TPU v7x, 32 devices: a whole 2x2x4 slice. The times are simulated.
32 devices in a mesh: cuts: 1, mode: 32 (over z, y, x, core).
Axes of the slice: x: 2, y: 2, z: 4, core: 2. Of those that a mesh axis runs over, the one named last changes fastest.
Arguments:
- branch_in: bfloat16 [4, 2, 2048, 1024], P(None, None, ('cuts', 'mode')), may hold values from -6 to 6
- column_order: int32 [4, 1024], replicated, may hold values from 0 to 1023, each once within a row
- gate_a: bfloat16 [2, 1024, 1024], P(None, 'mode'), may hold values from -0.125 to 0.125
- gate_b: bfloat16 [2, 1024, 1024], P(None, 'mode'), may hold values from -0.125 to 0.125
Outputs:
- joined: bfloat16 [2, 512, 2, 128], P(None, ('cuts', 'mode'))
Inputs may be any that keep to these rules, and one draw needn't show every extreme that they name: Each row of column_order names every column state once.
All inputs are finite; a program needn't handle non-finite values.
Results may differ from a plain program's by a relative error of at most 0.014.
Values may be sent and summed in bfloat16 or wider, within the bound.
No kernel may reach another device: no remote copies, remote signals or barrier semaphores. Data moves between devices by JAX's collectives and lax.ppermute only.
A program may use at most 128 MiB of HBM per device.

v0:
```python
import jax
import jax.numpy as jnp
from jax import lax
from jax.sharding import PartitionSpec as P

SHARED = 4096
KEPT = 4
CYCLES = 2


def partner(value, axis, bit):
    mask = 2**bit
    pairs = [(source, source ^ mask) for source in range(lax.axis_size(axis))]
    return lax.ppermute(value, axis, pairs)


def product_four(states, layer_block):
    branches, parts, row_count, width = states.shape
    real_in = states[:, 0].reshape(branches * row_count, width)
    imag_in = states[:, 1].reshape(branches * row_count, width)
    real_part = jnp.dot(real_in, layer_block[0], preferred_element_type=jnp.float32) - jnp.dot(
        imag_in, layer_block[1], preferred_element_type=jnp.float32
    )
    imag_part = jnp.dot(real_in, layer_block[1], preferred_element_type=jnp.float32) + jnp.dot(
        imag_in, layer_block[0], preferred_element_type=jnp.float32
    )
    joined_parts = jnp.stack(
        [
            real_part.reshape(branches, row_count, width),
            imag_part.reshape(branches, row_count, width),
        ],
        axis=1,
    )
    return joined_parts.astype(jnp.bfloat16)


def complex_rows(left_real, left_imag, right_real, right_imag):
    real_part = jnp.dot(left_real, right_real, preferred_element_type=jnp.float32) - jnp.dot(
        left_imag, right_imag, preferred_element_type=jnp.float32
    )
    imag_part = jnp.dot(left_real, right_imag, preferred_element_type=jnp.float32) + jnp.dot(
        left_imag, right_real, preferred_element_type=jnp.float32
    )
    return jnp.stack([real_part, imag_part], axis=1)


def read_bit(device_index, bit_number):
    return device_index // 2**bit_number % 2


def trade_axes(buffer, axis_bits, trader, device_index):
    for position, bit_number in enumerate(axis_bits):
        own_bit = read_bit(device_index, bit_number)
        kept_half = lax.dynamic_index_in_dim(buffer, own_bit, position, keepdims=False)
        sent_half = lax.dynamic_index_in_dim(buffer, 1 - own_bit, position, keepdims=False)
        received = trader(sent_half, bit_number)
        first_half = jnp.where(own_bit == 0, kept_half, received)
        second_half = jnp.where(own_bit == 0, received, kept_half)
        buffer = jnp.stack([first_half, second_half], axis=position)
    return buffer


def local(branch_in, column_order, gate_a, gate_b):
    join_scale = (2.0 * SHARED) ** (-0.5)
    devices_mode = lax.axis_size("mode")
    whole_a, whole_b = (
        lax.all_gather(gate_a, "mode", axis=1, tiled=True),
        lax.all_gather(gate_b, "mode", axis=1, tiled=True),
    )
    states = jnp.take_along_axis(branch_in, column_order[:, None, None, :], axis=3)
    for layer_number in range(2 * CYCLES):
        if layer_number > 0:
            states = lax.all_to_all(states, "mode", split_axis=3, concat_axis=3, tiled=True)
        states = product_four(states, whole_a if layer_number % 2 == 0 else whole_b)
    local_cells = states.shape[2] * states.shape[3]
    local_rows = local_cells // SHARED
    shared_rows = SHARED // devices_mode
    join_width = local_cells // (shared_rows * KEPT)
    results = []
    for pair_number in range(2):
        left_part = states[2 * pair_number].reshape(2, local_rows, SHARED)
        right_part = states[2 * pair_number + 1].reshape(2, shared_rows, KEPT, join_width)
        device_index = lax.axis_index("mode")
        total_bits = devices_mode.bit_length() - 1
        group_bits = total_bits - 4
        batch_bits = KEPT.bit_length() - 1
        groups = devices_mode // (4 * KEPT)
        span = 2 * shared_rows
        outer = SHARED // (span * groups)
        half_join = join_width // 2

        def left_trader(piece, bit_number):
            return partner(piece, "mode", bit_number)

        def right_trader(piece, bit_number):
            return partner(piece, "mode", bit_number)

        left_buffer = left_part.reshape(2, local_rows, outer, groups, span).transpose(3, 0, 1, 2, 4)
        left_buffer = left_buffer.reshape((2,) * group_bits + (1, 2, local_rows, outer, span))
        left_buffer = jnp.broadcast_to(
            left_buffer, (2,) * group_bits + (2, 2, local_rows, outer, span)
        )
        left_bits = [group_bits - position for position in range(group_bits)] + [0]
        left_buffer = trade_axes(left_buffer, left_bits, left_trader, device_index)
        left_block = left_buffer.reshape(devices_mode // (2 * KEPT), 2, local_rows, outer * span)
        left_block = left_block.transpose(1, 0, 2, 3).reshape(2, half_join, SHARED // groups)
        right_buffer = right_part.reshape(2, shared_rows, KEPT, 2, half_join).transpose(
            2, 3, 0, 1, 4
        )
        right_buffer = right_buffer.reshape((2,) * batch_bits + (1, 2, 2, shared_rows, half_join))
        right_buffer = jnp.broadcast_to(
            right_buffer, (2,) * batch_bits + (2, 2, 2, shared_rows, half_join)
        )
        right_bits = [total_bits - 1 - position for position in range(batch_bits)] + [
            total_bits - batch_bits - 1,
            0,
        ]
        right_buffer = trade_axes(right_buffer, right_bits, right_trader, device_index)
        right_block = right_buffer.reshape(2 * KEPT, 2, 2, shared_rows, half_join)
        right_block = right_block.transpose(2, 0, 1, 3, 4).reshape(2, SHARED // groups, half_join)
        running = complex_rows(left_block[0], left_block[1], right_block[0], right_block[1])
        for position in range(group_bits):
            bit_number = group_bits - position
            own_bit = read_bit(device_index, bit_number)
            row_count = running.shape[0]
            halves = running.reshape(2, row_count // 2, 2, half_join)
            kept_half = lax.dynamic_index_in_dim(halves, own_bit, 0, keepdims=False)
            sent_half = lax.dynamic_index_in_dim(halves, 1 - own_bit, 0, keepdims=False)
            running = kept_half + partner(
                sent_half.astype(jnp.bfloat16), "mode", bit_number
            ).astype(sent_half.dtype)
        rounded = (running * join_scale).astype(jnp.bfloat16)
        own_bit = read_bit(device_index, 0)
        halves = rounded.reshape(2, local_rows, 2, half_join)
        kept_half = lax.dynamic_index_in_dim(halves, own_bit, 0, keepdims=False)
        sent_half = lax.dynamic_index_in_dim(halves, 1 - own_bit, 0, keepdims=False)
        received = partner(sent_half, "mode", 0)
        first_half = jnp.where(own_bit == 0, kept_half, received)
        second_half = jnp.where(own_bit == 0, received, kept_half)
        finished = jnp.concatenate([first_half, second_half], axis=2)
        results.append(finished)
    return jnp.stack(results)


def solution(mesh):
    in_specs = (
        P(None, None, ("cuts", "mode"), None),
        P(),
        P(None, "mode", None),
        P(None, "mode", None),
    )
    out_specs = P(None, ("cuts", "mode"), None, None)
    return jax.shard_map(local, mesh=mesh, in_specs=in_specs, out_specs=out_specs, check_vma=False)
```

profile of v0, /device:TPU:0, one launch (start us, length us, event | category | flops | bytes accessed | tf_op | source)
XLA Modules:
  0.0 323.3 jit_solution(7350059804431820258)
XLA Ops:
  8.0 4.5 %copy.162 = bf16[4,2,64,1024]{2,1,3,0:T(2,128)(2,1)S(1)} copy(bf16[4,2,64,1024]{3,2,1,0:T(8,128)(2,1)} %param.4) | data formatting | bytes 2097152 | tf_op args[0]
  12.6 32.2 %gather_fusion = bf16[4096,2,64]{2,1,0:T(2,128)(2,1)} fusion(bf16[4,2,64,1024]{2,1,3,0:T(2,128)(2,1)S(1)} %copy.162, s32[4096]{0:T(1024)S(1)} %bitcast.334), kind=kCustom, calls=%fused_computation | custom fusion | bytes 2129920 | tf_op jit(solution)/shard_map/jit(take_along_axis)/gather | solution.py:70
  44.8 4.6 %copy.163 = bf16[4,1024,2,64]{1,3,0,2:T(8,128)(2,1)S(1)} copy(bf16[4,1024,2,64]{3,2,1,0:T(2,128)(2,1)} %bitcast.338) | data formatting | bytes 2097152 | tf_op jit(solution)/shard_map/jit(take_along_axis)/gather | solution.py:70
  49.7 25.2 %all-gather.3.cloned.1.call-done = bf16[2,1024,1024]{2,1,0:T(8,128)(2,1)} async-done(((bf16[2,32,1024]{2,1,0:T(8,128)(2,1)}), bf16[2,1024,1024]{2,1,0:T(8,128)(2,1)}) %all-gather.3.cloned.1.call-update) | async-done | bytes 4194320 | tf_op jit(solution)/shard_map/all_gather | solution.py:67
  77.2 2.3 fusion.8
  80.3 2.3 fusion.3
  82.6 2.3 fusion.9
  86.3 3.0 fusion.74
  90.8 35.0 %all_to_all.15 = bf16[32,2,8192]{2,1,0:T(2,128)(2,1)} all-to-all(bf16[32,2,8192]{2,1,0:T(2,128)(2,1)S(1)} %reshape.118), channel_id=1, replica_groups=mesh['cuts'=1,'mode'=32] {'mode'}, dimensions={0} | all-to-all | bytes 2097152 | tf_op jit(solution)/shard_map/all_to_all | solution.py:73
  125.8 4.5 %reshape.119 = bf16[1024,2,4,64]{3,2,1,0:T(4,128)(2,1)S(1)} reshape(bf16[32,2,8192]{2,1,0:T(2,128)(2,1)} %all_to_all.15) | data formatting | bytes 2097152
  134.1 8.4 %all-gather.5.cloned.1.call-done = bf16[2,1024,1024]{2,1,0:T(8,128)(2,1)} async-done(((bf16[2,32,1024]{2,1,0:T(8,128)(2,1)}), bf16[2,1024,1024]{2,1,0:T(8,128)(2,1)}) %all-gather.5.cloned.1.call-update) | async-done | bytes 4194320 | tf_op jit(solution)/shard_map/all_gather | solution.py:68
  144.8 2.3 fusion.10
  147.8 2.3 fusion.7
  150.2 2.3 fusion.11
  153.9 3.0 fusion.73
  158.3 29.5 %all_to_all.16 = bf16[32,2,8192]{2,1,0:T(2,128)(2,1)} all-to-all(bf16[32,2,8192]{2,1,0:T(2,128)(2,1)S(1)} %reshape.120), channel_id=1, replica_groups=mesh['cuts'=1,'mode'=32] {'mode'}, dimensions={0} | all-to-all | bytes 2097152 | tf_op jit(solution)/shard_map/all_to_all | solution.py:73
  187.8 4.5 %reshape.121 = bf16[1024,2,4,64]{3,2,1,0:T(4,128)(2,1)S(1)} reshape(bf16[32,2,8192]{2,1,0:T(2,128)(2,1)} %all_to_all.16) | data formatting | bytes 2097152
  196.2 2.3 fusion
  198.5 2.3 fusion.12
  201.6 2.3 fusion.2
  203.9 2.3 fusion.13
  207.6 3.0 fusion.72
  212.8 3.6 %all-to-all-start.2 = ((bf16[32,2,8192]{2,1,0:T(2,128)(2,1)}), bf16[32,2,8192]{2,1,0:T(2,128)(2,1)S(1)}, u32[]{:S(2)}, u32[]{:S(2)}) async-start(bf16[32,2,8192]{2,1,0:T(2,128)(2,1)} %reshape.122), calls=%async_computation.2 | async-start | bytes 2097152 | tf_op jit(solution)/shard_map/all_to_all | solution.py:73
  216.6 26.1 %all-to-all-done.2 = bf16[32,2,8192]{2,1,0:T(2,128)(2,1)S(1)} async-done(((bf16[32,2,8192]{2,1,0:T(2,128)(2,1)}), bf16[32,2,8192]{2,1,0:T(2,128)(2,1)S(1)}, u32[]{:S(2)}, u32[]{:S(2)}) %all-to-all-start.2) | async-done | bytes 1048608 | tf_op jit(solution)/shard_map/all_to_all | solution.py:73
  248.3 2.4 fusion.6
  250.7 2.3 fusion.4
  263.6 12.9 %collective-permute-done.2 = bf16[2,2,2,2,128,64]{4,5,3,2,1,0:T(8,128)(2,1)S(1)} collective-permute-done((bf16[2,2,2,2,128,64]{4,5,3,2,1,0:T(8,128)(2,1)S(1)}, bf16[2,2,2,2,128,64]{4,5,3,2,1,0:T(8,128)(2,1)S(1)}, u32[]{:S(2)}, u32[]{:S(2)}) %collective-permute-start.2) | collective-permute-done | bytes 262176 | tf_op jit(solution)/shard_map/ppermute | solution.py:14
  276.7 4.4 %collective-permute-done.10 = bf16[2,2,2,2,128,64]{4,5,3,2,1,0:T(8,128)(2,1)S(1)} collective-permute-done((bf16[2,2,2,2,128,64]{4,5,3,2,1,0:T(8,128)(2,1)S(1)}, bf16[2,2,2,2,128,64]{4,5,3,2,1,0:T(8,128)(2,1)S(1)}, u32[]{:S(2)}, u32[]{:S(2)}) %collective-permute-start.10) | collective-permute-done | bytes 262176 | tf_op jit(solution)/shard_map/ppermute | solution.py:14
  282.6 4.0 %collective-permute-done.3 = bf16[2,2,2,2,128,64]{4,5,3,2,1,0:T(8,128)(2,1)S(1)} collective-permute-done((bf16[2,2,2,2,128,64]{4,5,3,2,1,0:T(8,128)(2,1)S(1)}, bf16[2,2,2,2,128,64]{4,5,3,2,1,0:T(8,128)(2,1)S(1)}, u32[]{:S(2)}, u32[]{:S(2)}) %collective-permute-start.3) | collective-permute-done | bytes 262176 | tf_op jit(solution)/shard_map/ppermute | solution.py:14
  288.4 3.7 %collective-permute-done.11 = bf16[2,2,2,2,128,64]{4,5,3,2,1,0:T(8,128)(2,1)S(1)} collective-permute-done((bf16[2,2,2,2,128,64]{4,5,3,2,1,0:T(8,128)(2,1)S(1)}, bf16[2,2,2,2,128,64]{4,5,3,2,1,0:T(8,128)(2,1)S(1)}, u32[]{:S(2)}, u32[]{:S(2)}) %collective-permute-start.11) | collective-permute-done | bytes 262176 | tf_op jit(solution)/shard_map/ppermute | solution.py:14
  296.5 5.0 %collective-permute-done.12 = bf16[2,2,2,2,128,64]{4,5,3,2,1,0:T(8,128)(2,1)} collective-permute-done((bf16[2,2,2,2,128,64]{4,5,3,2,1,0:T(8,128)(2,1)S(1)}, bf16[2,2,2,2,128,64]{4,5,3,2,1,0:T(8,128)(2,1)}, u32[]{:S(2)}, u32[]{:S(2)}) %collective-permute-start.12) | collective-permute-done | bytes 262176 | tf_op jit(solution)/shard_map/ppermute | solution.py:14
  310.5 3.5 %collective-permute-done.14 = bf16[32,2,64]{2,0,1:T(8,128)(2,1)S(1)} collective-permute-done((bf16[32,2,64]{2,0,1:T(8,128)(2,1)S(1)}, bf16[32,2,64]{2,0,1:T(8,128)(2,1)S(1)}, u32[]{:S(2)}, u32[]{:S(2)}) %collective-permute-start.14) | collective-permute-done | bytes 8224 | tf_op jit(solution)/shard_map/ppermute | solution.py:14
  (145 shorter events, 60.1 us)
Async XLA Ops:
  6.5 6.0 %copy-start = (s32[4,1024]{1,0:T(4,128)S(1)}, s32[4,1024]{1,0:T(4,128)}, u32[]{:S(2)}) copy-start(s32[4,1024]{1,0:T(4,128)} %param.5) | copy-start | bytes 49156
  6.5 68.4 %all-gather.3.cloned.1.call-start = ((), (), s32[]{:S(2)}) async-start(), calls=%async_computation.3 | async-start | bytes 4325376 | tf_op jit(solution)/shard_map/all_gather | solution.py:67
  7.3 135.2 %all-gather.5.cloned.1.call-start = ((), (), s32[]{:S(2)}) async-start(), calls=%async_computation.4 | async-start | bytes 4325376 | tf_op jit(solution)/shard_map/all_gather | solution.py:68
  212.8 29.9 %all-to-all-start.2 = ((bf16[32,2,8192]{2,1,0:T(2,128)(2,1)}), bf16[32,2,8192]{2,1,0:T(2,128)(2,1)S(1)}, u32[]{:S(2)}, u32[]{:S(2)}) async-start(bf16[32,2,8192]{2,1,0:T(2,128)(2,1)} %reshape.122), calls=%async_computation.2 | async-start | bytes 2097152 | tf_op jit(solution)/shard_map/all_to_all | solution.py:73
  248.2 4.8 %copy-start.1 = (bf16[2,1024,1024]{2,1,0:T(8,128)(2,1)S(1)}, bf16[2,1024,1024]{2,1,0:T(8,128)(2,1)}, u32[]{:S(2)}) copy-start(bf16[2,1024,1024]{2,1,0:T(8,128)(2,1)} %all-gather.5.cloned.1.call-done) | copy-start | bytes 12582916
  255.5 21.0 %collective-permute-start.2 = (bf16[2,2,2,2,128,64]{4,5,3,2,1,0:T(8,128)(2,1)S(1)}, bf16[2,2,2,2,128,64]{4,5,3,2,1,0:T(8,128)(2,1)S(1)}, u32[]{:S(2)}, u32[]{:S(2)}) collective-permute-start(bf16[2,2,2,2,128,64]{4,5,3,2,1,0:T(8,128)(2,1)S(1)} %broadcast_in_dim.67), channel_id=1, source_target_pairs={{0,16},{1,17},{2,18},{3,19},{4,20},{5,21},{6,22},{7,23},{8,24},{9,... | collective-permute-start | bytes 786440 | tf_op jit(solution)/shard_map/ppermute | solution.py:14
  257.4 23.6 %collective-permute-start.10 = (bf16[2,2,2,2,128,64]{4,5,3,2,1,0:T(8,128)(2,1)S(1)}, bf16[2,2,2,2,128,64]{4,5,3,2,1,0:T(8,128)(2,1)S(1)}, u32[]{:S(2)}, u32[]{:S(2)}) collective-permute-start(bf16[2,2,2,2,128,64]{4,5,3,2,1,0:T(8,128)(2,1)S(1)} %broadcast_in_dim.76), channel_id=1, source_target_pairs={{0,16},{1,17},{2,18},{3,19},{4,20},{5,21},{6,22},{7,23},{8,24},{9,... | collective-permute-start | bytes 786440 | tf_op jit(solution)/shard_map/ppermute | solution.py:14
  260.6 20.5 %collective-permute-start = (bf16[2,2,16,8,256]{4,3,2,1,0:T(8,128)(2,1)S(1)}, bf16[2,2,16,8,256]{4,3,2,1,0:T(8,128)(2,1)S(1)}, u32[]{:S(2)}, u32[]{:S(2)}) collective-permute-start(bf16[2,2,16,8,256]{4,3,2,1,0:T(8,128)(2,1)S(1)} %broadcast_in_dim.62), channel_id=1, source_target_pairs={{0,2},{1,3},{2,0},{3,1},{4,6},{5,7},{6,4},{7,5},{8,10},{9,11},{10,... | collective-permute-start | bytes 786440 | tf_op jit(solution)/shard_map/ppermute | solution.py:14
  263.0 18.4 %collective-permute-start.8 = (bf16[2,2,16,8,256]{4,3,2,1,0:T(8,128)(2,1)S(1)}, bf16[2,2,16,8,256]{4,3,2,1,0:T(8,128)(2,1)S(1)}, u32[]{:S(2)}, u32[]{:S(2)}) collective-permute-start(bf16[2,2,16,8,256]{4,3,2,1,0:T(8,128)(2,1)S(1)} %broadcast_in_dim.71), channel_id=1, source_target_pairs={{0,2},{1,3},{2,0},{3,1},{4,6},{5,7},{6,4},{7,5},{8,10},{9,11},{10,... | collective-permute-start | bytes 786440 | tf_op jit(solution)/shard_map/ppermute | solution.py:14
  276.6 10.0 %collective-permute-start.3 = (bf16[2,2,2,2,128,64]{4,5,3,2,1,0:T(8,128)(2,1)S(1)}, bf16[2,2,2,2,128,64]{4,5,3,2,1,0:T(8,128)(2,1)S(1)}, u32[]{:S(2)}, u32[]{:S(2)}) collective-permute-start(bf16[2,2,2,2,128,64]{4,5,3,2,1,0:T(8,128)(2,1)S(1)} %fusion.35), channel_id=1, source_target_pairs={{0,8},{1,9},{2,10},{3,11},{4,12},{5,13},{6,14},{7,15},{8,0},{9,1},... | collective-permute-start | bytes 786440 | tf_op jit(solution)/shard_map/ppermute | solution.py:14
  281.1 11.0 %collective-permute-start.11 = (bf16[2,2,2,2,128,64]{4,5,3,2,1,0:T(8,128)(2,1)S(1)}, bf16[2,2,2,2,128,64]{4,5,3,2,1,0:T(8,128)(2,1)S(1)}, u32[]{:S(2)}, u32[]{:S(2)}) collective-permute-start(bf16[2,2,2,2,128,64]{4,5,3,2,1,0:T(8,128)(2,1)S(1)} %fusion.21), channel_id=1, source_target_pairs={{0,8},{1,9},{2,10},{3,11},{4,12},{5,13},{6,14},{7,15},{8,0},{9,1},... | collective-permute-start | bytes 786440 | tf_op jit(solution)/shard_map/ppermute | solution.py:14
  281.3 12.1 %collective-permute-start.1 = (bf16[2,2,16,8,256]{4,3,2,1,0:T(8,128)(2,1)S(1)}, bf16[2,2,16,8,256]{4,3,2,1,0:T(8,128)(2,1)S(1)}, u32[]{:S(2)}, u32[]{:S(2)}) collective-permute-start(bf16[2,2,16,8,256]{4,3,2,1,0:T(8,128)(2,1)S(1)} %fusion.39), channel_id=1, source_target_pairs={{0,1},{1,0},{2,3},{3,2},{4,5},{5,4},{6,7},{7,6},{8,9},{9,8},{10,11... | collective-permute-start | bytes 786440 | tf_op jit(solution)/shard_map/ppermute | solution.py:14
  282.2 11.7 %collective-permute-start.9 = (bf16[2,2,16,8,256]{4,3,2,1,0:T(8,128)(2,1)}, bf16[2,2,16,8,256]{4,3,2,1,0:T(8,128)(2,1)}, u32[]{:S(2)}, u32[]{:S(2)}) collective-permute-start(bf16[2,2,16,8,256]{4,3,2,1,0:T(8,128)(2,1)} %fusion.25), channel_id=1, source_target_pairs={{0,1},{1,0},{2,3},{3,2},{4,5},{5,4},{6,7},{7,6},{8,9},{9,8},{10,11... | collective-permute-start | bytes 786440 | tf_op jit(solution)/shard_map/ppermute | solution.py:14
  287.4 9.1 %collective-permute-start.4 = (bf16[2,2,2,2,128,64]{4,5,3,2,1,0:T(8,128)(2,1)}, bf16[2,2,2,2,128,64]{4,5,3,2,1,0:T(8,128)(2,1)S(1)}, u32[]{:S(2)}, u32[]{:S(2)}) collective-permute-start(bf16[2,2,2,2,128,64]{4,5,3,2,1,0:T(8,128)(2,1)} %fusion.31), channel_id=1, source_target_pairs={{0,4},{1,5},{2,6},{3,7},{4,0},{5,1},{6,2},{7,3},{8,12},{9,13},{10,... | collective-permute-start | bytes 786440 | tf_op jit(solution)/shard_map/ppermute | solution.py:14
  292.3 9.2 %collective-permute-start.12 = (bf16[2,2,2,2,128,64]{4,5,3,2,1,0:T(8,128)(2,1)S(1)}, bf16[2,2,2,2,128,64]{4,5,3,2,1,0:T(8,128)(2,1)}, u32[]{:S(2)}, u32[]{:S(2)}) collective-permute-start(bf16[2,2,2,2,128,64]{4,5,3,2,1,0:T(8,128)(2,1)S(1)} %bitcast.395), channel_id=1, source_target_pairs={{0,4},{1,5},{2,6},{3,7},{4,0},{5,1},{6,2},{7,3},{8,12},{9,13},{10,... | collective-permute-start | bytes 786440 | tf_op jit(solution)/shard_map/ppermute | solution.py:14
  302.6 1.6 collective-permute-start.5
  302.7 5.5 %collective-permute-start.13 = (bf16[2,2,2,2,128,64]{4,5,3,2,1,0:T(8,128)(2,1)S(1)}, bf16[2,2,2,2,128,64]{4,5,3,2,1,0:T(8,128)(2,1)S(1)}, u32[]{:S(2)}, u32[]{:S(2)}) collective-permute-start(bf16[2,2,2,2,128,64]{4,5,3,2,1,0:T(8,128)(2,1)S(1)} %bitcast.396), channel_id=1, source_target_pairs={{0,1},{1,0},{2,3},{3,2},{4,5},{5,4},{6,7},{7,6},{8,9},{9,8},{10,11... | collective-permute-start | bytes 786440 | tf_op jit(solution)/shard_map/ppermute | solution.py:14
  306.2 4.1 %collective-permute-start.6 = (bf16[32,2,64]{2,0,1:T(8,128)(2,1)S(1)}, bf16[32,2,64]{2,0,1:T(8,128)(2,1)S(1)}, u32[]{:S(2)}, u32[]{:S(2)}) collective-permute-start(bf16[32,2,64]{2,0,1:T(8,128)(2,1)S(1)} %fusion.61), channel_id=1, source_target_pairs={{0,2},{1,3},{2,0},{3,1},{4,6},{5,7},{6,4},{7,5},{8,10},{9,11},{10,... | collective-permute-start | bytes 24584 | tf_op jit(solution)/shard_map/ppermute | solution.py:14
  310.2 3.8 %collective-permute-start.14 = (bf16[32,2,64]{2,0,1:T(8,128)(2,1)S(1)}, bf16[32,2,64]{2,0,1:T(8,128)(2,1)S(1)}, u32[]{:S(2)}, u32[]{:S(2)}) collective-permute-start(bf16[32,2,64]{2,0,1:T(8,128)(2,1)S(1)} %fusion.62), channel_id=1, source_target_pairs={{0,2},{1,3},{2,0},{3,1},{4,6},{5,7},{6,4},{7,5},{8,10},{9,11},{10,... | collective-permute-start | bytes 24584 | tf_op jit(solution)/shard_map/ppermute | solution.py:14
  310.4 3.7 %collective-permute-start.7 = (bf16[16,2,64]{2,1,0:T(2,128)(2,1)S(1)}, bf16[16,2,64]{2,1,0:T(2,128)(2,1)S(1)}, u32[]{:S(2)}, u32[]{:S(2)}) collective-permute-start(bf16[16,2,64]{2,1,0:T(2,128)(2,1)S(1)} %bitcast.400), channel_id=1, source_target_pairs={{0,1},{1,0},{2,3},{3,2},{4,5},{5,4},{6,7},{7,6},{8,9},{9,8},{10,11... | collective-permute-start | bytes 12296 | tf_op jit(solution)/shard_map/ppermute | solution.py:14
  314.0 1.2 collective-permute-start.15
Sparse Core Ops, SparseCore 0:
  10.3 64.5 all-gather.2
  77.8 64.6 all-gather.4
where the time goes:
time: 329 us; the launch traced here: 323 us
  waiting for transfers between devices  97.6 us (30%)
  local copies, waits for them, and re-layouts  81.6 us (25%)
  blocking collectives  64.5 us (20%)
  matrix products  35.6 us (11%)
  between operations  14.9 us (5%)
  starting transfers between devices  14.7 us (4%)
  other arithmetic  14.4 us (4%)
    all_to_all x2, blocking collectives, local(): lax.all_to_all(states, 'mode', split_axis=3, concat_axis=3, tiled=True)  64.5 us
    gather x2, local copies, waits for them, and re-layouts, local(): jnp.take_along_axis(branch_in, column_order[:, None, None, :], axis=3)  36.9 us
    ppermute x16, waiting for transfers between devices, partner(): return lax.ppermute(value, axis, pairs)  36.6 us
    unnamed x28, local copies, waits for them, and re-layouts  27.6 us
    all_to_all x1, waiting for transfers between devices, local(): lax.all_to_all(states, 'mode', split_axis=3, concat_axis=3, tiled=True)  26.1 us
    all_gather x1, waiting for transfers between devices, local(): lax.all_gather(gate_a, 'mode', axis=1, tiled=True)  25.2 us
    ppermute x16, starting transfers between devices, partner(): return lax.ppermute(value, axis, pairs)  11 us
    dot_general x4, matrix products, product_four(): jnp.dot(real_in, layer_block[1], preferred_element_type=jnp.float32)  9.34 us
  transfers between devices with their start and end apart: 19, of which 12 were waited for; matrix products, arithmetic and copies ran while one was open for 24% of the time, Pallas kernels for 0%

commit v1 on v0

--- a/solution.py
+++ b/solution.py
@@ -1,11 +1,238 @@
+import functools
+
 import jax
 import jax.numpy as jnp
 from jax import lax
+from jax.experimental import pallas as pl
+from jax.experimental.pallas import tpu as pltpu
 from jax.sharding import PartitionSpec as P
 
 SHARED = 4096
 KEPT = 4
 CYCLES = 2
+LANES = 128
+VMEM_LIMIT = 56 * 1024 * 1024
+
+
+def whole(count):
+    return [pl.BlockSpec(memory_space=pltpu.VMEM)] * count
+
+
+def one_hot(shape, axis, wanted):
+    return (lax.broadcasted_iota(jnp.int32, shape, axis) == wanted).astype(jnp.bfloat16)
+
+
+def exact_dot(left, right):
+    return jnp.dot(left, right, preferred_element_type=jnp.float32)
+
+
+def order_kernel(order_ref, x_ref, o_ref):
+    width = x_ref.shape[1]
+    step = min(256, width)
+    for start in range(0, width, step):
+        picks = one_hot((width, step), 0, order_ref[:, start : start + step])
+        o_ref[:, start : start + step] = exact_dot(x_ref[...], picks).astype(jnp.bfloat16)
+
+
+def swap_sign(tiles, qs):
+    turned = pltpu.roll(tiles, qs, 1)
+    row = lax.broadcasted_iota(jnp.int32, tiles.shape, 1)
+    return jnp.where(row < qs, -turned, turned)
+
+
+def regroup_store(acc, first_lane, group, devices, tile_rows, x_ref, h_ref):
+    per = LANES // group
+    lane = lax.broadcasted_iota(jnp.int32, (tile_rows, LANES), 1) // group
+    for offset in range(0, acc.shape[1], LANES):
+        tile = acc[:, offset : offset + LANES].reshape(devices, tile_rows, LANES)
+        row_start = (first_lane + offset) // group * tile_rows
+        for block in range(devices // per):
+            parts = [tile[block * per + m] for m in range(per)]
+            bit = 1
+            while bit < per:
+                moved = list(parts)
+                keep = (lane // bit) % 2 == 0
+                for m in range(per):
+                    if m & bit:
+                        continue
+                    low, high = parts[m], parts[m | bit]
+                    moved[m] = jnp.where(keep, low, pltpu.roll(high, bit * group, 1))
+                    moved[m | bit] = jnp.where(keep, pltpu.roll(low, LANES - bit * group, 1), high)
+                parts = moved
+                bit *= 2
+            tiles = jnp.stack(parts)
+            rows = pl.ds(row_start, per * tile_rows)
+            lanes = pl.ds(block * LANES, LANES)
+            x_ref[rows, lanes] = tiles.reshape(per * tile_rows, LANES).astype(jnp.bfloat16)
+            turned = swap_sign(tiles, tile_rows // 2)
+            h_ref[rows, lanes] = turned.reshape(per * tile_rows, LANES).astype(jnp.bfloat16)
+
+
+def layers_kernel(sizes, is_left, x_ref, a_ref, b_ref, o_ref, xs, hs, last):
+    devices, qs, group, rows_each = sizes
+    tile_rows = 2 * qs
+    rows, width = x_ref.shape
+    first = x_ref[...].astype(jnp.float32).reshape(devices, tile_rows, width)
+    hs[0] = swap_sign(first, qs).reshape(rows, width).astype(jnp.bfloat16)
+    step = 256
+    for layer in range(2 * CYCLES):
+        gate = a_ref if layer % 2 == 0 else b_ref
+        here = x_ref if layer == 0 else xs.at[layer % 2]
+        turned = hs.at[layer % 2]
+        later = (layer + 1) % 2
+        for start in range(0, width, step):
+            cols = slice(start, start + step)
+            acc = exact_dot(here[...], gate[0, :, cols]) + exact_dot(turned[...], gate[1, :, cols])
+            if layer < 2 * CYCLES - 1:
+                regroup_store(acc, start, group, devices, tile_rows, xs.at[later], hs.at[later])
+            else:
+                last[:, cols] = acc.astype(jnp.bfloat16)
+    half = rows // 2
+    new = lax.broadcasted_iota(jnp.int32, (rows, rows), 0)
+    part, inner = new // half, new % half
+    if is_left:
+        v, r = inner // devices, inner % devices
+        picks = one_hot((rows, rows), 1, r * tile_rows + part * qs + v)
+        moved = exact_dot(picks, last[...]).astype(jnp.bfloat16)
+        span = 2 * rows_each
+        each = width * qs // rows_each
+        words = width // span
+        for start in range(0, width, step):
+            place = start + lax.broadcasted_iota(jnp.int32, (width, step), 1)
+            e, rest = place // each, place % each
+            h, w, qr = rest // (words * qs), rest % (words * qs) // qs, rest % qs
+            lanes = one_hot((width, step), 0, w * span + (e * qs + qr) * 2 + h)
+            sent = exact_dot(moved, lanes)
+            low_lane = lax.broadcasted_iota(jnp.int32, (half, LANES), 1) < LANES // 2
+            for offset in range(0, step, LANES):
+                real = sent[:half, offset : offset + LANES]
+                imag = sent[half:, offset : offset + LANES]
+                e0 = (start + offset) // each
+                even = jnp.where(low_lane, real, pltpu.roll(imag, LANES // 2, 1))
+                odd = jnp.where(low_lane, pltpu.roll(real, LANES // 2, 1), imag)
+                o_ref[e0 * half : (e0 + 1) * half, :] = even.astype(jnp.bfloat16)
+                o_ref[(e0 + 1) * half : (e0 + 2) * half, :] = odd.astype(jnp.bfloat16)
+    else:
+        r, q = inner // qs, inner % qs
+        picks = one_hot((rows, rows), 1, r * tile_rows + part * qs + q)
+        o_ref[...] = exact_dot(picks, last[...]).astype(jnp.bfloat16)
+
+
+def join_kernel(sizes, left_ref, right_ref, o_ref):
+    devices, us, vs = sizes
+    rows = us * devices
+    free = right_ref.shape[1] // (2 * KEPT)
+    left = left_ref[...].reshape(us, vs, devices, LANES)
+    left = jnp.concatenate([left[:, v].reshape(rows, LANES) for v in range(vs)], axis=1)
+    new = lax.broadcasted_iota(jnp.int32, (rows, rows), 0)
+    picks = one_hot((rows, rows), 1, new % us * devices + new // us)
+    left = exact_dot(picks, left).astype(jnp.bfloat16)
+    half = right_ref.shape[0] // 2
+    depth = half // vs
+    real, imag = right_ref[:half, :], right_ref[half:, :]
+    block = rows // KEPT
+    for g in range(KEPT):
+        stack = []
+        for v in range(vs):
+            r = [real[v * depth : (v + 1) * depth, (h * KEPT + g) * free :][:, :free] for h in range(2)]
+            i = [imag[v * depth : (v + 1) * depth, (h * KEPT + g) * free :][:, :free] for h in range(2)]
+            to_real = jnp.concatenate([r[0], r[1], -i[0], -i[1]], axis=0)
+            to_imag = jnp.concatenate([i[0], i[1], r[0], r[1]], axis=0)
+            stack.append(jnp.concatenate([to_real, to_imag], axis=1))
+        stack = jnp.concatenate(stack, axis=0)
+        part = exact_dot(left[g * block : (g + 1) * block, :], stack)
+        o_ref[g * block : (g + 1) * block, :] = part.astype(jnp.bfloat16)
+
+
+def call(kernel, out_shape, inputs, scratch=(), flops=0):
+    moved = sum(x.size * x.dtype.itemsize for x in inputs)
+    return pl.pallas_call(
+        kernel,
+        out_shape=jax.ShapeDtypeStruct(out_shape, jnp.bfloat16),
+        in_specs=whole(len(inputs)),
+        out_specs=whole(1)[0],
+        scratch_shapes=list(scratch),
+        compiler_params=pltpu.CompilerParams(vmem_limit_bytes=VMEM_LIMIT),
+        cost_estimate=pl.CostEstimate(flops=flops, bytes_accessed=moved, transcendentals=0),
+    )(*inputs)
+
+
+def tiles_fit(devices, rows_each, width):
+    pair_devices = devices // 2
+    if devices < 4 or devices & (devices - 1) or rows_each % pair_devices or width % 256:
+        return False
+    qs, group = rows_each // pair_devices, width // devices
+    return (
+        2 * qs == 8
+        and LANES % group == 0
+        and devices % (LANES // group) == 0
+        and qs == SHARED // width
+        and devices % 32 == 0
+        and 2 * width * qs // rows_each == LANES
+        and devices * rows_each * width // SHARED % (KEPT * LANES) == 0
+        and 2 * (devices * rows_each * width // SHARED) == width
+    )
+
+
+def fast(branch_in, column_order, gate_a, gate_b):
+    devices = lax.axis_size("mode")
+    me = lax.axis_index("mode")
+    rows_each, width = branch_in.shape[2:]
+    halves = devices // 2
+    qs, group = rows_each // halves, width // devices
+    tile_rows = 2 * qs
+    rows = devices * tile_rows
+    pair = me // halves
+    whole_a, whole_b = gather_gates(gate_a, gate_b)
+    cut = branch_in.reshape(2, 2, 2, halves, qs, width).transpose(1, 0, 3, 2, 4, 5)
+    cut = cut.reshape(2, devices, tile_rows, width)
+    states = []
+    for side in range(2):
+        got = lax.all_to_all(cut[side], "mode", split_axis=0, concat_axis=0, tiled=True)
+        order = lax.dynamic_slice_in_dim(column_order, 2 * pair + side, 1, 0)
+        states.append(
+            call(order_kernel, (rows, width), (order, got.reshape(rows, width)), flops=2 * rows * width * width)
+        )
+    sizes = (devices, qs, group, rows_each)
+    scratch = [pltpu.VMEM((2, rows, width), jnp.bfloat16)] * 2 + [pltpu.VMEM((rows, width), jnp.bfloat16)]
+    work = 2 * CYCLES * 4 * rows * width * width
+    left = call(
+        functools.partial(layers_kernel, sizes, True),
+        (halves * rows // 2, LANES),
+        (states[0], whole_a, whole_b),
+        scratch,
+        work,
+    )
+    groups = [[h * halves + e for e in range(halves)] for h in range(2)]
+    left = lax.all_to_all(
+        left.reshape(halves, rows // 2, LANES),
+        "mode",
+        split_axis=0,
+        concat_axis=0,
+        axis_index_groups=groups,
+        tiled=True,
+    )
+    right = call(
+        functools.partial(layers_kernel, sizes, False), (rows, width), (states[1], whole_a, whole_b), scratch, work
+    )
+    free = width // (2 * KEPT)
+    us = halves
+    partial_sums = call(
+        functools.partial(join_kernel, (devices, us, qs)),
+        (devices * us, 2 * free),
+        (left.reshape(halves * rows // 2, LANES), right),
+        flops=2 * devices * us * LANES * qs * 2 * free,
+    )
+    parts = lax.all_to_all(
+        partial_sums.reshape(devices, us, 2 * free), "mode", split_axis=0, concat_axis=0, tiled=True
+    )
+    parts = parts.reshape(2, halves, us, 2 * free).astype(jnp.float32)
+    join_scale = (2.0 * SHARED) ** (-0.5)
+    return (jnp.sum(parts, axis=1) * join_scale).astype(jnp.bfloat16).reshape(2, us, 2, free)
+
+
+def gather_gates(gate_a, gate_b):
+    return [lax.all_gather(gate, "mode", axis=1, tiled=True) for gate in (gate_a, gate_b)]
 
 
 def partner(value, axis, bit):
@@ -60,7 +287,7 @@
     return buffer
 
 
-def local(branch_in, column_order, gate_a, gate_b):
+def general(branch_in, column_order, gate_a, gate_b):
     join_scale = (2.0 * SHARED) ** (-0.5)
     devices_mode = lax.axis_size("mode")
     whole_a, whole_b = (
@@ -142,6 +369,13 @@
     return jnp.stack(results)
 
 
+def local(branch_in, column_order, gate_a, gate_b):
+    branches, _, rows_each, width = branch_in.shape
+    if branches == 4 and tiles_fit(lax.axis_size("mode"), rows_each, width):
+        return fast(branch_in, column_order, gate_a, gate_b)
+    return general(branch_in, column_order, gate_a, gate_b)
+
+
 def solution(mesh):
     in_specs = (
         P(None, None, ("cuts", "mode"), None),

time: 329 us -> 199 us (0.60); the launches traced: 323 us -> 199 us
  local copies, waits for them, and re-layouts: 81.6 us -> 6.36 us
  blocking collectives: 64.5 us -> 15.5 us
  matrix products: 35.6 us -> 0 us
  Pallas kernels: 0 us -> 28.9 us
  waiting for transfers between devices: 97.6 us -> 120 us
  other arithmetic: 14.4 us -> 0.05 us
    all_gather x2, waiting for transfers between devices: 33.6 us -> 102 us  [gather_gates(): lax.all_gather(gate, 'mode', axis=1, tiled=True)]
    all_to_all x2 -> x1, blocking collectives: 64.5 us -> 15.5 us  [fast(): lax.all_to_all(partial_sums.reshape(devices, us, 2 * free), 'mode', split...]
    gather x2 -> x0, local copies, waits for them, and re-layouts: 36.9 us -> none  [local(): jnp.take_along_axis(branch_in, column_order[:, None, None, :], axis=3)]
    ppermute x16 -> x0, waiting for transfers between devices: 36.6 us -> none  [partner(): return lax.ppermute(value, axis, pairs)]
    dot_general x24 -> x0, matrix products: 35.6 us -> none  [the longest x4 9.34 us: product_four(): jnp.dot(real_in, layer_block[1], preferred_element_type=jnp.float32)]
    pallas_call x0 -> x5, Pallas kernels: none -> 28.9 us  [call(): pl.pallas_call(kernel, out_shape=jax.ShapeDtypeStruct(out_shape, jnp.bflo...]
    unnamed x28 -> x8, local copies, waits for them, and re-layouts: 27.6 us -> 0.8 us
    ppermute x16 -> x0, starting transfers between devices: 11 us -> none  [partner(): return lax.ppermute(value, axis, pairs)]
  transfers between devices with their start and end apart: 19 -> 5, of which waited for: 12 -> 3; matrix products, arithmetic and copies ran while one was open for 24% -> 2% of each run, Pallas kernels for 0% -> 13%
where the time goes in v1:
time: 199 us
  waiting for transfers between devices  120 us (60%)
  Pallas kernels  28.9 us (15%)
  blocking collectives  15.5 us (8%)
  starting transfers between devices  14.2 us (7%)
  between operations  13.5 us (7%)
  local copies, waits for them, and re-layouts  6.36 us (3%)
    all_gather x2, waiting for transfers between devices, gather_gates(): lax.all_gather(gate, 'mode', axis=1, tiled=True)  102 us
    pallas_call x5, Pallas kernels, call(): pl.pallas_call(kernel, out_shape=jax.ShapeDtypeStruct(out_shape, jnp.bflo...  28.9 us
    all_to_all x2, waiting for transfers between devices, fast(): lax.all_to_all(cut[side], 'mode', split_axis=0, concat_axis=0, tiled=True)  17.1 us
    all_to_all x1, blocking collectives, fast(): lax.all_to_all(partial_sums.reshape(devices, us, 2 * free), 'mode', split...  15.5 us
    all_to_all x2, starting transfers between devices, fast(): lax.all_to_all(cut[side], 'mode', split_axis=0, concat_axis=0, tiled=True)  10.4 us
  transfers between devices with their start and end apart: 5, of which 3 were waited for; matrix products, arithmetic and copies ran while one was open for 2% of the time, Pallas kernels for 13%

profile of v1, /device:TPU:0, one launch (start us, length us, event | category | flops | bytes accessed | tf_op | source)
XLA Modules:
  0.0 198.7 jit_solution(14126119788964164489)
XLA Ops:
  6.5 0.0 all-gather.3.cloned.1.call-start
  6.5 0.7 all-gather.3.cloned.1.call-update
  7.3 0.0 all-gather.5.cloned.1.call-start
  7.3 0.7 all-gather.5.cloned.1.call-update
  8.0 1.5 reshape.31
  9.5 0.0 copy-start.3
  9.5 0.4 fusion
  9.9 0.3 copy.5
  10.2 1.0 squeeze.6
  11.2 7.3 %all-to-all-start = ((bf16[32,8,1024]{2,1,0:T(8,128)(2,1)}), bf16[32,8,1024]{2,1,0:T(8,128)(2,1)S(1)}, u32[]{:S(2)}, u32[]{:S(2)}) async-start(bf16[32,8,1024]{2,1,0:T(8,128)(2,1)} %squeeze.6), calls=%async_computation | async-start | bytes 1048576 | tf_op jit(solution)/shard_map/all_to_all | solution.py:191
  18.5 0.3 copy.6
  18.7 0.9 squeeze.7
  19.7 17.1 %all-to-all-done = bf16[32,8,1024]{2,1,0:T(8,128)(2,1)S(1)} async-done(((bf16[32,8,1024]{2,1,0:T(8,128)(2,1)}), bf16[32,8,1024]{2,1,0:T(8,128)(2,1)S(1)}, u32[]{:S(2)}, u32[]{:S(2)}) %all-to-all-start) | async-done | bytes 524320 | tf_op jit(solution)/shard_map/all_to_all | solution.py:191
  36.8 0.0 copy-start.2
  36.8 3.1 %all-to-all-start.2 = ((bf16[32,8,1024]{2,1,0:T(8,128)(2,1)}), bf16[32,8,1024]{2,1,0:T(8,128)(2,1)S(1)}, u32[]{:S(2)}, u32[]{:S(2)}) async-start(bf16[32,8,1024]{2,1,0:T(8,128)(2,1)} %squeeze.7), calls=%async_computation.2 | async-start | bytes 1048576 | tf_op jit(solution)/shard_map/all_to_all | solution.py:191
  39.9 0.0 copy-done.3
  39.9 0.6 constant_dynamic-slice_fusion
  40.5 0.0 copy-done.2
  40.5 2.6 %shard_map.46.x_ref = bf16[256,1024]{1,0:T(8,128)(2,1)} custom-call(s32[1,1024]{1,0:T(1,128)} %get-tuple-element.8.order_ref, bf16[256,1024]{1,0:T(8,128)(2,1)} %bitcast.15), custom_call_target="tpu_custom_call" | custom-call | flops 536870912 | bytes 528384 | tf_op jit(solution)/shard_map/pallas_call | solution.py:149
  43.1 38.3 %all-gather.3.cloned.1.call-done.a_ref = bf16[2,1024,1024]{2,1,0:T(8,128)(2,1)} async-done(((bf16[2,32,1024]{2,1,0:T(8,128)(2,1)}), bf16[2,1024,1024]{2,1,0:T(8,128)(2,1)}) %all-gather.3.cloned.1.call-update) | async-done | bytes 4194320 | tf_op jit(solution)/shard_map/all_gather | solution.py:235
  81.4 63.4 %all-gather.5.cloned.1.call-done.b_ref = bf16[2,1024,1024]{2,1,0:T(8,128)(2,1)} async-done(((bf16[2,32,1024]{2,1,0:T(8,128)(2,1)}), bf16[2,1024,1024]{2,1,0:T(8,128)(2,1)}) %all-gather.5.cloned.1.call-update) | async-done | bytes 4194320 | tf_op jit(solution)/shard_map/all_gather | solution.py:235
  144.8 11.0 %shard_map.47 = bf16[2048,128]{1,0:T(8,128)(2,1)} custom-call(bf16[256,1024]{1,0:T(8,128)(2,1)} %shard_map.46.x_ref, bf16[2,1024,1024]{2,1,0:T(8,128)(2,1)} %all-gather.3.cloned.1.call-done.a_ref, bf16[2,1024,1024]{2,1,0:T(8,128)(2,1)} %all-gather.5.cloned.1.call-done.b_ref), custom_call_target="tpu_custom_call" | custom-call | flops 4294967296 | bytes 8912896 | tf_op jit(solution)/shard_map/pallas_call | solution.py:149
  155.8 0.0 all-to-all-done.2
  155.8 3.8 %all-to-all-start.1 = ((bf16[16,128,128]{2,1,0:T(8,128)(2,1)}), bf16[16,128,128]{2,1,0:T(8,128)(2,1)S(1)}, u32[]{:S(2)}, u32[]{:S(2)}) async-start(bf16[16,128,128]{2,1,0:T(8,128)(2,1)} %bitcast.16), calls=%async_computation.1 | async-start | bytes 1048576 | tf_op jit(solution)/shard_map/all_to_all | solution.py:207
  159.6 0.0 copy-done.1
  159.6 2.6 %shard_map.48.x_ref = bf16[256,1024]{1,0:T(8,128)(2,1)} custom-call(s32[1,1024]{1,0:T(1,128)} %get-tuple-element.7.order_ref, bf16[256,1024]{1,0:T(8,128)(2,1)} %bitcast.14), custom_call_target="tpu_custom_call" | custom-call | flops 536870912 | bytes 528384 | tf_op jit(solution)/shard_map/pallas_call | solution.py:149
  162.2 10.2 %shard_map.49.right_ref = bf16[256,1024]{1,0:T(8,128)(2,1)} custom-call(bf16[256,1024]{1,0:T(8,128)(2,1)} %shard_map.48.x_ref, bf16[2,1024,1024]{2,1,0:T(8,128)(2,1)} %all-gather.3.cloned.1.call-done.a_ref, bf16[2,1024,1024]{2,1,0:T(8,128)(2,1)} %all-gather.5.cloned.1.call-done.b_ref), custom_call_target="tpu_custom_call" | custom-call | flops 4294967296 | bytes 8912896 | tf_op jit(solution)/shard_map/pallas_call | solution.py:149
  172.4 0.0 all-to-all-done.1
  172.4 0.8 copy-done
  173.2 2.5 %shard_map.50 = bf16[512,256]{1,0:T(8,128)(2,1)} custom-call(bf16[2048,128]{1,0:T(8,128)(2,1)} %bitcast.12, bf16[256,1024]{1,0:T(8,128)(2,1)} %shard_map.49.right_ref), custom_call_target="tpu_custom_call" | custom-call | flops 134217728 | bytes 1048576 | tf_op jit(solution)/shard_map/pallas_call | solution.py:149
  175.7 15.5 %all_to_all.20 = bf16[32,16,256]{2,1,0:T(8,128)(2,1)S(1)} all-to-all(bf16[32,16,256]{2,1,0:T(8,128)(2,1)} %bitcast.13), channel_id=1, replica_groups=mesh['cuts'=1,'mode'=32] {'mode'}, dimensions={0} | all-to-all | bytes 524288 | tf_op jit(solution)/shard_map/all_to_all | solution.py:226
  191.3 0.6 convert_element_type.16
  (4 shorter events, 0.1 us)
Async XLA Ops:
  6.5 74.8 %all-gather.3.cloned.1.call-start = ((), (), s32[]{:S(2)}) async-start(), calls=%async_computation.4 | async-start | bytes 4325376 | tf_op jit(solution)/shard_map/all_gather | solution.py:235
  7.3 137.5 %all-gather.5.cloned.1.call-start = ((), (), s32[]{:S(2)}) async-start(), calls=%async_computation.5 | async-start | bytes 4325376 | tf_op jit(solution)/shard_map/all_gather | solution.py:235
  9.5 30.4 %copy-start.3 = (s32[4,1024]{1,0:T(4,128)S(1)}, s32[4,1024]{1,0:T(4,128)}, u32[]{:S(2)}) copy-start(s32[4,1024]{1,0:T(4,128)} %param.5) | copy-start | bytes 49156
  11.2 25.6 %all-to-all-start = ((bf16[32,8,1024]{2,1,0:T(8,128)(2,1)}), bf16[32,8,1024]{2,1,0:T(8,128)(2,1)S(1)}, u32[]{:S(2)}, u32[]{:S(2)}) async-start(bf16[32,8,1024]{2,1,0:T(8,128)(2,1)} %squeeze.6), calls=%async_computation | async-start | bytes 1048576 | tf_op jit(solution)/shard_map/all_to_all | solution.py:191
  36.8 3.7 %copy-start.2 = (bf16[32,8,1024]{2,1,0:T(8,128)(2,1)}, bf16[32,8,1024]{2,1,0:T(8,128)(2,1)S(1)}, u32[]{:S(2)}) copy-start(bf16[32,8,1024]{2,1,0:T(8,128)(2,1)S(1)} %all-to-all-done) | copy-start | bytes 1572868
  36.8 119.0 %all-to-all-start.2 = ((bf16[32,8,1024]{2,1,0:T(8,128)(2,1)}), bf16[32,8,1024]{2,1,0:T(8,128)(2,1)S(1)}, u32[]{:S(2)}, u32[]{:S(2)}) async-start(bf16[32,8,1024]{2,1,0:T(8,128)(2,1)} %squeeze.7), calls=%async_computation.2 | async-start | bytes 1048576 | tf_op jit(solution)/shard_map/all_to_all | solution.py:191
  155.8 3.8 %copy-start.1 = (bf16[32,8,1024]{2,1,0:T(8,128)(2,1)}, bf16[32,8,1024]{2,1,0:T(8,128)(2,1)S(1)}, u32[]{:S(2)}) copy-start(bf16[32,8,1024]{2,1,0:T(8,128)(2,1)S(1)} %all-to-all-done.2) | copy-start | bytes 1572868
  155.8 16.6 %all-to-all-start.1 = ((bf16[16,128,128]{2,1,0:T(8,128)(2,1)}), bf16[16,128,128]{2,1,0:T(8,128)(2,1)S(1)}, u32[]{:S(2)}, u32[]{:S(2)}) async-start(bf16[16,128,128]{2,1,0:T(8,128)(2,1)} %bitcast.16), calls=%async_computation.1 | async-start | bytes 1048576 | tf_op jit(solution)/shard_map/all_to_all | solution.py:207
  172.4 0.8 copy-start
Sparse Core Ops, SparseCore 0:
  10.3 71.0 all-gather.2
  84.3 60.4 all-gather.4

commit v2 on v1

--- a/solution.py
+++ b/solution.py
@@ -68,15 +68,41 @@
             h_ref[rows, lanes] = turned.reshape(per * tile_rows, LANES).astype(jnp.bfloat16)
 
 
-def layers_kernel(sizes, is_left, x_ref, a_ref, b_ref, o_ref, xs, hs, last):
+def gate_copies(plan, blocks, whole_ref, sems):
+    me = lax.axis_index("mode")
+    copies = ([], [])
+    for (sources, gates), block in zip(plan, blocks):
+        for place, source in enumerate(sources):
+            device = me
+            for bit in source:
+                device = device + (1 - 2 * (me // 2**bit % 2)) * 2**bit
+            size = block.shape[3]
+            rows = pl.ds(pl.multiple_of(device * size, size), size)
+            for position, gate in enumerate(gates):
+                sem = sems.at[gate, len(copies[gate])]
+                copies[gate].append(
+                    pltpu.make_async_copy(block.at[position, place], whole_ref.at[gate, :, rows, :], sem)
+                )
+    return copies
+
+
+def layers_kernel(sizes, is_left, plan, x_ref, *refs):
     devices, qs, group, rows_each = sizes
+    blocks, (o_ref, xs, hs, last, whole_ref, sems) = refs[: len(plan)], refs[len(plan) :]
+    copies = gate_copies(plan, blocks, whole_ref, sems)
+    for gate in range(2):
+        for copy in copies[gate]:
+            copy.start()
     tile_rows = 2 * qs
     rows, width = x_ref.shape
     first = x_ref[...].astype(jnp.float32).reshape(devices, tile_rows, width)
     hs[0] = swap_sign(first, qs).reshape(rows, width).astype(jnp.bfloat16)
     step = 256
     for layer in range(2 * CYCLES):
-        gate = a_ref if layer % 2 == 0 else b_ref
+        if layer < 2:
+            for copy in copies[layer]:
+                copy.wait()
+        gate = whole_ref.at[layer % 2]
         here = x_ref if layer == 0 else xs.at[layer % 2]
         turned = hs.at[layer % 2]
         later = (layer + 1) % 2
@@ -144,17 +170,17 @@
         o_ref[g * block : (g + 1) * block, :] = part.astype(jnp.bfloat16)
 
 
-def call(kernel, out_shape, inputs, scratch=(), flops=0):
-    moved = sum(x.size * x.dtype.itemsize for x in inputs)
+def call(kernel, out_shape, inputs, scratch=(), flops=0, blocks=()):
+    moved = sum(x.size * x.dtype.itemsize for x in (*inputs, *blocks))
     return pl.pallas_call(
         kernel,
         out_shape=jax.ShapeDtypeStruct(out_shape, jnp.bfloat16),
-        in_specs=whole(len(inputs)),
+        in_specs=whole(len(inputs)) + [pl.BlockSpec(memory_space=pl.ANY)] * len(blocks),
         out_specs=whole(1)[0],
         scratch_shapes=list(scratch),
         compiler_params=pltpu.CompilerParams(vmem_limit_bytes=VMEM_LIMIT),
         cost_estimate=pl.CostEstimate(flops=flops, bytes_accessed=moved, transcendentals=0),
-    )(*inputs)
+    )(*inputs, *blocks)
 
 
 def tiles_fit(devices, rows_each, width):
@@ -183,7 +209,7 @@
     tile_rows = 2 * qs
     rows = devices * tile_rows
     pair = me // halves
-    whole_a, whole_b = gather_gates(gate_a, gate_b)
+    blocks, plan = gather_gates(gate_a, gate_b)
     cut = branch_in.reshape(2, 2, 2, halves, qs, width).transpose(1, 0, 3, 2, 4, 5)
     cut = cut.reshape(2, devices, tile_rows, width)
     states = []
@@ -194,14 +220,19 @@
             call(order_kernel, (rows, width), (order, got.reshape(rows, width)), flops=2 * rows * width * width)
         )
     sizes = (devices, qs, group, rows_each)
-    scratch = [pltpu.VMEM((2, rows, width), jnp.bfloat16)] * 2 + [pltpu.VMEM((rows, width), jnp.bfloat16)]
+    scratch = [pltpu.VMEM((2, rows, width), jnp.bfloat16)] * 2 + [
+        pltpu.VMEM((rows, width), jnp.bfloat16),
+        pltpu.VMEM((2, 2, width, width), jnp.bfloat16),
+        pltpu.SemaphoreType.DMA((2, devices)),
+    ]
     work = 2 * CYCLES * 4 * rows * width * width
     left = call(
-        functools.partial(layers_kernel, sizes, True),
+        functools.partial(layers_kernel, sizes, True, plan),
         (halves * rows // 2, LANES),
-        (states[0], whole_a, whole_b),
+        (states[0],),
         scratch,
         work,
+        blocks,
     )
     groups = [[h * halves + e for e in range(halves)] for h in range(2)]
     left = lax.all_to_all(
@@ -213,7 +244,7 @@
         tiled=True,
     )
     right = call(
-        functools.partial(layers_kernel, sizes, False), (rows, width), (states[1], whole_a, whole_b), scratch, work
+        functools.partial(layers_kernel, sizes, False, plan), (rows, width), (states[1],), scratch, work, blocks
     )
     free = width // (2 * KEPT)
     us = halves
@@ -231,8 +262,33 @@
     return (jnp.sum(parts, axis=1) * join_scale).astype(jnp.bfloat16).reshape(2, us, 2, free)
 
 
+def flip(value, bit):
+    pairs = [(source, source ^ 2**bit) for source in range(lax.axis_size("mode"))]
+    return lax.ppermute(value, "mode", pairs)
+
+
 def gather_gates(gate_a, gate_b):
-    return [lax.all_gather(gate, "mode", axis=1, tiled=True) for gate in (gate_a, gate_b)]
+    bits = lax.axis_size("mode").bit_length() - 1
+    own = jnp.stack([gate_a, gate_b])[:, None]
+    sets = [(jnp.concatenate([own, flip(own, 3)], axis=1), ((), (3,)))]
+    for bit in range(4, bits):
+        sets += [(flip(value, bit), tuple(source + (bit,) for source in sources)) for value, sources in sets]
+    blocks = []
+    for value, sources in sets:
+        over_x, over_y = flip(value, 1), flip(value, 2)
+        diagonal = flip(over_x[:1], 2), flip(over_y[1:], 1)
+        turned = [tuple(source + more for source in sources) for more in ((1,), (2,), (1, 2))]
+        blocks += [
+            (value, sources, (0, 1)),
+            (over_x, turned[0], (0, 1)),
+            (over_y, turned[1], (0, 1)),
+            (diagonal[0], turned[2], (0,)),
+            (diagonal[1], turned[2], (1,)),
+        ]
+    blocks += [
+        (flip(value, 0), tuple(source + (0,) for source in sources), gates) for value, sources, gates in blocks
+    ]
+    return [value for value, _, _ in blocks], tuple((sources, gates) for _, sources, gates in blocks)
 
 
 def partner(value, axis, bit):

time: 199 us -> 141 us (0.71)
  waiting for transfers between devices: 120 us -> 51.7 us
  starting transfers between devices: 14.2 us -> 30.1 us
  between operations: 13.5 us -> 0.27 us
  local copies, waits for them, and re-layouts: 6.36 us -> 11 us
    all_gather x2 -> x0, waiting for transfers between devices: 102 us -> none  [gather_gates(): lax.all_gather(gate, 'mode', axis=1, tiled=True)]
    ppermute x0 -> x20, waiting for transfers between devices: none -> 51.7 us  [flip(): return lax.ppermute(value, 'mode', pairs)]
    ppermute x0 -> x20, starting transfers between devices: none -> 18.1 us  [flip(): return lax.ppermute(value, 'mode', pairs)]
    all_to_all x2, waiting for transfers between devices: 17.1 us -> 0.01 us  [fast(): lax.all_to_all(cut[side], 'mode', split_axis=0, concat_axis=0, tiled=True)]
    unnamed x8 -> x30, local copies, waits for them, and re-layouts: 0.8 us -> 5.38 us
    all_to_all x2, starting transfers between devices: 10.4 us -> 8.14 us  [fast(): lax.all_to_all(cut[side], 'mode', split_axis=0, concat_axis=0, tiled=True)]
  transfers between devices with their start and end apart: 5 -> 23, of which waited for: 3 -> 5; matrix products, arithmetic and copies ran while one was open for 2% -> 4% of each run, Pallas kernels for 13% -> 19%
where the time goes in v2:
time: 141 us; the launch traced here: 140 us
  waiting for transfers between devices  51.7 us (37%)
  starting transfers between devices  30.1 us (21%)
  Pallas kernels  29.7 us (21%)
  blocking collectives  16.4 us (12%)
  local copies, waits for them, and re-layouts  11 us (8%)
    ppermute x20, waiting for transfers between devices, flip(): return lax.ppermute(value, 'mode', pairs)  51.7 us
    pallas_call x5, Pallas kernels, call(): pl.pallas_call(kernel, out_shape=jax.ShapeDtypeStruct(out_shape, jnp.bflo...  29.7 us
    ppermute x20, starting transfers between devices, flip(): return lax.ppermute(value, 'mode', pairs)  18.1 us
    all_to_all x1, blocking collectives, fast(): lax.all_to_all(partial_sums.reshape(devices, us, 2 * free), 'mode', split...  16.4 us
    all_to_all x2, starting transfers between devices, fast(): lax.all_to_all(cut[side], 'mode', split_axis=0, concat_axis=0, tiled=True)  8.14 us
    unnamed x30, local copies, waits for them, and re-layouts  5.38 us
    all_to_all x1, starting transfers between devices, fast(): lax.all_to_all(left.reshape(halves, rows // 2, LANES), 'mode', split_axis...  3.84 us
  transfers between devices with their start and end apart: 23, of which 5 were waited for; matrix products, arithmetic and copies ran while one was open for 4% of the time, Pallas kernels for 19%

profile of v2, /device:TPU:0, one launch (start us, length us, event | category | flops | bytes accessed | tf_op | source)
XLA Modules:
  0.0 140.1 jit_solution(17903589398168069117)
XLA Ops:
  0.0 1.0 maximum_bitcast_fusion
  1.0 3.1 %collective-permute-start = (bf16[2,1,2,32,1024]{4,3,2,1,0:T(8,128)(2,1)S(1)}, bf16[2,1,2,32,1024]{4,3,2,1,0:T(8,128)(2,1)S(1)}, u32[]{:S(2)}, u32[]{:S(2)}) collective-permute-start(bf16[2,1,2,32,1024]{4,3,2,1,0:T(8,128)(2,1)S(1)} %maximum_bitcast_fusion), channel_id=1, source_target_pairs={{0,8},{1,9},{2,10},{3,11},{4,12},{5,13},{6,14},{7,15},{8,0},{9,1},... | collective-permute-start | bytes 786440 | tf_op jit(solution)/shard_map/ppermute | solution.py:267
  4.1 1.5 %reshape.31 = bf16[2,2,2,16,4,1024]{5,4,3,2,1,0:T(4,128)(2,1)S(1)} reshape(bf16[4,2,64,1024]{3,2,1,0:T(8,128)(2,1)} %param.4) | data formatting | bytes 2097152 | tf_op jit(solution)/shard_map/reshape | solution.py:213
  5.5 4.8 %collective-permute-done = bf16[2,1,2,32,1024]{4,3,2,1,0:T(8,128)(2,1)S(1)} collective-permute-done((bf16[2,1,2,32,1024]{4,3,2,1,0:T(8,128)(2,1)S(1)}, bf16[2,1,2,32,1024]{4,3,2,1,0:T(8,128)(2,1)S(1)}, u32[]{:S(2)}, u32[]{:S(2)}) %collective-permute-start) | collective-permute-done | bytes 262176 | tf_op jit(solution)/shard_map/ppermute | solution.py:267
  10.5 2.8 %collective-permute-start.5 = (bf16[2,2,2,32,1024]{4,3,2,1,0:T(8,128)(2,1)S(1)}, bf16[2,2,2,32,1024]{4,3,2,1,0:T(8,128)(2,1)}, u32[]{:S(2)}, u32[]{:S(2)}) collective-permute-start(bf16[2,2,2,32,1024]{4,3,2,1,0:T(8,128)(2,1)S(1)} %pad_maximum_fusion.refs_0_), channel_id=1, source_target_pairs={{0,16},{1,17},{2,18},{3,19},{4,20},{5,21},{6,22},{7,23},{8,24},{9,... | collective-permute-start | bytes 1572872 | tf_op jit(solution)/shard_map/ppermute | solution.py:267
  13.3 1.5 %collective-permute-start.1 = (bf16[2,2,2,32,1024]{4,3,2,1,0:T(8,128)(2,1)S(1)}, bf16[2,2,2,32,1024]{4,3,2,1,0:T(8,128)(2,1)S(1)}, u32[]{:S(2)}, u32[]{:S(2)}) collective-permute-start(bf16[2,2,2,32,1024]{4,3,2,1,0:T(8,128)(2,1)S(1)} %pad_maximum_fusion.refs_0_), channel_id=1, source_target_pairs={{0,2},{1,3},{2,0},{3,1},{4,6},{5,7},{6,4},{7,5},{8,10},{9,11},{10,... | collective-permute-start | bytes 1572872 | tf_op jit(solution)/shard_map/ppermute | solution.py:267
  14.8 1.5 %collective-permute-start.2 = (bf16[2,2,2,32,1024]{4,3,2,1,0:T(8,128)(2,1)S(1)}, bf16[2,2,2,32,1024]{4,3,2,1,0:T(8,128)(2,1)S(1)}, u32[]{:S(2)}, u32[]{:S(2)}) collective-permute-start(bf16[2,2,2,32,1024]{4,3,2,1,0:T(8,128)(2,1)S(1)} %pad_maximum_fusion.refs_0_), channel_id=1, source_target_pairs={{0,4},{1,5},{2,6},{3,7},{4,0},{5,1},{6,2},{7,3},{8,12},{9,13},{10,... | collective-permute-start | bytes 1572872 | tf_op jit(solution)/shard_map/ppermute | solution.py:267
  17.0 1.0 squeeze.6
  17.9 2.6 %all-to-all-start = ((bf16[32,8,1024]{2,1,0:T(8,128)(2,1)}), bf16[32,8,1024]{2,1,0:T(8,128)(2,1)S(1)}, u32[]{:S(2)}, u32[]{:S(2)}) async-start(bf16[32,8,1024]{2,1,0:T(8,128)(2,1)} %squeeze.6), calls=%async_computation | async-start | bytes 1048576 | tf_op jit(solution)/shard_map/all_to_all | solution.py:217
  20.6 22.0 %collective-permute-done.5.refs_5_ = bf16[2,2,2,32,1024]{4,3,2,1,0:T(8,128)(2,1)} collective-permute-done((bf16[2,2,2,32,1024]{4,3,2,1,0:T(8,128)(2,1)S(1)}, bf16[2,2,2,32,1024]{4,3,2,1,0:T(8,128)(2,1)}, u32[]{:S(2)}, u32[]{:S(2)}) %collective-permute-start.5) | collective-permute-done | bytes 524320 | tf_op jit(solution)/shard_map/ppermute | solution.py:267
  42.5 1.5 %collective-permute-start.6 = (bf16[2,2,2,32,1024]{4,3,2,1,0:T(8,128)(2,1)}, bf16[2,2,2,32,1024]{4,3,2,1,0:T(8,128)(2,1)S(1)}, u32[]{:S(2)}, u32[]{:S(2)}) collective-permute-start(bf16[2,2,2,32,1024]{4,3,2,1,0:T(8,128)(2,1)} %collective-permute-done.5.refs_5_), channel_id=1, source_target_pairs={{0,2},{1,3},{2,0},{3,1},{4,6},{5,7},{6,4},{7,5},{8,10},{9,11},{10,... | collective-permute-start | bytes 1572872 | tf_op jit(solution)/shard_map/ppermute | solution.py:267
  44.0 1.5 %collective-permute-start.7 = (bf16[2,2,2,32,1024]{4,3,2,1,0:T(8,128)(2,1)}, bf16[2,2,2,32,1024]{4,3,2,1,0:T(8,128)(2,1)S(1)}, u32[]{:S(2)}, u32[]{:S(2)}) collective-permute-start(bf16[2,2,2,32,1024]{4,3,2,1,0:T(8,128)(2,1)} %collective-permute-done.5.refs_5_), channel_id=1, source_target_pairs={{0,4},{1,5},{2,6},{3,7},{4,0},{5,1},{6,2},{7,3},{8,12},{9,13},{10,... | collective-permute-start | bytes 1572872 | tf_op jit(solution)/shard_map/ppermute | solution.py:267
  46.8 15.3 %collective-permute-done.3.refs_3_ = bf16[1,2,2,32,1024]{4,3,2,1,0:T(8,128)(2,1)S(1)} collective-permute-done((bf16[1,2,2,32,1024]{4,3,2,1,0:T(8,128)(2,1)S(1)}, bf16[1,2,2,32,1024]{4,3,2,1,0:T(8,128)(2,1)S(1)}, u32[]{:S(2)}, u32[]{:S(2)}) %collective-permute-start.3) | collective-permute-done | bytes 262176 | tf_op jit(solution)/shard_map/ppermute | solution.py:267
  63.8 0.9 squeeze.7
  64.7 0.8 copy-done.2
  65.5 5.5 %all-to-all-start.2 = ((bf16[32,8,1024]{2,1,0:T(8,128)(2,1)}), bf16[32,8,1024]{2,1,0:T(8,128)(2,1)S(1)}, u32[]{:S(2)}, u32[]{:S(2)}) async-start(bf16[32,8,1024]{2,1,0:T(8,128)(2,1)} %squeeze.7), calls=%async_computation.2 | async-start | bytes 1048576 | tf_op jit(solution)/shard_map/all_to_all | solution.py:217
  71.1 1.0 copy-done.9
  72.5 1.7 %collective-permute-start.8 = (bf16[1,2,2,32,1024]{4,3,2,1,0:T(8,128)(2,1)S(1)}, bf16[1,2,2,32,1024]{4,3,2,1,0:T(8,128)(2,1)S(1)}, u32[]{:S(2)}, u32[]{:S(2)}) collective-permute-start(bf16[1,2,2,32,1024]{4,3,2,1,0:T(8,128)(2,1)S(1)} %slice.29), channel_id=1, source_target_pairs={{0,4},{1,5},{2,6},{3,7},{4,0},{5,1},{6,2},{7,3},{8,12},{9,13},{10,... | collective-permute-start | bytes 786440 | tf_op jit(solution)/shard_map/ppermute | solution.py:267
  74.2 1.5 %collective-permute-start.9 = (bf16[1,2,2,32,1024]{4,3,2,1,0:T(8,128)(2,1)S(1)}, bf16[1,2,2,32,1024]{4,3,2,1,0:T(8,128)(2,1)S(1)}, u32[]{:S(2)}, u32[]{:S(2)}) collective-permute-start(bf16[1,2,2,32,1024]{4,3,2,1,0:T(8,128)(2,1)S(1)} %slice.30), channel_id=1, source_target_pairs={{0,2},{1,3},{2,0},{3,1},{4,6},{5,7},{6,4},{7,5},{8,10},{9,11},{10,... | collective-permute-start | bytes 786440 | tf_op jit(solution)/shard_map/ppermute | solution.py:267
  76.2 8.9 %collective-permute-done.8.refs_8_ = bf16[1,2,2,32,1024]{4,3,2,1,0:T(8,128)(2,1)S(1)} collective-permute-done((bf16[1,2,2,32,1024]{4,3,2,1,0:T(8,128)(2,1)S(1)}, bf16[1,2,2,32,1024]{4,3,2,1,0:T(8,128)(2,1)S(1)}, u32[]{:S(2)}, u32[]{:S(2)}) %collective-permute-start.8) | collective-permute-done | bytes 262176 | tf_op jit(solution)/shard_map/ppermute | solution.py:267
  85.0 0.7 collective-permute-done.9.refs_9_
  85.8 0.7 copy-done.10
  87.1 2.6 %shard_map.46.x_ref = bf16[256,1024]{1,0:T(8,128)(2,1)} custom-call(s32[1,1024]{1,0:T(1,128)} %get-tuple-element.8.order_ref, bf16[256,1024]{1,0:T(8,128)(2,1)} %bitcast.18), custom_call_target="tpu_custom_call" | custom-call | flops 536870912 | bytes 528384 | tf_op jit(solution)/shard_map/pallas_call | solution.py:175
  89.8 0.8 copy-done.11
  90.6 11.3 %shard_map.47 = bf16[2048,128]{1,0:T(8,128)(2,1)} custom-call(bf16[256,1024]{1,0:T(8,128)(2,1)} %shard_map.46.x_ref, bf16[2,2,2,32,1024]{4,3,2,1,0:T(8,128)(2,1)} %copy-done.1, bf16[2,2,2,32,1024]{4,3,2,1,0:T(8,128)(2,1)} %copy-done.4, bf16[2,2,2,32,1024]{4,3,2,1,0:T(8,128)(2,1)} %copy-done.5, bf16[1,2,2,32,1024]{4,3,2,1,0:T(8,128)(2,1)} %copy-done.12, ...), custom_call_target="tpu_custom_call" | custom-call | flops 4294967296 | bytes 8912896 | tf_op jit(solution)/shard_map/pallas_call | solution.py:175
  101.9 0.8 copy-done.3
  102.7 3.8 %all-to-all-start.1 = ((bf16[16,128,128]{2,1,0:T(8,128)(2,1)}), bf16[16,128,128]{2,1,0:T(8,128)(2,1)S(1)}, u32[]{:S(2)}, u32[]{:S(2)}) async-start(bf16[16,128,128]{2,1,0:T(8,128)(2,1)} %bitcast.20), calls=%async_computation.1 | async-start | bytes 1048576 | tf_op jit(solution)/shard_map/all_to_all | solution.py:238
  106.5 2.6 %shard_map.48.x_ref = bf16[256,1024]{1,0:T(8,128)(2,1)} custom-call(s32[1,1024]{1,0:T(1,128)} %get-tuple-element.7.order_ref, bf16[256,1024]{1,0:T(8,128)(2,1)} %bitcast.19), custom_call_target="tpu_custom_call" | custom-call | flops 536870912 | bytes 528384 | tf_op jit(solution)/shard_map/pallas_call | solution.py:175
  109.2 10.6 %shard_map.49.right_ref = bf16[256,1024]{1,0:T(8,128)(2,1)} custom-call(bf16[256,1024]{1,0:T(8,128)(2,1)} %shard_map.48.x_ref, bf16[2,2,2,32,1024]{4,3,2,1,0:T(8,128)(2,1)} %copy-done.1, bf16[2,2,2,32,1024]{4,3,2,1,0:T(8,128)(2,1)} %copy-done.4, bf16[2,2,2,32,1024]{4,3,2,1,0:T(8,128)(2,1)} %copy-done.5, bf16[1,2,2,32,1024]{4,3,2,1,0:T(8,128)(2,1)} %copy-done.12, ...), custom_call_target="tpu_custom_call" | custom-call | flops 4294967296 | bytes 8912896 | tf_op jit(solution)/shard_map/pallas_call | solution.py:175
  119.8 0.8 copy-done
  120.6 2.5 %shard_map.50 = bf16[512,256]{1,0:T(8,128)(2,1)} custom-call(bf16[2048,128]{1,0:T(8,128)(2,1)} %bitcast.16, bf16[256,1024]{1,0:T(8,128)(2,1)} %shard_map.49.right_ref), custom_call_target="tpu_custom_call" | custom-call | flops 134217728 | bytes 1048576 | tf_op jit(solution)/shard_map/pallas_call | solution.py:175
  123.1 16.4 %all_to_all.20 = bf16[32,16,256]{2,1,0:T(8,128)(2,1)S(1)} all-to-all(bf16[32,16,256]{2,1,0:T(8,128)(2,1)} %bitcast.17), channel_id=1, replica_groups=mesh['cuts'=1,'mode'=32] {'mode'}, dimensions={0} | all-to-all | bytes 524288 | tf_op jit(solution)/shard_map/all_to_all | solution.py:257
  (66 shorter events, 5.9 us)
Async XLA Ops:
  1.0 9.4 %collective-permute-start = (bf16[2,1,2,32,1024]{4,3,2,1,0:T(8,128)(2,1)S(1)}, bf16[2,1,2,32,1024]{4,3,2,1,0:T(8,128)(2,1)S(1)}, u32[]{:S(2)}, u32[]{:S(2)}) collective-permute-start(bf16[2,1,2,32,1024]{4,3,2,1,0:T(8,128)(2,1)S(1)} %maximum_bitcast_fusion), channel_id=1, source_target_pairs={{0,8},{1,9},{2,10},{3,11},{4,12},{5,13},{6,14},{7,15},{8,0},{9,1},... | collective-permute-start | bytes 786440 | tf_op jit(solution)/shard_map/ppermute | solution.py:267
  10.4 36.3 %copy-start.1 = (bf16[2,2,2,32,1024]{4,3,2,1,0:T(8,128)(2,1)}, bf16[2,2,2,32,1024]{4,3,2,1,0:T(8,128)(2,1)S(1)}, u32[]{:S(2)}) copy-start(bf16[2,2,2,32,1024]{4,3,2,1,0:T(8,128)(2,1)S(1)} %pad_maximum_fusion.refs_0_) | copy-start | bytes 1572868
  10.5 32.1 %collective-permute-start.5 = (bf16[2,2,2,32,1024]{4,3,2,1,0:T(8,128)(2,1)S(1)}, bf16[2,2,2,32,1024]{4,3,2,1,0:T(8,128)(2,1)}, u32[]{:S(2)}, u32[]{:S(2)}) collective-permute-start(bf16[2,2,2,32,1024]{4,3,2,1,0:T(8,128)(2,1)S(1)} %pad_maximum_fusion.refs_0_), channel_id=1, source_target_pairs={{0,16},{1,17},{2,18},{3,19},{4,20},{5,21},{6,22},{7,23},{8,24},{9,... | collective-permute-start | bytes 1572872 | tf_op jit(solution)/shard_map/ppermute | solution.py:267
  13.3 32.2 %collective-permute-start.1 = (bf16[2,2,2,32,1024]{4,3,2,1,0:T(8,128)(2,1)S(1)}, bf16[2,2,2,32,1024]{4,3,2,1,0:T(8,128)(2,1)S(1)}, u32[]{:S(2)}, u32[]{:S(2)}) collective-permute-start(bf16[2,2,2,32,1024]{4,3,2,1,0:T(8,128)(2,1)S(1)} %pad_maximum_fusion.refs_0_), channel_id=1, source_target_pairs={{0,2},{1,3},{2,0},{3,1},{4,6},{5,7},{6,4},{7,5},{8,10},{9,11},{10,... | collective-permute-start | bytes 1572872 | tf_op jit(solution)/shard_map/ppermute | solution.py:267
  14.8 31.4 %collective-permute-start.2 = (bf16[2,2,2,32,1024]{4,3,2,1,0:T(8,128)(2,1)S(1)}, bf16[2,2,2,32,1024]{4,3,2,1,0:T(8,128)(2,1)S(1)}, u32[]{:S(2)}, u32[]{:S(2)}) collective-permute-start(bf16[2,2,2,32,1024]{4,3,2,1,0:T(8,128)(2,1)S(1)} %pad_maximum_fusion.refs_0_), channel_id=1, source_target_pairs={{0,4},{1,5},{2,6},{3,7},{4,0},{5,1},{6,2},{7,3},{8,12},{9,13},{10,... | collective-permute-start | bytes 1572872 | tf_op jit(solution)/shard_map/ppermute | solution.py:267
  17.9 46.8 %all-to-all-start = ((bf16[32,8,1024]{2,1,0:T(8,128)(2,1)}), bf16[32,8,1024]{2,1,0:T(8,128)(2,1)S(1)}, u32[]{:S(2)}, u32[]{:S(2)}) async-start(bf16[32,8,1024]{2,1,0:T(8,128)(2,1)} %squeeze.6), calls=%async_computation | async-start | bytes 1048576 | tf_op jit(solution)/shard_map/all_to_all | solution.py:217
  42.5 20.0 %collective-permute-start.6 = (bf16[2,2,2,32,1024]{4,3,2,1,0:T(8,128)(2,1)}, bf16[2,2,2,32,1024]{4,3,2,1,0:T(8,128)(2,1)S(1)}, u32[]{:S(2)}, u32[]{:S(2)}) collective-permute-start(bf16[2,2,2,32,1024]{4,3,2,1,0:T(8,128)(2,1)} %collective-permute-done.5.refs_5_), channel_id=1, source_target_pairs={{0,2},{1,3},{2,0},{3,1},{4,6},{5,7},{6,4},{7,5},{8,10},{9,11},{10,... | collective-permute-start | bytes 1572872 | tf_op jit(solution)/shard_map/ppermute | solution.py:267
  44.0 18.6 %collective-permute-start.7 = (bf16[2,2,2,32,1024]{4,3,2,1,0:T(8,128)(2,1)}, bf16[2,2,2,32,1024]{4,3,2,1,0:T(8,128)(2,1)S(1)}, u32[]{:S(2)}, u32[]{:S(2)}) collective-permute-start(bf16[2,2,2,32,1024]{4,3,2,1,0:T(8,128)(2,1)} %collective-permute-done.5.refs_5_), channel_id=1, source_target_pairs={{0,4},{1,5},{2,6},{3,7},{4,0},{5,1},{6,2},{7,3},{8,12},{9,13},{10,... | collective-permute-start | bytes 1572872 | tf_op jit(solution)/shard_map/ppermute | solution.py:267
  45.5 16.5 %copy-start.4 = (bf16[2,2,2,32,1024]{4,3,2,1,0:T(8,128)(2,1)}, bf16[2,2,2,32,1024]{4,3,2,1,0:T(8,128)(2,1)S(1)}, u32[]{:S(2)}) copy-start(bf16[2,2,2,32,1024]{4,3,2,1,0:T(8,128)(2,1)S(1)} %collective-permute-done.1.refs_1_) | copy-start | bytes 1572868
  45.5 16.5 %collective-permute-start.3 = (bf16[1,2,2,32,1024]{4,3,2,1,0:T(8,128)(2,1)S(1)}, bf16[1,2,2,32,1024]{4,3,2,1,0:T(8,128)(2,1)S(1)}, u32[]{:S(2)}, u32[]{:S(2)}) collective-permute-start(bf16[1,2,2,32,1024]{4,3,2,1,0:T(8,128)(2,1)S(1)} %slice.27), channel_id=1, source_target_pairs={{0,4},{1,5},{2,6},{3,7},{4,0},{5,1},{6,2},{7,3},{8,12},{9,13},{10,... | collective-permute-start | bytes 786440 | tf_op jit(solution)/shard_map/ppermute | solution.py:267
  46.1 26.0 %copy-start.5 = (bf16[2,2,2,32,1024]{4,3,2,1,0:T(8,128)(2,1)}, bf16[2,2,2,32,1024]{4,3,2,1,0:T(8,128)(2,1)S(1)}, u32[]{:S(2)}) copy-start(bf16[2,2,2,32,1024]{4,3,2,1,0:T(8,128)(2,1)S(1)} %collective-permute-done.2.refs_2_) | copy-start | bytes 1572868
  46.1 15.9 %collective-permute-start.4 = (bf16[1,2,2,32,1024]{4,3,2,1,0:T(8,128)(2,1)S(1)}, bf16[1,2,2,32,1024]{4,3,2,1,0:T(8,128)(2,1)}, u32[]{:S(2)}, u32[]{:S(2)}) collective-permute-start(bf16[1,2,2,32,1024]{4,3,2,1,0:T(8,128)(2,1)S(1)} %slice.28), channel_id=1, source_target_pairs={{0,2},{1,3},{2,0},{3,1},{4,6},{5,7},{6,4},{7,5},{8,10},{9,11},{10,... | collective-permute-start | bytes 786440 | tf_op jit(solution)/shard_map/ppermute | solution.py:267
  46.8 25.4 %collective-permute-start.10 = (bf16[2,2,2,32,1024]{4,3,2,1,0:T(8,128)(2,1)S(1)}, bf16[2,2,2,32,1024]{4,3,2,1,0:T(8,128)(2,1)}, u32[]{:S(2)}, u32[]{:S(2)}) collective-permute-start(bf16[2,2,2,32,1024]{4,3,2,1,0:T(8,128)(2,1)S(1)} %pad_maximum_fusion.refs_0_), channel_id=1, source_target_pairs={{0,1},{1,0},{2,3},{3,2},{4,5},{5,4},{6,7},{7,6},{8,9},{9,8},{10,11... | collective-permute-start | bytes 1572872 | tf_op jit(solution)/shard_map/ppermute | solution.py:267
  62.0 2.7 %copy-start.12 = (bf16[1,2,2,32,1024]{4,3,2,1,0:T(8,128)(2,1)}, bf16[1,2,2,32,1024]{4,3,2,1,0:T(8,128)(2,1)S(1)}, u32[]{:S(2)}) copy-start(bf16[1,2,2,32,1024]{4,3,2,1,0:T(8,128)(2,1)S(1)} %collective-permute-done.3.refs_3_) | copy-start | bytes 786436
  62.0 13.6 %collective-permute-start.15 = (bf16[2,2,2,32,1024]{4,3,2,1,0:T(8,128)(2,1)}, bf16[2,2,2,32,1024]{4,3,2,1,0:T(8,128)(2,1)}, u32[]{:S(2)}, u32[]{:S(2)}) collective-permute-start(bf16[2,2,2,32,1024]{4,3,2,1,0:T(8,128)(2,1)} %collective-permute-done.5.refs_5_), channel_id=1, source_target_pairs={{0,1},{1,0},{2,3},{3,2},{4,5},{5,4},{6,7},{7,6},{8,9},{9,8},{10,11... | collective-permute-start | bytes 1572872 | tf_op jit(solution)/shard_map/ppermute | solution.py:267
  62.0 13.6 %collective-permute-start.11 = (bf16[2,2,2,32,1024]{4,3,2,1,0:T(8,128)(2,1)S(1)}, bf16[2,2,2,32,1024]{4,3,2,1,0:T(8,128)(2,1)}, u32[]{:S(2)}, u32[]{:S(2)}) collective-permute-start(bf16[2,2,2,32,1024]{4,3,2,1,0:T(8,128)(2,1)S(1)} %collective-permute-done.1.refs_1_), channel_id=1, source_target_pairs={{0,1},{1,0},{2,3},{3,2},{4,5},{5,4},{6,7},{7,6},{8,9},{9,8},{10,11... | collective-permute-start | bytes 1572872 | tf_op jit(solution)/shard_map/ppermute | solution.py:267
  62.5 9.9 %collective-permute-start.13 = (bf16[1,2,2,32,1024]{4,3,2,1,0:T(8,128)(2,1)S(1)}, bf16[1,2,2,32,1024]{4,3,2,1,0:T(8,128)(2,1)}, u32[]{:S(2)}, u32[]{:S(2)}) collective-permute-start(bf16[1,2,2,32,1024]{4,3,2,1,0:T(8,128)(2,1)S(1)} %collective-permute-done.3.refs_3_), channel_id=1, source_target_pairs={{0,1},{1,0},{2,3},{3,2},{4,5},{5,4},{6,7},{7,6},{8,9},{9,8},{10,11... | collective-permute-start | bytes 786440 | tf_op jit(solution)/shard_map/ppermute | solution.py:267
  62.6 0.9 copy-start.8
  62.6 11.5 %collective-permute-start.14 = (bf16[1,2,2,32,1024]{4,3,2,1,0:T(8,128)(2,1)}, bf16[1,2,2,32,1024]{4,3,2,1,0:T(8,128)(2,1)}, u32[]{:S(2)}, u32[]{:S(2)}) collective-permute-start(bf16[1,2,2,32,1024]{4,3,2,1,0:T(8,128)(2,1)} %collective-permute-done.4.refs_4_), channel_id=1, source_target_pairs={{0,1},{1,0},{2,3},{3,2},{4,5},{5,4},{6,7},{7,6},{8,9},{9,8},{10,11... | collective-permute-start | bytes 786440 | tf_op jit(solution)/shard_map/ppermute | solution.py:267
  64.7 6.4 %copy-start.7 = (bf16[2,2,2,32,1024]{4,3,2,1,0:T(8,128)(2,1)S(1)}, bf16[2,2,2,32,1024]{4,3,2,1,0:T(8,128)(2,1)}, u32[]{:S(2)}) copy-start(bf16[2,2,2,32,1024]{4,3,2,1,0:T(8,128)(2,1)} %copy-done.6) | copy-start | bytes 1572868
  65.5 36.4 %all-to-all-start.2 = ((bf16[32,8,1024]{2,1,0:T(8,128)(2,1)}), bf16[32,8,1024]{2,1,0:T(8,128)(2,1)S(1)}, u32[]{:S(2)}, u32[]{:S(2)}) async-start(bf16[32,8,1024]{2,1,0:T(8,128)(2,1)} %squeeze.7), calls=%async_computation.2 | async-start | bytes 1048576 | tf_op jit(solution)/shard_map/all_to_all | solution.py:217
  71.1 1.0 copy-start.9
  72.2 17.5 %collective-permute-start.12 = (bf16[2,2,2,32,1024]{4,3,2,1,0:T(8,128)(2,1)S(1)}, bf16[2,2,2,32,1024]{4,3,2,1,0:T(8,128)(2,1)}, u32[]{:S(2)}, u32[]{:S(2)}) collective-permute-start(bf16[2,2,2,32,1024]{4,3,2,1,0:T(8,128)(2,1)S(1)} %collective-permute-done.2.refs_2_), channel_id=1, source_target_pairs={{0,1},{1,0},{2,3},{3,2},{4,5},{5,4},{6,7},{7,6},{8,9},{9,8},{10,11... | collective-permute-start | bytes 1572872 | tf_op jit(solution)/shard_map/ppermute | solution.py:267
  72.5 12.5 %collective-permute-start.8 = (bf16[1,2,2,32,1024]{4,3,2,1,0:T(8,128)(2,1)S(1)}, bf16[1,2,2,32,1024]{4,3,2,1,0:T(8,128)(2,1)S(1)}, u32[]{:S(2)}, u32[]{:S(2)}) collective-permute-start(bf16[1,2,2,32,1024]{4,3,2,1,0:T(8,128)(2,1)S(1)} %slice.29), channel_id=1, source_target_pairs={{0,4},{1,5},{2,6},{3,7},{4,0},{5,1},{6,2},{7,3},{8,12},{9,13},{10,... | collective-permute-start | bytes 786440 | tf_op jit(solution)/shard_map/ppermute | solution.py:267
  74.2 11.6 %collective-permute-start.9 = (bf16[1,2,2,32,1024]{4,3,2,1,0:T(8,128)(2,1)S(1)}, bf16[1,2,2,32,1024]{4,3,2,1,0:T(8,128)(2,1)S(1)}, u32[]{:S(2)}, u32[]{:S(2)}) collective-permute-start(bf16[1,2,2,32,1024]{4,3,2,1,0:T(8,128)(2,1)S(1)} %slice.30), channel_id=1, source_target_pairs={{0,2},{1,3},{2,0},{3,1},{4,6},{5,7},{6,4},{7,5},{8,10},{9,11},{10,... | collective-permute-start | bytes 786440 | tf_op jit(solution)/shard_map/ppermute | solution.py:267
  75.6 14.1 %collective-permute-start.16 = (bf16[2,2,2,32,1024]{4,3,2,1,0:T(8,128)(2,1)S(1)}, bf16[2,2,2,32,1024]{4,3,2,1,0:T(8,128)(2,1)}, u32[]{:S(2)}, u32[]{:S(2)}) collective-permute-start(bf16[2,2,2,32,1024]{4,3,2,1,0:T(8,128)(2,1)S(1)} %copy-done.7), channel_id=1, source_target_pairs={{0,1},{1,0},{2,3},{3,2},{4,5},{5,4},{6,7},{7,6},{8,9},{9,8},{10,11... | collective-permute-start | bytes 1572872 | tf_op jit(solution)/shard_map/ppermute | solution.py:267
  75.7 14.1 %collective-permute-start.17 = (bf16[2,2,2,32,1024]{4,3,2,1,0:T(8,128)(2,1)S(1)}, bf16[2,2,2,32,1024]{4,3,2,1,0:T(8,128)(2,1)S(1)}, u32[]{:S(2)}, u32[]{:S(2)}) collective-permute-start(bf16[2,2,2,32,1024]{4,3,2,1,0:T(8,128)(2,1)S(1)} %copy-done.9), channel_id=1, source_target_pairs={{0,1},{1,0},{2,3},{3,2},{4,5},{5,4},{6,7},{7,6},{8,9},{9,8},{10,11... | collective-permute-start | bytes 1572872 | tf_op jit(solution)/shard_map/ppermute | solution.py:267
  85.0 4.7 %copy-start.13 = (bf16[1,2,2,32,1024]{4,3,2,1,0:T(8,128)(2,1)}, bf16[1,2,2,32,1024]{4,3,2,1,0:T(8,128)(2,1)S(1)}, u32[]{:S(2)}) copy-start(bf16[1,2,2,32,1024]{4,3,2,1,0:T(8,128)(2,1)S(1)} %collective-permute-done.8.refs_8_) | copy-start | bytes 786436
  85.0 4.7 %collective-permute-start.18 = (bf16[1,2,2,32,1024]{4,3,2,1,0:T(8,128)(2,1)S(1)}, bf16[1,2,2,32,1024]{4,3,2,1,0:T(8,128)(2,1)}, u32[]{:S(2)}, u32[]{:S(2)}) collective-permute-start(bf16[1,2,2,32,1024]{4,3,2,1,0:T(8,128)(2,1)S(1)} %collective-permute-done.8.refs_8_), channel_id=1, source_target_pairs={{0,1},{1,0},{2,3},{3,2},{4,5},{5,4},{6,7},{7,6},{8,9},{9,8},{10,11... | collective-permute-start | bytes 786440 | tf_op jit(solution)/shard_map/ppermute | solution.py:267
  85.7 4.0 %copy-start.14 = (bf16[1,2,2,32,1024]{4,3,2,1,0:T(8,128)(2,1)}, bf16[1,2,2,32,1024]{4,3,2,1,0:T(8,128)(2,1)S(1)}, u32[]{:S(2)}) copy-start(bf16[1,2,2,32,1024]{4,3,2,1,0:T(8,128)(2,1)S(1)} %collective-permute-done.9.refs_9_) | copy-start | bytes 786436
  85.7 4.0 %collective-permute-start.19 = (bf16[1,2,2,32,1024]{4,3,2,1,0:T(8,128)(2,1)S(1)}, bf16[1,2,2,32,1024]{4,3,2,1,0:T(8,128)(2,1)}, u32[]{:S(2)}, u32[]{:S(2)}) collective-permute-start(bf16[1,2,2,32,1024]{4,3,2,1,0:T(8,128)(2,1)S(1)} %collective-permute-done.9.refs_9_), channel_id=1, source_target_pairs={{0,1},{1,0},{2,3},{3,2},{4,5},{5,4},{6,7},{7,6},{8,9},{9,8},{10,11... | collective-permute-start | bytes 786440 | tf_op jit(solution)/shard_map/ppermute | solution.py:267
  102.7 17.1 %all-to-all-start.1 = ((bf16[16,128,128]{2,1,0:T(8,128)(2,1)}), bf16[16,128,128]{2,1,0:T(8,128)(2,1)S(1)}, u32[]{:S(2)}, u32[]{:S(2)}) async-start(bf16[16,128,128]{2,1,0:T(8,128)(2,1)} %bitcast.20), calls=%async_computation.1 | async-start | bytes 1048576 | tf_op jit(solution)/shard_map/all_to_all | solution.py:238
  (6 other events, 4.7 us)

commit v3 on v2

--- a/solution.py
+++ b/solution.py
@@ -26,12 +26,19 @@
     return jnp.dot(left, right, preferred_element_type=jnp.float32)
 
 
-def order_kernel(order_ref, x_ref, o_ref):
-    width = x_ref.shape[1]
+def pack_kernel(side, qs, x_ref, order_ref, o_ref):
+    _, parts, rows_each, width = x_ref.shape
+    rows = parts * rows_each
     step = min(256, width)
-    for start in range(0, width, step):
-        picks = one_hot((width, step), 0, order_ref[:, start : start + step])
-        o_ref[:, start : start + step] = exact_dot(x_ref[...], picks).astype(jnp.bfloat16)
+    new = lax.broadcasted_iota(jnp.int32, (rows, rows), 0)
+    e, k, q = new // (parts * qs), new // qs % parts, new % qs
+    pack = one_hot((rows, rows), 1, k * rows_each + e * qs + q)
+    for pair in range(x_ref.shape[0] // 2):
+        branch = 2 * pair + side
+        packed = exact_dot(pack, x_ref[branch].reshape(rows, width)).astype(jnp.bfloat16)
+        for start in range(0, width, step):
+            picks = one_hot((width, step), 0, order_ref[branch : branch + 1, start : start + step])
+            o_ref[pair * rows : (pair + 1) * rows, start : start + step] = exact_dot(packed, picks).astype(jnp.bfloat16)
 
 
 def swap_sign(tiles, qs):
@@ -97,7 +104,7 @@
     rows, width = x_ref.shape
     first = x_ref[...].astype(jnp.float32).reshape(devices, tile_rows, width)
     hs[0] = swap_sign(first, qs).reshape(rows, width).astype(jnp.bfloat16)
-    step = 256
+    step = min(512, width)
     for layer in range(2 * CYCLES):
         if layer < 2:
             for copy in copies[layer]:
@@ -123,6 +130,7 @@
         span = 2 * rows_each
         each = width * qs // rows_each
         words = width // span
+        step = min(256, width)
         for start in range(0, width, step):
             place = start + lax.broadcasted_iota(jnp.int32, (width, step), 1)
             e, rest = place // each, place % each
@@ -202,23 +210,22 @@
 
 def fast(branch_in, column_order, gate_a, gate_b):
     devices = lax.axis_size("mode")
-    me = lax.axis_index("mode")
     rows_each, width = branch_in.shape[2:]
     halves = devices // 2
     qs, group = rows_each // halves, width // devices
     tile_rows = 2 * qs
     rows = devices * tile_rows
-    pair = me // halves
-    blocks, plan = gather_gates(gate_a, gate_b)
-    cut = branch_in.reshape(2, 2, 2, halves, qs, width).transpose(1, 0, 3, 2, 4, 5)
-    cut = cut.reshape(2, devices, tile_rows, width)
-    states = []
-    for side in range(2):
-        got = lax.all_to_all(cut[side], "mode", split_axis=0, concat_axis=0, tiled=True)
-        order = lax.dynamic_slice_in_dim(column_order, 2 * pair + side, 1, 0)
-        states.append(
-            call(order_kernel, (rows, width), (order, got.reshape(rows, width)), flops=2 * rows * width * width)
-        )
+    cut = [
+        call(
+            functools.partial(pack_kernel, side, qs),
+            (rows, width),
+            (branch_in, column_order),
+            flops=2 * rows * width * width,
+        ).reshape(devices, tile_rows, width)
+        for side in range(2)
+    ]
+    blocks, plan, *states = spread(gate_a, gate_b, cut)
+    states = [state.reshape(rows, width) for state in states]
     sizes = (devices, qs, group, rows_each)
     scratch = [pltpu.VMEM((2, rows, width), jnp.bfloat16)] * 2 + [
         pltpu.VMEM((rows, width), jnp.bfloat16),
@@ -235,14 +242,7 @@
         blocks,
     )
     groups = [[h * halves + e for e in range(halves)] for h in range(2)]
-    left = lax.all_to_all(
-        left.reshape(halves, rows // 2, LANES),
-        "mode",
-        split_axis=0,
-        concat_axis=0,
-        axis_index_groups=groups,
-        tiled=True,
-    )
+    left = trade(left.reshape(halves, rows // 2, LANES), groups)
     right = call(
         functools.partial(layers_kernel, sizes, False, plan), (rows, width), (states[1],), scratch, work, blocks
     )
@@ -254,9 +254,7 @@
         (left.reshape(halves * rows // 2, LANES), right),
         flops=2 * devices * us * LANES * qs * 2 * free,
     )
-    parts = lax.all_to_all(
-        partial_sums.reshape(devices, us, 2 * free), "mode", split_axis=0, concat_axis=0, tiled=True
-    )
+    parts = trade(partial_sums.reshape(devices, us, 2 * free))
     parts = parts.reshape(2, halves, us, 2 * free).astype(jnp.float32)
     join_scale = (2.0 * SHARED) ** (-0.5)
     return (jnp.sum(parts, axis=1) * join_scale).astype(jnp.bfloat16).reshape(2, us, 2, free)
@@ -267,28 +265,42 @@
     return lax.ppermute(value, "mode", pairs)
 
 
-def gather_gates(gate_a, gate_b):
+def plane(value, sources):
+    over_x, over_y = flip(value, 1), flip(value, 2)
+    diagonal = flip(over_x[:1], 2), flip(over_y[1:], 1)
+    turned = [tuple(source + more for source in sources) for more in ((1,), (2,), (1, 2))]
+    return [
+        (value, sources, (0, 1)),
+        (over_x, turned[0], (0, 1)),
+        (over_y, turned[1], (0, 1)),
+        (diagonal[0], turned[2], (0,)),
+        (diagonal[1], turned[2], (1,)),
+    ]
+
+
+def spread(gate_a, gate_b, cut):
     bits = lax.axis_size("mode").bit_length() - 1
     own = jnp.stack([gate_a, gate_b])[:, None]
     sets = [(jnp.concatenate([own, flip(own, 3)], axis=1), ((), (3,)))]
     for bit in range(4, bits):
         sets += [(flip(value, bit), tuple(source + (bit,) for source in sources)) for value, sources in sets]
-    blocks = []
-    for value, sources in sets:
-        over_x, over_y = flip(value, 1), flip(value, 2)
-        diagonal = flip(over_x[:1], 2), flip(over_y[1:], 1)
-        turned = [tuple(source + more for source in sources) for more in ((1,), (2,), (1, 2))]
-        blocks += [
-            (value, sources, (0, 1)),
-            (over_x, turned[0], (0, 1)),
-            (over_y, turned[1], (0, 1)),
-            (diagonal[0], turned[2], (0,)),
-            (diagonal[1], turned[2], (1,)),
-        ]
+    blocks, left = [], cut[0]
+    for number, (value, sources) in enumerate(sets):
+        if number:
+            value, left, *_ = lax.optimization_barrier((value, left, blocks[-2][0], blocks[-1][0]))
+        blocks += plane(value, sources)
+    left = trade(left)
+    right, *_ = lax.optimization_barrier((cut[1], blocks[-3][0], blocks[-4][0]))
+    right = trade(right)
     blocks += [
         (flip(value, 0), tuple(source + (0,) for source in sources), gates) for value, sources, gates in blocks
     ]
-    return [value for value, _, _ in blocks], tuple((sources, gates) for _, sources, gates in blocks)
+    plan = tuple((sources, gates) for _, sources, gates in blocks)
+    return [value for value, _, _ in blocks], plan, left, right
+
+
+def trade(value, groups=None):
+    return lax.all_to_all(value, "mode", split_axis=0, concat_axis=0, axis_index_groups=groups, tiled=True)
 
 
 def partner(value, axis, bit):

time: 141 us -> 137 us (0.972)
  local copies, waits for them, and re-layouts: 11 us -> 5.98 us
  waiting for transfers between devices: 51.7 us -> 48.4 us
  starting transfers between devices: 30.1 us -> 32.8 us
    ppermute x20, waiting for transfers between devices: 51.7 us -> 48.4 us  [flip(): return lax.ppermute(value, 'mode', pairs)]
    ppermute x20, starting transfers between devices: 18.1 us -> 20.2 us  [flip(): return lax.ppermute(value, 'mode', pairs)]
    squeeze x2 -> x0, local copies, waits for them, and re-layouts: 1.87 us -> none  [fast(): cut[side]]
    reshape x1 -> x0, local copies, waits for them, and re-layouts: 1.46 us -> none  [fast(): branch_in.reshape(2, 2, 2, halves, qs, width).transpose(1, 0, 3, 2, 4, 5)]
    unnamed x30 -> x36, local copies, waits for them, and re-layouts: 5.38 us -> 5.29 us
  transfers between devices with their start and end apart: 23 -> 23, of which waited for: 5 -> 8; matrix products, arithmetic and copies ran while one was open for 4% -> 0% of each run, Pallas kernels for 19% -> 21%
where the time goes in v3:
time: 137 us; the launch traced here: 136 us
  waiting for transfers between devices  48.4 us (35%)
  starting transfers between devices  32.8 us (24%)
  Pallas kernels  30.9 us (23%)
  blocking collectives  16.6 us (12%)
  local copies, waits for them, and re-layouts  5.98 us (4%)
    ppermute x20, waiting for transfers between devices, flip(): return lax.ppermute(value, 'mode', pairs)  48.4 us
    pallas_call x5, Pallas kernels, call(): pl.pallas_call(kernel, out_shape=jax.ShapeDtypeStruct(out_shape, jnp.bflo...  30.9 us
    ppermute x20, starting transfers between devices, flip(): return lax.ppermute(value, 'mode', pairs)  20.2 us
    all_to_all x1, blocking collectives, trade(): lax.all_to_all(value, 'mode', split_axis=0, concat_axis=0, axis_index_gro...  16.6 us
    all_to_all x3, starting transfers between devices, trade(): lax.all_to_all(value, 'mode', split_axis=0, concat_axis=0, axis_index_gro...  12.6 us
    unnamed x36, local copies, waits for them, and re-layouts  5.29 us
  transfers between devices with their start and end apart: 23, of which 8 were waited for; matrix products, arithmetic and copies ran while one was open for 0% of the time, Pallas kernels for 21%

profile of v3, /device:TPU:0, one launch (start us, length us, event | category | flops | bytes accessed | tf_op | source)
XLA Modules:
  0.0 136.1 jit_solution(13918231795149126814)
XLA Ops:
  0.0 1.0 maximum_bitcast_fusion
  1.0 3.1 %collective-permute-start = (bf16[2,1,2,32,1024]{4,3,2,1,0:T(8,128)(2,1)S(1)}, bf16[2,1,2,32,1024]{4,3,2,1,0:T(8,128)(2,1)S(1)}, u32[]{:S(2)}, u32[]{:S(2)}) collective-permute-start(bf16[2,1,2,32,1024]{4,3,2,1,0:T(8,128)(2,1)S(1)} %maximum_bitcast_fusion), channel_id=1, source_target_pairs={{0,8},{1,9},{2,10},{3,11},{4,12},{5,13},{6,14},{7,15},{8,0},{9,1},... | collective-permute-start | bytes 786440 | tf_op jit(solution)/shard_map/ppermute | solution.py:265
  4.1 6.3 %collective-permute-done = bf16[2,1,2,32,1024]{4,3,2,1,0:T(8,128)(2,1)S(1)} collective-permute-done((bf16[2,1,2,32,1024]{4,3,2,1,0:T(8,128)(2,1)S(1)}, bf16[2,1,2,32,1024]{4,3,2,1,0:T(8,128)(2,1)S(1)}, u32[]{:S(2)}, u32[]{:S(2)}) %collective-permute-start) | collective-permute-done | bytes 262176 | tf_op jit(solution)/shard_map/ppermute | solution.py:265
  10.5 1.7 %collective-permute-start.4 = (bf16[2,2,2,32,1024]{4,3,2,1,0:T(8,128)(2,1)S(1)}, bf16[2,2,2,32,1024]{4,3,2,1,0:T(8,128)(2,1)S(1)}, u32[]{:S(2)}, u32[]{:S(2)}) collective-permute-start(bf16[2,2,2,32,1024]{4,3,2,1,0:T(8,128)(2,1)S(1)} %pad_maximum_fusion.refs_0_), channel_id=1, source_target_pairs={{0,4},{1,5},{2,6},{3,7},{4,0},{5,1},{6,2},{7,3},{8,12},{9,13},{10,... | collective-permute-start | bytes 1572872 | tf_op jit(solution)/shard_map/ppermute | solution.py:265
  12.2 1.5 %collective-permute-start.2 = (bf16[2,2,2,32,1024]{4,3,2,1,0:T(8,128)(2,1)S(1)}, bf16[2,2,2,32,1024]{4,3,2,1,0:T(8,128)(2,1)S(1)}, u32[]{:S(2)}, u32[]{:S(2)}) collective-permute-start(bf16[2,2,2,32,1024]{4,3,2,1,0:T(8,128)(2,1)S(1)} %pad_maximum_fusion.refs_0_), channel_id=1, source_target_pairs={{0,2},{1,3},{2,0},{3,1},{4,6},{5,7},{6,4},{7,5},{8,10},{9,11},{10,... | collective-permute-start | bytes 1572872 | tf_op jit(solution)/shard_map/ppermute | solution.py:265
  13.7 2.6 %collective-permute-start.1 = (bf16[2,2,2,32,1024]{4,3,2,1,0:T(8,128)(2,1)S(1)}, bf16[2,2,2,32,1024]{4,3,2,1,0:T(8,128)(2,1)}, u32[]{:S(2)}, u32[]{:S(2)}) collective-permute-start(bf16[2,2,2,32,1024]{4,3,2,1,0:T(8,128)(2,1)S(1)} %pad_maximum_fusion.refs_0_), channel_id=1, source_target_pairs={{0,16},{1,17},{2,18},{3,19},{4,20},{5,21},{6,22},{7,23},{8,24},{9,... | collective-permute-start | bytes 1572872 | tf_op jit(solution)/shard_map/ppermute | solution.py:265
  16.3 7.3 %collective-permute-done.4.refs_2_ = bf16[2,2,2,32,1024]{4,3,2,1,0:T(8,128)(2,1)S(1)} collective-permute-done((bf16[2,2,2,32,1024]{4,3,2,1,0:T(8,128)(2,1)S(1)}, bf16[2,2,2,32,1024]{4,3,2,1,0:T(8,128)(2,1)S(1)}, u32[]{:S(2)}, u32[]{:S(2)}) %collective-permute-start.4) | collective-permute-done | bytes 524320 | tf_op jit(solution)/shard_map/ppermute | solution.py:265
  23.7 1.4 %collective-permute-start.5 = (bf16[1,2,2,32,1024]{4,3,2,1,0:T(8,128)(2,1)S(1)}, bf16[1,2,2,32,1024]{4,3,2,1,0:T(8,128)(2,1)S(1)}, u32[]{:S(2)}, u32[]{:S(2)}) collective-permute-start(bf16[1,2,2,32,1024]{4,3,2,1,0:T(8,128)(2,1)S(1)} %slice.17), channel_id=1, source_target_pairs={{0,2},{1,3},{2,0},{3,1},{4,6},{5,7},{6,4},{7,5},{8,10},{9,11},{10,... | collective-permute-start | bytes 786440 | tf_op jit(solution)/shard_map/ppermute | solution.py:265
  25.1 1.6 %collective-permute-start.3 = (bf16[1,2,2,32,1024]{4,3,2,1,0:T(8,128)(2,1)S(1)}, bf16[1,2,2,32,1024]{4,3,2,1,0:T(8,128)(2,1)S(1)}, u32[]{:S(2)}, u32[]{:S(2)}) collective-permute-start(bf16[1,2,2,32,1024]{4,3,2,1,0:T(8,128)(2,1)S(1)} %slice.16), channel_id=1, source_target_pairs={{0,4},{1,5},{2,6},{3,7},{4,0},{5,1},{6,2},{7,3},{8,12},{9,13},{10,... | collective-permute-start | bytes 786440 | tf_op jit(solution)/shard_map/ppermute | solution.py:265
  26.7 3.3 %shard_map.46 = bf16[256,1024]{1,0:T(8,128)(2,1)} custom-call(bf16[4,2,64,1024]{3,2,1,0:T(8,128)(2,1)} %x_ref.3, s32[4,1024]{1,0:T(4,128)} %order_ref.3), custom_call_target="tpu_custom_call" | custom-call | flops 536870912 | bytes 1064960 | tf_op jit(solution)/shard_map/pallas_call | solution.py:183
  29.9 8.2 %collective-permute-done.1.refs_5_ = bf16[2,2,2,32,1024]{4,3,2,1,0:T(8,128)(2,1)} collective-permute-done((bf16[2,2,2,32,1024]{4,3,2,1,0:T(8,128)(2,1)S(1)}, bf16[2,2,2,32,1024]{4,3,2,1,0:T(8,128)(2,1)}, u32[]{:S(2)}, u32[]{:S(2)}) %collective-permute-start.1) | collective-permute-done | bytes 524320 | tf_op jit(solution)/shard_map/ppermute | solution.py:265
  38.2 0.7 copy-done.13
  38.9 3.9 %all-to-all-start = ((bf16[32,8,1024]{2,1,0:T(8,128)(2,1)}), bf16[32,8,1024]{2,1,0:T(8,128)(2,1)S(1)}, u32[]{:S(2)}, u32[]{:S(2)}) async-start(bf16[32,8,1024]{2,1,0:T(8,128)(2,1)} %bitcast.19), calls=%async_computation | async-start | bytes 1048576 | tf_op jit(solution)/shard_map/all_to_all | solution.py:303
  42.8 1.8 %collective-permute-start.7 = (bf16[2,2,2,32,1024]{4,3,2,1,0:T(8,128)(2,1)}, bf16[2,2,2,32,1024]{4,3,2,1,0:T(8,128)(2,1)S(1)}, u32[]{:S(2)}, u32[]{:S(2)}) collective-permute-start(bf16[2,2,2,32,1024]{4,3,2,1,0:T(8,128)(2,1)} %collective-permute-done.1.refs_5_), channel_id=1, source_target_pairs={{0,4},{1,5},{2,6},{3,7},{4,0},{5,1},{6,2},{7,3},{8,12},{9,13},{10,... | collective-permute-start | bytes 1572872 | tf_op jit(solution)/shard_map/ppermute | solution.py:265
  44.6 1.5 %collective-permute-start.6 = (bf16[2,2,2,32,1024]{4,3,2,1,0:T(8,128)(2,1)}, bf16[2,2,2,32,1024]{4,3,2,1,0:T(8,128)(2,1)S(1)}, u32[]{:S(2)}, u32[]{:S(2)}) collective-permute-start(bf16[2,2,2,32,1024]{4,3,2,1,0:T(8,128)(2,1)} %collective-permute-done.1.refs_5_), channel_id=1, source_target_pairs={{0,2},{1,3},{2,0},{3,1},{4,6},{5,7},{6,4},{7,5},{8,10},{9,11},{10,... | collective-permute-start | bytes 1572872 | tf_op jit(solution)/shard_map/ppermute | solution.py:265
  46.7 15.8 %collective-permute-done.7.refs_7_ = bf16[2,2,2,32,1024]{4,3,2,1,0:T(8,128)(2,1)S(1)} collective-permute-done((bf16[2,2,2,32,1024]{4,3,2,1,0:T(8,128)(2,1)}, bf16[2,2,2,32,1024]{4,3,2,1,0:T(8,128)(2,1)S(1)}, u32[]{:S(2)}, u32[]{:S(2)}) %collective-permute-start.7) | collective-permute-done | bytes 524320 | tf_op jit(solution)/shard_map/ppermute | solution.py:265
  63.0 3.2 %shard_map.48 = bf16[256,1024]{1,0:T(8,128)(2,1)} custom-call(bf16[4,2,64,1024]{3,2,1,0:T(8,128)(2,1)} %x_ref.3, s32[4,1024]{1,0:T(4,128)} %order_ref.3), custom_call_target="tpu_custom_call" | custom-call | flops 536870912 | bytes 1064960 | tf_op jit(solution)/shard_map/pallas_call | solution.py:183
  66.3 0.8 copy-done.2
  67.1 4.5 %all-to-all-start.2 = ((bf16[32,8,1024]{2,1,0:T(8,128)(2,1)}), bf16[32,8,1024]{2,1,0:T(8,128)(2,1)S(1)}, u32[]{:S(2)}, u32[]{:S(2)}) async-start(bf16[32,8,1024]{2,1,0:T(8,128)(2,1)} %bitcast.18), calls=%async_computation.2 | async-start | bytes 1048576 | tf_op jit(solution)/shard_map/all_to_all | solution.py:303
  71.7 1.0 copy-done.8
  73.1 1.7 %collective-permute-start.9 = (bf16[1,2,2,32,1024]{4,3,2,1,0:T(8,128)(2,1)S(1)}, bf16[1,2,2,32,1024]{4,3,2,1,0:T(8,128)(2,1)S(1)}, u32[]{:S(2)}, u32[]{:S(2)}) collective-permute-start(bf16[1,2,2,32,1024]{4,3,2,1,0:T(8,128)(2,1)S(1)} %slice.19), channel_id=1, source_target_pairs={{0,2},{1,3},{2,0},{3,1},{4,6},{5,7},{6,4},{7,5},{8,10},{9,11},{10,... | collective-permute-start | bytes 786440 | tf_op jit(solution)/shard_map/ppermute | solution.py:265
  74.8 1.5 %collective-permute-start.8 = (bf16[1,2,2,32,1024]{4,3,2,1,0:T(8,128)(2,1)S(1)}, bf16[1,2,2,32,1024]{4,3,2,1,0:T(8,128)(2,1)S(1)}, u32[]{:S(2)}, u32[]{:S(2)}) collective-permute-start(bf16[1,2,2,32,1024]{4,3,2,1,0:T(8,128)(2,1)S(1)} %slice.18), channel_id=1, source_target_pairs={{0,4},{1,5},{2,6},{3,7},{4,0},{5,1},{6,2},{7,3},{8,12},{9,13},{10,... | collective-permute-start | bytes 786440 | tf_op jit(solution)/shard_map/ppermute | solution.py:265
  76.7 8.6 %collective-permute-done.9.refs_9_ = bf16[1,2,2,32,1024]{4,3,2,1,0:T(8,128)(2,1)S(1)} collective-permute-done((bf16[1,2,2,32,1024]{4,3,2,1,0:T(8,128)(2,1)S(1)}, bf16[1,2,2,32,1024]{4,3,2,1,0:T(8,128)(2,1)S(1)}, u32[]{:S(2)}, u32[]{:S(2)}) %collective-permute-start.9) | collective-permute-done | bytes 262176 | tf_op jit(solution)/shard_map/ppermute | solution.py:265
  85.9 0.9 collective-permute-done.19.refs_19_
  88.6 11.4 %shard_map.47 = bf16[2048,128]{1,0:T(8,128)(2,1)} custom-call(bf16[256,1024]{1,0:T(8,128)(2,1)} %bitcast.16, bf16[2,2,2,32,1024]{4,3,2,1,0:T(8,128)(2,1)} %copy-done.1, bf16[2,2,2,32,1024]{4,3,2,1,0:T(8,128)(2,1)} %copy-done.5, bf16[2,2,2,32,1024]{4,3,2,1,0:T(8,128)(2,1)} %copy-done.4, bf16[1,2,2,32,1024]{4,3,2,1,0:T(8,128)(2,1)} %copy-done.13, ...), custom_call_target="tpu_custom_call" | custom-call | flops 4294967296 | bytes 8912896 | tf_op jit(solution)/shard_map/pallas_call | solution.py:183
  99.9 0.8 copy-done.3
  100.8 4.2 %all-to-all-start.1 = ((bf16[16,128,128]{2,1,0:T(8,128)(2,1)}), bf16[16,128,128]{2,1,0:T(8,128)(2,1)S(1)}, u32[]{:S(2)}, u32[]{:S(2)}) async-start(bf16[16,128,128]{2,1,0:T(8,128)(2,1)} %bitcast.20), calls=%async_computation.1 | async-start | bytes 1048576 | tf_op jit(solution)/shard_map/all_to_all | solution.py:303
  104.9 10.6 %shard_map.49.right_ref = bf16[256,1024]{1,0:T(8,128)(2,1)} custom-call(bf16[256,1024]{1,0:T(8,128)(2,1)} %bitcast.17, bf16[2,2,2,32,1024]{4,3,2,1,0:T(8,128)(2,1)} %copy-done.1, bf16[2,2,2,32,1024]{4,3,2,1,0:T(8,128)(2,1)} %copy-done.5, bf16[2,2,2,32,1024]{4,3,2,1,0:T(8,128)(2,1)} %copy-done.4, bf16[1,2,2,32,1024]{4,3,2,1,0:T(8,128)(2,1)} %copy-done.13, ...), custom_call_target="tpu_custom_call" | custom-call | flops 4294967296 | bytes 8912896 | tf_op jit(solution)/shard_map/pallas_call | solution.py:183
  115.5 0.8 copy-done
  116.3 2.5 %shard_map.50 = bf16[512,256]{1,0:T(8,128)(2,1)} custom-call(bf16[2048,128]{1,0:T(8,128)(2,1)} %bitcast.14, bf16[256,1024]{1,0:T(8,128)(2,1)} %shard_map.49.right_ref), custom_call_target="tpu_custom_call" | custom-call | flops 134217728 | bytes 1048576 | tf_op jit(solution)/shard_map/pallas_call | solution.py:183
  118.8 16.6 %all_to_all.20 = bf16[32,16,256]{2,1,0:T(8,128)(2,1)S(1)} all-to-all(bf16[32,16,256]{2,1,0:T(8,128)(2,1)} %bitcast.15), channel_id=1, replica_groups=mesh['cuts'=1,'mode'=32] {'mode'}, dimensions={0} | all-to-all | bytes 524288 | tf_op jit(solution)/shard_map/all_to_all | solution.py:303
  135.4 0.6 convert_element_type.16
  (65 shorter events, 4.4 us)
Async XLA Ops:
  1.0 9.4 %collective-permute-start = (bf16[2,1,2,32,1024]{4,3,2,1,0:T(8,128)(2,1)S(1)}, bf16[2,1,2,32,1024]{4,3,2,1,0:T(8,128)(2,1)S(1)}, u32[]{:S(2)}, u32[]{:S(2)}) collective-permute-start(bf16[2,1,2,32,1024]{4,3,2,1,0:T(8,128)(2,1)S(1)} %maximum_bitcast_fusion), channel_id=1, source_target_pairs={{0,8},{1,9},{2,10},{3,11},{4,12},{5,13},{6,14},{7,15},{8,0},{9,1},... | collective-permute-start | bytes 786440 | tf_op jit(solution)/shard_map/ppermute | solution.py:265
  10.4 35.7 %copy-start.1 = (bf16[2,2,2,32,1024]{4,3,2,1,0:T(8,128)(2,1)}, bf16[2,2,2,32,1024]{4,3,2,1,0:T(8,128)(2,1)S(1)}, u32[]{:S(2)}) copy-start(bf16[2,2,2,32,1024]{4,3,2,1,0:T(8,128)(2,1)S(1)} %pad_maximum_fusion.refs_0_) | copy-start | bytes 1572868
  10.5 13.2 %collective-permute-start.4 = (bf16[2,2,2,32,1024]{4,3,2,1,0:T(8,128)(2,1)S(1)}, bf16[2,2,2,32,1024]{4,3,2,1,0:T(8,128)(2,1)S(1)}, u32[]{:S(2)}, u32[]{:S(2)}) collective-permute-start(bf16[2,2,2,32,1024]{4,3,2,1,0:T(8,128)(2,1)S(1)} %pad_maximum_fusion.refs_0_), channel_id=1, source_target_pairs={{0,4},{1,5},{2,6},{3,7},{4,0},{5,1},{6,2},{7,3},{8,12},{9,13},{10,... | collective-permute-start | bytes 1572872 | tf_op jit(solution)/shard_map/ppermute | solution.py:265
  12.2 12.9 %collective-permute-start.2 = (bf16[2,2,2,32,1024]{4,3,2,1,0:T(8,128)(2,1)S(1)}, bf16[2,2,2,32,1024]{4,3,2,1,0:T(8,128)(2,1)S(1)}, u32[]{:S(2)}, u32[]{:S(2)}) collective-permute-start(bf16[2,2,2,32,1024]{4,3,2,1,0:T(8,128)(2,1)S(1)} %pad_maximum_fusion.refs_0_), channel_id=1, source_target_pairs={{0,2},{1,3},{2,0},{3,1},{4,6},{5,7},{6,4},{7,5},{8,10},{9,11},{10,... | collective-permute-start | bytes 1572872 | tf_op jit(solution)/shard_map/ppermute | solution.py:265
  13.7 24.5 %collective-permute-start.1 = (bf16[2,2,2,32,1024]{4,3,2,1,0:T(8,128)(2,1)S(1)}, bf16[2,2,2,32,1024]{4,3,2,1,0:T(8,128)(2,1)}, u32[]{:S(2)}, u32[]{:S(2)}) collective-permute-start(bf16[2,2,2,32,1024]{4,3,2,1,0:T(8,128)(2,1)S(1)} %pad_maximum_fusion.refs_0_), channel_id=1, source_target_pairs={{0,16},{1,17},{2,18},{3,19},{4,20},{5,21},{6,22},{7,23},{8,24},{9,... | collective-permute-start | bytes 1572872 | tf_op jit(solution)/shard_map/ppermute | solution.py:265
  23.6 22.5 %copy-start.4 = (bf16[2,2,2,32,1024]{4,3,2,1,0:T(8,128)(2,1)}, bf16[2,2,2,32,1024]{4,3,2,1,0:T(8,128)(2,1)S(1)}, u32[]{:S(2)}) copy-start(bf16[2,2,2,32,1024]{4,3,2,1,0:T(8,128)(2,1)S(1)} %collective-permute-done.4.refs_2_) | copy-start | bytes 1572868
  23.7 14.5 %collective-permute-start.5 = (bf16[1,2,2,32,1024]{4,3,2,1,0:T(8,128)(2,1)S(1)}, bf16[1,2,2,32,1024]{4,3,2,1,0:T(8,128)(2,1)S(1)}, u32[]{:S(2)}, u32[]{:S(2)}) collective-permute-start(bf16[1,2,2,32,1024]{4,3,2,1,0:T(8,128)(2,1)S(1)} %slice.17), channel_id=1, source_target_pairs={{0,2},{1,3},{2,0},{3,1},{4,6},{5,7},{6,4},{7,5},{8,10},{9,11},{10,... | collective-permute-start | bytes 786440 | tf_op jit(solution)/shard_map/ppermute | solution.py:265
  25.1 21.6 %copy-start.5 = (bf16[2,2,2,32,1024]{4,3,2,1,0:T(8,128)(2,1)}, bf16[2,2,2,32,1024]{4,3,2,1,0:T(8,128)(2,1)S(1)}, u32[]{:S(2)}) copy-start(bf16[2,2,2,32,1024]{4,3,2,1,0:T(8,128)(2,1)S(1)} %collective-permute-done.2.refs_1_) | copy-start | bytes 1572868
  25.1 13.1 %collective-permute-start.3 = (bf16[1,2,2,32,1024]{4,3,2,1,0:T(8,128)(2,1)S(1)}, bf16[1,2,2,32,1024]{4,3,2,1,0:T(8,128)(2,1)S(1)}, u32[]{:S(2)}, u32[]{:S(2)}) collective-permute-start(bf16[1,2,2,32,1024]{4,3,2,1,0:T(8,128)(2,1)S(1)} %slice.16), channel_id=1, source_target_pairs={{0,4},{1,5},{2,6},{3,7},{4,0},{5,1},{6,2},{7,3},{8,12},{9,13},{10,... | collective-permute-start | bytes 786440 | tf_op jit(solution)/shard_map/ppermute | solution.py:265
  38.2 24.3 %copy-start.12 = (bf16[1,2,2,32,1024]{4,3,2,1,0:T(8,128)(2,1)}, bf16[1,2,2,32,1024]{4,3,2,1,0:T(8,128)(2,1)S(1)}, u32[]{:S(2)}) copy-start(bf16[1,2,2,32,1024]{4,3,2,1,0:T(8,128)(2,1)S(1)} %collective-permute-done.5.refs_4_) | copy-start | bytes 786436
  38.9 27.3 %all-to-all-start = ((bf16[32,8,1024]{2,1,0:T(8,128)(2,1)}), bf16[32,8,1024]{2,1,0:T(8,128)(2,1)S(1)}, u32[]{:S(2)}, u32[]{:S(2)}) async-start(bf16[32,8,1024]{2,1,0:T(8,128)(2,1)} %bitcast.19), calls=%async_computation | async-start | bytes 1048576 | tf_op jit(solution)/shard_map/all_to_all | solution.py:303
  42.8 19.7 %collective-permute-start.7 = (bf16[2,2,2,32,1024]{4,3,2,1,0:T(8,128)(2,1)}, bf16[2,2,2,32,1024]{4,3,2,1,0:T(8,128)(2,1)S(1)}, u32[]{:S(2)}, u32[]{:S(2)}) collective-permute-start(bf16[2,2,2,32,1024]{4,3,2,1,0:T(8,128)(2,1)} %collective-permute-done.1.refs_5_), channel_id=1, source_target_pairs={{0,4},{1,5},{2,6},{3,7},{4,0},{5,1},{6,2},{7,3},{8,12},{9,13},{10,... | collective-permute-start | bytes 1572872 | tf_op jit(solution)/shard_map/ppermute | solution.py:265
  44.6 17.9 %collective-permute-start.6 = (bf16[2,2,2,32,1024]{4,3,2,1,0:T(8,128)(2,1)}, bf16[2,2,2,32,1024]{4,3,2,1,0:T(8,128)(2,1)S(1)}, u32[]{:S(2)}, u32[]{:S(2)}) collective-permute-start(bf16[2,2,2,32,1024]{4,3,2,1,0:T(8,128)(2,1)} %collective-permute-done.1.refs_5_), channel_id=1, source_target_pairs={{0,2},{1,3},{2,0},{3,1},{4,6},{5,7},{6,4},{7,5},{8,10},{9,11},{10,... | collective-permute-start | bytes 1572872 | tf_op jit(solution)/shard_map/ppermute | solution.py:265
  46.1 26.6 %collective-permute-start.10 = (bf16[2,2,2,32,1024]{4,3,2,1,0:T(8,128)(2,1)S(1)}, bf16[2,2,2,32,1024]{4,3,2,1,0:T(8,128)(2,1)}, u32[]{:S(2)}, u32[]{:S(2)}) collective-permute-start(bf16[2,2,2,32,1024]{4,3,2,1,0:T(8,128)(2,1)S(1)} %pad_maximum_fusion.refs_0_), channel_id=1, source_target_pairs={{0,1},{1,0},{2,3},{3,2},{4,5},{5,4},{6,7},{7,6},{8,9},{9,8},{10,11... | collective-permute-start | bytes 1572872 | tf_op jit(solution)/shard_map/ppermute | solution.py:265
  46.1 28.6 %collective-permute-start.12 = (bf16[2,2,2,32,1024]{4,3,2,1,0:T(8,128)(2,1)S(1)}, bf16[2,2,2,32,1024]{4,3,2,1,0:T(8,128)(2,1)}, u32[]{:S(2)}, u32[]{:S(2)}) collective-permute-start(bf16[2,2,2,32,1024]{4,3,2,1,0:T(8,128)(2,1)S(1)} %collective-permute-done.4.refs_2_), channel_id=1, source_target_pairs={{0,1},{1,0},{2,3},{3,2},{4,5},{5,4},{6,7},{7,6},{8,9},{9,8},{10,11... | collective-permute-start | bytes 1572872 | tf_op jit(solution)/shard_map/ppermute | solution.py:265
  46.6 29.6 %collective-permute-start.11 = (bf16[2,2,2,32,1024]{4,3,2,1,0:T(8,128)(2,1)S(1)}, bf16[2,2,2,32,1024]{4,3,2,1,0:T(8,128)(2,1)}, u32[]{:S(2)}, u32[]{:S(2)}) collective-permute-start(bf16[2,2,2,32,1024]{4,3,2,1,0:T(8,128)(2,1)S(1)} %collective-permute-done.2.refs_1_), channel_id=1, source_target_pairs={{0,1},{1,0},{2,3},{3,2},{4,5},{5,4},{6,7},{7,6},{8,9},{9,8},{10,11... | collective-permute-start | bytes 1572872 | tf_op jit(solution)/shard_map/ppermute | solution.py:265
  62.5 13.7 %copy-start.6 = (bf16[2,2,2,32,1024]{4,3,2,1,0:T(8,128)(2,1)}, bf16[2,2,2,32,1024]{4,3,2,1,0:T(8,128)(2,1)S(1)}, u32[]{:S(2)}) copy-start(bf16[2,2,2,32,1024]{4,3,2,1,0:T(8,128)(2,1)S(1)} %collective-permute-done.7.refs_7_) | copy-start | bytes 1572868
  62.5 10.6 %collective-permute-start.14 = (bf16[1,2,2,32,1024]{4,3,2,1,0:T(8,128)(2,1)S(1)}, bf16[1,2,2,32,1024]{4,3,2,1,0:T(8,128)(2,1)}, u32[]{:S(2)}, u32[]{:S(2)}) collective-permute-start(bf16[1,2,2,32,1024]{4,3,2,1,0:T(8,128)(2,1)S(1)} %collective-permute-done.5.refs_4_), channel_id=1, source_target_pairs={{0,1},{1,0},{2,3},{3,2},{4,5},{5,4},{6,7},{7,6},{8,9},{9,8},{10,11... | collective-permute-start | bytes 786440 | tf_op jit(solution)/shard_map/ppermute | solution.py:265
  62.5 3.7 %copy-start.7 = (bf16[2,2,2,32,1024]{4,3,2,1,0:T(8,128)(2,1)}, bf16[2,2,2,32,1024]{4,3,2,1,0:T(8,128)(2,1)S(1)}, u32[]{:S(2)}) copy-start(bf16[2,2,2,32,1024]{4,3,2,1,0:T(8,128)(2,1)S(1)} %collective-permute-done.6.refs_6_) | copy-start | bytes 1572868
  62.5 13.7 %collective-permute-start.13 = (bf16[1,2,2,32,1024]{4,3,2,1,0:T(8,128)(2,1)}, bf16[1,2,2,32,1024]{4,3,2,1,0:T(8,128)(2,1)}, u32[]{:S(2)}, u32[]{:S(2)}) collective-permute-start(bf16[1,2,2,32,1024]{4,3,2,1,0:T(8,128)(2,1)} %copy-done.13), channel_id=1, source_target_pairs={{0,1},{1,0},{2,3},{3,2},{4,5},{5,4},{6,7},{7,6},{8,9},{9,8},{10,11... | collective-permute-start | bytes 786440 | tf_op jit(solution)/shard_map/ppermute | solution.py:265
  67.1 32.8 %all-to-all-start.2 = ((bf16[32,8,1024]{2,1,0:T(8,128)(2,1)}), bf16[32,8,1024]{2,1,0:T(8,128)(2,1)S(1)}, u32[]{:S(2)}, u32[]{:S(2)}) async-start(bf16[32,8,1024]{2,1,0:T(8,128)(2,1)} %bitcast.18), calls=%async_computation.2 | async-start | bytes 1048576 | tf_op jit(solution)/shard_map/all_to_all | solution.py:303
  72.8 13.2 %collective-permute-start.15 = (bf16[2,2,2,32,1024]{4,3,2,1,0:T(8,128)(2,1)}, bf16[2,2,2,32,1024]{4,3,2,1,0:T(8,128)(2,1)S(1)}, u32[]{:S(2)}, u32[]{:S(2)}) collective-permute-start(bf16[2,2,2,32,1024]{4,3,2,1,0:T(8,128)(2,1)} %collective-permute-done.1.refs_5_), channel_id=1, source_target_pairs={{0,1},{1,0},{2,3},{3,2},{4,5},{5,4},{6,7},{7,6},{8,9},{9,8},{10,11... | collective-permute-start | bytes 1572872 | tf_op jit(solution)/shard_map/ppermute | solution.py:265
  73.1 12.3 %collective-permute-start.9 = (bf16[1,2,2,32,1024]{4,3,2,1,0:T(8,128)(2,1)S(1)}, bf16[1,2,2,32,1024]{4,3,2,1,0:T(8,128)(2,1)S(1)}, u32[]{:S(2)}, u32[]{:S(2)}) collective-permute-start(bf16[1,2,2,32,1024]{4,3,2,1,0:T(8,128)(2,1)S(1)} %slice.19), channel_id=1, source_target_pairs={{0,2},{1,3},{2,0},{3,1},{4,6},{5,7},{6,4},{7,5},{8,10},{9,11},{10,... | collective-permute-start | bytes 786440 | tf_op jit(solution)/shard_map/ppermute | solution.py:265
  74.8 11.2 %collective-permute-start.8 = (bf16[1,2,2,32,1024]{4,3,2,1,0:T(8,128)(2,1)S(1)}, bf16[1,2,2,32,1024]{4,3,2,1,0:T(8,128)(2,1)S(1)}, u32[]{:S(2)}, u32[]{:S(2)}) collective-permute-start(bf16[1,2,2,32,1024]{4,3,2,1,0:T(8,128)(2,1)S(1)} %slice.18), channel_id=1, source_target_pairs={{0,4},{1,5},{2,6},{3,7},{4,0},{5,1},{6,2},{7,3},{8,12},{9,13},{10,... | collective-permute-start | bytes 786440 | tf_op jit(solution)/shard_map/ppermute | solution.py:265
  76.2 11.2 %collective-permute-start.17 = (bf16[2,2,2,32,1024]{4,3,2,1,0:T(8,128)(2,1)S(1)}, bf16[2,2,2,32,1024]{4,3,2,1,0:T(8,128)(2,1)S(1)}, u32[]{:S(2)}, u32[]{:S(2)}) collective-permute-start(bf16[2,2,2,32,1024]{4,3,2,1,0:T(8,128)(2,1)S(1)} %collective-permute-done.7.refs_7_), channel_id=1, source_target_pairs={{0,1},{1,0},{2,3},{3,2},{4,5},{5,4},{6,7},{7,6},{8,9},{9,8},{10,11... | collective-permute-start | bytes 1572872 | tf_op jit(solution)/shard_map/ppermute | solution.py:265
  76.2 11.2 %collective-permute-start.16 = (bf16[2,2,2,32,1024]{4,3,2,1,0:T(8,128)(2,1)S(1)}, bf16[2,2,2,32,1024]{4,3,2,1,0:T(8,128)(2,1)S(1)}, u32[]{:S(2)}, u32[]{:S(2)}) collective-permute-start(bf16[2,2,2,32,1024]{4,3,2,1,0:T(8,128)(2,1)S(1)} %copy-done.8), channel_id=1, source_target_pairs={{0,1},{1,0},{2,3},{3,2},{4,5},{5,4},{6,7},{7,6},{8,9},{9,8},{10,11... | collective-permute-start | bytes 1572872 | tf_op jit(solution)/shard_map/ppermute | solution.py:265
  85.3 2.1 %copy-start.14 = (bf16[1,2,2,32,1024]{4,3,2,1,0:T(8,128)(2,1)}, bf16[1,2,2,32,1024]{4,3,2,1,0:T(8,128)(2,1)S(1)}, u32[]{:S(2)}) copy-start(bf16[1,2,2,32,1024]{4,3,2,1,0:T(8,128)(2,1)S(1)} %collective-permute-done.9.refs_9_) | copy-start | bytes 786436
  85.3 1.5 %collective-permute-start.19 = (bf16[1,2,2,32,1024]{4,3,2,1,0:T(8,128)(2,1)S(1)}, bf16[1,2,2,32,1024]{4,3,2,1,0:T(8,128)(2,1)S(1)}, u32[]{:S(2)}, u32[]{:S(2)}) collective-permute-start(bf16[1,2,2,32,1024]{4,3,2,1,0:T(8,128)(2,1)S(1)} %collective-permute-done.9.refs_9_), channel_id=1, source_target_pairs={{0,1},{1,0},{2,3},{3,2},{4,5},{5,4},{6,7},{7,6},{8,9},{9,8},{10,11... | collective-permute-start | bytes 786440 | tf_op jit(solution)/shard_map/ppermute | solution.py:265
  85.9 1.6 %copy-start.15 = (bf16[1,2,2,32,1024]{4,3,2,1,0:T(8,128)(2,1)}, bf16[1,2,2,32,1024]{4,3,2,1,0:T(8,128)(2,1)S(1)}, u32[]{:S(2)}) copy-start(bf16[1,2,2,32,1024]{4,3,2,1,0:T(8,128)(2,1)S(1)} %collective-permute-done.8.refs_8_) | copy-start | bytes 786436
  85.9 1.5 %collective-permute-start.18 = (bf16[1,2,2,32,1024]{4,3,2,1,0:T(8,128)(2,1)S(1)}, bf16[1,2,2,32,1024]{4,3,2,1,0:T(8,128)(2,1)S(1)}, u32[]{:S(2)}, u32[]{:S(2)}) collective-permute-start(bf16[1,2,2,32,1024]{4,3,2,1,0:T(8,128)(2,1)S(1)} %collective-permute-done.8.refs_8_), channel_id=1, source_target_pairs={{0,1},{1,0},{2,3},{3,2},{4,5},{5,4},{6,7},{7,6},{8,9},{9,8},{10,11... | collective-permute-start | bytes 786440 | tf_op jit(solution)/shard_map/ppermute | solution.py:265
  85.9 1.6 %copy-start.9 = (bf16[2,2,2,32,1024]{4,3,2,1,0:T(8,128)(2,1)}, bf16[2,2,2,32,1024]{4,3,2,1,0:T(8,128)(2,1)S(1)}, u32[]{:S(2)}) copy-start(bf16[2,2,2,32,1024]{4,3,2,1,0:T(8,128)(2,1)S(1)} %collective-permute-done.15.refs_15_) | copy-start | bytes 1572868
  100.8 14.7 %all-to-all-start.1 = ((bf16[16,128,128]{2,1,0:T(8,128)(2,1)}), bf16[16,128,128]{2,1,0:T(8,128)(2,1)S(1)}, u32[]{:S(2)}, u32[]{:S(2)}) async-start(bf16[16,128,128]{2,1,0:T(8,128)(2,1)} %bitcast.20), calls=%async_computation.1 | async-start | bytes 1048576 | tf_op jit(solution)/shard_map/all_to_all | solution.py:303
  (9 other events, 7.7 us)

commit v4 on v3

--- a/solution.py
+++ b/solution.py
@@ -26,19 +26,24 @@
     return jnp.dot(left, right, preferred_element_type=jnp.float32)
 
 
-def pack_kernel(side, qs, x_ref, order_ref, o_ref):
+def pack_kernel(qs, x_ref, order_ref, o_ref, ordered):
     _, parts, rows_each, width = x_ref.shape
     rows = parts * rows_each
     step = min(256, width)
-    new = lax.broadcasted_iota(jnp.int32, (rows, rows), 0)
-    e, k, q = new // (parts * qs), new // qs % parts, new % qs
-    pack = one_hot((rows, rows), 1, k * rows_each + e * qs + q)
+    new = lax.broadcasted_iota(jnp.int32, (2 * rows, 2 * rows), 0)
+    e, side = new // (2 * parts * qs), new // (parts * qs) % 2
+    k, q = new // qs % parts, new % qs
+    pack = one_hot((2 * rows, 2 * rows), 1, side * rows + k * rows_each + e * qs + q)
     for pair in range(x_ref.shape[0] // 2):
-        branch = 2 * pair + side
-        packed = exact_dot(pack, x_ref[branch].reshape(rows, width)).astype(jnp.bfloat16)
-        for start in range(0, width, step):
-            picks = one_hot((width, step), 0, order_ref[branch : branch + 1, start : start + step])
-            o_ref[pair * rows : (pair + 1) * rows, start : start + step] = exact_dot(packed, picks).astype(jnp.bfloat16)
+        for side in range(2):
+            branch = 2 * pair + side
+            values = x_ref[branch].reshape(rows, width)
+            for start in range(0, width, step):
+                picks = one_hot((width, step), 0, order_ref[branch : branch + 1, start : start + step])
+                found = exact_dot(values, picks).astype(jnp.bfloat16)
+                ordered[side * rows : (side + 1) * rows, start : start + step] = found
+        packed = exact_dot(pack, ordered[...]).astype(jnp.bfloat16)
+        o_ref[2 * pair * rows : 2 * (pair + 1) * rows, :] = packed
 
 
 def swap_sign(tiles, qs):
@@ -101,8 +106,10 @@
         for copy in copies[gate]:
             copy.start()
     tile_rows = 2 * qs
-    rows, width = x_ref.shape
-    first = x_ref[...].astype(jnp.float32).reshape(devices, tile_rows, width)
+    rows, width = x_ref.shape[0] // 2, x_ref.shape[1]
+    first = x_ref[...].astype(jnp.float32).reshape(devices, 2 * tile_rows, width)
+    first = first[:, :tile_rows] if is_left else first[:, tile_rows:]
+    xs[0] = first.reshape(rows, width).astype(jnp.bfloat16)
     hs[0] = swap_sign(first, qs).reshape(rows, width).astype(jnp.bfloat16)
     step = min(512, width)
     for layer in range(2 * CYCLES):
@@ -110,8 +117,7 @@
             for copy in copies[layer]:
                 copy.wait()
         gate = whole_ref.at[layer % 2]
-        here = x_ref if layer == 0 else xs.at[layer % 2]
-        turned = hs.at[layer % 2]
+        here, turned = xs.at[layer % 2], hs.at[layer % 2]
         later = (layer + 1) % 2
         for start in range(0, width, step):
             cols = slice(start, start + step)
@@ -215,17 +221,15 @@
     qs, group = rows_each // halves, width // devices
     tile_rows = 2 * qs
     rows = devices * tile_rows
-    cut = [
-        call(
-            functools.partial(pack_kernel, side, qs),
-            (rows, width),
-            (branch_in, column_order),
-            flops=2 * rows * width * width,
-        ).reshape(devices, tile_rows, width)
-        for side in range(2)
-    ]
-    blocks, plan, *states = spread(gate_a, gate_b, cut)
-    states = [state.reshape(rows, width) for state in states]
+    packed = call(
+        functools.partial(pack_kernel, qs),
+        (2 * rows, width),
+        (branch_in, column_order),
+        [pltpu.VMEM((4 * rows_each, width), jnp.bfloat16)],
+        8 * rows * width * width,
+    )
+    blocks, plan, states = spread(gate_a, gate_b, packed.reshape(devices, 2 * tile_rows, width))
+    states = states.reshape(2 * rows, width)
     sizes = (devices, qs, group, rows_each)
     scratch = [pltpu.VMEM((2, rows, width), jnp.bfloat16)] * 2 + [
         pltpu.VMEM((rows, width), jnp.bfloat16),
@@ -236,7 +240,7 @@
     left = call(
         functools.partial(layers_kernel, sizes, True, plan),
         (halves * rows // 2, LANES),
-        (states[0],),
+        (states,),
         scratch,
         work,
         blocks,
@@ -244,7 +248,7 @@
     groups = [[h * halves + e for e in range(halves)] for h in range(2)]
     left = trade(left.reshape(halves, rows // 2, LANES), groups)
     right = call(
-        functools.partial(layers_kernel, sizes, False, plan), (rows, width), (states[1],), scratch, work, blocks
+        functools.partial(layers_kernel, sizes, False, plan), (rows, width), (states,), scratch, work, blocks
     )
     free = width // (2 * KEPT)
     us = halves
@@ -260,8 +264,9 @@
     return (jnp.sum(parts, axis=1) * join_scale).astype(jnp.bfloat16).reshape(2, us, 2, free)
 
 
-def flip(value, bit):
-    pairs = [(source, source ^ 2**bit) for source in range(lax.axis_size("mode"))]
+def flip(value, *bits):
+    mask = sum(2**bit for bit in bits)
+    pairs = [(source, source ^ mask) for source in range(lax.axis_size("mode"))]
     return lax.ppermute(value, "mode", pairs)
 
 
@@ -278,25 +283,27 @@
     ]
 
 
-def spread(gate_a, gate_b, cut):
+def spread(gate_a, gate_b, packed):
     bits = lax.axis_size("mode").bit_length() - 1
     own = jnp.stack([gate_a, gate_b])[:, None]
     sets = [(jnp.concatenate([own, flip(own, 3)], axis=1), ((), (3,)))]
     for bit in range(4, bits):
-        sets += [(flip(value, bit), tuple(source + (bit,) for source in sources)) for value, sources in sets]
-    blocks, left = [], cut[0]
+        far = [flip(own, *source, bit) for _, sources in sets for source in sources]
+        if bit == 4:
+            first, far[0], packed = lax.optimization_barrier((sets[0][0], far[0], packed))
+            sets = [(first, sets[0][1])]
+        more = [tuple(source + (bit,) for source in sources) for _, sources in sets]
+        sets += [(jnp.concatenate(far[2 * n : 2 * n + 2], axis=1), sources) for n, sources in enumerate(more)]
+    blocks = []
     for number, (value, sources) in enumerate(sets):
         if number:
-            value, left, *_ = lax.optimization_barrier((value, left, blocks[-2][0], blocks[-1][0]))
+            value, *_ = lax.optimization_barrier((value, blocks[-2][0], blocks[-1][0]))
         blocks += plane(value, sources)
-    left = trade(left)
-    right, *_ = lax.optimization_barrier((cut[1], blocks[-3][0], blocks[-4][0]))
-    right = trade(right)
-    blocks += [
-        (flip(value, 0), tuple(source + (0,) for source in sources), gates) for value, sources, gates in blocks
-    ]
+    near = [(flip(value, 0), tuple(source + (0,) for source in sources), gates) for value, sources, gates in blocks]
+    packed, _ = lax.optimization_barrier((packed, near[-5][0]))
+    blocks += near
     plan = tuple((sources, gates) for _, sources, gates in blocks)
-    return [value for value, _, _ in blocks], plan, left, right
+    return [value for value, _, _ in blocks], plan, trade(packed)
 
 
 def trade(value, groups=None):

time: 137 us -> 133 us (0.971)
  starting transfers between devices: 32.8 us -> 28.1 us
  waiting for transfers between devices: 48.4 us -> 52.3 us
  Pallas kernels: 30.9 us -> 28.8 us
    all_to_all x3 -> x2, starting transfers between devices: 12.6 us -> 8.07 us  [trade(): lax.all_to_all(value, 'mode', split_axis=0, concat_axis=0, axis_index_gro...]
    ppermute x20 -> x21, waiting for transfers between devices: 48.4 us -> 52.2 us  [flip(): return lax.ppermute(value, 'mode', pairs)]
    pallas_call x5 -> x4, Pallas kernels: 30.9 us -> 28.8 us  [call(): pl.pallas_call(kernel, out_shape=jax.ShapeDtypeStruct(out_shape, jnp.bflo...]
    unnamed x36 -> x44, local copies, waits for them, and re-layouts: 5.29 us -> 4.29 us
    ppermute x20 -> x21, starting transfers between devices: 20.2 us -> 20.1 us  [flip(): return lax.ppermute(value, 'mode', pairs)]
  transfers between devices with their start and end apart: 23 -> 23, of which waited for: 8 -> 12; matrix products, arithmetic and copies ran while one was open for 0% -> 0% of each run, Pallas kernels for 21% -> 11%
where the time goes in v4:
time: 133 us; the launch traced here: 132 us
  waiting for transfers between devices  52.3 us (39%)
  Pallas kernels  28.8 us (22%)
  starting transfers between devices  28.1 us (21%)
  blocking collectives  16.5 us (12%)
  local copies, waits for them, and re-layouts  4.98 us (4%)
    ppermute x21, waiting for transfers between devices, flip(): return lax.ppermute(value, 'mode', pairs)  52.2 us
    pallas_call x4, Pallas kernels, call(): pl.pallas_call(kernel, out_shape=jax.ShapeDtypeStruct(out_shape, jnp.bflo...  28.8 us
    ppermute x21, starting transfers between devices, flip(): return lax.ppermute(value, 'mode', pairs)  20.1 us
    all_to_all x1, blocking collectives, trade(): lax.all_to_all(value, 'mode', split_axis=0, concat_axis=0, axis_index_gro...  16.5 us
    all_to_all x2, starting transfers between devices, trade(): lax.all_to_all(value, 'mode', split_axis=0, concat_axis=0, axis_index_gro...  8.07 us
    unnamed x44, local copies, waits for them, and re-layouts  4.29 us
  transfers between devices with their start and end apart: 23, of which 12 were waited for; matrix products, arithmetic and copies ran while one was open for 0% of the time, Pallas kernels for 11%

profile of v4, /device:TPU:0, one launch (start us, length us, event | category | flops | bytes accessed | tf_op | source)
XLA Modules:
  0.0 132.1 jit_solution(11487108460137019688)
XLA Ops:
  0.0 1.0 maximum_bitcast_fusion
  1.0 3.1 %collective-permute-start = (bf16[2,1,2,32,1024]{4,3,2,1,0:T(8,128)(2,1)S(1)}, bf16[2,1,2,32,1024]{4,3,2,1,0:T(8,128)(2,1)S(1)}, u32[]{:S(2)}, u32[]{:S(2)}) collective-permute-start(bf16[2,1,2,32,1024]{4,3,2,1,0:T(8,128)(2,1)S(1)} %maximum_bitcast_fusion), channel_id=1, source_target_pairs={{0,8},{1,9},{2,10},{3,11},{4,12},{5,13},{6,14},{7,15},{8,0},{9,1},... | collective-permute-start | bytes 786440 | tf_op jit(solution)/shard_map/ppermute | solution.py:270
  4.1 2.6 %collective-permute-start.1 = (bf16[2,1,2,32,1024]{4,3,2,1,0:T(8,128)(2,1)S(1)}, bf16[2,1,2,32,1024]{4,3,2,1,0:T(8,128)(2,1)S(1)}, u32[]{:S(2)}, u32[]{:S(2)}) collective-permute-start(bf16[2,1,2,32,1024]{4,3,2,1,0:T(8,128)(2,1)S(1)} %maximum_bitcast_fusion), channel_id=1, source_target_pairs={{0,16},{1,17},{2,18},{3,19},{4,20},{5,21},{6,22},{7,23},{8,24},{9,... | collective-permute-start | bytes 786440 | tf_op jit(solution)/shard_map/ppermute | solution.py:270
  6.7 4.0 %shard_map.46 = bf16[512,1024]{1,0:T(8,128)(2,1)} custom-call(bf16[4,2,64,1024]{3,2,1,0:T(8,128)(2,1)} %x_ref.1, s32[4,1024]{1,0:T(4,128)} %order_ref.1), custom_call_target="tpu_custom_call" | custom-call | flops 2147483648 | bytes 1064960 | tf_op jit(solution)/shard_map/pallas_call | solution.py:189
  10.7 5.2 %collective-permute-done = bf16[2,1,2,32,1024]{4,3,2,1,0:T(8,128)(2,1)S(1)} collective-permute-done((bf16[2,1,2,32,1024]{4,3,2,1,0:T(8,128)(2,1)S(1)}, bf16[2,1,2,32,1024]{4,3,2,1,0:T(8,128)(2,1)S(1)}, u32[]{:S(2)}, u32[]{:S(2)}) %collective-permute-start) | collective-permute-done | bytes 262176 | tf_op jit(solution)/shard_map/ppermute | solution.py:270
  16.0 2.5 %collective-permute-done.1 = bf16[2,1,2,32,1024]{4,3,2,1,0:T(8,128)(2,1)S(1)} collective-permute-done((bf16[2,1,2,32,1024]{4,3,2,1,0:T(8,128)(2,1)S(1)}, bf16[2,1,2,32,1024]{4,3,2,1,0:T(8,128)(2,1)S(1)}, u32[]{:S(2)}, u32[]{:S(2)}) %collective-permute-start.1) | collective-permute-done | bytes 262176 | tf_op jit(solution)/shard_map/ppermute | solution.py:270
  18.4 1.5 %collective-permute-start.5 = (bf16[2,2,2,32,1024]{4,3,2,1,0:T(8,128)(2,1)S(1)}, bf16[2,2,2,32,1024]{4,3,2,1,0:T(8,128)(2,1)S(1)}, u32[]{:S(2)}, u32[]{:S(2)}) collective-permute-start(bf16[2,2,2,32,1024]{4,3,2,1,0:T(8,128)(2,1)S(1)} %pad_maximum_fusion.refs_0_), channel_id=1, source_target_pairs={{0,4},{1,5},{2,6},{3,7},{4,0},{5,1},{6,2},{7,3},{8,12},{9,13},{10,... | collective-permute-start | bytes 1572872 | tf_op jit(solution)/shard_map/ppermute | solution.py:270
  19.9 1.5 %collective-permute-start.3 = (bf16[2,2,2,32,1024]{4,3,2,1,0:T(8,128)(2,1)S(1)}, bf16[2,2,2,32,1024]{4,3,2,1,0:T(8,128)(2,1)S(1)}, u32[]{:S(2)}, u32[]{:S(2)}) collective-permute-start(bf16[2,2,2,32,1024]{4,3,2,1,0:T(8,128)(2,1)S(1)} %pad_maximum_fusion.refs_0_), channel_id=1, source_target_pairs={{0,2},{1,3},{2,0},{3,1},{4,6},{5,7},{6,4},{7,5},{8,10},{9,11},{10,... | collective-permute-start | bytes 1572872 | tf_op jit(solution)/shard_map/ppermute | solution.py:270
  21.4 2.5 %collective-permute-start.2 = (bf16[2,1,2,32,1024]{4,3,2,1,0:T(8,128)(2,1)S(1)}, bf16[2,1,2,32,1024]{4,3,2,1,0:T(8,128)(2,1)S(1)}, u32[]{:S(2)}, u32[]{:S(2)}) collective-permute-start(bf16[2,1,2,32,1024]{4,3,2,1,0:T(8,128)(2,1)S(1)} %maximum_bitcast_fusion), channel_id=1, source_target_pairs={{0,24},{1,25},{2,26},{3,27},{4,28},{5,29},{6,30},{7,31},{8,16},{9,... | collective-permute-start | bytes 786440 | tf_op jit(solution)/shard_map/ppermute | solution.py:270
  23.9 5.5 %collective-permute-done.5.refs_2_ = bf16[2,2,2,32,1024]{4,3,2,1,0:T(8,128)(2,1)S(1)} collective-permute-done((bf16[2,2,2,32,1024]{4,3,2,1,0:T(8,128)(2,1)S(1)}, bf16[2,2,2,32,1024]{4,3,2,1,0:T(8,128)(2,1)S(1)}, u32[]{:S(2)}, u32[]{:S(2)}) %collective-permute-start.5) | collective-permute-done | bytes 524320 | tf_op jit(solution)/shard_map/ppermute | solution.py:270
  29.4 1.6 %collective-permute-start.6 = (bf16[1,2,2,32,1024]{4,3,2,1,0:T(8,128)(2,1)S(1)}, bf16[1,2,2,32,1024]{4,3,2,1,0:T(8,128)(2,1)S(1)}, u32[]{:S(2)}, u32[]{:S(2)}) collective-permute-start(bf16[1,2,2,32,1024]{4,3,2,1,0:T(8,128)(2,1)S(1)} %slice.17), channel_id=1, source_target_pairs={{0,2},{1,3},{2,0},{3,1},{4,6},{5,7},{6,4},{7,5},{8,10},{9,11},{10,... | collective-permute-start | bytes 786440 | tf_op jit(solution)/shard_map/ppermute | solution.py:270
  31.0 1.6 %collective-permute-done.3.refs_1_ = bf16[2,2,2,32,1024]{4,3,2,1,0:T(8,128)(2,1)S(1)} collective-permute-done((bf16[2,2,2,32,1024]{4,3,2,1,0:T(8,128)(2,1)S(1)}, bf16[2,2,2,32,1024]{4,3,2,1,0:T(8,128)(2,1)S(1)}, u32[]{:S(2)}, u32[]{:S(2)}) %collective-permute-start.3) | collective-permute-done | bytes 524320 | tf_op jit(solution)/shard_map/ppermute | solution.py:270
  33.3 2.6 %collective-permute-done.6.refs_4_ = bf16[1,2,2,32,1024]{4,3,2,1,0:T(8,128)(2,1)S(1)} collective-permute-done((bf16[1,2,2,32,1024]{4,3,2,1,0:T(8,128)(2,1)S(1)}, bf16[1,2,2,32,1024]{4,3,2,1,0:T(8,128)(2,1)S(1)}, u32[]{:S(2)}, u32[]{:S(2)}) %collective-permute-start.6) | collective-permute-done | bytes 262176 | tf_op jit(solution)/shard_map/ppermute | solution.py:270
  35.9 3.2 %collective-permute-done.4.refs_3_ = bf16[1,2,2,32,1024]{4,3,2,1,0:T(8,128)(2,1)S(1)} collective-permute-done((bf16[1,2,2,32,1024]{4,3,2,1,0:T(8,128)(2,1)S(1)}, bf16[1,2,2,32,1024]{4,3,2,1,0:T(8,128)(2,1)S(1)}, u32[]{:S(2)}, u32[]{:S(2)}) %collective-permute-start.4) | collective-permute-done | bytes 262176 | tf_op jit(solution)/shard_map/ppermute | solution.py:270
  39.1 0.7 copy-done.15
  39.8 1.9 %collective-permute-done.7.refs_15_ = bf16[2,2,2,32,1024]{4,3,2,1,0:T(8,128)(2,1)S(1)} collective-permute-done((bf16[2,2,2,32,1024]{4,3,2,1,0:T(8,128)(2,1)S(1)}, bf16[2,2,2,32,1024]{4,3,2,1,0:T(8,128)(2,1)S(1)}, u32[]{:S(2)}, u32[]{:S(2)}) %collective-permute-start.7) | collective-permute-done | bytes 524320 | tf_op jit(solution)/shard_map/ppermute | solution.py:270
  41.7 0.8 copy-done.8
  42.5 4.1 %all-to-all-start = ((bf16[32,16,1024]{2,1,0:T(8,128)(2,1)}), bf16[32,16,1024]{2,1,0:T(8,128)(2,1)S(1)}, u32[]{:S(2)}, u32[]{:S(2)}) async-start(bf16[32,16,1024]{2,1,0:T(8,128)(2,1)} %bitcast.3), calls=%async_computation | async-start | bytes 2097152 | tf_op jit(solution)/shard_map/all_to_all | solution.py:310
  46.5 1.8 %collective-permute-start.9 = (bf16[2,2,2,32,1024]{4,3,2,1,0:T(8,128)(2,1)S(1)}, bf16[2,2,2,32,1024]{4,3,2,1,0:T(8,128)(2,1)S(1)}, u32[]{:S(2)}, u32[]{:S(2)}) collective-permute-start(bf16[2,2,2,32,1024]{4,3,2,1,0:T(8,128)(2,1)S(1)} %pad_maximum_fusion.1.refs_5_), channel_id=1, source_target_pairs={{0,4},{1,5},{2,6},{3,7},{4,0},{5,1},{6,2},{7,3},{8,12},{9,13},{10,... | collective-permute-start | bytes 1572872 | tf_op jit(solution)/shard_map/ppermute | solution.py:270
  48.4 1.5 %collective-permute-start.8 = (bf16[2,2,2,32,1024]{4,3,2,1,0:T(8,128)(2,1)S(1)}, bf16[2,2,2,32,1024]{4,3,2,1,0:T(8,128)(2,1)S(1)}, u32[]{:S(2)}, u32[]{:S(2)}) collective-permute-start(bf16[2,2,2,32,1024]{4,3,2,1,0:T(8,128)(2,1)S(1)} %pad_maximum_fusion.1.refs_5_), channel_id=1, source_target_pairs={{0,2},{1,3},{2,0},{3,1},{4,6},{5,7},{6,4},{7,5},{8,10},{9,11},{10,... | collective-permute-start | bytes 1572872 | tf_op jit(solution)/shard_map/ppermute | solution.py:270
  50.4 21.3 %collective-permute-done.9.refs_7_ = bf16[2,2,2,32,1024]{4,3,2,1,0:T(8,128)(2,1)S(1)} collective-permute-done((bf16[2,2,2,32,1024]{4,3,2,1,0:T(8,128)(2,1)S(1)}, bf16[2,2,2,32,1024]{4,3,2,1,0:T(8,128)(2,1)S(1)}, u32[]{:S(2)}, u32[]{:S(2)}) %collective-permute-start.9) | collective-permute-done | bytes 524320 | tf_op jit(solution)/shard_map/ppermute | solution.py:270
  72.4 1.4 %collective-permute-start.11 = (bf16[1,2,2,32,1024]{4,3,2,1,0:T(8,128)(2,1)S(1)}, bf16[1,2,2,32,1024]{4,3,2,1,0:T(8,128)(2,1)S(1)}, u32[]{:S(2)}, u32[]{:S(2)}) collective-permute-start(bf16[1,2,2,32,1024]{4,3,2,1,0:T(8,128)(2,1)S(1)} %slice.19), channel_id=1, source_target_pairs={{0,2},{1,3},{2,0},{3,1},{4,6},{5,7},{6,4},{7,5},{8,10},{9,11},{10,... | collective-permute-start | bytes 786440 | tf_op jit(solution)/shard_map/ppermute | solution.py:270
  74.6 6.0 %collective-permute-done.11.refs_9_ = bf16[1,2,2,32,1024]{4,3,2,1,0:T(8,128)(2,1)S(1)} collective-permute-done((bf16[1,2,2,32,1024]{4,3,2,1,0:T(8,128)(2,1)S(1)}, bf16[1,2,2,32,1024]{4,3,2,1,0:T(8,128)(2,1)S(1)}, u32[]{:S(2)}, u32[]{:S(2)}) %collective-permute-start.11) | collective-permute-done | bytes 262176 | tf_op jit(solution)/shard_map/ppermute | solution.py:270
  80.7 1.0 collective-permute-done.10.refs_8_
  82.2 1.0 collective-permute-done.19.refs_18_
  84.0 0.8 copy-done.12
  85.3 11.5 %shard_map.47 = bf16[2048,128]{1,0:T(8,128)(2,1)} custom-call(bf16[512,1024]{1,0:T(8,128)(2,1)} %bitcast.14, bf16[2,2,2,32,1024]{4,3,2,1,0:T(8,128)(2,1)} %copy-done.2, bf16[2,2,2,32,1024]{4,3,2,1,0:T(8,128)(2,1)} %copy-done.5, bf16[2,2,2,32,1024]{4,3,2,1,0:T(8,128)(2,1)} %copy-done.4, bf16[1,2,2,32,1024]{4,3,2,1,0:T(8,128)(2,1)} %copy-done.15, ...), custom_call_target="tpu_custom_call" | custom-call | flops 4294967296 | bytes 9437184 | tf_op jit(solution)/shard_map/pallas_call | solution.py:189
  96.8 4.0 %all-to-all-start.1 = ((bf16[16,128,128]{2,1,0:T(8,128)(2,1)}), bf16[16,128,128]{2,1,0:T(8,128)(2,1)S(1)}, u32[]{:S(2)}, u32[]{:S(2)}) async-start(bf16[16,128,128]{2,1,0:T(8,128)(2,1)} %bitcast.16), calls=%async_computation.1 | async-start | bytes 1048576 | tf_op jit(solution)/shard_map/all_to_all | solution.py:310
  100.8 10.8 %shard_map.48.right_ref = bf16[256,1024]{1,0:T(8,128)(2,1)} custom-call(bf16[512,1024]{1,0:T(8,128)(2,1)} %bitcast.15, bf16[2,2,2,32,1024]{4,3,2,1,0:T(8,128)(2,1)} %copy-done.2, bf16[2,2,2,32,1024]{4,3,2,1,0:T(8,128)(2,1)} %copy-done.5, bf16[2,2,2,32,1024]{4,3,2,1,0:T(8,128)(2,1)} %copy-done.4, bf16[1,2,2,32,1024]{4,3,2,1,0:T(8,128)(2,1)} %copy-done.15, ...), custom_call_target="tpu_custom_call" | custom-call | flops 4294967296 | bytes 9437184 | tf_op jit(solution)/shard_map/pallas_call | solution.py:189
  111.6 0.8 copy-done
  112.4 2.5 %shard_map.49 = bf16[512,256]{1,0:T(8,128)(2,1)} custom-call(bf16[2048,128]{1,0:T(8,128)(2,1)} %bitcast.12, bf16[256,1024]{1,0:T(8,128)(2,1)} %shard_map.48.right_ref), custom_call_target="tpu_custom_call" | custom-call | flops 134217728 | bytes 1048576 | tf_op jit(solution)/shard_map/pallas_call | solution.py:189
  114.9 16.5 %all_to_all.15 = bf16[32,16,256]{2,1,0:T(8,128)(2,1)S(1)} all-to-all(bf16[32,16,256]{2,1,0:T(8,128)(2,1)} %bitcast.13), channel_id=1, replica_groups=mesh['cuts'=1,'mode'=32] {'mode'}, dimensions={0} | all-to-all | bytes 524288 | tf_op jit(solution)/shard_map/all_to_all | solution.py:310
  (73 shorter events, 5.2 us)
Async XLA Ops:
  1.0 14.9 %collective-permute-start = (bf16[2,1,2,32,1024]{4,3,2,1,0:T(8,128)(2,1)S(1)}, bf16[2,1,2,32,1024]{4,3,2,1,0:T(8,128)(2,1)S(1)}, u32[]{:S(2)}, u32[]{:S(2)}) collective-permute-start(bf16[2,1,2,32,1024]{4,3,2,1,0:T(8,128)(2,1)S(1)} %maximum_bitcast_fusion), channel_id=1, source_target_pairs={{0,8},{1,9},{2,10},{3,11},{4,12},{5,13},{6,14},{7,15},{8,0},{9,1},... | collective-permute-start | bytes 786440 | tf_op jit(solution)/shard_map/ppermute | solution.py:270
  4.1 14.3 %collective-permute-start.1 = (bf16[2,1,2,32,1024]{4,3,2,1,0:T(8,128)(2,1)S(1)}, bf16[2,1,2,32,1024]{4,3,2,1,0:T(8,128)(2,1)S(1)}, u32[]{:S(2)}, u32[]{:S(2)}) collective-permute-start(bf16[2,1,2,32,1024]{4,3,2,1,0:T(8,128)(2,1)S(1)} %maximum_bitcast_fusion), channel_id=1, source_target_pairs={{0,16},{1,17},{2,18},{3,19},{4,20},{5,21},{6,22},{7,23},{8,24},{9,... | collective-permute-start | bytes 786440 | tf_op jit(solution)/shard_map/ppermute | solution.py:270
  15.9 33.9 %copy-start.2 = (bf16[2,2,2,32,1024]{4,3,2,1,0:T(8,128)(2,1)}, bf16[2,2,2,32,1024]{4,3,2,1,0:T(8,128)(2,1)S(1)}, u32[]{:S(2)}) copy-start(bf16[2,2,2,32,1024]{4,3,2,1,0:T(8,128)(2,1)S(1)} %pad_maximum_fusion.refs_0_) | copy-start | bytes 1572868
  18.4 11.0 %collective-permute-start.5 = (bf16[2,2,2,32,1024]{4,3,2,1,0:T(8,128)(2,1)S(1)}, bf16[2,2,2,32,1024]{4,3,2,1,0:T(8,128)(2,1)S(1)}, u32[]{:S(2)}, u32[]{:S(2)}) collective-permute-start(bf16[2,2,2,32,1024]{4,3,2,1,0:T(8,128)(2,1)S(1)} %pad_maximum_fusion.refs_0_), channel_id=1, source_target_pairs={{0,4},{1,5},{2,6},{3,7},{4,0},{5,1},{6,2},{7,3},{8,12},{9,13},{10,... | collective-permute-start | bytes 1572872 | tf_op jit(solution)/shard_map/ppermute | solution.py:270
  19.9 12.7 %collective-permute-start.3 = (bf16[2,2,2,32,1024]{4,3,2,1,0:T(8,128)(2,1)S(1)}, bf16[2,2,2,32,1024]{4,3,2,1,0:T(8,128)(2,1)S(1)}, u32[]{:S(2)}, u32[]{:S(2)}) collective-permute-start(bf16[2,2,2,32,1024]{4,3,2,1,0:T(8,128)(2,1)S(1)} %pad_maximum_fusion.refs_0_), channel_id=1, source_target_pairs={{0,2},{1,3},{2,0},{3,1},{4,6},{5,7},{6,4},{7,5},{8,10},{9,11},{10,... | collective-permute-start | bytes 1572872 | tf_op jit(solution)/shard_map/ppermute | solution.py:270
  21.4 11.8 %collective-permute-start.2 = (bf16[2,1,2,32,1024]{4,3,2,1,0:T(8,128)(2,1)S(1)}, bf16[2,1,2,32,1024]{4,3,2,1,0:T(8,128)(2,1)S(1)}, u32[]{:S(2)}, u32[]{:S(2)}) collective-permute-start(bf16[2,1,2,32,1024]{4,3,2,1,0:T(8,128)(2,1)S(1)} %maximum_bitcast_fusion), channel_id=1, source_target_pairs={{0,24},{1,25},{2,26},{3,27},{4,28},{5,29},{6,30},{7,31},{8,16},{9,... | collective-permute-start | bytes 786440 | tf_op jit(solution)/shard_map/ppermute | solution.py:270
  29.4 20.4 %copy-start.4 = (bf16[2,2,2,32,1024]{4,3,2,1,0:T(8,128)(2,1)}, bf16[2,2,2,32,1024]{4,3,2,1,0:T(8,128)(2,1)S(1)}, u32[]{:S(2)}) copy-start(bf16[2,2,2,32,1024]{4,3,2,1,0:T(8,128)(2,1)S(1)} %collective-permute-done.5.refs_2_) | copy-start | bytes 1572868
  29.4 6.4 %collective-permute-start.6 = (bf16[1,2,2,32,1024]{4,3,2,1,0:T(8,128)(2,1)S(1)}, bf16[1,2,2,32,1024]{4,3,2,1,0:T(8,128)(2,1)S(1)}, u32[]{:S(2)}, u32[]{:S(2)}) collective-permute-start(bf16[1,2,2,32,1024]{4,3,2,1,0:T(8,128)(2,1)S(1)} %slice.17), channel_id=1, source_target_pairs={{0,2},{1,3},{2,0},{3,1},{4,6},{5,7},{6,4},{7,5},{8,10},{9,11},{10,... | collective-permute-start | bytes 786440 | tf_op jit(solution)/shard_map/ppermute | solution.py:270
  32.6 39.1 %copy-start.5 = (bf16[2,2,2,32,1024]{4,3,2,1,0:T(8,128)(2,1)}, bf16[2,2,2,32,1024]{4,3,2,1,0:T(8,128)(2,1)S(1)}, u32[]{:S(2)}) copy-start(bf16[2,2,2,32,1024]{4,3,2,1,0:T(8,128)(2,1)S(1)} %collective-permute-done.3.refs_1_) | copy-start | bytes 1572868
  32.6 6.4 %collective-permute-start.4 = (bf16[1,2,2,32,1024]{4,3,2,1,0:T(8,128)(2,1)S(1)}, bf16[1,2,2,32,1024]{4,3,2,1,0:T(8,128)(2,1)S(1)}, u32[]{:S(2)}, u32[]{:S(2)}) collective-permute-start(bf16[1,2,2,32,1024]{4,3,2,1,0:T(8,128)(2,1)S(1)} %slice.16), channel_id=1, source_target_pairs={{0,4},{1,5},{2,6},{3,7},{4,0},{5,1},{6,2},{7,3},{8,12},{9,13},{10,... | collective-permute-start | bytes 786440 | tf_op jit(solution)/shard_map/ppermute | solution.py:270
  33.3 15.1 %copy-start.3 = (bf16[2,2,2,32,1024]{4,3,2,1,0:T(8,128)(2,1)}, bf16[2,2,2,32,1024]{4,3,2,1,0:T(8,128)(2,1)S(1)}, u32[]{:S(2)}) copy-start(bf16[2,2,2,32,1024]{4,3,2,1,0:T(8,128)(2,1)S(1)} %pad_maximum_fusion.1.refs_5_) | copy-start | bytes 1572868
  35.9 14.5 %copy-start.14 = (bf16[1,2,2,32,1024]{4,3,2,1,0:T(8,128)(2,1)}, bf16[1,2,2,32,1024]{4,3,2,1,0:T(8,128)(2,1)S(1)}, u32[]{:S(2)}) copy-start(bf16[1,2,2,32,1024]{4,3,2,1,0:T(8,128)(2,1)S(1)} %collective-permute-done.6.refs_4_) | copy-start | bytes 786436
  39.8 1.9 %collective-permute-start.7 = (bf16[2,2,2,32,1024]{4,3,2,1,0:T(8,128)(2,1)S(1)}, bf16[2,2,2,32,1024]{4,3,2,1,0:T(8,128)(2,1)S(1)}, u32[]{:S(2)}, u32[]{:S(2)}) collective-permute-start(bf16[2,2,2,32,1024]{4,3,2,1,0:T(8,128)(2,1)S(1)} %pad_maximum_fusion.1.refs_5_), channel_id=1, source_target_pairs={{0,1},{1,0},{2,3},{3,2},{4,5},{5,4},{6,7},{7,6},{8,9},{9,8},{10,11... | collective-permute-start | bytes 1572872 | tf_op jit(solution)/shard_map/ppermute | solution.py:270
  42.5 41.5 %all-to-all-start = ((bf16[32,16,1024]{2,1,0:T(8,128)(2,1)}), bf16[32,16,1024]{2,1,0:T(8,128)(2,1)S(1)}, u32[]{:S(2)}, u32[]{:S(2)}) async-start(bf16[32,16,1024]{2,1,0:T(8,128)(2,1)} %bitcast.3), calls=%async_computation | async-start | bytes 2097152 | tf_op jit(solution)/shard_map/all_to_all | solution.py:310
  46.5 25.1 %collective-permute-start.9 = (bf16[2,2,2,32,1024]{4,3,2,1,0:T(8,128)(2,1)S(1)}, bf16[2,2,2,32,1024]{4,3,2,1,0:T(8,128)(2,1)S(1)}, u32[]{:S(2)}, u32[]{:S(2)}) collective-permute-start(bf16[2,2,2,32,1024]{4,3,2,1,0:T(8,128)(2,1)S(1)} %pad_maximum_fusion.1.refs_5_), channel_id=1, source_target_pairs={{0,4},{1,5},{2,6},{3,7},{4,0},{5,1},{6,2},{7,3},{8,12},{9,13},{10,... | collective-permute-start | bytes 1572872 | tf_op jit(solution)/shard_map/ppermute | solution.py:270
  48.4 23.3 %collective-permute-start.8 = (bf16[2,2,2,32,1024]{4,3,2,1,0:T(8,128)(2,1)S(1)}, bf16[2,2,2,32,1024]{4,3,2,1,0:T(8,128)(2,1)S(1)}, u32[]{:S(2)}, u32[]{:S(2)}) collective-permute-start(bf16[2,2,2,32,1024]{4,3,2,1,0:T(8,128)(2,1)S(1)} %pad_maximum_fusion.1.refs_5_), channel_id=1, source_target_pairs={{0,2},{1,3},{2,0},{3,1},{4,6},{5,7},{6,4},{7,5},{8,10},{9,11},{10,... | collective-permute-start | bytes 1572872 | tf_op jit(solution)/shard_map/ppermute | solution.py:270
  49.8 22.5 %collective-permute-start.12 = (bf16[2,2,2,32,1024]{4,3,2,1,0:T(8,128)(2,1)S(1)}, bf16[2,2,2,32,1024]{4,3,2,1,0:T(8,128)(2,1)S(1)}, u32[]{:S(2)}, u32[]{:S(2)}) collective-permute-start(bf16[2,2,2,32,1024]{4,3,2,1,0:T(8,128)(2,1)S(1)} %pad_maximum_fusion.refs_0_), channel_id=1, source_target_pairs={{0,1},{1,0},{2,3},{3,2},{4,5},{5,4},{6,7},{7,6},{8,9},{9,8},{10,11... | collective-permute-start | bytes 1572872 | tf_op jit(solution)/shard_map/ppermute | solution.py:270
  49.9 24.2 %collective-permute-start.14 = (bf16[2,2,2,32,1024]{4,3,2,1,0:T(8,128)(2,1)S(1)}, bf16[2,2,2,32,1024]{4,3,2,1,0:T(8,128)(2,1)S(1)}, u32[]{:S(2)}, u32[]{:S(2)}) collective-permute-start(bf16[2,2,2,32,1024]{4,3,2,1,0:T(8,128)(2,1)S(1)} %collective-permute-done.5.refs_2_), channel_id=1, source_target_pairs={{0,1},{1,0},{2,3},{3,2},{4,5},{5,4},{6,7},{7,6},{8,9},{9,8},{10,11... | collective-permute-start | bytes 1572872 | tf_op jit(solution)/shard_map/ppermute | solution.py:270
  50.4 23.4 %collective-permute-start.16 = (bf16[1,2,2,32,1024]{4,3,2,1,0:T(8,128)(2,1)S(1)}, bf16[1,2,2,32,1024]{4,3,2,1,0:T(8,128)(2,1)S(1)}, u32[]{:S(2)}, u32[]{:S(2)}) collective-permute-start(bf16[1,2,2,32,1024]{4,3,2,1,0:T(8,128)(2,1)S(1)} %collective-permute-done.6.refs_4_), channel_id=1, source_target_pairs={{0,1},{1,0},{2,3},{3,2},{4,5},{5,4},{6,7},{7,6},{8,9},{9,8},{10,11... | collective-permute-start | bytes 786440 | tf_op jit(solution)/shard_map/ppermute | solution.py:270
  71.7 2.4 %collective-permute-start.15 = (bf16[1,2,2,32,1024]{4,3,2,1,0:T(8,128)(2,1)}, bf16[1,2,2,32,1024]{4,3,2,1,0:T(8,128)(2,1)S(1)}, u32[]{:S(2)}, u32[]{:S(2)}) collective-permute-start(bf16[1,2,2,32,1024]{4,3,2,1,0:T(8,128)(2,1)} %copy-done.15), channel_id=1, source_target_pairs={{0,1},{1,0},{2,3},{3,2},{4,5},{5,4},{6,7},{7,6},{8,9},{9,8},{10,11... | collective-permute-start | bytes 786440 | tf_op jit(solution)/shard_map/ppermute | solution.py:270
  71.7 11.5 %copy-start.7 = (bf16[2,2,2,32,1024]{4,3,2,1,0:T(8,128)(2,1)}, bf16[2,2,2,32,1024]{4,3,2,1,0:T(8,128)(2,1)S(1)}, u32[]{:S(2)}) copy-start(bf16[2,2,2,32,1024]{4,3,2,1,0:T(8,128)(2,1)S(1)} %collective-permute-done.8.refs_6_) | copy-start | bytes 1572868
  71.7 9.9 %collective-permute-start.13 = (bf16[2,2,2,32,1024]{4,3,2,1,0:T(8,128)(2,1)S(1)}, bf16[2,2,2,32,1024]{4,3,2,1,0:T(8,128)(2,1)S(1)}, u32[]{:S(2)}, u32[]{:S(2)}) collective-permute-start(bf16[2,2,2,32,1024]{4,3,2,1,0:T(8,128)(2,1)S(1)} %collective-permute-done.3.refs_1_), channel_id=1, source_target_pairs={{0,1},{1,0},{2,3},{3,2},{4,5},{5,4},{6,7},{7,6},{8,9},{9,8},{10,11... | collective-permute-start | bytes 1572872 | tf_op jit(solution)/shard_map/ppermute | solution.py:270
  72.4 10.9 %copy-start.9 = (bf16[2,2,2,32,1024]{4,3,2,1,0:T(8,128)(2,1)}, bf16[2,2,2,32,1024]{4,3,2,1,0:T(8,128)(2,1)S(1)}, u32[]{:S(2)}) copy-start(bf16[2,2,2,32,1024]{4,3,2,1,0:T(8,128)(2,1)S(1)} %collective-permute-done.12.refs_10_) | copy-start | bytes 1572868
  72.4 8.3 %collective-permute-start.11 = (bf16[1,2,2,32,1024]{4,3,2,1,0:T(8,128)(2,1)S(1)}, bf16[1,2,2,32,1024]{4,3,2,1,0:T(8,128)(2,1)S(1)}, u32[]{:S(2)}, u32[]{:S(2)}) collective-permute-start(bf16[1,2,2,32,1024]{4,3,2,1,0:T(8,128)(2,1)S(1)} %slice.19), channel_id=1, source_target_pairs={{0,2},{1,3},{2,0},{3,1},{4,6},{5,7},{6,4},{7,5},{8,10},{9,11},{10,... | collective-permute-start | bytes 786440 | tf_op jit(solution)/shard_map/ppermute | solution.py:270
  73.7 9.5 %copy-start.16 = (bf16[1,2,2,32,1024]{4,3,2,1,0:T(8,128)(2,1)}, bf16[1,2,2,32,1024]{4,3,2,1,0:T(8,128)(2,1)S(1)}, u32[]{:S(2)}) copy-start(bf16[1,2,2,32,1024]{4,3,2,1,0:T(8,128)(2,1)S(1)} %collective-permute-done.16.refs_14_) | copy-start | bytes 786436
  73.7 8.0 %collective-permute-start.10 = (bf16[1,2,2,32,1024]{4,3,2,1,0:T(8,128)(2,1)S(1)}, bf16[1,2,2,32,1024]{4,3,2,1,0:T(8,128)(2,1)S(1)}, u32[]{:S(2)}, u32[]{:S(2)}) collective-permute-start(bf16[1,2,2,32,1024]{4,3,2,1,0:T(8,128)(2,1)S(1)} %slice.18), channel_id=1, source_target_pairs={{0,4},{1,5},{2,6},{3,7},{4,0},{5,1},{6,2},{7,3},{8,12},{9,13},{10,... | collective-permute-start | bytes 786440 | tf_op jit(solution)/shard_map/ppermute | solution.py:270
  74.0 9.2 %copy-start.10 = (bf16[2,2,2,32,1024]{4,3,2,1,0:T(8,128)(2,1)}, bf16[2,2,2,32,1024]{4,3,2,1,0:T(8,128)(2,1)S(1)}, u32[]{:S(2)}) copy-start(bf16[2,2,2,32,1024]{4,3,2,1,0:T(8,128)(2,1)S(1)} %collective-permute-done.14.refs_12_) | copy-start | bytes 1572868
  74.0 9.2 %collective-permute-start.18 = (bf16[2,2,2,32,1024]{4,3,2,1,0:T(8,128)(2,1)S(1)}, bf16[2,2,2,32,1024]{4,3,2,1,0:T(8,128)(2,1)S(1)}, u32[]{:S(2)}, u32[]{:S(2)}) collective-permute-start(bf16[2,2,2,32,1024]{4,3,2,1,0:T(8,128)(2,1)S(1)} %collective-permute-done.9.refs_7_), channel_id=1, source_target_pairs={{0,1},{1,0},{2,3},{3,2},{4,5},{5,4},{6,7},{7,6},{8,9},{9,8},{10,11... | collective-permute-start | bytes 1572872 | tf_op jit(solution)/shard_map/ppermute | solution.py:270
  74.1 9.8 %collective-permute-start.17 = (bf16[2,2,2,32,1024]{4,3,2,1,0:T(8,128)(2,1)S(1)}, bf16[2,2,2,32,1024]{4,3,2,1,0:T(8,128)(2,1)S(1)}, u32[]{:S(2)}, u32[]{:S(2)}) collective-permute-start(bf16[2,2,2,32,1024]{4,3,2,1,0:T(8,128)(2,1)S(1)} %collective-permute-done.8.refs_6_), channel_id=1, source_target_pairs={{0,1},{1,0},{2,3},{3,2},{4,5},{5,4},{6,7},{7,6},{8,9},{9,8},{10,11... | collective-permute-start | bytes 1572872 | tf_op jit(solution)/shard_map/ppermute | solution.py:270
  80.7 1.5 %collective-permute-start.20 = (bf16[1,2,2,32,1024]{4,3,2,1,0:T(8,128)(2,1)S(1)}, bf16[1,2,2,32,1024]{4,3,2,1,0:T(8,128)(2,1)S(1)}, u32[]{:S(2)}, u32[]{:S(2)}) collective-permute-start(bf16[1,2,2,32,1024]{4,3,2,1,0:T(8,128)(2,1)S(1)} %collective-permute-done.11.refs_9_), channel_id=1, source_target_pairs={{0,1},{1,0},{2,3},{3,2},{4,5},{5,4},{6,7},{7,6},{8,9},{9,8},{10,11... | collective-permute-start | bytes 786440 | tf_op jit(solution)/shard_map/ppermute | solution.py:270
  81.7 1.5 %collective-permute-start.19 = (bf16[1,2,2,32,1024]{4,3,2,1,0:T(8,128)(2,1)S(1)}, bf16[1,2,2,32,1024]{4,3,2,1,0:T(8,128)(2,1)S(1)}, u32[]{:S(2)}, u32[]{:S(2)}) collective-permute-start(bf16[1,2,2,32,1024]{4,3,2,1,0:T(8,128)(2,1)S(1)} %collective-permute-done.10.refs_8_), channel_id=1, source_target_pairs={{0,1},{1,0},{2,3},{3,2},{4,5},{5,4},{6,7},{7,6},{8,9},{9,8},{10,11... | collective-permute-start | bytes 786440 | tf_op jit(solution)/shard_map/ppermute | solution.py:270
  96.8 14.8 %all-to-all-start.1 = ((bf16[16,128,128]{2,1,0:T(8,128)(2,1)}), bf16[16,128,128]{2,1,0:T(8,128)(2,1)S(1)}, u32[]{:S(2)}, u32[]{:S(2)}) async-start(bf16[16,128,128]{2,1,0:T(8,128)(2,1)} %bitcast.16), calls=%async_computation.1 | async-start | bytes 1048576 | tf_op jit(solution)/shard_map/all_to_all | solution.py:310
  (13 other events, 25.9 us)

commit v5 on v4

--- a/solution.py
+++ b/solution.py
@@ -270,8 +270,8 @@
     return lax.ppermute(value, "mode", pairs)
 
 
-def plane(value, sources):
-    over_x, over_y = flip(value, 1), flip(value, 2)
+def plane(value, sources, early):
+    over_x, over_y, *_ = lax.optimization_barrier((flip(value, 1), flip(value, 2), *early))
     diagonal = flip(over_x[:1], 2), flip(over_y[1:], 1)
     turned = [tuple(source + more for source in sources) for more in ((1,), (2,), (1, 2))]
     return [
@@ -286,22 +286,26 @@
 def spread(gate_a, gate_b, packed):
     bits = lax.axis_size("mode").bit_length() - 1
     own = jnp.stack([gate_a, gate_b])[:, None]
-    sets = [(jnp.concatenate([own, flip(own, 3)], axis=1), ((), (3,)))]
-    for bit in range(4, bits):
-        far = [flip(own, *source, bit) for _, sources in sets for source in sources]
-        if bit == 4:
-            first, far[0], packed = lax.optimization_barrier((sets[0][0], far[0], packed))
-            sets = [(first, sets[0][1])]
-        more = [tuple(source + (bit,) for source in sources) for _, sources in sets]
-        sets += [(jnp.concatenate(far[2 * n : 2 * n + 2], axis=1), sources) for n, sources in enumerate(more)]
+    far = [()]
+    for bit in range(3, bits):
+        far += [source + (bit,) for source in far]
+    far = sorted(far[1:], key=len)
+    came = [flip(own, *source) for source in far]
+    sets = [(own, ((),))]
+    for start in range(0, len(far), 2):
+        value = jnp.concatenate(came[start : start + 2], axis=1)
+        sets.append((value, tuple(far[start : start + 2])))
     blocks = []
     for number, (value, sources) in enumerate(sets):
-        if number:
-            value, *_ = lax.optimization_barrier((value, blocks[-2][0], blocks[-1][0]))
-        blocks += plane(value, sources)
-    near = [(flip(value, 0), tuple(source + (0,) for source in sources), gates) for value, sources, gates in blocks]
-    packed, _ = lax.optimization_barrier((packed, near[-5][0]))
-    blocks += near
+        if number == 1:
+            value, packed, *_ = lax.optimization_barrier((value, packed, blocks[-2][0], blocks[-1][0]))
+        elif number:
+            value, *_ = lax.optimization_barrier((value, blocks[-4][0], blocks[-3][0]))
+        early = [later for later, _ in sets[2:]] if number == 1 else []
+        blocks += plane(value, sources, early)
+    blocks += [
+        (flip(value, 0), tuple(source + (0,) for source in sources), gates) for value, sources, gates in blocks
+    ]
     plan = tuple((sources, gates) for _, sources, gates in blocks)
     return [value for value, _, _ in blocks], plan, trade(packed)
 

time: 133 us -> 131 us (0.985)
  starting transfers between devices: 28.1 us -> 44.2 us
  waiting for transfers between devices: 52.3 us -> 37.6 us
  blocking collectives: 16.5 us -> 14.7 us
    ppermute x21 -> x30, waiting for transfers between devices: 52.2 us -> 37.6 us  [flip(): return lax.ppermute(value, 'mode', pairs)]
    all_to_all x2, starting transfers between devices: 8.07 us -> 16.9 us  [trade(): lax.all_to_all(value, 'mode', split_axis=0, concat_axis=0, axis_index_gro...]
    ppermute x21 -> x30, starting transfers between devices: 20.1 us -> 27.3 us  [flip(): return lax.ppermute(value, 'mode', pairs)]
    all_to_all x1, blocking collectives: 16.5 us -> 14.7 us  [trade(): lax.all_to_all(value, 'mode', split_axis=0, concat_axis=0, axis_index_gro...]
    unnamed x44 -> x56, local copies, waits for them, and re-layouts: 4.29 us -> 3.26 us
  transfers between devices with their start and end apart: 23 -> 32, of which waited for: 12 -> 15; matrix products, arithmetic and copies ran while one was open for 0% -> 0% of each run, Pallas kernels for 11% -> 11%
where the time goes in v5:
time: 131 us
  starting transfers between devices  44.2 us (34%)
  waiting for transfers between devices  37.6 us (29%)
  Pallas kernels  28.8 us (22%)
  blocking collectives  14.7 us (11%)
  local copies, waits for them, and re-layouts  3.95 us (3%)
    ppermute x30, waiting for transfers between devices, flip(): return lax.ppermute(value, 'mode', pairs)  37.6 us
    pallas_call x4, Pallas kernels, call(): pl.pallas_call(kernel, out_shape=jax.ShapeDtypeStruct(out_shape, jnp.bflo...  28.8 us
    ppermute x30, starting transfers between devices, flip(): return lax.ppermute(value, 'mode', pairs)  27.3 us
    all_to_all x2, starting transfers between devices, trade(): lax.all_to_all(value, 'mode', split_axis=0, concat_axis=0, axis_index_gro...  16.9 us
    all_to_all x1, blocking collectives, trade(): lax.all_to_all(value, 'mode', split_axis=0, concat_axis=0, axis_index_gro...  14.7 us
    unnamed x56, local copies, waits for them, and re-layouts  3.26 us
  transfers between devices with their start and end apart: 32, of which 15 were waited for; matrix products, arithmetic and copies ran while one was open for 0% of the time, Pallas kernels for 11%

profile of v5, /device:TPU:0, one launch (start us, length us, event | category | flops | bytes accessed | tf_op | source)
XLA Modules:
  0.0 130.7 jit_solution(2770052180705605147)
XLA Ops:
  0.0 1.0 maximum_bitcast_fusion.refs_0_
  1.0 3.0 %collective-permute-start.3 = (bf16[2,1,2,32,1024]{4,3,2,1,0:T(8,128)(2,1)S(1)}, bf16[2,1,2,32,1024]{4,3,2,1,0:T(8,128)(2,1)S(1)}, u32[]{:S(2)}, u32[]{:S(2)}) collective-permute-start(bf16[2,1,2,32,1024]{4,3,2,1,0:T(8,128)(2,1)S(1)} %maximum_bitcast_fusion.refs_0_), channel_id=1, source_target_pairs={{0,4},{1,5},{2,6},{3,7},{4,0},{5,1},{6,2},{7,3},{8,12},{9,13},{10,... | collective-permute-start | bytes 786440 | tf_op jit(solution)/shard_map/ppermute | solution.py:270
  4.0 1.5 %collective-permute-start.2 = (bf16[2,1,2,32,1024]{4,3,2,1,0:T(8,128)(2,1)S(1)}, bf16[2,1,2,32,1024]{4,3,2,1,0:T(8,128)(2,1)S(1)}, u32[]{:S(2)}, u32[]{:S(2)}) collective-permute-start(bf16[2,1,2,32,1024]{4,3,2,1,0:T(8,128)(2,1)S(1)} %maximum_bitcast_fusion.refs_0_), channel_id=1, source_target_pairs={{0,2},{1,3},{2,0},{3,1},{4,6},{5,7},{6,4},{7,5},{8,10},{9,11},{10,... | collective-permute-start | bytes 786440 | tf_op jit(solution)/shard_map/ppermute | solution.py:270
  5.5 2.6 %collective-permute-start.1 = (bf16[2,1,2,32,1024]{4,3,2,1,0:T(8,128)(2,1)S(1)}, bf16[2,1,2,32,1024]{4,3,2,1,0:T(8,128)(2,1)S(1)}, u32[]{:S(2)}, u32[]{:S(2)}) collective-permute-start(bf16[2,1,2,32,1024]{4,3,2,1,0:T(8,128)(2,1)S(1)} %maximum_bitcast_fusion.refs_0_), channel_id=1, source_target_pairs={{0,16},{1,17},{2,18},{3,19},{4,20},{5,21},{6,22},{7,23},{8,24},{9,... | collective-permute-start | bytes 786440 | tf_op jit(solution)/shard_map/ppermute | solution.py:270
  8.1 1.6 %collective-permute-start = (bf16[2,1,2,32,1024]{4,3,2,1,0:T(8,128)(2,1)S(1)}, bf16[2,1,2,32,1024]{4,3,2,1,0:T(8,128)(2,1)S(1)}, u32[]{:S(2)}, u32[]{:S(2)}) collective-permute-start(bf16[2,1,2,32,1024]{4,3,2,1,0:T(8,128)(2,1)S(1)} %maximum_bitcast_fusion.refs_0_), channel_id=1, source_target_pairs={{0,8},{1,9},{2,10},{3,11},{4,12},{5,13},{6,14},{7,15},{8,0},{9,1},... | collective-permute-start | bytes 786440 | tf_op jit(solution)/shard_map/ppermute | solution.py:270
  10.3 1.5 %collective-permute-done.2.refs_1_ = bf16[2,1,2,32,1024]{4,3,2,1,0:T(8,128)(2,1)S(1)} collective-permute-done((bf16[2,1,2,32,1024]{4,3,2,1,0:T(8,128)(2,1)S(1)}, bf16[2,1,2,32,1024]{4,3,2,1,0:T(8,128)(2,1)S(1)}, u32[]{:S(2)}, u32[]{:S(2)}) %collective-permute-start.2) | collective-permute-done | bytes 262176 | tf_op jit(solution)/shard_map/ppermute | solution.py:270
  11.8 1.6 %collective-permute-start.5 = (bf16[1,1,2,32,1024]{4,3,2,1,0:T(8,128)(2,1)S(1)}, bf16[1,1,2,32,1024]{4,3,2,1,0:T(8,128)(2,1)S(1)}, u32[]{:S(2)}, u32[]{:S(2)}) collective-permute-start(bf16[1,1,2,32,1024]{4,3,2,1,0:T(8,128)(2,1)S(1)} %slice.19), channel_id=1, source_target_pairs={{0,2},{1,3},{2,0},{3,1},{4,6},{5,7},{6,4},{7,5},{8,10},{9,11},{10,... | collective-permute-start | bytes 393224 | tf_op jit(solution)/shard_map/ppermute | solution.py:270
  13.9 4.0 %shard_map.46 = bf16[512,1024]{1,0:T(8,128)(2,1)} custom-call(bf16[4,2,64,1024]{3,2,1,0:T(8,128)(2,1)} %x_ref.1, s32[4,1024]{1,0:T(4,128)} %order_ref.1), custom_call_target="tpu_custom_call" | custom-call | flops 2147483648 | bytes 1064960 | tf_op jit(solution)/shard_map/pallas_call | solution.py:189
  17.9 1.7 %collective-permute-done.1 = bf16[2,1,2,32,1024]{4,3,2,1,0:T(8,128)(2,1)S(1)} collective-permute-done((bf16[2,1,2,32,1024]{4,3,2,1,0:T(8,128)(2,1)S(1)}, bf16[2,1,2,32,1024]{4,3,2,1,0:T(8,128)(2,1)S(1)}, u32[]{:S(2)}, u32[]{:S(2)}) %collective-permute-start.1) | collective-permute-done | bytes 262176 | tf_op jit(solution)/shard_map/ppermute | solution.py:270
  19.9 3.6 %all-to-all-start = ((bf16[32,16,1024]{2,1,0:T(8,128)(2,1)}), bf16[32,16,1024]{2,1,0:T(8,128)(2,1)S(1)}, u32[]{:S(2)}, u32[]{:S(2)}) async-start(bf16[32,16,1024]{2,1,0:T(8,128)(2,1)} %bitcast.3), calls=%async_computation | async-start | bytes 2097152 | tf_op jit(solution)/shard_map/all_to_all | solution.py:314
  23.5 1.8 %collective-permute-start.7 = (bf16[2,2,2,32,1024]{4,3,2,1,0:T(8,128)(2,1)S(1)}, bf16[2,2,2,32,1024]{4,3,2,1,0:T(8,128)(2,1)S(1)}, u32[]{:S(2)}, u32[]{:S(2)}) collective-permute-start(bf16[2,2,2,32,1024]{4,3,2,1,0:T(8,128)(2,1)S(1)} %pad_maximum_fusion.refs_5_), channel_id=1, source_target_pairs={{0,4},{1,5},{2,6},{3,7},{4,0},{5,1},{6,2},{7,3},{8,12},{9,13},{10,... | collective-permute-start | bytes 1572872 | tf_op jit(solution)/shard_map/ppermute | solution.py:270
  25.3 1.5 %collective-permute-start.6 = (bf16[2,2,2,32,1024]{4,3,2,1,0:T(8,128)(2,1)S(1)}, bf16[2,2,2,32,1024]{4,3,2,1,0:T(8,128)(2,1)S(1)}, u32[]{:S(2)}, u32[]{:S(2)}) collective-permute-start(bf16[2,2,2,32,1024]{4,3,2,1,0:T(8,128)(2,1)S(1)} %pad_maximum_fusion.refs_5_), channel_id=1, source_target_pairs={{0,2},{1,3},{2,0},{3,1},{4,6},{5,7},{6,4},{7,5},{8,10},{9,11},{10,... | collective-permute-start | bytes 1572872 | tf_op jit(solution)/shard_map/ppermute | solution.py:270
  26.8 3.4 %collective-permute-start.8 = (bf16[2,1,2,32,1024]{4,3,2,1,0:T(8,128)(2,1)S(1)}, bf16[2,1,2,32,1024]{4,3,2,1,0:T(8,128)(2,1)S(1)}, u32[]{:S(2)}, u32[]{:S(2)}) collective-permute-start(bf16[2,1,2,32,1024]{4,3,2,1,0:T(8,128)(2,1)S(1)} %maximum_bitcast_fusion.refs_0_), channel_id=1, source_target_pairs={{0,24},{1,25},{2,26},{3,27},{4,28},{5,29},{6,30},{7,31},{8,16},{9,... | collective-permute-start | bytes 786440 | tf_op jit(solution)/shard_map/ppermute | solution.py:270
  30.7 20.0 %collective-permute-done.8.refs_10_ = bf16[2,1,2,32,1024]{4,3,2,1,0:T(8,128)(2,1)S(1)} collective-permute-done((bf16[2,1,2,32,1024]{4,3,2,1,0:T(8,128)(2,1)S(1)}, bf16[2,1,2,32,1024]{4,3,2,1,0:T(8,128)(2,1)S(1)}, u32[]{:S(2)}, u32[]{:S(2)}) %collective-permute-start.8) | collective-permute-done | bytes 262176 | tf_op jit(solution)/shard_map/ppermute | solution.py:270
  51.3 1.5 %collective-permute-start.12 = (bf16[2,1,2,32,1024]{4,3,2,1,0:T(8,128)(2,1)S(1)}, bf16[2,1,2,32,1024]{4,3,2,1,0:T(8,128)(2,1)S(1)}, u32[]{:S(2)}, u32[]{:S(2)}) collective-permute-start(bf16[2,1,2,32,1024]{4,3,2,1,0:T(8,128)(2,1)S(1)} %collective-permute-done.8.refs_10_), channel_id=1, source_target_pairs={{0,4},{1,5},{2,6},{3,7},{4,0},{5,1},{6,2},{7,3},{8,12},{9,13},{10,... | collective-permute-start | bytes 786440 | tf_op jit(solution)/shard_map/ppermute | solution.py:270
  52.8 1.5 %collective-permute-start.11 = (bf16[2,1,2,32,1024]{4,3,2,1,0:T(8,128)(2,1)S(1)}, bf16[2,1,2,32,1024]{4,3,2,1,0:T(8,128)(2,1)S(1)}, u32[]{:S(2)}, u32[]{:S(2)}) collective-permute-start(bf16[2,1,2,32,1024]{4,3,2,1,0:T(8,128)(2,1)S(1)} %collective-permute-done.8.refs_10_), channel_id=1, source_target_pairs={{0,2},{1,3},{2,0},{3,1},{4,6},{5,7},{6,4},{7,5},{8,10},{9,11},{10,... | collective-permute-start | bytes 786440 | tf_op jit(solution)/shard_map/ppermute | solution.py:270
  54.3 1.6 %collective-permute-done.18.refs_18_ = bf16[1,1,2,32,1024]{4,3,2,1,0:T(8,128)(2,1)S(1)} collective-permute-done((bf16[1,1,2,32,1024]{4,3,2,1,0:T(8,128)(2,1)}, bf16[1,1,2,32,1024]{4,3,2,1,0:T(8,128)(2,1)S(1)}, u32[]{:S(2)}, u32[]{:S(2)}) %collective-permute-start.18) | collective-permute-done | bytes 131104 | tf_op jit(solution)/shard_map/ppermute | solution.py:270
  57.0 3.0 %collective-permute-done.12.refs_12_ = bf16[2,1,2,32,1024]{4,3,2,1,0:T(8,128)(2,1)S(1)} collective-permute-done((bf16[2,1,2,32,1024]{4,3,2,1,0:T(8,128)(2,1)S(1)}, bf16[2,1,2,32,1024]{4,3,2,1,0:T(8,128)(2,1)S(1)}, u32[]{:S(2)}, u32[]{:S(2)}) %collective-permute-start.12) | collective-permute-done | bytes 262176 | tf_op jit(solution)/shard_map/ppermute | solution.py:270
  60.0 1.7 %collective-permute-start.9 = (bf16[1,2,2,32,1024]{4,3,2,1,0:T(8,128)(2,1)S(1)}, bf16[1,2,2,32,1024]{4,3,2,1,0:T(8,128)(2,1)S(1)}, u32[]{:S(2)}, u32[]{:S(2)}) collective-permute-start(bf16[1,2,2,32,1024]{4,3,2,1,0:T(8,128)(2,1)S(1)} %slice.20), channel_id=1, source_target_pairs={{0,4},{1,5},{2,6},{3,7},{4,0},{5,1},{6,2},{7,3},{8,12},{9,13},{10,... | collective-permute-start | bytes 786440 | tf_op jit(solution)/shard_map/ppermute | solution.py:270
  62.0 1.5 %collective-permute-start.14 = (bf16[1,1,2,32,1024]{4,3,2,1,0:T(8,128)(2,1)S(1)}, bf16[1,1,2,32,1024]{4,3,2,1,0:T(8,128)(2,1)S(1)}, u32[]{:S(2)}, u32[]{:S(2)}) collective-permute-start(bf16[1,1,2,32,1024]{4,3,2,1,0:T(8,128)(2,1)S(1)} %slice.23), channel_id=1, source_target_pairs={{0,2},{1,3},{2,0},{3,1},{4,6},{5,7},{6,4},{7,5},{8,10},{9,11},{10,... | collective-permute-start | bytes 393224 | tf_op jit(solution)/shard_map/ppermute | solution.py:270
  64.1 3.5 %collective-permute-done.10.refs_9_ = bf16[1,2,2,32,1024]{4,3,2,1,0:T(8,128)(2,1)S(1)} collective-permute-done((bf16[1,2,2,32,1024]{4,3,2,1,0:T(8,128)(2,1)S(1)}, bf16[1,2,2,32,1024]{4,3,2,1,0:T(8,128)(2,1)S(1)}, u32[]{:S(2)}, u32[]{:S(2)}) %collective-permute-start.10) | collective-permute-done | bytes 262176 | tf_op jit(solution)/shard_map/ppermute | solution.py:270
  67.6 1.6 %collective-permute-done.9.refs_8_ = bf16[1,2,2,32,1024]{4,3,2,1,0:T(8,128)(2,1)S(1)} collective-permute-done((bf16[1,2,2,32,1024]{4,3,2,1,0:T(8,128)(2,1)S(1)}, bf16[1,2,2,32,1024]{4,3,2,1,0:T(8,128)(2,1)S(1)}, u32[]{:S(2)}, u32[]{:S(2)}) %collective-permute-start.9) | collective-permute-done | bytes 262176 | tf_op jit(solution)/shard_map/ppermute | solution.py:270
  69.9 0.9 collective-permute-done.13.refs_13_
  70.8 0.8 collective-permute-done.29.refs_29_
  73.0 0.9 collective-permute-done.23.refs_23_
  75.1 0.8 copy-done.11
  76.3 11.5 %shard_map.47 = bf16[2048,128]{1,0:T(8,128)(2,1)} custom-call(bf16[512,1024]{1,0:T(8,128)(2,1)} %bitcast.14, bf16[2,1,2,32,1024]{4,3,2,1,0:T(8,128)(2,1)} %copy-done.3, bf16[2,1,2,32,1024]{4,3,2,1,0:T(8,128)(2,1)} %copy-done.7, bf16[2,1,2,32,1024]{4,3,2,1,0:T(8,128)(2,1)} %copy-done.6, bf16[1,1,2,32,1024]{4,3,2,1,0:T(8,128)(2,1)} %collective-permute-done.4.refs_3_, ...), custom_call_target="tpu_custom_call" | custom-call | flops 4294967296 | bytes 9437184 | tf_op jit(solution)/shard_map/pallas_call | solution.py:189
  87.9 13.3 %all-to-all-start.1 = ((bf16[16,128,128]{2,1,0:T(8,128)(2,1)}), bf16[16,128,128]{2,1,0:T(8,128)(2,1)S(1)}, u32[]{:S(2)}, u32[]{:S(2)}) async-start(bf16[16,128,128]{2,1,0:T(8,128)(2,1)} %bitcast.16), calls=%async_computation.1 | async-start | bytes 1048576 | tf_op jit(solution)/shard_map/all_to_all | solution.py:314
  101.2 10.8 %shard_map.48.right_ref = bf16[256,1024]{1,0:T(8,128)(2,1)} custom-call(bf16[512,1024]{1,0:T(8,128)(2,1)} %bitcast.15, bf16[2,1,2,32,1024]{4,3,2,1,0:T(8,128)(2,1)} %copy-done.3, bf16[2,1,2,32,1024]{4,3,2,1,0:T(8,128)(2,1)} %copy-done.7, bf16[2,1,2,32,1024]{4,3,2,1,0:T(8,128)(2,1)} %copy-done.6, bf16[1,1,2,32,1024]{4,3,2,1,0:T(8,128)(2,1)} %collective-permute-done.4.refs_3_, ...), custom_call_target="tpu_custom_call" | custom-call | flops 4294967296 | bytes 9437184 | tf_op jit(solution)/shard_map/pallas_call | solution.py:189
  112.0 0.8 copy-done
  112.8 2.5 %shard_map.49 = bf16[512,256]{1,0:T(8,128)(2,1)} custom-call(bf16[2048,128]{1,0:T(8,128)(2,1)} %bitcast.12, bf16[256,1024]{1,0:T(8,128)(2,1)} %shard_map.48.right_ref), custom_call_target="tpu_custom_call" | custom-call | flops 134217728 | bytes 1048576 | tf_op jit(solution)/shard_map/pallas_call | solution.py:189
  115.3 14.7 %all_to_all.15 = bf16[32,16,256]{2,1,0:T(8,128)(2,1)S(1)} all-to-all(bf16[32,16,256]{2,1,0:T(8,128)(2,1)} %bitcast.13), channel_id=1, replica_groups=mesh['cuts'=1,'mode'=32] {'mode'}, dimensions={0} | all-to-all | bytes 524288 | tf_op jit(solution)/shard_map/all_to_all | solution.py:314
  (104 shorter events, 8.7 us)
Async XLA Ops:
  1.0 9.3 %collective-permute-start.3 = (bf16[2,1,2,32,1024]{4,3,2,1,0:T(8,128)(2,1)S(1)}, bf16[2,1,2,32,1024]{4,3,2,1,0:T(8,128)(2,1)S(1)}, u32[]{:S(2)}, u32[]{:S(2)}) collective-permute-start(bf16[2,1,2,32,1024]{4,3,2,1,0:T(8,128)(2,1)S(1)} %maximum_bitcast_fusion.refs_0_), channel_id=1, source_target_pairs={{0,4},{1,5},{2,6},{3,7},{4,0},{5,1},{6,2},{7,3},{8,12},{9,13},{10,... | collective-permute-start | bytes 786440 | tf_op jit(solution)/shard_map/ppermute | solution.py:270
  4.0 7.8 %collective-permute-start.2 = (bf16[2,1,2,32,1024]{4,3,2,1,0:T(8,128)(2,1)S(1)}, bf16[2,1,2,32,1024]{4,3,2,1,0:T(8,128)(2,1)S(1)}, u32[]{:S(2)}, u32[]{:S(2)}) collective-permute-start(bf16[2,1,2,32,1024]{4,3,2,1,0:T(8,128)(2,1)S(1)} %maximum_bitcast_fusion.refs_0_), channel_id=1, source_target_pairs={{0,2},{1,3},{2,0},{3,1},{4,6},{5,7},{6,4},{7,5},{8,10},{9,11},{10,... | collective-permute-start | bytes 786440 | tf_op jit(solution)/shard_map/ppermute | solution.py:270
  5.5 14.1 %collective-permute-start.1 = (bf16[2,1,2,32,1024]{4,3,2,1,0:T(8,128)(2,1)S(1)}, bf16[2,1,2,32,1024]{4,3,2,1,0:T(8,128)(2,1)S(1)}, u32[]{:S(2)}, u32[]{:S(2)}) collective-permute-start(bf16[2,1,2,32,1024]{4,3,2,1,0:T(8,128)(2,1)S(1)} %maximum_bitcast_fusion.refs_0_), channel_id=1, source_target_pairs={{0,16},{1,17},{2,18},{3,19},{4,20},{5,21},{6,22},{7,23},{8,24},{9,... | collective-permute-start | bytes 786440 | tf_op jit(solution)/shard_map/ppermute | solution.py:270
  8.1 11.7 %collective-permute-start = (bf16[2,1,2,32,1024]{4,3,2,1,0:T(8,128)(2,1)S(1)}, bf16[2,1,2,32,1024]{4,3,2,1,0:T(8,128)(2,1)S(1)}, u32[]{:S(2)}, u32[]{:S(2)}) collective-permute-start(bf16[2,1,2,32,1024]{4,3,2,1,0:T(8,128)(2,1)S(1)} %maximum_bitcast_fusion.refs_0_), channel_id=1, source_target_pairs={{0,8},{1,9},{2,10},{3,11},{4,12},{5,13},{6,14},{7,15},{8,0},{9,1},... | collective-permute-start | bytes 786440 | tf_op jit(solution)/shard_map/ppermute | solution.py:270
  11.8 8.1 %collective-permute-start.5 = (bf16[1,1,2,32,1024]{4,3,2,1,0:T(8,128)(2,1)S(1)}, bf16[1,1,2,32,1024]{4,3,2,1,0:T(8,128)(2,1)S(1)}, u32[]{:S(2)}, u32[]{:S(2)}) collective-permute-start(bf16[1,1,2,32,1024]{4,3,2,1,0:T(8,128)(2,1)S(1)} %slice.19), channel_id=1, source_target_pairs={{0,2},{1,3},{2,0},{3,1},{4,6},{5,7},{6,4},{7,5},{8,10},{9,11},{10,... | collective-permute-start | bytes 393224 | tf_op jit(solution)/shard_map/ppermute | solution.py:270
  13.4 6.5 %collective-permute-start.4 = (bf16[1,1,2,32,1024]{4,3,2,1,0:T(8,128)(2,1)S(1)}, bf16[1,1,2,32,1024]{4,3,2,1,0:T(8,128)(2,1)}, u32[]{:S(2)}, u32[]{:S(2)}) collective-permute-start(bf16[1,1,2,32,1024]{4,3,2,1,0:T(8,128)(2,1)S(1)} %slice.18), channel_id=1, source_target_pairs={{0,4},{1,5},{2,6},{3,7},{4,0},{5,1},{6,2},{7,3},{8,12},{9,13},{10,... | collective-permute-start | bytes 393224 | tf_op jit(solution)/shard_map/ppermute | solution.py:270
  19.9 55.1 %all-to-all-start = ((bf16[32,16,1024]{2,1,0:T(8,128)(2,1)}), bf16[32,16,1024]{2,1,0:T(8,128)(2,1)S(1)}, u32[]{:S(2)}, u32[]{:S(2)}) async-start(bf16[32,16,1024]{2,1,0:T(8,128)(2,1)} %bitcast.3), calls=%async_computation | async-start | bytes 2097152 | tf_op jit(solution)/shard_map/all_to_all | solution.py:314
  23.5 27.2 %collective-permute-start.7 = (bf16[2,2,2,32,1024]{4,3,2,1,0:T(8,128)(2,1)S(1)}, bf16[2,2,2,32,1024]{4,3,2,1,0:T(8,128)(2,1)S(1)}, u32[]{:S(2)}, u32[]{:S(2)}) collective-permute-start(bf16[2,2,2,32,1024]{4,3,2,1,0:T(8,128)(2,1)S(1)} %pad_maximum_fusion.refs_5_), channel_id=1, source_target_pairs={{0,4},{1,5},{2,6},{3,7},{4,0},{5,1},{6,2},{7,3},{8,12},{9,13},{10,... | collective-permute-start | bytes 1572872 | tf_op jit(solution)/shard_map/ppermute | solution.py:270
  25.3 25.9 %collective-permute-start.6 = (bf16[2,2,2,32,1024]{4,3,2,1,0:T(8,128)(2,1)S(1)}, bf16[2,2,2,32,1024]{4,3,2,1,0:T(8,128)(2,1)S(1)}, u32[]{:S(2)}, u32[]{:S(2)}) collective-permute-start(bf16[2,2,2,32,1024]{4,3,2,1,0:T(8,128)(2,1)S(1)} %pad_maximum_fusion.refs_5_), channel_id=1, source_target_pairs={{0,2},{1,3},{2,0},{3,1},{4,6},{5,7},{6,4},{7,5},{8,10},{9,11},{10,... | collective-permute-start | bytes 1572872 | tf_op jit(solution)/shard_map/ppermute | solution.py:270
  26.8 23.9 %collective-permute-start.8 = (bf16[2,1,2,32,1024]{4,3,2,1,0:T(8,128)(2,1)S(1)}, bf16[2,1,2,32,1024]{4,3,2,1,0:T(8,128)(2,1)S(1)}, u32[]{:S(2)}, u32[]{:S(2)}) collective-permute-start(bf16[2,1,2,32,1024]{4,3,2,1,0:T(8,128)(2,1)S(1)} %maximum_bitcast_fusion.refs_0_), channel_id=1, source_target_pairs={{0,24},{1,25},{2,26},{3,27},{4,28},{5,29},{6,30},{7,31},{8,16},{9,... | collective-permute-start | bytes 786440 | tf_op jit(solution)/shard_map/ppermute | solution.py:270
  30.2 22.6 %collective-permute-start.15 = (bf16[2,1,2,32,1024]{4,3,2,1,0:T(8,128)(2,1)S(1)}, bf16[2,1,2,32,1024]{4,3,2,1,0:T(8,128)(2,1)}, u32[]{:S(2)}, u32[]{:S(2)}) collective-permute-start(bf16[2,1,2,32,1024]{4,3,2,1,0:T(8,128)(2,1)S(1)} %maximum_bitcast_fusion.refs_0_), channel_id=1, source_target_pairs={{0,1},{1,0},{2,3},{3,2},{4,5},{5,4},{6,7},{7,6},{8,9},{9,8},{10,11... | collective-permute-start | bytes 786440 | tf_op jit(solution)/shard_map/ppermute | solution.py:270
  30.2 26.3 %collective-permute-start.16 = (bf16[2,1,2,32,1024]{4,3,2,1,0:T(8,128)(2,1)S(1)}, bf16[2,1,2,32,1024]{4,3,2,1,0:T(8,128)(2,1)S(1)}, u32[]{:S(2)}, u32[]{:S(2)}) collective-permute-start(bf16[2,1,2,32,1024]{4,3,2,1,0:T(8,128)(2,1)S(1)} %collective-permute-done.2.refs_1_), channel_id=1, source_target_pairs={{0,1},{1,0},{2,3},{3,2},{4,5},{5,4},{6,7},{7,6},{8,9},{9,8},{10,11... | collective-permute-start | bytes 786440 | tf_op jit(solution)/shard_map/ppermute | solution.py:270
  50.7 12.9 %collective-permute-start.20 = (bf16[2,2,2,32,1024]{4,3,2,1,0:T(8,128)(2,1)S(1)}, bf16[2,2,2,32,1024]{4,3,2,1,0:T(8,128)(2,1)S(1)}, u32[]{:S(2)}, u32[]{:S(2)}) collective-permute-start(bf16[2,2,2,32,1024]{4,3,2,1,0:T(8,128)(2,1)S(1)} %pad_maximum_fusion.refs_5_), channel_id=1, source_target_pairs={{0,1},{1,0},{2,3},{3,2},{4,5},{5,4},{6,7},{7,6},{8,9},{9,8},{10,11... | collective-permute-start | bytes 1572872 | tf_op jit(solution)/shard_map/ppermute | solution.py:270
  50.7 3.5 %collective-permute-start.19 = (bf16[1,1,2,32,1024]{4,3,2,1,0:T(8,128)(2,1)S(1)}, bf16[1,1,2,32,1024]{4,3,2,1,0:T(8,128)(2,1)S(1)}, u32[]{:S(2)}, u32[]{:S(2)}) collective-permute-start(bf16[1,1,2,32,1024]{4,3,2,1,0:T(8,128)(2,1)S(1)} %collective-permute-done.5.refs_4_), channel_id=1, source_target_pairs={{0,1},{1,0},{2,3},{3,2},{4,5},{5,4},{6,7},{7,6},{8,9},{9,8},{10,11... | collective-permute-start | bytes 393224 | tf_op jit(solution)/shard_map/ppermute | solution.py:270
  51.3 8.7 %collective-permute-start.12 = (bf16[2,1,2,32,1024]{4,3,2,1,0:T(8,128)(2,1)S(1)}, bf16[2,1,2,32,1024]{4,3,2,1,0:T(8,128)(2,1)S(1)}, u32[]{:S(2)}, u32[]{:S(2)}) collective-permute-start(bf16[2,1,2,32,1024]{4,3,2,1,0:T(8,128)(2,1)S(1)} %collective-permute-done.8.refs_10_), channel_id=1, source_target_pairs={{0,4},{1,5},{2,6},{3,7},{4,0},{5,1},{6,2},{7,3},{8,12},{9,13},{10,... | collective-permute-start | bytes 786440 | tf_op jit(solution)/shard_map/ppermute | solution.py:270
  52.8 9.2 %collective-permute-start.11 = (bf16[2,1,2,32,1024]{4,3,2,1,0:T(8,128)(2,1)S(1)}, bf16[2,1,2,32,1024]{4,3,2,1,0:T(8,128)(2,1)S(1)}, u32[]{:S(2)}, u32[]{:S(2)}) collective-permute-start(bf16[2,1,2,32,1024]{4,3,2,1,0:T(8,128)(2,1)S(1)} %collective-permute-done.8.refs_10_), channel_id=1, source_target_pairs={{0,2},{1,3},{2,0},{3,1},{4,6},{5,7},{6,4},{7,5},{8,10},{9,11},{10,... | collective-permute-start | bytes 786440 | tf_op jit(solution)/shard_map/ppermute | solution.py:270
  54.3 1.6 %collective-permute-start.18 = (bf16[1,1,2,32,1024]{4,3,2,1,0:T(8,128)(2,1)}, bf16[1,1,2,32,1024]{4,3,2,1,0:T(8,128)(2,1)S(1)}, u32[]{:S(2)}, u32[]{:S(2)}) collective-permute-start(bf16[1,1,2,32,1024]{4,3,2,1,0:T(8,128)(2,1)} %collective-permute-done.4.refs_3_), channel_id=1, source_target_pairs={{0,1},{1,0},{2,3},{3,2},{4,5},{5,4},{6,7},{7,6},{8,9},{9,8},{10,11... | collective-permute-start | bytes 393224 | tf_op jit(solution)/shard_map/ppermute | solution.py:270
  55.8 6.2 %collective-permute-start.17 = (bf16[2,1,2,32,1024]{4,3,2,1,0:T(8,128)(2,1)S(1)}, bf16[2,1,2,32,1024]{4,3,2,1,0:T(8,128)(2,1)S(1)}, u32[]{:S(2)}, u32[]{:S(2)}) collective-permute-start(bf16[2,1,2,32,1024]{4,3,2,1,0:T(8,128)(2,1)S(1)} %collective-permute-done.3.refs_2_), channel_id=1, source_target_pairs={{0,1},{1,0},{2,3},{3,2},{4,5},{5,4},{6,7},{7,6},{8,9},{9,8},{10,11... | collective-permute-start | bytes 786440 | tf_op jit(solution)/shard_map/ppermute | solution.py:270
  56.5 11.1 %collective-permute-start.10 = (bf16[1,2,2,32,1024]{4,3,2,1,0:T(8,128)(2,1)S(1)}, bf16[1,2,2,32,1024]{4,3,2,1,0:T(8,128)(2,1)S(1)}, u32[]{:S(2)}, u32[]{:S(2)}) collective-permute-start(bf16[1,2,2,32,1024]{4,3,2,1,0:T(8,128)(2,1)S(1)} %slice.21), channel_id=1, source_target_pairs={{0,2},{1,3},{2,0},{3,1},{4,6},{5,7},{6,4},{7,5},{8,10},{9,11},{10,... | collective-permute-start | bytes 786440 | tf_op jit(solution)/shard_map/ppermute | solution.py:270
  60.0 9.2 %collective-permute-start.9 = (bf16[1,2,2,32,1024]{4,3,2,1,0:T(8,128)(2,1)S(1)}, bf16[1,2,2,32,1024]{4,3,2,1,0:T(8,128)(2,1)S(1)}, u32[]{:S(2)}, u32[]{:S(2)}) collective-permute-start(bf16[1,2,2,32,1024]{4,3,2,1,0:T(8,128)(2,1)S(1)} %slice.20), channel_id=1, source_target_pairs={{0,4},{1,5},{2,6},{3,7},{4,0},{5,1},{6,2},{7,3},{8,12},{9,13},{10,... | collective-permute-start | bytes 786440 | tf_op jit(solution)/shard_map/ppermute | solution.py:270
  62.0 7.3 %collective-permute-start.25 = (bf16[2,1,2,32,1024]{4,3,2,1,0:T(8,128)(2,1)S(1)}, bf16[2,1,2,32,1024]{4,3,2,1,0:T(8,128)(2,1)S(1)}, u32[]{:S(2)}, u32[]{:S(2)}) collective-permute-start(bf16[2,1,2,32,1024]{4,3,2,1,0:T(8,128)(2,1)S(1)} %collective-permute-done.8.refs_10_), channel_id=1, source_target_pairs={{0,1},{1,0},{2,3},{3,2},{4,5},{5,4},{6,7},{7,6},{8,9},{9,8},{10,11... | collective-permute-start | bytes 786440 | tf_op jit(solution)/shard_map/ppermute | solution.py:270
  62.0 7.8 %collective-permute-start.14 = (bf16[1,1,2,32,1024]{4,3,2,1,0:T(8,128)(2,1)S(1)}, bf16[1,1,2,32,1024]{4,3,2,1,0:T(8,128)(2,1)S(1)}, u32[]{:S(2)}, u32[]{:S(2)}) collective-permute-start(bf16[1,1,2,32,1024]{4,3,2,1,0:T(8,128)(2,1)S(1)} %slice.23), channel_id=1, source_target_pairs={{0,2},{1,3},{2,0},{3,1},{4,6},{5,7},{6,4},{7,5},{8,10},{9,11},{10,... | collective-permute-start | bytes 393224 | tf_op jit(solution)/shard_map/ppermute | solution.py:270
  63.6 7.2 %collective-permute-start.13 = (bf16[1,1,2,32,1024]{4,3,2,1,0:T(8,128)(2,1)S(1)}, bf16[1,1,2,32,1024]{4,3,2,1,0:T(8,128)(2,1)S(1)}, u32[]{:S(2)}, u32[]{:S(2)}) collective-permute-start(bf16[1,1,2,32,1024]{4,3,2,1,0:T(8,128)(2,1)S(1)} %slice.22), channel_id=1, source_target_pairs={{0,4},{1,5},{2,6},{3,7},{4,0},{5,1},{6,2},{7,3},{8,12},{9,13},{10,... | collective-permute-start | bytes 393224 | tf_op jit(solution)/shard_map/ppermute | solution.py:270
  67.6 4.9 %collective-permute-start.24 = (bf16[1,2,2,32,1024]{4,3,2,1,0:T(8,128)(2,1)S(1)}, bf16[1,2,2,32,1024]{4,3,2,1,0:T(8,128)(2,1)S(1)}, u32[]{:S(2)}, u32[]{:S(2)}) collective-permute-start(bf16[1,2,2,32,1024]{4,3,2,1,0:T(8,128)(2,1)S(1)} %collective-permute-done.10.refs_9_), channel_id=1, source_target_pairs={{0,1},{1,0},{2,3},{3,2},{4,5},{5,4},{6,7},{7,6},{8,9},{9,8},{10,11... | collective-permute-start | bytes 786440 | tf_op jit(solution)/shard_map/ppermute | solution.py:270
  69.2 5.1 %collective-permute-start.21 = (bf16[2,2,2,32,1024]{4,3,2,1,0:T(8,128)(2,1)S(1)}, bf16[2,2,2,32,1024]{4,3,2,1,0:T(8,128)(2,1)S(1)}, u32[]{:S(2)}, u32[]{:S(2)}) collective-permute-start(bf16[2,2,2,32,1024]{4,3,2,1,0:T(8,128)(2,1)S(1)} %collective-permute-done.6.refs_6_), channel_id=1, source_target_pairs={{0,1},{1,0},{2,3},{3,2},{4,5},{5,4},{6,7},{7,6},{8,9},{9,8},{10,11... | collective-permute-start | bytes 1572872 | tf_op jit(solution)/shard_map/ppermute | solution.py:270
  69.3 5.8 %collective-permute-start.22 = (bf16[2,2,2,32,1024]{4,3,2,1,0:T(8,128)(2,1)S(1)}, bf16[2,2,2,32,1024]{4,3,2,1,0:T(8,128)(2,1)S(1)}, u32[]{:S(2)}, u32[]{:S(2)}) collective-permute-start(bf16[2,2,2,32,1024]{4,3,2,1,0:T(8,128)(2,1)S(1)} %collective-permute-done.7.refs_7_), channel_id=1, source_target_pairs={{0,1},{1,0},{2,3},{3,2},{4,5},{5,4},{6,7},{7,6},{8,9},{9,8},{10,11... | collective-permute-start | bytes 1572872 | tf_op jit(solution)/shard_map/ppermute | solution.py:270
  69.8 1.8 %collective-permute-start.29 = (bf16[1,1,2,32,1024]{4,3,2,1,0:T(8,128)(2,1)S(1)}, bf16[1,1,2,32,1024]{4,3,2,1,0:T(8,128)(2,1)}, u32[]{:S(2)}, u32[]{:S(2)}) collective-permute-start(bf16[1,1,2,32,1024]{4,3,2,1,0:T(8,128)(2,1)S(1)} %collective-permute-done.14.refs_14_), channel_id=1, source_target_pairs={{0,1},{1,0},{2,3},{3,2},{4,5},{5,4},{6,7},{7,6},{8,9},{9,8},{10,11... | collective-permute-start | bytes 393224 | tf_op jit(solution)/shard_map/ppermute | solution.py:270
  70.8 1.6 %collective-permute-start.28 = (bf16[1,1,2,32,1024]{4,3,2,1,0:T(8,128)(2,1)S(1)}, bf16[1,1,2,32,1024]{4,3,2,1,0:T(8,128)(2,1)}, u32[]{:S(2)}, u32[]{:S(2)}) collective-permute-start(bf16[1,1,2,32,1024]{4,3,2,1,0:T(8,128)(2,1)S(1)} %collective-permute-done.13.refs_13_), channel_id=1, source_target_pairs={{0,1},{1,0},{2,3},{3,2},{4,5},{5,4},{6,7},{7,6},{8,9},{9,8},{10,11... | collective-permute-start | bytes 393224 | tf_op jit(solution)/shard_map/ppermute | solution.py:270
  71.6 2.3 %collective-permute-start.26 = (bf16[2,1,2,32,1024]{4,3,2,1,0:T(8,128)(2,1)S(1)}, bf16[2,1,2,32,1024]{4,3,2,1,0:T(8,128)(2,1)S(1)}, u32[]{:S(2)}, u32[]{:S(2)}) collective-permute-start(bf16[2,1,2,32,1024]{4,3,2,1,0:T(8,128)(2,1)S(1)} %collective-permute-done.11.refs_11_), channel_id=1, source_target_pairs={{0,1},{1,0},{2,3},{3,2},{4,5},{5,4},{6,7},{7,6},{8,9},{9,8},{10,11... | collective-permute-start | bytes 786440 | tf_op jit(solution)/shard_map/ppermute | solution.py:270
  72.4 1.5 %collective-permute-start.23 = (bf16[1,2,2,32,1024]{4,3,2,1,0:T(8,128)(2,1)S(1)}, bf16[1,2,2,32,1024]{4,3,2,1,0:T(8,128)(2,1)S(1)}, u32[]{:S(2)}, u32[]{:S(2)}) collective-permute-start(bf16[1,2,2,32,1024]{4,3,2,1,0:T(8,128)(2,1)S(1)} %collective-permute-done.9.refs_8_), channel_id=1, source_target_pairs={{0,1},{1,0},{2,3},{3,2},{4,5},{5,4},{6,7},{7,6},{8,9},{9,8},{10,11... | collective-permute-start | bytes 786440 | tf_op jit(solution)/shard_map/ppermute | solution.py:270
  72.5 1.8 %collective-permute-start.27 = (bf16[2,1,2,32,1024]{4,3,2,1,0:T(8,128)(2,1)S(1)}, bf16[2,1,2,32,1024]{4,3,2,1,0:T(8,128)(2,1)S(1)}, u32[]{:S(2)}, u32[]{:S(2)}) collective-permute-start(bf16[2,1,2,32,1024]{4,3,2,1,0:T(8,128)(2,1)S(1)} %collective-permute-done.12.refs_12_), channel_id=1, source_target_pairs={{0,1},{1,0},{2,3},{3,2},{4,5},{5,4},{6,7},{7,6},{8,9},{9,8},{10,11... | collective-permute-start | bytes 786440 | tf_op jit(solution)/shard_map/ppermute | solution.py:270
  87.9 24.1 %all-to-all-start.1 = ((bf16[16,128,128]{2,1,0:T(8,128)(2,1)}), bf16[16,128,128]{2,1,0:T(8,128)(2,1)S(1)}, u32[]{:S(2)}, u32[]{:S(2)}) async-start(bf16[16,128,128]{2,1,0:T(8,128)(2,1)} %bitcast.16), calls=%async_computation.1 | async-start | bytes 1048576 | tf_op jit(solution)/shard_map/all_to_all | solution.py:314
  (28 other events, 299.9 us)

commit v6 on v4

--- a/solution.py
+++ b/solution.py
@@ -11,7 +11,7 @@
 KEPT = 4
 CYCLES = 2
 LANES = 128
-VMEM_LIMIT = 56 * 1024 * 1024
+VMEM_LIMIT = 24 * 1024 * 1024
 
 
 def whole(count):
@@ -286,21 +286,19 @@
 def spread(gate_a, gate_b, packed):
     bits = lax.axis_size("mode").bit_length() - 1
     own = jnp.stack([gate_a, gate_b])[:, None]
-    sets = [(jnp.concatenate([own, flip(own, 3)], axis=1), ((), (3,)))]
-    for bit in range(4, bits):
-        far = [flip(own, *source, bit) for _, sources in sets for source in sources]
-        if bit == 4:
-            first, far[0], packed = lax.optimization_barrier((sets[0][0], far[0], packed))
-            sets = [(first, sets[0][1])]
-        more = [tuple(source + (bit,) for source in sources) for _, sources in sets]
-        sets += [(jnp.concatenate(far[2 * n : 2 * n + 2], axis=1), sources) for n, sources in enumerate(more)]
-    blocks = []
-    for number, (value, sources) in enumerate(sets):
-        if number:
-            value, *_ = lax.optimization_barrier((value, blocks[-2][0], blocks[-1][0]))
-        blocks += plane(value, sources)
-    near = [(flip(value, 0), tuple(source + (0,) for source in sources), gates) for value, sources, gates in blocks]
-    packed, _ = lax.optimization_barrier((packed, near[-5][0]))
+    blocks = plane(own, ((),))
+    far = [()]
+    for bit in range(3, bits):
+        far += [source + (bit,) for source in far]
+    far = tuple(far[1:])
+    value = jnp.concatenate([flip(own, *source) for source in far], axis=1)
+    value, packed, *_ = lax.optimization_barrier((value, packed, blocks[-2][0], blocks[-1][0]))
+    blocks += plane(value, far)
+    near = []
+    for number, (value, sources, gates) in enumerate(blocks):
+        if number >= len(blocks) - 2:
+            value, *_ = lax.optimization_barrier((value, *[earlier for earlier, _, _ in near[: len(blocks) - 2]]))
+        near.append((flip(value, 0), tuple(source + (0,) for source in sources), gates))
     blocks += near
     plan = tuple((sources, gates) for _, sources, gates in blocks)
     return [value for value, _, _ in blocks], plan, trade(packed)

time: 133 us -> 169 us (1.27)
  local copies, waits for them, and re-layouts: 4.98 us -> 39.5 us
  starting transfers between devices: 28.1 us -> 23.7 us
  waiting for transfers between devices: 52.3 us -> 55.7 us
  Pallas kernels: 28.8 us -> 31.5 us
    unnamed x44 -> x92, local copies, waits for them, and re-layouts: 4.29 us -> 38.9 us
    ppermute x21, waiting for transfers between devices: 52.2 us -> 55.7 us  [flip(): return lax.ppermute(value, 'mode', pairs)]
    ppermute x21, starting transfers between devices: 20.1 us -> 17.1 us  [flip(): return lax.ppermute(value, 'mode', pairs)]
    pallas_call x4, Pallas kernels: 28.8 us -> 31.5 us  [call(): pl.pallas_call(kernel, out_shape=jax.ShapeDtypeStruct(out_shape, jnp.bflo...]
  transfers between devices with their start and end apart: 23 -> 23, of which waited for: 12 -> 9; matrix products, arithmetic and copies ran while one was open for 0% -> 0% of each run, Pallas kernels for 11% -> 10%
where the time goes in v6:
time: 169 us; the launch traced here: 168 us
  waiting for transfers between devices  55.7 us (33%)
  local copies, waits for them, and re-layouts  39.5 us (23%)
  Pallas kernels  31.5 us (19%)
  starting transfers between devices  23.7 us (14%)
  blocking collectives  16.2 us (10%)
    ppermute x21, waiting for transfers between devices, flip(): return lax.ppermute(value, 'mode', pairs)  55.7 us
    unnamed x92, local copies, waits for them, and re-layouts  38.9 us
    pallas_call x4, Pallas kernels, call(): pl.pallas_call(kernel, out_shape=jax.ShapeDtypeStruct(out_shape, jnp.bflo...  31.5 us
    ppermute x21, starting transfers between devices, flip(): return lax.ppermute(value, 'mode', pairs)  17.1 us
    all_to_all x1, blocking collectives, trade(): lax.all_to_all(value, 'mode', split_axis=0, concat_axis=0, axis_index_gro...  16.2 us
    all_to_all x2, starting transfers between devices, trade(): lax.all_to_all(value, 'mode', split_axis=0, concat_axis=0, axis_index_gro...  6.62 us
  transfers between devices with their start and end apart: 23, of which 9 were waited for; matrix products, arithmetic and copies ran while one was open for 0% of the time, Pallas kernels for 10%

profile of v6, /device:TPU:0, one launch (start us, length us, event | category | flops | bytes accessed | tf_op | source)
XLA Modules:
  0.0 168.0 jit_solution(11530212734962160223)
XLA Ops:
  0.0 1.0 maximum_bitcast_fusion.refs_0_
  1.0 3.0 %collective-permute-start.5 = (bf16[2,1,2,32,1024]{4,3,2,1,0:T(8,128)(2,1)S(1)}, bf16[2,1,2,32,1024]{4,3,2,1,0:T(8,128)(2,1)S(1)}, u32[]{:S(2)}, u32[]{:S(2)}) collective-permute-start(bf16[2,1,2,32,1024]{4,3,2,1,0:T(8,128)(2,1)S(1)} %maximum_bitcast_fusion.refs_0_), channel_id=1, source_target_pairs={{0,4},{1,5},{2,6},{3,7},{4,0},{5,1},{6,2},{7,3},{8,12},{9,13},{10,... | collective-permute-start | bytes 786440 | tf_op jit(solution)/shard_map/ppermute | solution.py:270
  4.0 1.5 collective-permute-start.3
  5.5 3.6 %collective-permute-start.2 = (bf16[2,1,2,32,1024]{4,3,2,1,0:T(8,128)(2,1)S(1)}, bf16[2,1,2,32,1024]{4,3,2,1,0:T(8,128)(2,1)S(1)}, u32[]{:S(2)}, u32[]{:S(2)}) collective-permute-start(bf16[2,1,2,32,1024]{4,3,2,1,0:T(8,128)(2,1)S(1)} %maximum_bitcast_fusion.refs_0_), channel_id=1, source_target_pairs={{0,24},{1,25},{2,26},{3,27},{4,28},{5,29},{6,30},{7,31},{8,16},{9,... | collective-permute-start | bytes 786440 | tf_op jit(solution)/shard_map/ppermute | solution.py:270
  9.9 1.2 copy-done.8
  11.2 2.8 %shard_map.46 = bf16[512,1024]{1,0:T(8,128)(2,1)} custom-call(bf16[4,2,64,1024]{3,2,1,0:T(8,128)(2,1)S(1)} %copy-done.8, s32[4,1024]{1,0:T(4,128)S(1)} %copy-done.45), custom_call_target="tpu_custom_call" | custom-call | flops 2147483648 | bytes 1064960 | tf_op jit(solution)/shard_map/pallas_call | solution.py:189
  14.9 1.8 %collective-permute-done.2 = bf16[2,1,2,32,1024]{4,3,2,1,0:T(8,128)(2,1)S(1)} collective-permute-done((bf16[2,1,2,32,1024]{4,3,2,1,0:T(8,128)(2,1)S(1)}, bf16[2,1,2,32,1024]{4,3,2,1,0:T(8,128)(2,1)S(1)}, u32[]{:S(2)}, u32[]{:S(2)}) %collective-permute-start.2) | collective-permute-done | bytes 262176 | tf_op jit(solution)/shard_map/ppermute | solution.py:270
  16.7 14.2 %collective-permute-done.1 = bf16[2,1,2,32,1024]{4,3,2,1,0:T(8,128)(2,1)S(1)} collective-permute-done((bf16[2,1,2,32,1024]{4,3,2,1,0:T(8,128)(2,1)S(1)}, bf16[2,1,2,32,1024]{4,3,2,1,0:T(8,128)(2,1)S(1)}, u32[]{:S(2)}, u32[]{:S(2)}) %collective-permute-start.1) | collective-permute-done | bytes 262176 | tf_op jit(solution)/shard_map/ppermute | solution.py:270
  31.0 2.8 %all-to-all-start = ((bf16[32,16,1024]{2,1,0:T(8,128)(2,1)}), bf16[32,16,1024]{2,1,0:T(8,128)(2,1)S(1)}, u32[]{:S(2)}, u32[]{:S(2)}) async-start(bf16[32,16,1024]{2,1,0:T(8,128)(2,1)} %bitcast.3), calls=%async_computation | async-start | bytes 2097152 | tf_op jit(solution)/shard_map/all_to_all | solution.py:308
  33.9 1.8 %collective-permute-start.8 = (bf16[2,3,2,32,1024]{4,3,2,1,0:T(8,128)(2,1)S(1)}, bf16[2,3,2,32,1024]{4,3,2,1,0:T(8,128)(2,1)S(1)}, u32[]{:S(2)}, u32[]{:S(2)}) collective-permute-start(bf16[2,3,2,32,1024]{4,3,2,1,0:T(8,128)(2,1)S(1)} %pad_maximum_fusion.refs_5_), channel_id=1, source_target_pairs={{0,4},{1,5},{2,6},{3,7},{4,0},{5,1},{6,2},{7,3},{8,12},{9,13},{10,... | collective-permute-start | bytes 2359304 | tf_op jit(solution)/shard_map/ppermute | solution.py:270
  35.7 1.5 collective-permute-start.7
  37.7 27.1 %collective-permute-done.8.refs_7_ = bf16[2,3,2,32,1024]{4,3,2,1,0:T(8,128)(2,1)S(1)} collective-permute-done((bf16[2,3,2,32,1024]{4,3,2,1,0:T(8,128)(2,1)S(1)}, bf16[2,3,2,32,1024]{4,3,2,1,0:T(8,128)(2,1)S(1)}, u32[]{:S(2)}, u32[]{:S(2)}) %collective-permute-start.8) | collective-permute-done | bytes 786464 | tf_op jit(solution)/shard_map/ppermute | solution.py:270
  65.4 3.0 %collective-permute-done.15.refs_14_ = bf16[1,1,2,32,1024]{4,3,2,1,0:T(8,128)(2,1)S(1)} collective-permute-done((bf16[1,1,2,32,1024]{4,3,2,1,0:T(8,128)(2,1)S(1)}, bf16[1,1,2,32,1024]{4,3,2,1,0:T(8,128)(2,1)S(1)}, u32[]{:S(2)}, u32[]{:S(2)}) %collective-permute-start.15) | collective-permute-done | bytes 131104 | tf_op jit(solution)/shard_map/ppermute | solution.py:270
  71.9 1.5 collective-permute-start.10
  75.4 7.9 %collective-permute-done.10.refs_9_ = bf16[1,3,2,32,1024]{4,3,2,1,0:T(8,128)(2,1)S(1)} collective-permute-done((bf16[1,3,2,32,1024]{4,3,2,1,0:T(8,128)(2,1)S(1)}, bf16[1,3,2,32,1024]{4,3,2,1,0:T(8,128)(2,1)S(1)}, u32[]{:S(2)}, u32[]{:S(2)}) %collective-permute-start.10) | collective-permute-done | bytes 393248 | tf_op jit(solution)/shard_map/ppermute | solution.py:270
  88.6 1.1 copy-done.1
  89.8 1.1 copy-done.4
  90.9 1.1 copy-done.10
  92.0 1.1 copy-done.13
  93.2 1.1 copy-done.16
  94.3 1.0 copy-done.21
  95.3 1.0 copy-done.24
  101.0 14.8 %shard_map.47 = bf16[2048,128]{1,0:T(8,128)(2,1)} custom-call(bf16[512,1024]{1,0:T(8,128)(2,1)S(1)} %bitcast.14, bf16[2,1,2,32,1024]{4,3,2,1,0:T(8,128)(2,1)S(1)} %maximum_bitcast_fusion.refs_0_, bf16[2,1,2,32,1024]{4,3,2,1,0:T(8,128)(2,1)S(1)} %collective-permute-done.3.refs_1_, bf16[2,1,2,32,1024]{4,3,2,1,0:T(8,128)(2,1)S(1)} %collective-permute-done.5.refs_2_, ...), custom_call_target="tpu_custom_call" | custom-call | flops 4294967296 | bytes 9437184 | tf_op jit(solution)/shard_map/pallas_call | solution.py:189
  117.3 3.8 %all-to-all-start.1 = ((bf16[16,128,128]{2,1,0:T(8,128)(2,1)}), bf16[16,128,128]{2,1,0:T(8,128)(2,1)S(1)}, u32[]{:S(2)}, u32[]{:S(2)}) async-start(bf16[16,128,128]{2,1,0:T(8,128)(2,1)} %bitcast.5), calls=%async_computation.1 | async-start | bytes 1048576 | tf_op jit(solution)/shard_map/all_to_all | solution.py:308
  121.1 1.1 copy-done.2
  122.2 1.1 copy-done.5
  124.3 1.1 copy-done.11
  125.4 1.1 copy-done.14
  126.6 1.1 copy-done.17
  129.7 1.0 copy-done.25
  137.3 13.3 %shard_map.48.right_ref = bf16[256,1024]{1,0:T(8,128)(2,1)S(1)} custom-call(bf16[512,1024]{1,0:T(8,128)(2,1)S(1)} %bitcast.15, bf16[2,1,2,32,1024]{4,3,2,1,0:T(8,128)(2,1)S(1)} %maximum_bitcast_fusion.refs_0_, bf16[2,1,2,32,1024]{4,3,2,1,0:T(8,128)(2,1)S(1)} %copy-done.7, bf16[2,1,2,32,1024]{4,3,2,1,0:T(8,128)(2,1)S(1)} %collective-permute-done.5.refs_2_, ...), custom_call_target="tpu_custom_call" | custom-call | flops 4294967296 | bytes 9437184 | tf_op jit(solution)/shard_map/pallas_call | solution.py:189
  151.1 16.2 %all_to_all.15 = bf16[32,16,256]{2,1,0:T(8,128)(2,1)S(1)} all-to-all(bf16[32,16,256]{2,1,0:T(8,128)(2,1)S(1)} %bitcast.13), channel_id=1, replica_groups=mesh['cuts'=1,'mode'=32] {'mode'}, dimensions={0} | all-to-all | bytes 524288 | tf_op jit(solution)/shard_map/all_to_all | solution.py:308
  (120 shorter events, 30.6 us)
Async XLA Ops:
  0.0 9.9 %copy-start.45 = (s32[4,1024]{1,0:T(4,128)S(1)}, s32[4,1024]{1,0:T(4,128)}, u32[]{:S(2)}) copy-start(s32[4,1024]{1,0:T(4,128)} %order_ref.1) | copy-start | bytes 49156
  1.0 12.9 %collective-permute-start.5 = (bf16[2,1,2,32,1024]{4,3,2,1,0:T(8,128)(2,1)S(1)}, bf16[2,1,2,32,1024]{4,3,2,1,0:T(8,128)(2,1)S(1)}, u32[]{:S(2)}, u32[]{:S(2)}) collective-permute-start(bf16[2,1,2,32,1024]{4,3,2,1,0:T(8,128)(2,1)S(1)} %maximum_bitcast_fusion.refs_0_), channel_id=1, source_target_pairs={{0,4},{1,5},{2,6},{3,7},{4,0},{5,1},{6,2},{7,3},{8,12},{9,13},{10,... | collective-permute-start | bytes 786440 | tf_op jit(solution)/shard_map/ppermute | solution.py:270
  4.0 10.5 %collective-permute-start.3 = (bf16[2,1,2,32,1024]{4,3,2,1,0:T(8,128)(2,1)S(1)}, bf16[2,1,2,32,1024]{4,3,2,1,0:T(8,128)(2,1)S(1)}, u32[]{:S(2)}, u32[]{:S(2)}) collective-permute-start(bf16[2,1,2,32,1024]{4,3,2,1,0:T(8,128)(2,1)S(1)} %maximum_bitcast_fusion.refs_0_), channel_id=1, source_target_pairs={{0,2},{1,3},{2,0},{3,1},{4,6},{5,7},{6,4},{7,5},{8,10},{9,11},{10,... | collective-permute-start | bytes 786440 | tf_op jit(solution)/shard_map/ppermute | solution.py:270
  5.5 11.1 %collective-permute-start.2 = (bf16[2,1,2,32,1024]{4,3,2,1,0:T(8,128)(2,1)S(1)}, bf16[2,1,2,32,1024]{4,3,2,1,0:T(8,128)(2,1)S(1)}, u32[]{:S(2)}, u32[]{:S(2)}) collective-permute-start(bf16[2,1,2,32,1024]{4,3,2,1,0:T(8,128)(2,1)S(1)} %maximum_bitcast_fusion.refs_0_), channel_id=1, source_target_pairs={{0,24},{1,25},{2,26},{3,27},{4,28},{5,29},{6,30},{7,31},{8,16},{9,... | collective-permute-start | bytes 786440 | tf_op jit(solution)/shard_map/ppermute | solution.py:270
  9.1 21.7 %collective-permute-start.1 = (bf16[2,1,2,32,1024]{4,3,2,1,0:T(8,128)(2,1)S(1)}, bf16[2,1,2,32,1024]{4,3,2,1,0:T(8,128)(2,1)S(1)}, u32[]{:S(2)}, u32[]{:S(2)}) collective-permute-start(bf16[2,1,2,32,1024]{4,3,2,1,0:T(8,128)(2,1)S(1)} %maximum_bitcast_fusion.refs_0_), channel_id=1, source_target_pairs={{0,16},{1,17},{2,18},{3,19},{4,20},{5,21},{6,22},{7,23},{8,24},{9,... | collective-permute-start | bytes 786440 | tf_op jit(solution)/shard_map/ppermute | solution.py:270
  9.1 21.7 %collective-permute-start = (bf16[2,1,2,32,1024]{4,3,2,1,0:T(8,128)(2,1)S(1)}, bf16[2,1,2,32,1024]{4,3,2,1,0:T(8,128)(2,1)S(1)}, u32[]{:S(2)}, u32[]{:S(2)}) collective-permute-start(bf16[2,1,2,32,1024]{4,3,2,1,0:T(8,128)(2,1)S(1)} %maximum_bitcast_fusion.refs_0_), channel_id=1, source_target_pairs={{0,8},{1,9},{2,10},{3,11},{4,12},{5,13},{6,14},{7,15},{8,0},{9,1},... | collective-permute-start | bytes 786440 | tf_op jit(solution)/shard_map/ppermute | solution.py:270
  9.9 1.2 copy-start.8
  13.9 17.0 %collective-permute-start.6 = (bf16[1,1,2,32,1024]{4,3,2,1,0:T(8,128)(2,1)S(1)}, bf16[1,1,2,32,1024]{4,3,2,1,0:T(8,128)(2,1)S(1)}, u32[]{:S(2)}, u32[]{:S(2)}) collective-permute-start(bf16[1,1,2,32,1024]{4,3,2,1,0:T(8,128)(2,1)S(1)} %slice.17), channel_id=1, source_target_pairs={{0,2},{1,3},{2,0},{3,1},{4,6},{5,7},{6,4},{7,5},{8,10},{9,11},{10,... | collective-permute-start | bytes 393224 | tf_op jit(solution)/shard_map/ppermute | solution.py:270
  14.5 74.1 %copy-start.6 = (bf16[2,1,2,32,1024]{4,3,2,1,0:T(8,128)(2,1)}, bf16[2,1,2,32,1024]{4,3,2,1,0:T(8,128)(2,1)S(1)}, u32[]{:S(2)}) copy-start(bf16[2,1,2,32,1024]{4,3,2,1,0:T(8,128)(2,1)S(1)} %collective-permute-done.3.refs_1_) | copy-start | bytes 786436
  14.6 16.4 %collective-permute-start.4 = (bf16[1,1,2,32,1024]{4,3,2,1,0:T(8,128)(2,1)S(1)}, bf16[1,1,2,32,1024]{4,3,2,1,0:T(8,128)(2,1)S(1)}, u32[]{:S(2)}, u32[]{:S(2)}) collective-permute-start(bf16[1,1,2,32,1024]{4,3,2,1,0:T(8,128)(2,1)S(1)} %slice.16), channel_id=1, source_target_pairs={{0,4},{1,5},{2,6},{3,7},{4,0},{5,1},{6,2},{7,3},{8,12},{9,13},{10,... | collective-permute-start | bytes 393224 | tf_op jit(solution)/shard_map/ppermute | solution.py:270
  31.0 57.6 %copy-start.37 = (bf16[1,1,2,32,1024]{4,3,2,1,0:T(8,128)(2,1)}, bf16[1,1,2,32,1024]{4,3,2,1,0:T(8,128)(2,1)S(1)}, u32[]{:S(2)}) copy-start(bf16[1,1,2,32,1024]{4,3,2,1,0:T(8,128)(2,1)S(1)} %collective-permute-done.4.refs_3_) | copy-start | bytes 393220
  31.0 57.6 %all-to-all-start = ((bf16[32,16,1024]{2,1,0:T(8,128)(2,1)}), bf16[32,16,1024]{2,1,0:T(8,128)(2,1)S(1)}, u32[]{:S(2)}, u32[]{:S(2)}) async-start(bf16[32,16,1024]{2,1,0:T(8,128)(2,1)} %bitcast.3), calls=%async_computation | async-start | bytes 2097152 | tf_op jit(solution)/shard_map/all_to_all | solution.py:308
  33.9 31.0 %collective-permute-start.8 = (bf16[2,3,2,32,1024]{4,3,2,1,0:T(8,128)(2,1)S(1)}, bf16[2,3,2,32,1024]{4,3,2,1,0:T(8,128)(2,1)S(1)}, u32[]{:S(2)}, u32[]{:S(2)}) collective-permute-start(bf16[2,3,2,32,1024]{4,3,2,1,0:T(8,128)(2,1)S(1)} %pad_maximum_fusion.refs_5_), channel_id=1, source_target_pairs={{0,4},{1,5},{2,6},{3,7},{4,0},{5,1},{6,2},{7,3},{8,12},{9,13},{10,... | collective-permute-start | bytes 2359304 | tf_op jit(solution)/shard_map/ppermute | solution.py:270
  35.7 29.1 %collective-permute-start.7 = (bf16[2,3,2,32,1024]{4,3,2,1,0:T(8,128)(2,1)S(1)}, bf16[2,3,2,32,1024]{4,3,2,1,0:T(8,128)(2,1)S(1)}, u32[]{:S(2)}, u32[]{:S(2)}) collective-permute-start(bf16[2,3,2,32,1024]{4,3,2,1,0:T(8,128)(2,1)S(1)} %pad_maximum_fusion.refs_5_), channel_id=1, source_target_pairs={{0,2},{1,3},{2,0},{3,1},{4,6},{5,7},{6,4},{7,5},{8,10},{9,11},{10,... | collective-permute-start | bytes 2359304 | tf_op jit(solution)/shard_map/ppermute | solution.py:270
  37.2 28.2 %collective-permute-start.11 = (bf16[2,1,2,32,1024]{4,3,2,1,0:T(8,128)(2,1)S(1)}, bf16[2,1,2,32,1024]{4,3,2,1,0:T(8,128)(2,1)S(1)}, u32[]{:S(2)}, u32[]{:S(2)}) collective-permute-start(bf16[2,1,2,32,1024]{4,3,2,1,0:T(8,128)(2,1)S(1)} %maximum_bitcast_fusion.refs_0_), channel_id=1, source_target_pairs={{0,1},{1,0},{2,3},{3,2},{4,5},{5,4},{6,7},{7,6},{8,9},{9,8},{10,11... | collective-permute-start | bytes 786440 | tf_op jit(solution)/shard_map/ppermute | solution.py:270
  37.2 32.0 %collective-permute-start.13 = (bf16[2,1,2,32,1024]{4,3,2,1,0:T(8,128)(2,1)S(1)}, bf16[2,1,2,32,1024]{4,3,2,1,0:T(8,128)(2,1)S(1)}, u32[]{:S(2)}, u32[]{:S(2)}) collective-permute-start(bf16[2,1,2,32,1024]{4,3,2,1,0:T(8,128)(2,1)S(1)} %collective-permute-done.5.refs_2_), channel_id=1, source_target_pairs={{0,1},{1,0},{2,3},{3,2},{4,5},{5,4},{6,7},{7,6},{8,9},{9,8},{10,11... | collective-permute-start | bytes 786440 | tf_op jit(solution)/shard_map/ppermute | solution.py:270
  37.7 36.8 %collective-permute-start.16 = (bf16[2,3,2,32,1024]{4,3,2,1,0:T(8,128)(2,1)S(1)}, bf16[2,3,2,32,1024]{4,3,2,1,0:T(8,128)(2,1)S(1)}, u32[]{:S(2)}, u32[]{:S(2)}) collective-permute-start(bf16[2,3,2,32,1024]{4,3,2,1,0:T(8,128)(2,1)S(1)} %pad_maximum_fusion.refs_5_), channel_id=1, source_target_pairs={{0,1},{1,0},{2,3},{3,2},{4,5},{5,4},{6,7},{7,6},{8,9},{9,8},{10,11... | collective-permute-start | bytes 2359304 | tf_op jit(solution)/shard_map/ppermute | solution.py:270
  64.8 8.6 %copy-start = (bf16[2,3,2,32,1024]{4,3,2,1,0:T(8,128)(2,1)}, bf16[2,3,2,32,1024]{4,3,2,1,0:T(8,128)(2,1)S(1)}, u32[]{:S(2)}) copy-start(bf16[2,3,2,32,1024]{4,3,2,1,0:T(8,128)(2,1)S(1)} %collective-permute-done.8.refs_7_) | copy-start | bytes 2359300
  64.8 18.5 %collective-permute-start.18 = (bf16[2,3,2,32,1024]{4,3,2,1,0:T(8,128)(2,1)S(1)}, bf16[2,3,2,32,1024]{4,3,2,1,0:T(8,128)(2,1)S(1)}, u32[]{:S(2)}, u32[]{:S(2)}) collective-permute-start(bf16[2,3,2,32,1024]{4,3,2,1,0:T(8,128)(2,1)S(1)} %collective-permute-done.8.refs_7_), channel_id=1, source_target_pairs={{0,1},{1,0},{2,3},{3,2},{4,5},{5,4},{6,7},{7,6},{8,9},{9,8},{10,11... | collective-permute-start | bytes 2359304 | tf_op jit(solution)/shard_map/ppermute | solution.py:270
  64.8 8.6 %copy-start.3 = (bf16[2,3,2,32,1024]{4,3,2,1,0:T(8,128)(2,1)}, bf16[2,3,2,32,1024]{4,3,2,1,0:T(8,128)(2,1)S(1)}, u32[]{:S(2)}) copy-start(bf16[2,3,2,32,1024]{4,3,2,1,0:T(8,128)(2,1)S(1)} %collective-permute-done.7.refs_6_) | copy-start | bytes 2359300
  64.8 19.4 %collective-permute-start.17 = (bf16[2,3,2,32,1024]{4,3,2,1,0:T(8,128)(2,1)S(1)}, bf16[2,3,2,32,1024]{4,3,2,1,0:T(8,128)(2,1)S(1)}, u32[]{:S(2)}, u32[]{:S(2)}) collective-permute-start(bf16[2,3,2,32,1024]{4,3,2,1,0:T(8,128)(2,1)S(1)} %collective-permute-done.7.refs_6_), channel_id=1, source_target_pairs={{0,1},{1,0},{2,3},{3,2},{4,5},{5,4},{6,7},{7,6},{8,9},{9,8},{10,11... | collective-permute-start | bytes 2359304 | tf_op jit(solution)/shard_map/ppermute | solution.py:270
  65.3 3.1 %collective-permute-start.15 = (bf16[1,1,2,32,1024]{4,3,2,1,0:T(8,128)(2,1)S(1)}, bf16[1,1,2,32,1024]{4,3,2,1,0:T(8,128)(2,1)S(1)}, u32[]{:S(2)}, u32[]{:S(2)}) collective-permute-start(bf16[1,1,2,32,1024]{4,3,2,1,0:T(8,128)(2,1)S(1)} %collective-permute-done.6.refs_4_), channel_id=1, source_target_pairs={{0,1},{1,0},{2,3},{3,2},{4,5},{5,4},{6,7},{7,6},{8,9},{9,8},{10,11... | collective-permute-start | bytes 393224 | tf_op jit(solution)/shard_map/ppermute | solution.py:270
  69.1 4.4 %collective-permute-start.12 = (bf16[2,1,2,32,1024]{4,3,2,1,0:T(8,128)(2,1)S(1)}, bf16[2,1,2,32,1024]{4,3,2,1,0:T(8,128)(2,1)S(1)}, u32[]{:S(2)}, u32[]{:S(2)}) collective-permute-start(bf16[2,1,2,32,1024]{4,3,2,1,0:T(8,128)(2,1)S(1)} %collective-permute-done.3.refs_1_), channel_id=1, source_target_pairs={{0,1},{1,0},{2,3},{3,2},{4,5},{5,4},{6,7},{7,6},{8,9},{9,8},{10,11... | collective-permute-start | bytes 786440 | tf_op jit(solution)/shard_map/ppermute | solution.py:270
  69.9 1.4 collective-permute-start.14
  71.9 11.4 %collective-permute-start.10 = (bf16[1,3,2,32,1024]{4,3,2,1,0:T(8,128)(2,1)S(1)}, bf16[1,3,2,32,1024]{4,3,2,1,0:T(8,128)(2,1)S(1)}, u32[]{:S(2)}, u32[]{:S(2)}) collective-permute-start(bf16[1,3,2,32,1024]{4,3,2,1,0:T(8,128)(2,1)S(1)} %slice.19), channel_id=1, source_target_pairs={{0,2},{1,3},{2,0},{3,1},{4,6},{5,7},{6,4},{7,5},{8,10},{9,11},{10,... | collective-permute-start | bytes 1179656 | tf_op jit(solution)/shard_map/ppermute | solution.py:270
  74.2 11.1 %collective-permute-start.9 = (bf16[1,3,2,32,1024]{4,3,2,1,0:T(8,128)(2,1)S(1)}, bf16[1,3,2,32,1024]{4,3,2,1,0:T(8,128)(2,1)S(1)}, u32[]{:S(2)}, u32[]{:S(2)}) collective-permute-start(bf16[1,3,2,32,1024]{4,3,2,1,0:T(8,128)(2,1)S(1)} %slice.18), channel_id=1, source_target_pairs={{0,4},{1,5},{2,6},{3,7},{4,0},{5,1},{6,2},{7,3},{8,12},{9,13},{10,... | collective-permute-start | bytes 1179656 | tf_op jit(solution)/shard_map/ppermute | solution.py:270
  85.2 1.7 %collective-permute-start.19 = (bf16[1,3,2,32,1024]{4,3,2,1,0:T(8,128)(2,1)S(1)}, bf16[1,3,2,32,1024]{4,3,2,1,0:T(8,128)(2,1)S(1)}, u32[]{:S(2)}, u32[]{:S(2)}) collective-permute-start(bf16[1,3,2,32,1024]{4,3,2,1,0:T(8,128)(2,1)S(1)} %collective-permute-done.9.refs_8_), channel_id=1, source_target_pairs={{0,1},{1,0},{2,3},{3,2},{4,5},{5,4},{6,7},{7,6},{8,9},{9,8},{10,11... | collective-permute-start | bytes 1179656 | tf_op jit(solution)/shard_map/ppermute | solution.py:270
  86.0 1.9 %collective-permute-start.20 = (bf16[1,3,2,32,1024]{4,3,2,1,0:T(8,128)(2,1)S(1)}, bf16[1,3,2,32,1024]{4,3,2,1,0:T(8,128)(2,1)S(1)}, u32[]{:S(2)}, u32[]{:S(2)}) collective-permute-start(bf16[1,3,2,32,1024]{4,3,2,1,0:T(8,128)(2,1)S(1)} %collective-permute-done.10.refs_9_), channel_id=1, source_target_pairs={{0,1},{1,0},{2,3},{3,2},{4,5},{5,4},{6,7},{7,6},{8,9},{9,8},{10,11... | collective-permute-start | bytes 1179656 | tf_op jit(solution)/shard_map/ppermute | solution.py:270
  88.6 1.1 copy-start.1
  89.8 1.1 copy-start.4
  117.3 33.2 %all-to-all-start.1 = ((bf16[16,128,128]{2,1,0:T(8,128)(2,1)}), bf16[16,128,128]{2,1,0:T(8,128)(2,1)S(1)}, u32[]{:S(2)}, u32[]{:S(2)}) async-start(bf16[16,128,128]{2,1,0:T(8,128)(2,1)} %bitcast.5), calls=%async_computation.1 | async-start | bytes 1048576 | tf_op jit(solution)/shard_map/all_to_all | solution.py:308
  121.1 1.1 copy-start.2
  (37 other events, 34.3 us)

commit v7 on v5

--- a/solution.py
+++ b/solution.py
@@ -11,7 +11,7 @@
 KEPT = 4
 CYCLES = 2
 LANES = 128
-VMEM_LIMIT = 56 * 1024 * 1024
+MEBI = 1024 * 1024
 
 
 def whole(count):
@@ -52,7 +52,8 @@
     return jnp.where(row < qs, -turned, turned)
 
 
-def regroup_store(acc, first_lane, group, devices, tile_rows, x_ref, h_ref):
+def regroup_store(acc, first_lane, group, devices, tile_rows, x_ref):
+    width = x_ref.shape[1] // 2
     per = LANES // group
     lane = lax.broadcasted_iota(jnp.int32, (tile_rows, LANES), 1) // group
     for offset in range(0, acc.shape[1], LANES):
@@ -77,7 +78,7 @@
             lanes = pl.ds(block * LANES, LANES)
             x_ref[rows, lanes] = tiles.reshape(per * tile_rows, LANES).astype(jnp.bfloat16)
             turned = swap_sign(tiles, tile_rows // 2)
-            h_ref[rows, lanes] = turned.reshape(per * tile_rows, LANES).astype(jnp.bfloat16)
+            x_ref[rows, pl.ds(width + block * LANES, LANES)] = turned.reshape(per * tile_rows, LANES).astype(jnp.bfloat16)
 
 
 def gate_copies(plan, blocks, whole_ref, sems):
@@ -100,7 +101,7 @@
 
 def layers_kernel(sizes, is_left, plan, x_ref, *refs):
     devices, qs, group, rows_each = sizes
-    blocks, (o_ref, xs, hs, last, whole_ref, sems) = refs[: len(plan)], refs[len(plan) :]
+    blocks, (o_ref, xs, last, whole_ref, sems) = refs[: len(plan)], refs[len(plan) :]
     copies = gate_copies(plan, blocks, whole_ref, sems)
     for gate in range(2):
         for copy in copies[gate]:
@@ -109,21 +110,20 @@
     rows, width = x_ref.shape[0] // 2, x_ref.shape[1]
     first = x_ref[...].astype(jnp.float32).reshape(devices, 2 * tile_rows, width)
     first = first[:, :tile_rows] if is_left else first[:, tile_rows:]
-    xs[0] = first.reshape(rows, width).astype(jnp.bfloat16)
-    hs[0] = swap_sign(first, qs).reshape(rows, width).astype(jnp.bfloat16)
+    xs[0, :, :width] = first.reshape(rows, width).astype(jnp.bfloat16)
+    xs[0, :, width:] = swap_sign(first, qs).reshape(rows, width).astype(jnp.bfloat16)
     step = min(512, width)
     for layer in range(2 * CYCLES):
         if layer < 2:
             for copy in copies[layer]:
                 copy.wait()
         gate = whole_ref.at[layer % 2]
-        here, turned = xs.at[layer % 2], hs.at[layer % 2]
-        later = (layer + 1) % 2
+        here, later = xs.at[layer % 2], xs.at[(layer + 1) % 2]
         for start in range(0, width, step):
             cols = slice(start, start + step)
-            acc = exact_dot(here[...], gate[0, :, cols]) + exact_dot(turned[...], gate[1, :, cols])
+            acc = exact_dot(here[...], gate[:, :, cols].reshape(2 * width, step))
             if layer < 2 * CYCLES - 1:
-                regroup_store(acc, start, group, devices, tile_rows, xs.at[later], hs.at[later])
+                regroup_store(acc, start, group, devices, tile_rows, later)
             else:
                 last[:, cols] = acc.astype(jnp.bfloat16)
     half = rows // 2
@@ -184,7 +184,7 @@
         o_ref[g * block : (g + 1) * block, :] = part.astype(jnp.bfloat16)
 
 
-def call(kernel, out_shape, inputs, scratch=(), flops=0, blocks=()):
+def call(kernel, out_shape, inputs, scratch=(), flops=0, blocks=(), grant=24):
     moved = sum(x.size * x.dtype.itemsize for x in (*inputs, *blocks))
     return pl.pallas_call(
         kernel,
@@ -192,7 +192,7 @@
         in_specs=whole(len(inputs)) + [pl.BlockSpec(memory_space=pl.ANY)] * len(blocks),
         out_specs=whole(1)[0],
         scratch_shapes=list(scratch),
-        compiler_params=pltpu.CompilerParams(vmem_limit_bytes=VMEM_LIMIT),
+        compiler_params=pltpu.CompilerParams(vmem_limit_bytes=grant * MEBI),
         cost_estimate=pl.CostEstimate(flops=flops, bytes_accessed=moved, transcendentals=0),
     )(*inputs, *blocks)
 
@@ -231,7 +231,8 @@
     blocks, plan, states = spread(gate_a, gate_b, packed.reshape(devices, 2 * tile_rows, width))
     states = states.reshape(2 * rows, width)
     sizes = (devices, qs, group, rows_each)
-    scratch = [pltpu.VMEM((2, rows, width), jnp.bfloat16)] * 2 + [
+    scratch = [
+        pltpu.VMEM((2, rows, 2 * width), jnp.bfloat16),
         pltpu.VMEM((rows, width), jnp.bfloat16),
         pltpu.VMEM((2, 2, width, width), jnp.bfloat16),
         pltpu.SemaphoreType.DMA((2, devices)),
@@ -244,11 +245,12 @@
         scratch,
         work,
         blocks,
+        56,
     )
     groups = [[h * halves + e for e in range(halves)] for h in range(2)]
     left = trade(left.reshape(halves, rows // 2, LANES), groups)
     right = call(
-        functools.partial(layers_kernel, sizes, False, plan), (rows, width), (states,), scratch, work, blocks
+        functools.partial(layers_kernel, sizes, False, plan), (rows, width), (states,), scratch, work, blocks, 56
     )
     free = width // (2 * KEPT)
     us = halves
@@ -300,12 +302,18 @@
         if number == 1:
             value, packed, *_ = lax.optimization_barrier((value, packed, blocks[-2][0], blocks[-1][0]))
         elif number:
-            value, *_ = lax.optimization_barrier((value, blocks[-4][0], blocks[-3][0]))
+            value, *_ = lax.optimization_barrier((value, blocks[-2][0], blocks[-1][0]))
         early = [later for later, _ in sets[2:]] if number == 1 else []
         blocks += plane(value, sources, early)
-    blocks += [
-        (flip(value, 0), tuple(source + (0,) for source in sources), gates) for value, sources, gates in blocks
-    ]
+    packed, *_ = lax.optimization_barrier((packed, *[value for value, _ in sets[1:]]))
+    last = [len(blocks) - 2, len(blocks) - 1]
+    near = {}
+    for number in [number for number in range(len(blocks)) if number not in last] + last:
+        value, sources, gates = blocks[number]
+        if number in last:
+            value, *_ = lax.optimization_barrier((value, *[near[n][0] for n in near if n not in last]))
+        near[number] = (flip(value, 0), tuple(source + (0,) for source in sources), gates)
+    blocks += near.values()
     plan = tuple((sources, gates) for _, sources, gates in blocks)
     return [value for value, _, _ in blocks], plan, trade(packed)
 

time: 131 us -> 137 us (1.046)
  waiting for transfers between devices: 37.6 us -> 58.7 us
  starting transfers between devices: 44.2 us -> 28.8 us
  Pallas kernels: 28.8 us -> 25.7 us
  blocking collectives: 14.7 us -> 16.3 us
    ppermute x30, waiting for transfers between devices: 37.6 us -> 58.7 us  [flip(): return lax.ppermute(value, 'mode', pairs)]
    all_to_all x2, starting transfers between devices: 16.9 us -> 7.26 us  [trade(): lax.all_to_all(value, 'mode', split_axis=0, concat_axis=0, axis_index_gro...]
    ppermute x30, starting transfers between devices: 27.3 us -> 21.5 us  [flip(): return lax.ppermute(value, 'mode', pairs)]
    pallas_call x4, Pallas kernels: 28.8 us -> 25.7 us  [call(): pl.pallas_call(kernel, out_shape=jax.ShapeDtypeStruct(out_shape, jnp.bflo...]
    all_to_all x1, blocking collectives: 14.7 us -> 16.3 us  [trade(): lax.all_to_all(value, 'mode', split_axis=0, concat_axis=0, axis_index_gro...]
    unnamed x56 -> x71, local copies, waits for them, and re-layouts: 3.26 us -> 4.33 us
  transfers between devices with their start and end apart: 32 -> 32, of which waited for: 15 -> 12; matrix products, arithmetic and copies ran while one was open for 0% -> 0% of each run, Pallas kernels for 11% -> 10%
where the time goes in v7:
time: 137 us; the launch traced here: 136 us
  waiting for transfers between devices  58.7 us (43%)
  starting transfers between devices  28.8 us (21%)
  Pallas kernels  25.7 us (19%)
  blocking collectives  16.3 us (12%)
  local copies, waits for them, and re-layouts  5.04 us (4%)
    ppermute x30, waiting for transfers between devices, flip(): return lax.ppermute(value, 'mode', pairs)  58.7 us
    pallas_call x4, Pallas kernels, call(): pl.pallas_call(kernel, out_shape=jax.ShapeDtypeStruct(out_shape, jnp.bflo...  25.7 us
    ppermute x30, starting transfers between devices, flip(): return lax.ppermute(value, 'mode', pairs)  21.5 us
    all_to_all x1, blocking collectives, trade(): lax.all_to_all(value, 'mode', split_axis=0, concat_axis=0, axis_index_gro...  16.3 us
    all_to_all x2, starting transfers between devices, trade(): lax.all_to_all(value, 'mode', split_axis=0, concat_axis=0, axis_index_gro...  7.26 us
    unnamed x71, local copies, waits for them, and re-layouts  4.33 us
  transfers between devices with their start and end apart: 32, of which 12 were waited for; matrix products, arithmetic and copies ran while one was open for 0% of the time, Pallas kernels for 10%

profile of v7, /device:TPU:0, one launch (start us, length us, event | category | flops | bytes accessed | tf_op | source)
XLA Modules:
  0.0 136.1 jit_solution(11952435504786024023)
XLA Ops:
  0.0 1.0 maximum_bitcast_fusion.refs_0_
  1.0 3.0 %collective-permute-start.3 = (bf16[2,1,2,32,1024]{4,3,2,1,0:T(8,128)(2,1)S(1)}, bf16[2,1,2,32,1024]{4,3,2,1,0:T(8,128)(2,1)S(1)}, u32[]{:S(2)}, u32[]{:S(2)}) collective-permute-start(bf16[2,1,2,32,1024]{4,3,2,1,0:T(8,128)(2,1)S(1)} %maximum_bitcast_fusion.refs_0_), channel_id=1, source_target_pairs={{0,4},{1,5},{2,6},{3,7},{4,0},{5,1},{6,2},{7,3},{8,12},{9,13},{10,... | collective-permute-start | bytes 786440 | tf_op jit(solution)/shard_map/ppermute | solution.py:272
  4.1 1.5 %collective-permute-start.2 = (bf16[2,1,2,32,1024]{4,3,2,1,0:T(8,128)(2,1)S(1)}, bf16[2,1,2,32,1024]{4,3,2,1,0:T(8,128)(2,1)S(1)}, u32[]{:S(2)}, u32[]{:S(2)}) collective-permute-start(bf16[2,1,2,32,1024]{4,3,2,1,0:T(8,128)(2,1)S(1)} %maximum_bitcast_fusion.refs_0_), channel_id=1, source_target_pairs={{0,2},{1,3},{2,0},{3,1},{4,6},{5,7},{6,4},{7,5},{8,10},{9,11},{10,... | collective-permute-start | bytes 786440 | tf_op jit(solution)/shard_map/ppermute | solution.py:272
  5.5 1.6 %collective-permute-start = (bf16[2,1,2,32,1024]{4,3,2,1,0:T(8,128)(2,1)S(1)}, bf16[2,1,2,32,1024]{4,3,2,1,0:T(8,128)(2,1)S(1)}, u32[]{:S(2)}, u32[]{:S(2)}) collective-permute-start(bf16[2,1,2,32,1024]{4,3,2,1,0:T(8,128)(2,1)S(1)} %maximum_bitcast_fusion.refs_0_), channel_id=1, source_target_pairs={{0,8},{1,9},{2,10},{3,11},{4,12},{5,13},{6,14},{7,15},{8,0},{9,1},... | collective-permute-start | bytes 786440 | tf_op jit(solution)/shard_map/ppermute | solution.py:272
  7.1 2.5 %collective-permute-start.6 = (bf16[2,1,2,32,1024]{4,3,2,1,0:T(8,128)(2,1)S(1)}, bf16[2,1,2,32,1024]{4,3,2,1,0:T(8,128)(2,1)S(1)}, u32[]{:S(2)}, u32[]{:S(2)}) collective-permute-start(bf16[2,1,2,32,1024]{4,3,2,1,0:T(8,128)(2,1)S(1)} %maximum_bitcast_fusion.refs_0_), channel_id=1, source_target_pairs={{0,24},{1,25},{2,26},{3,27},{4,28},{5,29},{6,30},{7,31},{8,16},{9,... | collective-permute-start | bytes 786440 | tf_op jit(solution)/shard_map/ppermute | solution.py:272
  9.7 1.2 copy-done.1
  10.9 2.8 %shard_map.46 = bf16[512,1024]{1,0:T(8,128)(2,1)} custom-call(bf16[4,2,64,1024]{3,2,1,0:T(8,128)(2,1)S(1)} %copy-done.1, s32[4,1024]{1,0:T(4,128)S(1)} %copy-done.2), custom_call_target="tpu_custom_call" | custom-call | flops 2147483648 | bytes 1064960 | tf_op jit(solution)/shard_map/pallas_call | solution.py:189
  13.8 0.6 collective-permute-start.5
  14.9 17.1 %collective-permute-done.1 = bf16[2,1,2,32,1024]{4,3,2,1,0:T(8,128)(2,1)S(1)} collective-permute-done((bf16[2,1,2,32,1024]{4,3,2,1,0:T(8,128)(2,1)S(1)}, bf16[2,1,2,32,1024]{4,3,2,1,0:T(8,128)(2,1)S(1)}, u32[]{:S(2)}, u32[]{:S(2)}) %collective-permute-start.1) | collective-permute-done | bytes 262176 | tf_op jit(solution)/shard_map/ppermute | solution.py:272
  32.1 0.8 copy-done.27
  33.1 3.0 %all-to-all-start = ((bf16[32,16,1024]{2,1,0:T(8,128)(2,1)}), bf16[32,16,1024]{2,1,0:T(8,128)(2,1)S(1)}, u32[]{:S(2)}, u32[]{:S(2)}) async-start(bf16[32,16,1024]{2,1,0:T(8,128)(2,1)} %bitcast.3), calls=%async_computation | async-start | bytes 2097152 | tf_op jit(solution)/shard_map/all_to_all | solution.py:322
  36.1 1.8 %collective-permute-start.8 = (bf16[2,2,2,32,1024]{4,3,2,1,0:T(8,128)(2,1)S(1)}, bf16[2,2,2,32,1024]{4,3,2,1,0:T(8,128)(2,1)S(1)}, u32[]{:S(2)}, u32[]{:S(2)}) collective-permute-start(bf16[2,2,2,32,1024]{4,3,2,1,0:T(8,128)(2,1)S(1)} %constant_dynamic-update-slice_fusion.refs_5_), channel_id=1, source_target_pairs={{0,4},{1,5},{2,6},{3,7},{4,0},{5,1},{6,2},{7,3},{8,12},{9,13},{10,... | collective-permute-start | bytes 1572872 | tf_op jit(solution)/shard_map/ppermute | solution.py:272
  37.9 1.5 %collective-permute-start.7 = (bf16[2,2,2,32,1024]{4,3,2,1,0:T(8,128)(2,1)S(1)}, bf16[2,2,2,32,1024]{4,3,2,1,0:T(8,128)(2,1)S(1)}, u32[]{:S(2)}, u32[]{:S(2)}) collective-permute-start(bf16[2,2,2,32,1024]{4,3,2,1,0:T(8,128)(2,1)S(1)} %constant_dynamic-update-slice_fusion.refs_5_), channel_id=1, source_target_pairs={{0,2},{1,3},{2,0},{3,1},{4,6},{5,7},{6,4},{7,5},{8,10},{9,11},{10,... | collective-permute-start | bytes 1572872 | tf_op jit(solution)/shard_map/ppermute | solution.py:272
  39.4 21.9 %collective-permute-done.8.refs_7_ = bf16[2,2,2,32,1024]{4,3,2,1,0:T(8,128)(2,1)S(1)} collective-permute-done((bf16[2,2,2,32,1024]{4,3,2,1,0:T(8,128)(2,1)S(1)}, bf16[2,2,2,32,1024]{4,3,2,1,0:T(8,128)(2,1)S(1)}, u32[]{:S(2)}, u32[]{:S(2)}) %collective-permute-start.8) | collective-permute-done | bytes 524320 | tf_op jit(solution)/shard_map/ppermute | solution.py:272
  61.3 1.4 collective-permute-start.10
  62.6 1.0 collective-permute-start.9
  64.2 4.8 %collective-permute-done.10.refs_9_ = bf16[1,2,2,32,1024]{4,3,2,1,0:T(8,128)(2,1)S(1)} collective-permute-done((bf16[1,2,2,32,1024]{4,3,2,1,0:T(8,128)(2,1)S(1)}, bf16[1,2,2,32,1024]{4,3,2,1,0:T(8,128)(2,1)S(1)}, u32[]{:S(2)}, u32[]{:S(2)}) %collective-permute-start.10) | collective-permute-done | bytes 262176 | tf_op jit(solution)/shard_map/ppermute | solution.py:272
  69.0 1.5 %collective-permute-done.9.refs_8_ = bf16[1,2,2,32,1024]{4,3,2,1,0:T(8,128)(2,1)S(1)} collective-permute-done((bf16[1,2,2,32,1024]{4,3,2,1,0:T(8,128)(2,1)S(1)}, bf16[1,2,2,32,1024]{4,3,2,1,0:T(8,128)(2,1)S(1)}, u32[]{:S(2)}, u32[]{:S(2)}) %collective-permute-start.9) | collective-permute-done | bytes 262176 | tf_op jit(solution)/shard_map/ppermute | solution.py:272
  71.2 0.7 collective-permute-start.12
  72.3 0.7 collective-permute-start.11
  73.7 5.7 %collective-permute-done.12.refs_12_ = bf16[2,1,2,32,1024]{4,3,2,1,0:T(8,128)(2,1)S(1)} collective-permute-done((bf16[2,1,2,32,1024]{4,3,2,1,0:T(8,128)(2,1)S(1)}, bf16[2,1,2,32,1024]{4,3,2,1,0:T(8,128)(2,1)S(1)}, u32[]{:S(2)}, u32[]{:S(2)}) %collective-permute-start.12) | collective-permute-done | bytes 262176 | tf_op jit(solution)/shard_map/ppermute | solution.py:272
  79.5 1.2 collective-permute-done.11.refs_11_
  81.4 0.8 collective-permute-done.23.refs_23_
  82.9 1.2 collective-permute-start.13
  84.1 3.7 %collective-permute-done.14.refs_14_ = bf16[1,1,2,32,1024]{4,3,2,1,0:T(8,128)(2,1)S(1)} collective-permute-done((bf16[1,1,2,32,1024]{4,3,2,1,0:T(8,128)(2,1)S(1)}, bf16[1,1,2,32,1024]{4,3,2,1,0:T(8,128)(2,1)S(1)}, u32[]{:S(2)}, u32[]{:S(2)}) %collective-permute-start.14) | collective-permute-done | bytes 131104 | tf_op jit(solution)/shard_map/ppermute | solution.py:272
  88.7 0.8 collective-permute-done.28.refs_28_
  90.8 11.6 %shard_map.47 = bf16[2048,128]{1,0:T(8,128)(2,1)} custom-call(bf16[512,1024]{1,0:T(8,128)(2,1)} %bitcast.14, bf16[2,1,2,32,1024]{4,3,2,1,0:T(8,128)(2,1)} %copy-done.4, bf16[2,1,2,32,1024]{4,3,2,1,0:T(8,128)(2,1)} %copy-done.9, bf16[2,1,2,32,1024]{4,3,2,1,0:T(8,128)(2,1)} %copy-done.8, bf16[1,1,2,32,1024]{4,3,2,1,0:T(8,128)(2,1)} %copy-done.27, ...), custom_call_target="tpu_custom_call" | custom-call | flops 4294967296 | bytes 9437184 | tf_op jit(solution)/shard_map/pallas_call | solution.py:189
  102.4 4.3 %all-to-all-start.1 = ((bf16[16,128,128]{2,1,0:T(8,128)(2,1)}), bf16[16,128,128]{2,1,0:T(8,128)(2,1)S(1)}, u32[]{:S(2)}, u32[]{:S(2)}) async-start(bf16[16,128,128]{2,1,0:T(8,128)(2,1)} %bitcast.16), calls=%async_computation.1 | async-start | bytes 1048576 | tf_op jit(solution)/shard_map/all_to_all | solution.py:322
  106.6 10.8 %shard_map.48.right_ref = bf16[256,1024]{1,0:T(8,128)(2,1)} custom-call(bf16[512,1024]{1,0:T(8,128)(2,1)} %bitcast.15, bf16[2,1,2,32,1024]{4,3,2,1,0:T(8,128)(2,1)} %copy-done.4, bf16[2,1,2,32,1024]{4,3,2,1,0:T(8,128)(2,1)} %copy-done.9, bf16[2,1,2,32,1024]{4,3,2,1,0:T(8,128)(2,1)} %copy-done.8, bf16[1,1,2,32,1024]{4,3,2,1,0:T(8,128)(2,1)} %copy-done.27, ...), custom_call_target="tpu_custom_call" | custom-call | flops 4294967296 | bytes 9437184 | tf_op jit(solution)/shard_map/pallas_call | solution.py:189
  117.5 1.0 copy-done
  119.1 16.3 %all_to_all.15 = bf16[32,16,256]{2,1,0:T(8,128)(2,1)S(1)} all-to-all(bf16[32,16,256]{2,1,0:T(8,128)(2,1)S(1)} %bitcast.13), channel_id=1, replica_groups=mesh['cuts'=1,'mode'=32] {'mode'}, dimensions={0} | all-to-all | bytes 524288 | tf_op jit(solution)/shard_map/all_to_all | solution.py:322
  135.4 0.6 convert_element_type.16
  (119 shorter events, 7.2 us)
Async XLA Ops:
  1.0 12.7 %collective-permute-start.3 = (bf16[2,1,2,32,1024]{4,3,2,1,0:T(8,128)(2,1)S(1)}, bf16[2,1,2,32,1024]{4,3,2,1,0:T(8,128)(2,1)S(1)}, u32[]{:S(2)}, u32[]{:S(2)}) collective-permute-start(bf16[2,1,2,32,1024]{4,3,2,1,0:T(8,128)(2,1)S(1)} %maximum_bitcast_fusion.refs_0_), channel_id=1, source_target_pairs={{0,4},{1,5},{2,6},{3,7},{4,0},{5,1},{6,2},{7,3},{8,12},{9,13},{10,... | collective-permute-start | bytes 786440 | tf_op jit(solution)/shard_map/ppermute | solution.py:272
  4.1 9.7 %collective-permute-start.2 = (bf16[2,1,2,32,1024]{4,3,2,1,0:T(8,128)(2,1)S(1)}, bf16[2,1,2,32,1024]{4,3,2,1,0:T(8,128)(2,1)S(1)}, u32[]{:S(2)}, u32[]{:S(2)}) collective-permute-start(bf16[2,1,2,32,1024]{4,3,2,1,0:T(8,128)(2,1)S(1)} %maximum_bitcast_fusion.refs_0_), channel_id=1, source_target_pairs={{0,2},{1,3},{2,0},{3,1},{4,6},{5,7},{6,4},{7,5},{8,10},{9,11},{10,... | collective-permute-start | bytes 786440 | tf_op jit(solution)/shard_map/ppermute | solution.py:272
  5.5 9.3 %collective-permute-start = (bf16[2,1,2,32,1024]{4,3,2,1,0:T(8,128)(2,1)S(1)}, bf16[2,1,2,32,1024]{4,3,2,1,0:T(8,128)(2,1)S(1)}, u32[]{:S(2)}, u32[]{:S(2)}) collective-permute-start(bf16[2,1,2,32,1024]{4,3,2,1,0:T(8,128)(2,1)S(1)} %maximum_bitcast_fusion.refs_0_), channel_id=1, source_target_pairs={{0,8},{1,9},{2,10},{3,11},{4,12},{5,13},{6,14},{7,15},{8,0},{9,1},... | collective-permute-start | bytes 786440 | tf_op jit(solution)/shard_map/ppermute | solution.py:272
  7.1 25.0 %collective-permute-start.6 = (bf16[2,1,2,32,1024]{4,3,2,1,0:T(8,128)(2,1)S(1)}, bf16[2,1,2,32,1024]{4,3,2,1,0:T(8,128)(2,1)S(1)}, u32[]{:S(2)}, u32[]{:S(2)}) collective-permute-start(bf16[2,1,2,32,1024]{4,3,2,1,0:T(8,128)(2,1)S(1)} %maximum_bitcast_fusion.refs_0_), channel_id=1, source_target_pairs={{0,24},{1,25},{2,26},{3,27},{4,28},{5,29},{6,30},{7,31},{8,16},{9,... | collective-permute-start | bytes 786440 | tf_op jit(solution)/shard_map/ppermute | solution.py:272
  9.6 22.4 %collective-permute-start.1 = (bf16[2,1,2,32,1024]{4,3,2,1,0:T(8,128)(2,1)S(1)}, bf16[2,1,2,32,1024]{4,3,2,1,0:T(8,128)(2,1)S(1)}, u32[]{:S(2)}, u32[]{:S(2)}) collective-permute-start(bf16[2,1,2,32,1024]{4,3,2,1,0:T(8,128)(2,1)S(1)} %maximum_bitcast_fusion.refs_0_), channel_id=1, source_target_pairs={{0,16},{1,17},{2,18},{3,19},{4,20},{5,21},{6,22},{7,23},{8,24},{9,... | collective-permute-start | bytes 786440 | tf_op jit(solution)/shard_map/ppermute | solution.py:272
  13.8 18.3 %collective-permute-start.5 = (bf16[1,1,2,32,1024]{4,3,2,1,0:T(8,128)(2,1)S(1)}, bf16[1,1,2,32,1024]{4,3,2,1,0:T(8,128)(2,1)S(1)}, u32[]{:S(2)}, u32[]{:S(2)}) collective-permute-start(bf16[1,1,2,32,1024]{4,3,2,1,0:T(8,128)(2,1)S(1)} %slice.19), channel_id=1, source_target_pairs={{0,2},{1,3},{2,0},{3,1},{4,6},{5,7},{6,4},{7,5},{8,10},{9,11},{10,... | collective-permute-start | bytes 393224 | tf_op jit(solution)/shard_map/ppermute | solution.py:272
  14.4 17.7 %collective-permute-start.4 = (bf16[1,1,2,32,1024]{4,3,2,1,0:T(8,128)(2,1)S(1)}, bf16[1,1,2,32,1024]{4,3,2,1,0:T(8,128)(2,1)S(1)}, u32[]{:S(2)}, u32[]{:S(2)}) collective-permute-start(bf16[1,1,2,32,1024]{4,3,2,1,0:T(8,128)(2,1)S(1)} %slice.18), channel_id=1, source_target_pairs={{0,4},{1,5},{2,6},{3,7},{4,0},{5,1},{6,2},{7,3},{8,12},{9,13},{10,... | collective-permute-start | bytes 393224 | tf_op jit(solution)/shard_map/ppermute | solution.py:272
  33.1 56.7 %all-to-all-start = ((bf16[32,16,1024]{2,1,0:T(8,128)(2,1)}), bf16[32,16,1024]{2,1,0:T(8,128)(2,1)S(1)}, u32[]{:S(2)}, u32[]{:S(2)}) async-start(bf16[32,16,1024]{2,1,0:T(8,128)(2,1)} %bitcast.3), calls=%async_computation | async-start | bytes 2097152 | tf_op jit(solution)/shard_map/all_to_all | solution.py:322
  36.1 25.1 %collective-permute-start.8 = (bf16[2,2,2,32,1024]{4,3,2,1,0:T(8,128)(2,1)S(1)}, bf16[2,2,2,32,1024]{4,3,2,1,0:T(8,128)(2,1)S(1)}, u32[]{:S(2)}, u32[]{:S(2)}) collective-permute-start(bf16[2,2,2,32,1024]{4,3,2,1,0:T(8,128)(2,1)S(1)} %constant_dynamic-update-slice_fusion.refs_5_), channel_id=1, source_target_pairs={{0,4},{1,5},{2,6},{3,7},{4,0},{5,1},{6,2},{7,3},{8,12},{9,13},{10,... | collective-permute-start | bytes 1572872 | tf_op jit(solution)/shard_map/ppermute | solution.py:272
  37.9 23.3 %collective-permute-start.7 = (bf16[2,2,2,32,1024]{4,3,2,1,0:T(8,128)(2,1)S(1)}, bf16[2,2,2,32,1024]{4,3,2,1,0:T(8,128)(2,1)S(1)}, u32[]{:S(2)}, u32[]{:S(2)}) collective-permute-start(bf16[2,2,2,32,1024]{4,3,2,1,0:T(8,128)(2,1)S(1)} %constant_dynamic-update-slice_fusion.refs_5_), channel_id=1, source_target_pairs={{0,2},{1,3},{2,0},{3,1},{4,6},{5,7},{6,4},{7,5},{8,10},{9,11},{10,... | collective-permute-start | bytes 1572872 | tf_op jit(solution)/shard_map/ppermute | solution.py:272
  61.3 7.8 %collective-permute-start.10 = (bf16[1,2,2,32,1024]{4,3,2,1,0:T(8,128)(2,1)S(1)}, bf16[1,2,2,32,1024]{4,3,2,1,0:T(8,128)(2,1)S(1)}, u32[]{:S(2)}, u32[]{:S(2)}) collective-permute-start(bf16[1,2,2,32,1024]{4,3,2,1,0:T(8,128)(2,1)S(1)} %slice.21), channel_id=1, source_target_pairs={{0,2},{1,3},{2,0},{3,1},{4,6},{5,7},{6,4},{7,5},{8,10},{9,11},{10,... | collective-permute-start | bytes 786440 | tf_op jit(solution)/shard_map/ppermute | solution.py:272
  62.6 7.9 %collective-permute-start.9 = (bf16[1,2,2,32,1024]{4,3,2,1,0:T(8,128)(2,1)S(1)}, bf16[1,2,2,32,1024]{4,3,2,1,0:T(8,128)(2,1)S(1)}, u32[]{:S(2)}, u32[]{:S(2)}) collective-permute-start(bf16[1,2,2,32,1024]{4,3,2,1,0:T(8,128)(2,1)S(1)} %slice.20), channel_id=1, source_target_pairs={{0,4},{1,5},{2,6},{3,7},{4,0},{5,1},{6,2},{7,3},{8,12},{9,13},{10,... | collective-permute-start | bytes 786440 | tf_op jit(solution)/shard_map/ppermute | solution.py:272
  63.6 7.0 %collective-permute-start.15 = (bf16[2,1,2,32,1024]{4,3,2,1,0:T(8,128)(2,1)S(1)}, bf16[2,1,2,32,1024]{4,3,2,1,0:T(8,128)(2,1)S(1)}, u32[]{:S(2)}, u32[]{:S(2)}) collective-permute-start(bf16[2,1,2,32,1024]{4,3,2,1,0:T(8,128)(2,1)S(1)} %maximum_bitcast_fusion.refs_0_), channel_id=1, source_target_pairs={{0,1},{1,0},{2,3},{3,2},{4,5},{5,4},{6,7},{7,6},{8,9},{9,8},{10,11... | collective-permute-start | bytes 786440 | tf_op jit(solution)/shard_map/ppermute | solution.py:272
  63.6 9.9 %collective-permute-start.20 = (bf16[2,2,2,32,1024]{4,3,2,1,0:T(8,128)(2,1)S(1)}, bf16[2,2,2,32,1024]{4,3,2,1,0:T(8,128)(2,1)S(1)}, u32[]{:S(2)}, u32[]{:S(2)}) collective-permute-start(bf16[2,2,2,32,1024]{4,3,2,1,0:T(8,128)(2,1)S(1)} %constant_dynamic-update-slice_fusion.refs_5_), channel_id=1, source_target_pairs={{0,1},{1,0},{2,3},{3,2},{4,5},{5,4},{6,7},{7,6},{8,9},{9,8},{10,11... | collective-permute-start | bytes 1572872 | tf_op jit(solution)/shard_map/ppermute | solution.py:272
  64.1 7.0 %collective-permute-start.19 = (bf16[1,1,2,32,1024]{4,3,2,1,0:T(8,128)(2,1)S(1)}, bf16[1,1,2,32,1024]{4,3,2,1,0:T(8,128)(2,1)S(1)}, u32[]{:S(2)}, u32[]{:S(2)}) collective-permute-start(bf16[1,1,2,32,1024]{4,3,2,1,0:T(8,128)(2,1)S(1)} %collective-permute-done.5.refs_4_), channel_id=1, source_target_pairs={{0,1},{1,0},{2,3},{3,2},{4,5},{5,4},{6,7},{7,6},{8,9},{9,8},{10,11... | collective-permute-start | bytes 393224 | tf_op jit(solution)/shard_map/ppermute | solution.py:272
  69.0 3.9 %collective-permute-start.16 = (bf16[2,1,2,32,1024]{4,3,2,1,0:T(8,128)(2,1)S(1)}, bf16[2,1,2,32,1024]{4,3,2,1,0:T(8,128)(2,1)}, u32[]{:S(2)}, u32[]{:S(2)}) collective-permute-start(bf16[2,1,2,32,1024]{4,3,2,1,0:T(8,128)(2,1)S(1)} %collective-permute-done.2.refs_1_), channel_id=1, source_target_pairs={{0,1},{1,0},{2,3},{3,2},{4,5},{5,4},{6,7},{7,6},{8,9},{9,8},{10,11... | collective-permute-start | bytes 786440 | tf_op jit(solution)/shard_map/ppermute | solution.py:272
  70.6 2.5 %collective-permute-start.17 = (bf16[2,1,2,32,1024]{4,3,2,1,0:T(8,128)(2,1)S(1)}, bf16[2,1,2,32,1024]{4,3,2,1,0:T(8,128)(2,1)S(1)}, u32[]{:S(2)}, u32[]{:S(2)}) collective-permute-start(bf16[2,1,2,32,1024]{4,3,2,1,0:T(8,128)(2,1)S(1)} %collective-permute-done.3.refs_2_), channel_id=1, source_target_pairs={{0,1},{1,0},{2,3},{3,2},{4,5},{5,4},{6,7},{7,6},{8,9},{9,8},{10,11... | collective-permute-start | bytes 786440 | tf_op jit(solution)/shard_map/ppermute | solution.py:272
  70.6 1.7 %collective-permute-start.18 = (bf16[1,1,2,32,1024]{4,3,2,1,0:T(8,128)(2,1)S(1)}, bf16[1,1,2,32,1024]{4,3,2,1,0:T(8,128)(2,1)S(1)}, u32[]{:S(2)}, u32[]{:S(2)}) collective-permute-start(bf16[1,1,2,32,1024]{4,3,2,1,0:T(8,128)(2,1)S(1)} %copy-done.28), channel_id=1, source_target_pairs={{0,1},{1,0},{2,3},{3,2},{4,5},{5,4},{6,7},{7,6},{8,9},{9,8},{10,11... | collective-permute-start | bytes 393224 | tf_op jit(solution)/shard_map/ppermute | solution.py:272
  71.2 8.3 %collective-permute-start.12 = (bf16[2,1,2,32,1024]{4,3,2,1,0:T(8,128)(2,1)S(1)}, bf16[2,1,2,32,1024]{4,3,2,1,0:T(8,128)(2,1)S(1)}, u32[]{:S(2)}, u32[]{:S(2)}) collective-permute-start(bf16[2,1,2,32,1024]{4,3,2,1,0:T(8,128)(2,1)S(1)} %copy-done.16), channel_id=1, source_target_pairs={{0,4},{1,5},{2,6},{3,7},{4,0},{5,1},{6,2},{7,3},{8,12},{9,13},{10,... | collective-permute-start | bytes 786440 | tf_op jit(solution)/shard_map/ppermute | solution.py:272
  72.3 8.4 %collective-permute-start.11 = (bf16[2,1,2,32,1024]{4,3,2,1,0:T(8,128)(2,1)S(1)}, bf16[2,1,2,32,1024]{4,3,2,1,0:T(8,128)(2,1)S(1)}, u32[]{:S(2)}, u32[]{:S(2)}) collective-permute-start(bf16[2,1,2,32,1024]{4,3,2,1,0:T(8,128)(2,1)S(1)} %copy-done.16), channel_id=1, source_target_pairs={{0,2},{1,3},{2,0},{3,1},{4,6},{5,7},{6,4},{7,5},{8,10},{9,11},{10,... | collective-permute-start | bytes 786440 | tf_op jit(solution)/shard_map/ppermute | solution.py:272
  73.0 9.9 %collective-permute-start.21 = (bf16[2,2,2,32,1024]{4,3,2,1,0:T(8,128)(2,1)S(1)}, bf16[2,2,2,32,1024]{4,3,2,1,0:T(8,128)(2,1)S(1)}, u32[]{:S(2)}, u32[]{:S(2)}) collective-permute-start(bf16[2,2,2,32,1024]{4,3,2,1,0:T(8,128)(2,1)S(1)} %collective-permute-done.7.refs_6_), channel_id=1, source_target_pairs={{0,1},{1,0},{2,3},{3,2},{4,5},{5,4},{6,7},{7,6},{8,9},{9,8},{10,11... | collective-permute-start | bytes 1572872 | tf_op jit(solution)/shard_map/ppermute | solution.py:272
  73.1 7.6 %collective-permute-start.24 = (bf16[1,2,2,32,1024]{4,3,2,1,0:T(8,128)(2,1)S(1)}, bf16[1,2,2,32,1024]{4,3,2,1,0:T(8,128)(2,1)S(1)}, u32[]{:S(2)}, u32[]{:S(2)}) collective-permute-start(bf16[1,2,2,32,1024]{4,3,2,1,0:T(8,128)(2,1)S(1)} %collective-permute-done.10.refs_9_), channel_id=1, source_target_pairs={{0,1},{1,0},{2,3},{3,2},{4,5},{5,4},{6,7},{7,6},{8,9},{9,8},{10,11... | collective-permute-start | bytes 786440 | tf_op jit(solution)/shard_map/ppermute | solution.py:272
  73.6 10.5 %collective-permute-start.22 = (bf16[2,2,2,32,1024]{4,3,2,1,0:T(8,128)(2,1)S(1)}, bf16[2,2,2,32,1024]{4,3,2,1,0:T(8,128)(2,1)S(1)}, u32[]{:S(2)}, u32[]{:S(2)}) collective-permute-start(bf16[2,2,2,32,1024]{4,3,2,1,0:T(8,128)(2,1)S(1)} %collective-permute-done.8.refs_7_), channel_id=1, source_target_pairs={{0,1},{1,0},{2,3},{3,2},{4,5},{5,4},{6,7},{7,6},{8,9},{9,8},{10,11... | collective-permute-start | bytes 1572872 | tf_op jit(solution)/shard_map/ppermute | solution.py:272
  79.5 1.8 %collective-permute-start.25 = (bf16[2,1,2,32,1024]{4,3,2,1,0:T(8,128)(2,1)S(1)}, bf16[2,1,2,32,1024]{4,3,2,1,0:T(8,128)(2,1)S(1)}, u32[]{:S(2)}, u32[]{:S(2)}) collective-permute-start(bf16[2,1,2,32,1024]{4,3,2,1,0:T(8,128)(2,1)S(1)} %copy-done.16), channel_id=1, source_target_pairs={{0,1},{1,0},{2,3},{3,2},{4,5},{5,4},{6,7},{7,6},{8,9},{9,8},{10,11... | collective-permute-start | bytes 786440 | tf_op jit(solution)/shard_map/ppermute | solution.py:272
  80.7 1.5 %collective-permute-start.23 = (bf16[1,2,2,32,1024]{4,3,2,1,0:T(8,128)(2,1)S(1)}, bf16[1,2,2,32,1024]{4,3,2,1,0:T(8,128)(2,1)S(1)}, u32[]{:S(2)}, u32[]{:S(2)}) collective-permute-start(bf16[1,2,2,32,1024]{4,3,2,1,0:T(8,128)(2,1)S(1)} %collective-permute-done.9.refs_8_), channel_id=1, source_target_pairs={{0,1},{1,0},{2,3},{3,2},{4,5},{5,4},{6,7},{7,6},{8,9},{9,8},{10,11... | collective-permute-start | bytes 786440 | tf_op jit(solution)/shard_map/ppermute | solution.py:272
  80.7 7.1 %collective-permute-start.26 = (bf16[2,1,2,32,1024]{4,3,2,1,0:T(8,128)(2,1)S(1)}, bf16[2,1,2,32,1024]{4,3,2,1,0:T(8,128)(2,1)S(1)}, u32[]{:S(2)}, u32[]{:S(2)}) collective-permute-start(bf16[2,1,2,32,1024]{4,3,2,1,0:T(8,128)(2,1)S(1)} %collective-permute-done.11.refs_11_), channel_id=1, source_target_pairs={{0,1},{1,0},{2,3},{3,2},{4,5},{5,4},{6,7},{7,6},{8,9},{9,8},{10,11... | collective-permute-start | bytes 786440 | tf_op jit(solution)/shard_map/ppermute | solution.py:272
  81.3 6.5 %collective-permute-start.27 = (bf16[2,1,2,32,1024]{4,3,2,1,0:T(8,128)(2,1)S(1)}, bf16[2,1,2,32,1024]{4,3,2,1,0:T(8,128)(2,1)S(1)}, u32[]{:S(2)}, u32[]{:S(2)}) collective-permute-start(bf16[2,1,2,32,1024]{4,3,2,1,0:T(8,128)(2,1)S(1)} %collective-permute-done.12.refs_12_), channel_id=1, source_target_pairs={{0,1},{1,0},{2,3},{3,2},{4,5},{5,4},{6,7},{7,6},{8,9},{9,8},{10,11... | collective-permute-start | bytes 786440 | tf_op jit(solution)/shard_map/ppermute | solution.py:272
  82.3 5.5 %collective-permute-start.14 = (bf16[1,1,2,32,1024]{4,3,2,1,0:T(8,128)(2,1)S(1)}, bf16[1,1,2,32,1024]{4,3,2,1,0:T(8,128)(2,1)S(1)}, u32[]{:S(2)}, u32[]{:S(2)}) collective-permute-start(bf16[1,1,2,32,1024]{4,3,2,1,0:T(8,128)(2,1)S(1)} %slice.23), channel_id=1, source_target_pairs={{0,2},{1,3},{2,0},{3,1},{4,6},{5,7},{6,4},{7,5},{8,10},{9,11},{10,... | collective-permute-start | bytes 393224 | tf_op jit(solution)/shard_map/ppermute | solution.py:272
  82.9 5.3 %collective-permute-start.13 = (bf16[1,1,2,32,1024]{4,3,2,1,0:T(8,128)(2,1)S(1)}, bf16[1,1,2,32,1024]{4,3,2,1,0:T(8,128)(2,1)S(1)}, u32[]{:S(2)}, u32[]{:S(2)}) collective-permute-start(bf16[1,1,2,32,1024]{4,3,2,1,0:T(8,128)(2,1)S(1)} %slice.22), channel_id=1, source_target_pairs={{0,4},{1,5},{2,6},{3,7},{4,0},{5,1},{6,2},{7,3},{8,12},{9,13},{10,... | collective-permute-start | bytes 393224 | tf_op jit(solution)/shard_map/ppermute | solution.py:272
  88.2 1.3 collective-permute-start.28
  88.2 1.5 %collective-permute-start.29 = (bf16[1,1,2,32,1024]{4,3,2,1,0:T(8,128)(2,1)S(1)}, bf16[1,1,2,32,1024]{4,3,2,1,0:T(8,128)(2,1)S(1)}, u32[]{:S(2)}, u32[]{:S(2)}) collective-permute-start(bf16[1,1,2,32,1024]{4,3,2,1,0:T(8,128)(2,1)S(1)} %collective-permute-done.14.refs_14_), channel_id=1, source_target_pairs={{0,1},{1,0},{2,3},{3,2},{4,5},{5,4},{6,7},{7,6},{8,9},{9,8},{10,11... | collective-permute-start | bytes 393224 | tf_op jit(solution)/shard_map/ppermute | solution.py:272
  102.4 15.1 %all-to-all-start.1 = ((bf16[16,128,128]{2,1,0:T(8,128)(2,1)}), bf16[16,128,128]{2,1,0:T(8,128)(2,1)S(1)}, u32[]{:S(2)}, u32[]{:S(2)}) async-start(bf16[16,128,128]{2,1,0:T(8,128)(2,1)} %bitcast.16), calls=%async_computation.1 | async-start | bytes 1048576 | tf_op jit(solution)/shard_map/all_to_all | solution.py:322
  (35 other events, 416.2 us)

commit v8 on v6

--- a/solution.py
+++ b/solution.py
@@ -11,7 +11,7 @@
 KEPT = 4
 CYCLES = 2
 LANES = 128
-VMEM_LIMIT = 24 * 1024 * 1024
+MEBI = 1024 * 1024
 
 
 def whole(count):
@@ -48,11 +48,12 @@
 
 def swap_sign(tiles, qs):
     turned = pltpu.roll(tiles, qs, 1)
-    row = lax.broadcasted_iota(jnp.int32, tiles.shape, 1)
-    return jnp.where(row < qs, -turned, turned)
-
-
-def regroup_store(acc, first_lane, group, devices, tile_rows, x_ref, h_ref):
+    row = lax.broadcasted_iota(jnp.int32, (1,) + tiles.shape[1:], 1)
+    return turned * jnp.where(row < qs, -1.0, 1.0)
+
+
+def regroup_store(acc, first_lane, group, devices, tile_rows, x_ref):
+    width = x_ref.shape[1] // 2
     per = LANES // group
     lane = lax.broadcasted_iota(jnp.int32, (tile_rows, LANES), 1) // group
     for offset in range(0, acc.shape[1], LANES):
@@ -68,8 +69,12 @@
                     if m & bit:
                         continue
                     low, high = parts[m], parts[m | bit]
-                    moved[m] = jnp.where(keep, low, pltpu.roll(high, bit * group, 1))
-                    moved[m | bit] = jnp.where(keep, pltpu.roll(low, LANES - bit * group, 1), high)
+                    if 2 * bit * group == LANES:
+                        up = down = pltpu.roll(jnp.where(keep, high, low), LANES // 2, 1)
+                    else:
+                        up, down = pltpu.roll(high, bit * group, 1), pltpu.roll(low, LANES - bit * group, 1)
+                    moved[m] = jnp.where(keep, low, up)
+                    moved[m | bit] = jnp.where(keep, down, high)
                 parts = moved
                 bit *= 2
             tiles = jnp.stack(parts)
@@ -77,7 +82,7 @@
             lanes = pl.ds(block * LANES, LANES)
             x_ref[rows, lanes] = tiles.reshape(per * tile_rows, LANES).astype(jnp.bfloat16)
             turned = swap_sign(tiles, tile_rows // 2)
-            h_ref[rows, lanes] = turned.reshape(per * tile_rows, LANES).astype(jnp.bfloat16)
+            x_ref[rows, pl.ds(width + block * LANES, LANES)] = turned.reshape(per * tile_rows, LANES).astype(jnp.bfloat16)
 
 
 def gate_copies(plan, blocks, whole_ref, sems):
@@ -100,7 +105,7 @@
 
 def layers_kernel(sizes, is_left, plan, x_ref, *refs):
     devices, qs, group, rows_each = sizes
-    blocks, (o_ref, xs, hs, last, whole_ref, sems) = refs[: len(plan)], refs[len(plan) :]
+    blocks, (o_ref, xs, last, whole_ref, sems) = refs[: len(plan)], refs[len(plan) :]
     copies = gate_copies(plan, blocks, whole_ref, sems)
     for gate in range(2):
         for copy in copies[gate]:
@@ -109,21 +114,20 @@
     rows, width = x_ref.shape[0] // 2, x_ref.shape[1]
     first = x_ref[...].astype(jnp.float32).reshape(devices, 2 * tile_rows, width)
     first = first[:, :tile_rows] if is_left else first[:, tile_rows:]
-    xs[0] = first.reshape(rows, width).astype(jnp.bfloat16)
-    hs[0] = swap_sign(first, qs).reshape(rows, width).astype(jnp.bfloat16)
+    xs[0, :, :width] = first.reshape(rows, width).astype(jnp.bfloat16)
+    xs[0, :, width:] = swap_sign(first, qs).reshape(rows, width).astype(jnp.bfloat16)
     step = min(512, width)
     for layer in range(2 * CYCLES):
         if layer < 2:
             for copy in copies[layer]:
                 copy.wait()
         gate = whole_ref.at[layer % 2]
-        here, turned = xs.at[layer % 2], hs.at[layer % 2]
-        later = (layer + 1) % 2
+        here, later = xs.at[layer % 2], xs.at[(layer + 1) % 2]
         for start in range(0, width, step):
             cols = slice(start, start + step)
-            acc = exact_dot(here[...], gate[0, :, cols]) + exact_dot(turned[...], gate[1, :, cols])
+            acc = exact_dot(here[...], gate[:, :, cols].reshape(2 * width, step))
             if layer < 2 * CYCLES - 1:
-                regroup_store(acc, start, group, devices, tile_rows, xs.at[later], hs.at[later])
+                regroup_store(acc, start, group, devices, tile_rows, later)
             else:
                 last[:, cols] = acc.astype(jnp.bfloat16)
     half = rows // 2
@@ -184,7 +188,7 @@
         o_ref[g * block : (g + 1) * block, :] = part.astype(jnp.bfloat16)
 
 
-def call(kernel, out_shape, inputs, scratch=(), flops=0, blocks=()):
+def call(kernel, out_shape, inputs, scratch=(), flops=0, blocks=(), grant=24):
     moved = sum(x.size * x.dtype.itemsize for x in (*inputs, *blocks))
     return pl.pallas_call(
         kernel,
@@ -192,7 +196,7 @@
         in_specs=whole(len(inputs)) + [pl.BlockSpec(memory_space=pl.ANY)] * len(blocks),
         out_specs=whole(1)[0],
         scratch_shapes=list(scratch),
-        compiler_params=pltpu.CompilerParams(vmem_limit_bytes=VMEM_LIMIT),
+        compiler_params=pltpu.CompilerParams(vmem_limit_bytes=grant * MEBI),
         cost_estimate=pl.CostEstimate(flops=flops, bytes_accessed=moved, transcendentals=0),
     )(*inputs, *blocks)
 
@@ -231,7 +235,8 @@
     blocks, plan, states = spread(gate_a, gate_b, packed.reshape(devices, 2 * tile_rows, width))
     states = states.reshape(2 * rows, width)
     sizes = (devices, qs, group, rows_each)
-    scratch = [pltpu.VMEM((2, rows, width), jnp.bfloat16)] * 2 + [
+    scratch = [
+        pltpu.VMEM((2, rows, 2 * width), jnp.bfloat16),
         pltpu.VMEM((rows, width), jnp.bfloat16),
         pltpu.VMEM((2, 2, width, width), jnp.bfloat16),
         pltpu.SemaphoreType.DMA((2, devices)),
@@ -244,11 +249,12 @@
         scratch,
         work,
         blocks,
+        56,
     )
     groups = [[h * halves + e for e in range(halves)] for h in range(2)]
     left = trade(left.reshape(halves, rows // 2, LANES), groups)
     right = call(
-        functools.partial(layers_kernel, sizes, False, plan), (rows, width), (states,), scratch, work, blocks
+        functools.partial(layers_kernel, sizes, False, plan), (rows, width), (states,), scratch, work, blocks, 56
     )
     free = width // (2 * KEPT)
     us = halves
@@ -292,16 +298,19 @@
         far += [source + (bit,) for source in far]
     far = tuple(far[1:])
     value = jnp.concatenate([flip(own, *source) for source in far], axis=1)
-    value, packed, *_ = lax.optimization_barrier((value, packed, blocks[-2][0], blocks[-1][0]))
+    states = trade(packed)
+    value, *_ = lax.optimization_barrier((value, packed, blocks[-2][0], blocks[-1][0]))
     blocks += plane(value, far)
     near = []
     for number, (value, sources, gates) in enumerate(blocks):
         if number >= len(blocks) - 2:
-            value, *_ = lax.optimization_barrier((value, *[earlier for earlier, _, _ in near[: len(blocks) - 2]]))
+            value, states, *_ = lax.optimization_barrier(
+                (value, states, *[earlier for earlier, _, _ in near[: len(blocks) - 2]])
+            )
         near.append((flip(value, 0), tuple(source + (0,) for source in sources), gates))
     blocks += near
     plan = tuple((sources, gates) for _, sources, gates in blocks)
-    return [value for value, _, _ in blocks], plan, trade(packed)
+    return [value for value, _, _ in blocks], plan, states
 
 
 def trade(value, groups=None):

time: 169 us -> 146 us (0.86)
  local copies, waits for them, and re-layouts: 39.5 us -> 6.65 us
  waiting for transfers between devices: 55.7 us -> 69.7 us
  Pallas kernels: 31.5 us -> 26 us
  starting transfers between devices: 23.7 us -> 27.8 us
    unnamed x92 -> x50, local copies, waits for them, and re-layouts: 38.9 us -> 5.97 us
    ppermute x21, waiting for transfers between devices: 55.7 us -> 69.7 us  [flip(): return lax.ppermute(value, 'mode', pairs)]
    pallas_call x4, Pallas kernels: 31.5 us -> 26 us  [call(): pl.pallas_call(kernel, out_shape=jax.ShapeDtypeStruct(out_shape, jnp.bflo...]
    all_to_all x2, starting transfers between devices: 6.62 us -> 11.1 us  [trade(): lax.all_to_all(value, 'mode', split_axis=0, concat_axis=0, axis_index_gro...]
  transfers between devices with their start and end apart: 23 -> 23, of which waited for: 9 -> 11; matrix products, arithmetic and copies ran while one was open for 0% -> 0% of each run, Pallas kernels for 10% -> 8%
where the time goes in v8:
time: 146 us; the launch traced here: 145 us
  waiting for transfers between devices  69.7 us (48%)
  starting transfers between devices  27.8 us (19%)
  Pallas kernels  26 us (18%)
  blocking collectives  14.6 us (10%)
  local copies, waits for them, and re-layouts  6.65 us (5%)
    ppermute x21, waiting for transfers between devices, flip(): return lax.ppermute(value, 'mode', pairs)  69.7 us
    pallas_call x4, Pallas kernels, call(): pl.pallas_call(kernel, out_shape=jax.ShapeDtypeStruct(out_shape, jnp.bflo...  26 us
    ppermute x21, starting transfers between devices, flip(): return lax.ppermute(value, 'mode', pairs)  16.8 us
    all_to_all x1, blocking collectives, trade(): lax.all_to_all(value, 'mode', split_axis=0, concat_axis=0, axis_index_gro...  14.6 us
    all_to_all x2, starting transfers between devices, trade(): lax.all_to_all(value, 'mode', split_axis=0, concat_axis=0, axis_index_gro...  11.1 us
    unnamed x50, local copies, waits for them, and re-layouts  5.97 us
  transfers between devices with their start and end apart: 23, of which 11 were waited for; matrix products, arithmetic and copies ran while one was open for 0% of the time, Pallas kernels for 8%

profile of v8, /device:TPU:0, one launch (start us, length us, event | category | flops | bytes accessed | tf_op | source)
XLA Modules:
  0.0 145.3 jit_solution(11244631685412393026)
XLA Ops:
  0.0 1.2 copy-done.1
  1.2 0.7 copy-done.2
  1.9 2.8 %shard_map.46 = bf16[512,1024]{1,0:T(8,128)(2,1)} custom-call(bf16[4,2,64,1024]{3,2,1,0:T(8,128)(2,1)S(1)} %copy-done.1, s32[4,1024]{1,0:T(4,128)S(1)} %copy-done.2), custom_call_target="tpu_custom_call" | custom-call | flops 2147483648 | bytes 1064960 | tf_op jit(solution)/shard_map/pallas_call | solution.py:193
  4.7 7.3 %all-to-all-start = ((bf16[32,16,1024]{2,1,0:T(8,128)(2,1)}), bf16[32,16,1024]{2,1,0:T(8,128)(2,1)S(1)}, u32[]{:S(2)}, u32[]{:S(2)}) async-start(bf16[32,16,1024]{2,1,0:T(8,128)(2,1)} %bitcast.3), calls=%async_computation | async-start | bytes 2097152 | tf_op jit(solution)/shard_map/all_to_all | solution.py:317
  12.1 1.8 %collective-permute-start.5 = (bf16[2,1,2,32,1024]{4,3,2,1,0:T(8,128)(2,1)S(1)}, bf16[2,1,2,32,1024]{4,3,2,1,0:T(8,128)(2,1)S(1)}, u32[]{:S(2)}, u32[]{:S(2)}) collective-permute-start(bf16[2,1,2,32,1024]{4,3,2,1,0:T(8,128)(2,1)S(1)} %maximum_bitcast_fusion.refs_0_), channel_id=1, source_target_pairs={{0,4},{1,5},{2,6},{3,7},{4,0},{5,1},{6,2},{7,3},{8,12},{9,13},{10,... | collective-permute-start | bytes 786440 | tf_op jit(solution)/shard_map/ppermute | solution.py:276
  13.9 1.5 %collective-permute-start.3 = (bf16[2,1,2,32,1024]{4,3,2,1,0:T(8,128)(2,1)S(1)}, bf16[2,1,2,32,1024]{4,3,2,1,0:T(8,128)(2,1)S(1)}, u32[]{:S(2)}, u32[]{:S(2)}) collective-permute-start(bf16[2,1,2,32,1024]{4,3,2,1,0:T(8,128)(2,1)S(1)} %maximum_bitcast_fusion.refs_0_), channel_id=1, source_target_pairs={{0,2},{1,3},{2,0},{3,1},{4,6},{5,7},{6,4},{7,5},{8,10},{9,11},{10,... | collective-permute-start | bytes 786440 | tf_op jit(solution)/shard_map/ppermute | solution.py:276
  15.4 3.4 %collective-permute-start.2 = (bf16[2,1,2,32,1024]{4,3,2,1,0:T(8,128)(2,1)S(1)}, bf16[2,1,2,32,1024]{4,3,2,1,0:T(8,128)(2,1)S(1)}, u32[]{:S(2)}, u32[]{:S(2)}) collective-permute-start(bf16[2,1,2,32,1024]{4,3,2,1,0:T(8,128)(2,1)S(1)} %maximum_bitcast_fusion.refs_0_), channel_id=1, source_target_pairs={{0,24},{1,25},{2,26},{3,27},{4,28},{5,29},{6,30},{7,31},{8,16},{9,... | collective-permute-start | bytes 786440 | tf_op jit(solution)/shard_map/ppermute | solution.py:276
  18.8 1.0 collective-permute-start
  19.8 9.6 %collective-permute-done.5.refs_2_ = bf16[2,1,2,32,1024]{4,3,2,1,0:T(8,128)(2,1)S(1)} collective-permute-done((bf16[2,1,2,32,1024]{4,3,2,1,0:T(8,128)(2,1)S(1)}, bf16[2,1,2,32,1024]{4,3,2,1,0:T(8,128)(2,1)S(1)}, u32[]{:S(2)}, u32[]{:S(2)}) %collective-permute-start.5) | collective-permute-done | bytes 262176 | tf_op jit(solution)/shard_map/ppermute | solution.py:276
  29.4 1.8 %collective-permute-start.6 = (bf16[1,1,2,32,1024]{4,3,2,1,0:T(8,128)(2,1)S(1)}, bf16[1,1,2,32,1024]{4,3,2,1,0:T(8,128)(2,1)S(1)}, u32[]{:S(2)}, u32[]{:S(2)}) collective-permute-start(bf16[1,1,2,32,1024]{4,3,2,1,0:T(8,128)(2,1)S(1)} %slice.17), channel_id=1, source_target_pairs={{0,2},{1,3},{2,0},{3,1},{4,6},{5,7},{6,4},{7,5},{8,10},{9,11},{10,... | collective-permute-start | bytes 393224 | tf_op jit(solution)/shard_map/ppermute | solution.py:276
  31.6 8.1 %collective-permute-done.2 = bf16[2,1,2,32,1024]{4,3,2,1,0:T(8,128)(2,1)S(1)} collective-permute-done((bf16[2,1,2,32,1024]{4,3,2,1,0:T(8,128)(2,1)S(1)}, bf16[2,1,2,32,1024]{4,3,2,1,0:T(8,128)(2,1)S(1)}, u32[]{:S(2)}, u32[]{:S(2)}) %collective-permute-start.2) | collective-permute-done | bytes 262176 | tf_op jit(solution)/shard_map/ppermute | solution.py:276
  39.7 21.0 %collective-permute-done.1 = bf16[2,1,2,32,1024]{4,3,2,1,0:T(8,128)(2,1)S(1)} collective-permute-done((bf16[2,1,2,32,1024]{4,3,2,1,0:T(8,128)(2,1)S(1)}, bf16[2,1,2,32,1024]{4,3,2,1,0:T(8,128)(2,1)S(1)}, u32[]{:S(2)}, u32[]{:S(2)}) %collective-permute-start.1) | collective-permute-done | bytes 262176 | tf_op jit(solution)/shard_map/ppermute | solution.py:276
  60.9 1.6 %collective-permute-start.9 = (bf16[2,3,2,32,1024]{4,3,2,1,0:T(8,128)(2,1)S(1)}, bf16[2,3,2,32,1024]{4,3,2,1,0:T(8,128)(2,1)S(1)}, u32[]{:S(2)}, u32[]{:S(2)}) collective-permute-start(bf16[2,3,2,32,1024]{4,3,2,1,0:T(8,128)(2,1)S(1)} %pad_maximum_fusion.refs_5_), channel_id=1, source_target_pairs={{0,2},{1,3},{2,0},{3,1},{4,6},{5,7},{6,4},{7,5},{8,10},{9,11},{10,... | collective-permute-start | bytes 2359304 | tf_op jit(solution)/shard_map/ppermute | solution.py:276
  62.5 1.4 collective-permute-start.7
  64.5 15.6 %collective-permute-done.9.refs_6_ = bf16[2,3,2,32,1024]{4,3,2,1,0:T(8,128)(2,1)S(1)} collective-permute-done((bf16[2,3,2,32,1024]{4,3,2,1,0:T(8,128)(2,1)S(1)}, bf16[2,3,2,32,1024]{4,3,2,1,0:T(8,128)(2,1)S(1)}, u32[]{:S(2)}, u32[]{:S(2)}) %collective-permute-start.9) | collective-permute-done | bytes 786464 | tf_op jit(solution)/shard_map/ppermute | solution.py:276
  80.1 1.2 collective-permute-done.7.refs_7_
  81.8 1.9 %collective-permute-done.15.refs_14_ = bf16[1,1,2,32,1024]{4,3,2,1,0:T(8,128)(2,1)S(1)} collective-permute-done((bf16[1,1,2,32,1024]{4,3,2,1,0:T(8,128)(2,1)S(1)}, bf16[1,1,2,32,1024]{4,3,2,1,0:T(8,128)(2,1)S(1)}, u32[]{:S(2)}, u32[]{:S(2)}) %collective-permute-start.15) | collective-permute-done | bytes 131104 | tf_op jit(solution)/shard_map/ppermute | solution.py:276
  84.3 0.7 copy-done.19
  85.2 1.2 collective-permute-done.14.refs_13_
  86.4 1.4 collective-permute-start.10
  87.9 0.6 collective-permute-start.8
  88.5 9.0 %collective-permute-done.10.refs_8_ = bf16[1,3,2,32,1024]{4,3,2,1,0:T(8,128)(2,1)S(1)} collective-permute-done((bf16[1,3,2,32,1024]{4,3,2,1,0:T(8,128)(2,1)S(1)}, bf16[1,3,2,32,1024]{4,3,2,1,0:T(8,128)(2,1)S(1)}, u32[]{:S(2)}, u32[]{:S(2)}) %collective-permute-start.10) | collective-permute-done | bytes 393248 | tf_op jit(solution)/shard_map/ppermute | solution.py:276
  97.6 0.9 copy-done.13
  99.4 1.2 collective-permute-done.20.refs_19_
  101.4 0.6 copy-done.17
  101.9 11.7 %shard_map.47 = bf16[2048,128]{1,0:T(8,128)(2,1)} custom-call(bf16[512,1024]{1,0:T(8,128)(2,1)} %bitcast.14, bf16[2,1,2,32,1024]{4,3,2,1,0:T(8,128)(2,1)} %copy-done.5, bf16[2,1,2,32,1024]{4,3,2,1,0:T(8,128)(2,1)} %copy-done.11, bf16[2,1,2,32,1024]{4,3,2,1,0:T(8,128)(2,1)} %copy-done.10, bf16[1,1,2,32,1024]{4,3,2,1,0:T(8,128)(2,1)} %copy-done.22, ...), custom_call_target="tpu_custom_call" | custom-call | flops 4294967296 | bytes 9437184 | tf_op jit(solution)/shard_map/pallas_call | solution.py:193
  113.6 3.8 %all-to-all-start.1 = ((bf16[16,128,128]{2,1,0:T(8,128)(2,1)}), bf16[16,128,128]{2,1,0:T(8,128)(2,1)S(1)}, u32[]{:S(2)}, u32[]{:S(2)}) async-start(bf16[16,128,128]{2,1,0:T(8,128)(2,1)} %bitcast.16), calls=%async_computation.1 | async-start | bytes 1048576 | tf_op jit(solution)/shard_map/all_to_all | solution.py:317
  117.4 10.9 %shard_map.48.right_ref = bf16[256,1024]{1,0:T(8,128)(2,1)} custom-call(bf16[512,1024]{1,0:T(8,128)(2,1)} %bitcast.15, bf16[2,1,2,32,1024]{4,3,2,1,0:T(8,128)(2,1)} %copy-done.5, bf16[2,1,2,32,1024]{4,3,2,1,0:T(8,128)(2,1)} %copy-done.11, bf16[2,1,2,32,1024]{4,3,2,1,0:T(8,128)(2,1)} %copy-done.10, bf16[1,1,2,32,1024]{4,3,2,1,0:T(8,128)(2,1)} %copy-done.22, ...), custom_call_target="tpu_custom_call" | custom-call | flops 4294967296 | bytes 9437184 | tf_op jit(solution)/shard_map/pallas_call | solution.py:193
  128.4 1.0 copy-done
  129.4 0.6 shard_map.49
  130.0 14.6 %all_to_all.15 = bf16[32,16,256]{2,1,0:T(8,128)(2,1)S(1)} all-to-all(bf16[32,16,256]{2,1,0:T(8,128)(2,1)S(1)} %bitcast.13), channel_id=1, replica_groups=mesh['cuts'=1,'mode'=32] {'mode'}, dimensions={0} | all-to-all | bytes 524288 | tf_op jit(solution)/shard_map/all_to_all | solution.py:317
  144.7 0.6 convert_element_type.16
  (78 shorter events, 4.3 us)
Async XLA Ops:
  4.7 93.8 %all-to-all-start = ((bf16[32,16,1024]{2,1,0:T(8,128)(2,1)}), bf16[32,16,1024]{2,1,0:T(8,128)(2,1)S(1)}, u32[]{:S(2)}, u32[]{:S(2)}) async-start(bf16[32,16,1024]{2,1,0:T(8,128)(2,1)} %bitcast.3), calls=%async_computation | async-start | bytes 2097152 | tf_op jit(solution)/shard_map/all_to_all | solution.py:317
  12.1 51.8 %copy-start.5 = (bf16[2,1,2,32,1024]{4,3,2,1,0:T(8,128)(2,1)}, bf16[2,1,2,32,1024]{4,3,2,1,0:T(8,128)(2,1)S(1)}, u32[]{:S(2)}) copy-start(bf16[2,1,2,32,1024]{4,3,2,1,0:T(8,128)(2,1)S(1)} %maximum_bitcast_fusion.refs_0_) | copy-start | bytes 786436
  12.1 17.3 %collective-permute-start.5 = (bf16[2,1,2,32,1024]{4,3,2,1,0:T(8,128)(2,1)S(1)}, bf16[2,1,2,32,1024]{4,3,2,1,0:T(8,128)(2,1)S(1)}, u32[]{:S(2)}, u32[]{:S(2)}) collective-permute-start(bf16[2,1,2,32,1024]{4,3,2,1,0:T(8,128)(2,1)S(1)} %maximum_bitcast_fusion.refs_0_), channel_id=1, source_target_pairs={{0,4},{1,5},{2,6},{3,7},{4,0},{5,1},{6,2},{7,3},{8,12},{9,13},{10,... | collective-permute-start | bytes 786440 | tf_op jit(solution)/shard_map/ppermute | solution.py:276
  13.9 17.2 %collective-permute-start.3 = (bf16[2,1,2,32,1024]{4,3,2,1,0:T(8,128)(2,1)S(1)}, bf16[2,1,2,32,1024]{4,3,2,1,0:T(8,128)(2,1)S(1)}, u32[]{:S(2)}, u32[]{:S(2)}) collective-permute-start(bf16[2,1,2,32,1024]{4,3,2,1,0:T(8,128)(2,1)S(1)} %maximum_bitcast_fusion.refs_0_), channel_id=1, source_target_pairs={{0,2},{1,3},{2,0},{3,1},{4,6},{5,7},{6,4},{7,5},{8,10},{9,11},{10,... | collective-permute-start | bytes 786440 | tf_op jit(solution)/shard_map/ppermute | solution.py:276
  15.4 24.3 %collective-permute-start.2 = (bf16[2,1,2,32,1024]{4,3,2,1,0:T(8,128)(2,1)S(1)}, bf16[2,1,2,32,1024]{4,3,2,1,0:T(8,128)(2,1)S(1)}, u32[]{:S(2)}, u32[]{:S(2)}) collective-permute-start(bf16[2,1,2,32,1024]{4,3,2,1,0:T(8,128)(2,1)S(1)} %maximum_bitcast_fusion.refs_0_), channel_id=1, source_target_pairs={{0,24},{1,25},{2,26},{3,27},{4,28},{5,29},{6,30},{7,31},{8,16},{9,... | collective-permute-start | bytes 786440 | tf_op jit(solution)/shard_map/ppermute | solution.py:276
  18.8 42.0 %collective-permute-start.1 = (bf16[2,1,2,32,1024]{4,3,2,1,0:T(8,128)(2,1)S(1)}, bf16[2,1,2,32,1024]{4,3,2,1,0:T(8,128)(2,1)S(1)}, u32[]{:S(2)}, u32[]{:S(2)}) collective-permute-start(bf16[2,1,2,32,1024]{4,3,2,1,0:T(8,128)(2,1)S(1)} %maximum_bitcast_fusion.refs_0_), channel_id=1, source_target_pairs={{0,16},{1,17},{2,18},{3,19},{4,20},{5,21},{6,22},{7,23},{8,24},{9,... | collective-permute-start | bytes 786440 | tf_op jit(solution)/shard_map/ppermute | solution.py:276
  18.8 42.0 %collective-permute-start = (bf16[2,1,2,32,1024]{4,3,2,1,0:T(8,128)(2,1)S(1)}, bf16[2,1,2,32,1024]{4,3,2,1,0:T(8,128)(2,1)S(1)}, u32[]{:S(2)}, u32[]{:S(2)}) collective-permute-start(bf16[2,1,2,32,1024]{4,3,2,1,0:T(8,128)(2,1)S(1)} %maximum_bitcast_fusion.refs_0_), channel_id=1, source_target_pairs={{0,8},{1,9},{2,10},{3,11},{4,12},{5,13},{6,14},{7,15},{8,0},{9,1},... | collective-permute-start | bytes 786440 | tf_op jit(solution)/shard_map/ppermute | solution.py:276
  29.4 34.6 %copy-start.10 = (bf16[2,1,2,32,1024]{4,3,2,1,0:T(8,128)(2,1)}, bf16[2,1,2,32,1024]{4,3,2,1,0:T(8,128)(2,1)S(1)}, u32[]{:S(2)}) copy-start(bf16[2,1,2,32,1024]{4,3,2,1,0:T(8,128)(2,1)S(1)} %collective-permute-done.5.refs_2_) | copy-start | bytes 786436
  29.4 31.5 %collective-permute-start.6 = (bf16[1,1,2,32,1024]{4,3,2,1,0:T(8,128)(2,1)S(1)}, bf16[1,1,2,32,1024]{4,3,2,1,0:T(8,128)(2,1)S(1)}, u32[]{:S(2)}, u32[]{:S(2)}) collective-permute-start(bf16[1,1,2,32,1024]{4,3,2,1,0:T(8,128)(2,1)S(1)} %slice.17), channel_id=1, source_target_pairs={{0,2},{1,3},{2,0},{3,1},{4,6},{5,7},{6,4},{7,5},{8,10},{9,11},{10,... | collective-permute-start | bytes 393224 | tf_op jit(solution)/shard_map/ppermute | solution.py:276
  31.1 52.6 %copy-start.11 = (bf16[2,1,2,32,1024]{4,3,2,1,0:T(8,128)(2,1)}, bf16[2,1,2,32,1024]{4,3,2,1,0:T(8,128)(2,1)S(1)}, u32[]{:S(2)}) copy-start(bf16[2,1,2,32,1024]{4,3,2,1,0:T(8,128)(2,1)S(1)} %collective-permute-done.3.refs_1_) | copy-start | bytes 786436
  31.2 29.8 %collective-permute-start.4 = (bf16[1,1,2,32,1024]{4,3,2,1,0:T(8,128)(2,1)S(1)}, bf16[1,1,2,32,1024]{4,3,2,1,0:T(8,128)(2,1)S(1)}, u32[]{:S(2)}, u32[]{:S(2)}) collective-permute-start(bf16[1,1,2,32,1024]{4,3,2,1,0:T(8,128)(2,1)S(1)} %slice.16), channel_id=1, source_target_pairs={{0,4},{1,5},{2,6},{3,7},{4,0},{5,1},{6,2},{7,3},{8,12},{9,13},{10,... | collective-permute-start | bytes 393224 | tf_op jit(solution)/shard_map/ppermute | solution.py:276
  60.9 27.0 %copy-start.4 = (bf16[2,3,2,32,1024]{4,3,2,1,0:T(8,128)(2,1)}, bf16[2,3,2,32,1024]{4,3,2,1,0:T(8,128)(2,1)S(1)}, u32[]{:S(2)}) copy-start(bf16[2,3,2,32,1024]{4,3,2,1,0:T(8,128)(2,1)S(1)} %pad_maximum_fusion.refs_5_) | copy-start | bytes 2359300
  60.9 24.3 %copy-start.21 = (bf16[1,1,2,32,1024]{4,3,2,1,0:T(8,128)(2,1)}, bf16[1,1,2,32,1024]{4,3,2,1,0:T(8,128)(2,1)S(1)}, u32[]{:S(2)}) copy-start(bf16[1,1,2,32,1024]{4,3,2,1,0:T(8,128)(2,1)S(1)} %collective-permute-done.6.refs_4_) | copy-start | bytes 393220
  60.9 24.3 %copy-start.22 = (bf16[1,1,2,32,1024]{4,3,2,1,0:T(8,128)(2,1)}, bf16[1,1,2,32,1024]{4,3,2,1,0:T(8,128)(2,1)S(1)}, u32[]{:S(2)}) copy-start(bf16[1,1,2,32,1024]{4,3,2,1,0:T(8,128)(2,1)S(1)} %collective-permute-done.4.refs_3_) | copy-start | bytes 393220
  60.9 19.1 %collective-permute-start.9 = (bf16[2,3,2,32,1024]{4,3,2,1,0:T(8,128)(2,1)S(1)}, bf16[2,3,2,32,1024]{4,3,2,1,0:T(8,128)(2,1)S(1)}, u32[]{:S(2)}, u32[]{:S(2)}) collective-permute-start(bf16[2,3,2,32,1024]{4,3,2,1,0:T(8,128)(2,1)S(1)} %pad_maximum_fusion.refs_5_), channel_id=1, source_target_pairs={{0,2},{1,3},{2,0},{3,1},{4,6},{5,7},{6,4},{7,5},{8,10},{9,11},{10,... | collective-permute-start | bytes 2359304 | tf_op jit(solution)/shard_map/ppermute | solution.py:276
  62.5 18.8 %collective-permute-start.7 = (bf16[2,3,2,32,1024]{4,3,2,1,0:T(8,128)(2,1)S(1)}, bf16[2,3,2,32,1024]{4,3,2,1,0:T(8,128)(2,1)S(1)}, u32[]{:S(2)}, u32[]{:S(2)}) collective-permute-start(bf16[2,3,2,32,1024]{4,3,2,1,0:T(8,128)(2,1)S(1)} %pad_maximum_fusion.refs_5_), channel_id=1, source_target_pairs={{0,4},{1,5},{2,6},{3,7},{4,0},{5,1},{6,2},{7,3},{8,12},{9,13},{10,... | collective-permute-start | bytes 2359304 | tf_op jit(solution)/shard_map/ppermute | solution.py:276
  63.9 17.4 %collective-permute-start.11 = (bf16[2,1,2,32,1024]{4,3,2,1,0:T(8,128)(2,1)S(1)}, bf16[2,1,2,32,1024]{4,3,2,1,0:T(8,128)(2,1)S(1)}, u32[]{:S(2)}, u32[]{:S(2)}) collective-permute-start(bf16[2,1,2,32,1024]{4,3,2,1,0:T(8,128)(2,1)S(1)} %maximum_bitcast_fusion.refs_0_), channel_id=1, source_target_pairs={{0,1},{1,0},{2,3},{3,2},{4,5},{5,4},{6,7},{7,6},{8,9},{9,8},{10,11... | collective-permute-start | bytes 786440 | tf_op jit(solution)/shard_map/ppermute | solution.py:276
  63.9 19.9 %collective-permute-start.13 = (bf16[2,1,2,32,1024]{4,3,2,1,0:T(8,128)(2,1)S(1)}, bf16[2,1,2,32,1024]{4,3,2,1,0:T(8,128)(2,1)S(1)}, u32[]{:S(2)}, u32[]{:S(2)}) collective-permute-start(bf16[2,1,2,32,1024]{4,3,2,1,0:T(8,128)(2,1)S(1)} %collective-permute-done.5.refs_2_), channel_id=1, source_target_pairs={{0,1},{1,0},{2,3},{3,2},{4,5},{5,4},{6,7},{7,6},{8,9},{9,8},{10,11... | collective-permute-start | bytes 786440 | tf_op jit(solution)/shard_map/ppermute | solution.py:276
  64.4 24.1 %collective-permute-start.16 = (bf16[2,3,2,32,1024]{4,3,2,1,0:T(8,128)(2,1)S(1)}, bf16[2,3,2,32,1024]{4,3,2,1,0:T(8,128)(2,1)S(1)}, u32[]{:S(2)}, u32[]{:S(2)}) collective-permute-start(bf16[2,3,2,32,1024]{4,3,2,1,0:T(8,128)(2,1)S(1)} %pad_maximum_fusion.refs_5_), channel_id=1, source_target_pairs={{0,1},{1,0},{2,3},{3,2},{4,5},{5,4},{6,7},{7,6},{8,9},{9,8},{10,11... | collective-permute-start | bytes 2359304 | tf_op jit(solution)/shard_map/ppermute | solution.py:276
  80.1 17.5 %collective-permute-start.17 = (bf16[2,3,2,32,1024]{4,3,2,1,0:T(8,128)(2,1)S(1)}, bf16[2,3,2,32,1024]{4,3,2,1,0:T(8,128)(2,1)S(1)}, u32[]{:S(2)}, u32[]{:S(2)}) collective-permute-start(bf16[2,3,2,32,1024]{4,3,2,1,0:T(8,128)(2,1)S(1)} %collective-permute-done.9.refs_6_), channel_id=1, source_target_pairs={{0,1},{1,0},{2,3},{3,2},{4,5},{5,4},{6,7},{7,6},{8,9},{9,8},{10,11... | collective-permute-start | bytes 2359304 | tf_op jit(solution)/shard_map/ppermute | solution.py:276
  81.3 19.8 %copy-start.7 = (bf16[2,3,2,32,1024]{4,3,2,1,0:T(8,128)(2,1)}, bf16[2,3,2,32,1024]{4,3,2,1,0:T(8,128)(2,1)S(1)}, u32[]{:S(2)}) copy-start(bf16[2,3,2,32,1024]{4,3,2,1,0:T(8,128)(2,1)S(1)} %collective-permute-done.7.refs_7_) | copy-start | bytes 2359300
  81.3 17.2 %collective-permute-start.18 = (bf16[2,3,2,32,1024]{4,3,2,1,0:T(8,128)(2,1)S(1)}, bf16[2,3,2,32,1024]{4,3,2,1,0:T(8,128)(2,1)}, u32[]{:S(2)}, u32[]{:S(2)}) collective-permute-start(bf16[2,3,2,32,1024]{4,3,2,1,0:T(8,128)(2,1)S(1)} %collective-permute-done.7.refs_7_), channel_id=1, source_target_pairs={{0,1},{1,0},{2,3},{3,2},{4,5},{5,4},{6,7},{7,6},{8,9},{9,8},{10,11... | collective-permute-start | bytes 2359304 | tf_op jit(solution)/shard_map/ppermute | solution.py:276
  81.3 2.4 %collective-permute-start.15 = (bf16[1,1,2,32,1024]{4,3,2,1,0:T(8,128)(2,1)S(1)}, bf16[1,1,2,32,1024]{4,3,2,1,0:T(8,128)(2,1)S(1)}, u32[]{:S(2)}, u32[]{:S(2)}) collective-permute-start(bf16[1,1,2,32,1024]{4,3,2,1,0:T(8,128)(2,1)S(1)} %collective-permute-done.6.refs_4_), channel_id=1, source_target_pairs={{0,1},{1,0},{2,3},{3,2},{4,5},{5,4},{6,7},{7,6},{8,9},{9,8},{10,11... | collective-permute-start | bytes 393224 | tf_op jit(solution)/shard_map/ppermute | solution.py:276
  83.7 4.2 %collective-permute-start.12 = (bf16[2,1,2,32,1024]{4,3,2,1,0:T(8,128)(2,1)S(1)}, bf16[2,1,2,32,1024]{4,3,2,1,0:T(8,128)(2,1)S(1)}, u32[]{:S(2)}, u32[]{:S(2)}) collective-permute-start(bf16[2,1,2,32,1024]{4,3,2,1,0:T(8,128)(2,1)S(1)} %collective-permute-done.3.refs_1_), channel_id=1, source_target_pairs={{0,1},{1,0},{2,3},{3,2},{4,5},{5,4},{6,7},{7,6},{8,9},{9,8},{10,11... | collective-permute-start | bytes 786440 | tf_op jit(solution)/shard_map/ppermute | solution.py:276
  85.1 1.3 collective-permute-start.14
  86.4 11.2 %collective-permute-start.10 = (bf16[1,3,2,32,1024]{4,3,2,1,0:T(8,128)(2,1)S(1)}, bf16[1,3,2,32,1024]{4,3,2,1,0:T(8,128)(2,1)S(1)}, u32[]{:S(2)}, u32[]{:S(2)}) collective-permute-start(bf16[1,3,2,32,1024]{4,3,2,1,0:T(8,128)(2,1)S(1)} %slice.19), channel_id=1, source_target_pairs={{0,4},{1,5},{2,6},{3,7},{4,0},{5,1},{6,2},{7,3},{8,12},{9,13},{10,... | collective-permute-start | bytes 1179656 | tf_op jit(solution)/shard_map/ppermute | solution.py:276
  87.9 9.7 %copy-start.20 = (bf16[2,1,2,32,1024]{4,3,2,1,0:T(8,128)(2,1)}, bf16[2,1,2,32,1024]{4,3,2,1,0:T(8,128)(2,1)S(1)}, u32[]{:S(2)}) copy-start(bf16[2,1,2,32,1024]{4,3,2,1,0:T(8,128)(2,1)S(1)} %collective-permute-done.12.refs_11_) | copy-start | bytes 786436
  87.9 11.0 %collective-permute-start.8 = (bf16[1,3,2,32,1024]{4,3,2,1,0:T(8,128)(2,1)S(1)}, bf16[1,3,2,32,1024]{4,3,2,1,0:T(8,128)(2,1)S(1)}, u32[]{:S(2)}, u32[]{:S(2)}) collective-permute-start(bf16[1,3,2,32,1024]{4,3,2,1,0:T(8,128)(2,1)S(1)} %slice.18), channel_id=1, source_target_pairs={{0,2},{1,3},{2,0},{3,1},{4,6},{5,7},{6,4},{7,5},{8,10},{9,11},{10,... | collective-permute-start | bytes 1179656 | tf_op jit(solution)/shard_map/ppermute | solution.py:276
  88.5 9.1 %copy-start.12 = (bf16[2,3,2,32,1024]{4,3,2,1,0:T(8,128)(2,1)}, bf16[2,3,2,32,1024]{4,3,2,1,0:T(8,128)(2,1)S(1)}, u32[]{:S(2)}) copy-start(bf16[2,3,2,32,1024]{4,3,2,1,0:T(8,128)(2,1)S(1)} %collective-permute-done.16.refs_15_) | copy-start | bytes 2359300
  98.9 1.7 %collective-permute-start.20 = (bf16[1,3,2,32,1024]{4,3,2,1,0:T(8,128)(2,1)S(1)}, bf16[1,3,2,32,1024]{4,3,2,1,0:T(8,128)(2,1)S(1)}, u32[]{:S(2)}, u32[]{:S(2)}) collective-permute-start(bf16[1,3,2,32,1024]{4,3,2,1,0:T(8,128)(2,1)S(1)} %collective-permute-done.8.refs_9_), channel_id=1, source_target_pairs={{0,1},{1,0},{2,3},{3,2},{4,5},{5,4},{6,7},{7,6},{8,9},{9,8},{10,11... | collective-permute-start | bytes 1179656 | tf_op jit(solution)/shard_map/ppermute | solution.py:276
  98.9 2.3 %collective-permute-start.19 = (bf16[1,3,2,32,1024]{4,3,2,1,0:T(8,128)(2,1)S(1)}, bf16[1,3,2,32,1024]{4,3,2,1,0:T(8,128)(2,1)S(1)}, u32[]{:S(2)}, u32[]{:S(2)}) collective-permute-start(bf16[1,3,2,32,1024]{4,3,2,1,0:T(8,128)(2,1)S(1)} %collective-permute-done.10.refs_8_), channel_id=1, source_target_pairs={{0,1},{1,0},{2,3},{3,2},{4,5},{5,4},{6,7},{7,6},{8,9},{9,8},{10,11... | collective-permute-start | bytes 1179656 | tf_op jit(solution)/shard_map/ppermute | solution.py:276
  113.6 14.7 %all-to-all-start.1 = ((bf16[16,128,128]{2,1,0:T(8,128)(2,1)}), bf16[16,128,128]{2,1,0:T(8,128)(2,1)S(1)}, u32[]{:S(2)}, u32[]{:S(2)}) async-start(bf16[16,128,128]{2,1,0:T(8,128)(2,1)} %bitcast.16), calls=%async_computation.1 | async-start | bytes 1048576 | tf_op jit(solution)/shard_map/all_to_all | solution.py:317
  (16 other events, 41.7 us)

commit v9 on v8

--- a/solution.py
+++ b/solution.py
@@ -26,24 +26,20 @@
     return jnp.dot(left, right, preferred_element_type=jnp.float32)
 
 
-def pack_kernel(qs, x_ref, order_ref, o_ref, ordered):
+def pack_kernel(qs, x_ref, order_ref, left_ref, right_ref):
     _, parts, rows_each, width = x_ref.shape
     rows = parts * rows_each
     step = min(256, width)
-    new = lax.broadcasted_iota(jnp.int32, (2 * rows, 2 * rows), 0)
-    e, side = new // (2 * parts * qs), new // (parts * qs) % 2
-    k, q = new // qs % parts, new % qs
-    pack = one_hot((2 * rows, 2 * rows), 1, side * rows + k * rows_each + e * qs + q)
-    for pair in range(x_ref.shape[0] // 2):
-        for side in range(2):
-            branch = 2 * pair + side
-            values = x_ref[branch].reshape(rows, width)
-            for start in range(0, width, step):
-                picks = one_hot((width, step), 0, order_ref[branch : branch + 1, start : start + step])
-                found = exact_dot(values, picks).astype(jnp.bfloat16)
-                ordered[side * rows : (side + 1) * rows, start : start + step] = found
-        packed = exact_dot(pack, ordered[...]).astype(jnp.bfloat16)
-        o_ref[2 * pair * rows : 2 * (pair + 1) * rows, :] = packed
+    new = lax.broadcasted_iota(jnp.int32, (rows, rows), 0)
+    e, k, q = new // (parts * qs), new // qs % parts, new % qs
+    pack = one_hot((rows, rows), 1, k * rows_each + e * qs + q)
+    for branch in range(x_ref.shape[0]):
+        o_ref = (left_ref, right_ref)[branch % 2]
+        place = branch // 2 * rows
+        packed = exact_dot(pack, x_ref[branch].reshape(rows, width)).astype(jnp.bfloat16)
+        for start in range(0, width, step):
+            picks = one_hot((width, step), 0, order_ref[branch : branch + 1, start : start + step])
+            o_ref[place : place + rows, start : start + step] = exact_dot(packed, picks).astype(jnp.bfloat16)
 
 
 def swap_sign(tiles, qs):
@@ -111,10 +107,9 @@
         for copy in copies[gate]:
             copy.start()
     tile_rows = 2 * qs
-    rows, width = x_ref.shape[0] // 2, x_ref.shape[1]
-    first = x_ref[...].astype(jnp.float32).reshape(devices, 2 * tile_rows, width)
-    first = first[:, :tile_rows] if is_left else first[:, tile_rows:]
-    xs[0, :, :width] = first.reshape(rows, width).astype(jnp.bfloat16)
+    rows, width = x_ref.shape
+    first = x_ref[...].astype(jnp.float32).reshape(devices, tile_rows, width)
+    xs[0, :, :width] = x_ref[...]
     xs[0, :, width:] = swap_sign(first, qs).reshape(rows, width).astype(jnp.bfloat16)
     step = min(512, width)
     for layer in range(2 * CYCLES):
@@ -188,13 +183,14 @@
         o_ref[g * block : (g + 1) * block, :] = part.astype(jnp.bfloat16)
 
 
-def call(kernel, out_shape, inputs, scratch=(), flops=0, blocks=(), grant=24):
+def call(kernel, out_shape, inputs, scratch=(), flops=0, blocks=(), grant=24, outputs=0):
     moved = sum(x.size * x.dtype.itemsize for x in (*inputs, *blocks))
+    out = jax.ShapeDtypeStruct(out_shape, jnp.bfloat16)
     return pl.pallas_call(
         kernel,
-        out_shape=jax.ShapeDtypeStruct(out_shape, jnp.bfloat16),
+        out_shape=[out] * outputs if outputs else out,
         in_specs=whole(len(inputs)) + [pl.BlockSpec(memory_space=pl.ANY)] * len(blocks),
-        out_specs=whole(1)[0],
+        out_specs=whole(outputs) if outputs else whole(1)[0],
         scratch_shapes=list(scratch),
         compiler_params=pltpu.CompilerParams(vmem_limit_bytes=grant * MEBI),
         cost_estimate=pl.CostEstimate(flops=flops, bytes_accessed=moved, transcendentals=0),
@@ -227,13 +223,14 @@
     rows = devices * tile_rows
     packed = call(
         functools.partial(pack_kernel, qs),
-        (2 * rows, width),
+        (rows, width),
         (branch_in, column_order),
-        [pltpu.VMEM((4 * rows_each, width), jnp.bfloat16)],
-        8 * rows * width * width,
-    )
-    blocks, plan, states = spread(gate_a, gate_b, packed.reshape(devices, 2 * tile_rows, width))
-    states = states.reshape(2 * rows, width)
+        flops=8 * rows * width * width,
+        outputs=2,
+    )
+    packed = [side.reshape(devices, tile_rows, width) for side in packed]
+    blocks, plan, *states = spread(gate_a, gate_b, packed)
+    states = [state.reshape(rows, width) for state in states]
     sizes = (devices, qs, group, rows_each)
     scratch = [
         pltpu.VMEM((2, rows, 2 * width), jnp.bfloat16),
@@ -245,7 +242,7 @@
     left = call(
         functools.partial(layers_kernel, sizes, True, plan),
         (halves * rows // 2, LANES),
-        (states,),
+        (states[0],),
         scratch,
         work,
         blocks,
@@ -254,7 +251,7 @@
     groups = [[h * halves + e for e in range(halves)] for h in range(2)]
     left = trade(left.reshape(halves, rows // 2, LANES), groups)
     right = call(
-        functools.partial(layers_kernel, sizes, False, plan), (rows, width), (states,), scratch, work, blocks, 56
+        functools.partial(layers_kernel, sizes, False, plan), (rows, width), (states[1],), scratch, work, blocks, 56
     )
     free = width // (2 * KEPT)
     us = halves
@@ -292,25 +289,29 @@
 def spread(gate_a, gate_b, packed):
     bits = lax.axis_size("mode").bit_length() - 1
     own = jnp.stack([gate_a, gate_b])[:, None]
-    blocks = plane(own, ((),))
     far = [()]
     for bit in range(3, bits):
         far += [source + (bit,) for source in far]
-    far = tuple(far[1:])
-    value = jnp.concatenate([flip(own, *source) for source in far], axis=1)
-    states = trade(packed)
-    value, *_ = lax.optimization_barrier((value, packed, blocks[-2][0], blocks[-1][0]))
-    blocks += plane(value, far)
+    came = [flip(own, *source) for source in far[1:]]
+    left, *rest = lax.optimization_barrier((packed[0], *came[1:]))
+    sets = [(own, ((),)), (came[0], tuple(far[1:2]))]
+    if rest:
+        sets.append((jnp.concatenate(rest, axis=1), tuple(far[2:])))
+    blocks = []
+    for number, (value, sources) in enumerate(sets):
+        if number:
+            value, *_ = lax.optimization_barrier((value, *packed, blocks[-2][0], blocks[-1][0]))
+        blocks += plane(value, sources)
+    right, *_ = lax.optimization_barrier((packed[1], blocks[-4][0], blocks[-3][0]))
+    last = len(blocks) - 2
     near = []
     for number, (value, sources, gates) in enumerate(blocks):
-        if number >= len(blocks) - 2:
-            value, states, *_ = lax.optimization_barrier(
-                (value, states, *[earlier for earlier, _, _ in near[: len(blocks) - 2]])
-            )
+        if number >= last:
+            value, *_ = lax.optimization_barrier((value, *[earlier for earlier, _, _ in near[:last]]))
         near.append((flip(value, 0), tuple(source + (0,) for source in sources), gates))
     blocks += near
     plan = tuple((sources, gates) for _, sources, gates in blocks)
-    return [value for value, _, _ in blocks], plan, states
+    return [value for value, _, _ in blocks], plan, trade(left), trade(right)
 
 
 def trade(value, groups=None):

time: 146 us -> 130 us (0.89)
  waiting for transfers between devices: 69.7 us -> 41.8 us
  starting transfers between devices: 27.8 us -> 37.8 us
  blocking collectives: 14.6 us -> 16.5 us
    ppermute x21 -> x30, waiting for transfers between devices: 69.7 us -> 41.8 us  [flip(): return lax.ppermute(value, 'mode', pairs)]
    ppermute x21 -> x30, starting transfers between devices: 16.8 us -> 25.9 us  [flip(): return lax.ppermute(value, 'mode', pairs)]
    all_to_all x1, blocking collectives: 14.6 us -> 16.5 us  [trade(): lax.all_to_all(value, 'mode', split_axis=0, concat_axis=0, axis_index_gro...]
    unnamed x50 -> x62, local copies, waits for them, and re-layouts: 5.97 us -> 4.53 us
    all_to_all x2 -> x3, starting transfers between devices: 11.1 us -> 11.9 us  [trade(): lax.all_to_all(value, 'mode', split_axis=0, concat_axis=0, axis_index_gro...]
  transfers between devices with their start and end apart: 23 -> 33, of which waited for: 11 -> 13; matrix products, arithmetic and copies ran while one was open for 0% -> 1% of each run, Pallas kernels for 8% -> 20%
where the time goes in v9:
time: 130 us
  waiting for transfers between devices  41.8 us (32%)
  starting transfers between devices  37.8 us (29%)
  Pallas kernels  25.9 us (20%)
  blocking collectives  16.5 us (13%)
  local copies, waits for them, and re-layouts  6.12 us (5%)
    ppermute x30, waiting for transfers between devices, flip(): return lax.ppermute(value, 'mode', pairs)  41.8 us
    pallas_call x4, Pallas kernels, call(): pl.pallas_call(kernel, out_shape=[out] * outputs if outputs else out, in_...  25.9 us
    ppermute x30, starting transfers between devices, flip(): return lax.ppermute(value, 'mode', pairs)  25.9 us
    all_to_all x1, blocking collectives, trade(): lax.all_to_all(value, 'mode', split_axis=0, concat_axis=0, axis_index_gro...  16.5 us
    all_to_all x3, starting transfers between devices, trade(): lax.all_to_all(value, 'mode', split_axis=0, concat_axis=0, axis_index_gro...  11.9 us
    unnamed x62, local copies, waits for them, and re-layouts  4.53 us
  transfers between devices with their start and end apart: 33, of which 13 were waited for; matrix products, arithmetic and copies ran while one was open for 1% of the time, Pallas kernels for 20%

profile of v9, /device:TPU:0, one launch (start us, length us, event | category | flops | bytes accessed | tf_op | source)
XLA Modules:
  0.0 129.7 jit_solution(15881012954068015759)
XLA Ops:
  0.0 1.1 maximum_bitcast_fusion.refs_0_
  1.1 3.0 %collective-permute-start.3 = (bf16[2,1,2,32,1024]{4,3,2,1,0:T(8,128)(2,1)S(1)}, bf16[2,1,2,32,1024]{4,3,2,1,0:T(8,128)(2,1)S(1)}, u32[]{:S(2)}, u32[]{:S(2)}) collective-permute-start(bf16[2,1,2,32,1024]{4,3,2,1,0:T(8,128)(2,1)S(1)} %maximum_bitcast_fusion.refs_0_), channel_id=1, source_target_pairs={{0,4},{1,5},{2,6},{3,7},{4,0},{5,1},{6,2},{7,3},{8,12},{9,13},{10,... | collective-permute-start | bytes 786440 | tf_op jit(solution)/shard_map/ppermute | solution.py:273
  4.1 1.5 %collective-permute-start.2 = (bf16[2,1,2,32,1024]{4,3,2,1,0:T(8,128)(2,1)S(1)}, bf16[2,1,2,32,1024]{4,3,2,1,0:T(8,128)(2,1)S(1)}, u32[]{:S(2)}, u32[]{:S(2)}) collective-permute-start(bf16[2,1,2,32,1024]{4,3,2,1,0:T(8,128)(2,1)S(1)} %maximum_bitcast_fusion.refs_0_), channel_id=1, source_target_pairs={{0,2},{1,3},{2,0},{3,1},{4,6},{5,7},{6,4},{7,5},{8,10},{9,11},{10,... | collective-permute-start | bytes 786440 | tf_op jit(solution)/shard_map/ppermute | solution.py:273
  5.6 1.6 %collective-permute-start.6 = (bf16[2,1,2,32,1024]{4,3,2,1,0:T(8,128)(2,1)S(1)}, bf16[2,1,2,32,1024]{4,3,2,1,0:T(8,128)(2,1)S(1)}, u32[]{:S(2)}, u32[]{:S(2)}) collective-permute-start(bf16[2,1,2,32,1024]{4,3,2,1,0:T(8,128)(2,1)S(1)} %maximum_bitcast_fusion.refs_0_), channel_id=1, source_target_pairs={{0,8},{1,9},{2,10},{3,11},{4,12},{5,13},{6,14},{7,15},{8,0},{9,1},... | collective-permute-start | bytes 786440 | tf_op jit(solution)/shard_map/ppermute | solution.py:273
  7.2 2.5 %collective-permute-start.1 = (bf16[2,1,2,32,1024]{4,3,2,1,0:T(8,128)(2,1)S(1)}, bf16[2,1,2,32,1024]{4,3,2,1,0:T(8,128)(2,1)S(1)}, u32[]{:S(2)}, u32[]{:S(2)}) collective-permute-start(bf16[2,1,2,32,1024]{4,3,2,1,0:T(8,128)(2,1)S(1)} %maximum_bitcast_fusion.refs_0_), channel_id=1, source_target_pairs={{0,24},{1,25},{2,26},{3,27},{4,28},{5,29},{6,30},{7,31},{8,16},{9,... | collective-permute-start | bytes 786440 | tf_op jit(solution)/shard_map/ppermute | solution.py:273
  10.5 1.8 %collective-permute-start.5 = (bf16[1,1,2,32,1024]{4,3,2,1,0:T(8,128)(2,1)S(1)}, bf16[1,1,2,32,1024]{4,3,2,1,0:T(8,128)(2,1)S(1)}, u32[]{:S(2)}, u32[]{:S(2)}) collective-permute-start(bf16[1,1,2,32,1024]{4,3,2,1,0:T(8,128)(2,1)S(1)} %slice.25), channel_id=1, source_target_pairs={{0,2},{1,3},{2,0},{3,1},{4,6},{5,7},{6,4},{7,5},{8,10},{9,11},{10,... | collective-permute-start | bytes 393224 | tf_op jit(solution)/shard_map/ppermute | solution.py:273
  12.2 1.6 %collective-permute-start.4 = (bf16[1,1,2,32,1024]{4,3,2,1,0:T(8,128)(2,1)S(1)}, bf16[1,1,2,32,1024]{4,3,2,1,0:T(8,128)(2,1)S(1)}, u32[]{:S(2)}, u32[]{:S(2)}) collective-permute-start(bf16[1,1,2,32,1024]{4,3,2,1,0:T(8,128)(2,1)S(1)} %slice.24), channel_id=1, source_target_pairs={{0,4},{1,5},{2,6},{3,7},{4,0},{5,1},{6,2},{7,3},{8,12},{9,13},{10,... | collective-permute-start | bytes 393224 | tf_op jit(solution)/shard_map/ppermute | solution.py:273
  13.8 0.7 copy-done.2
  14.6 3.0 %shard_map.46 = (bf16[256,1024]{1,0:T(8,128)(2,1)}, bf16[256,1024]{1,0:T(8,128)(2,1)}) custom-call(bf16[4,2,64,1024]{3,2,1,0:T(8,128)(2,1)S(1)} %copy-done.1, s32[4,1024]{1,0:T(4,128)S(1)} %copy-done.2), custom_call_target="tpu_custom_call" | custom-call | flops 2147483648 | bytes 1064960 | tf_op jit(solution)/shard_map/pallas_call | solution.py:189
  17.6 1.2 collective-permute-start.8
  19.4 3.3 %collective-permute-done.1 = bf16[2,1,2,32,1024]{4,3,2,1,0:T(8,128)(2,1)S(1)} collective-permute-done((bf16[2,1,2,32,1024]{4,3,2,1,0:T(8,128)(2,1)S(1)}, bf16[2,1,2,32,1024]{4,3,2,1,0:T(8,128)(2,1)S(1)}, u32[]{:S(2)}, u32[]{:S(2)}) %collective-permute-start.1) | collective-permute-done | bytes 262176 | tf_op jit(solution)/shard_map/ppermute | solution.py:273
  22.6 9.5 %collective-permute-done = bf16[2,1,2,32,1024]{4,3,2,1,0:T(8,128)(2,1)S(1)} collective-permute-done((bf16[2,1,2,32,1024]{4,3,2,1,0:T(8,128)(2,1)S(1)}, bf16[2,1,2,32,1024]{4,3,2,1,0:T(8,128)(2,1)S(1)}, u32[]{:S(2)}, u32[]{:S(2)}) %collective-permute-start) | collective-permute-done | bytes 262176 | tf_op jit(solution)/shard_map/ppermute | solution.py:273
  32.1 3.0 %all-to-all-start = ((bf16[32,8,1024]{2,1,0:T(8,128)(2,1)}), bf16[32,8,1024]{2,1,0:T(8,128)(2,1)S(1)}, u32[]{:S(2)}, u32[]{:S(2)}) async-start(bf16[32,8,1024]{2,1,0:T(8,128)(2,1)} %bitcast), calls=%async_computation | async-start | bytes 1048576 | tf_op jit(solution)/shard_map/all_to_all | solution.py:318
  35.2 1.8 %collective-permute-start.10 = (bf16[1,1,2,32,1024]{4,3,2,1,0:T(8,128)(2,1)S(1)}, bf16[1,1,2,32,1024]{4,3,2,1,0:T(8,128)(2,1)S(1)}, u32[]{:S(2)}, u32[]{:S(2)}) collective-permute-start(bf16[1,1,2,32,1024]{4,3,2,1,0:T(8,128)(2,1)S(1)} %slice.27), channel_id=1, source_target_pairs={{0,2},{1,3},{2,0},{3,1},{4,6},{5,7},{6,4},{7,5},{8,10},{9,11},{10,... | collective-permute-start | bytes 393224 | tf_op jit(solution)/shard_map/ppermute | solution.py:273
  37.0 0.9 slice.26
  37.9 1.5 %collective-permute-start.9 = (bf16[1,1,2,32,1024]{4,3,2,1,0:T(8,128)(2,1)S(1)}, bf16[1,1,2,32,1024]{4,3,2,1,0:T(8,128)(2,1)}, u32[]{:S(2)}, u32[]{:S(2)}) collective-permute-start(bf16[1,1,2,32,1024]{4,3,2,1,0:T(8,128)(2,1)S(1)} %slice.26), channel_id=1, source_target_pairs={{0,4},{1,5},{2,6},{3,7},{4,0},{5,1},{6,2},{7,3},{8,12},{9,13},{10,... | collective-permute-start | bytes 393224 | tf_op jit(solution)/shard_map/ppermute | solution.py:273
  40.1 4.9 %collective-permute-done.10.refs_9_ = bf16[1,1,2,32,1024]{4,3,2,1,0:T(8,128)(2,1)S(1)} collective-permute-done((bf16[1,1,2,32,1024]{4,3,2,1,0:T(8,128)(2,1)S(1)}, bf16[1,1,2,32,1024]{4,3,2,1,0:T(8,128)(2,1)S(1)}, u32[]{:S(2)}, u32[]{:S(2)}) %collective-permute-start.10) | collective-permute-done | bytes 131104 | tf_op jit(solution)/shard_map/ppermute | solution.py:273
  45.6 1.1 collective-permute-start.12
  48.0 0.9 collective-permute-done.19.refs_19_
  49.4 1.1 collective-permute-done.18.refs_18_
  51.3 8.6 %collective-permute-done.12.refs_12_ = bf16[2,2,2,32,1024]{4,3,2,1,0:T(8,128)(2,1)S(1)} collective-permute-done((bf16[2,2,2,32,1024]{4,3,2,1,0:T(8,128)(2,1)S(1)}, bf16[2,2,2,32,1024]{4,3,2,1,0:T(8,128)(2,1)S(1)}, u32[]{:S(2)}, u32[]{:S(2)}) %collective-permute-start.12) | collective-permute-done | bytes 524320 | tf_op jit(solution)/shard_map/ppermute | solution.py:273
  62.1 5.1 %all-to-all-start.2 = ((bf16[32,8,1024]{2,1,0:T(8,128)(2,1)}), bf16[32,8,1024]{2,1,0:T(8,128)(2,1)S(1)}, u32[]{:S(2)}, u32[]{:S(2)}) async-start(bf16[32,8,1024]{2,1,0:T(8,128)(2,1)} %bitcast.5), calls=%async_computation.2 | async-start | bytes 1048576 | tf_op jit(solution)/shard_map/all_to_all | solution.py:318
  67.3 1.8 %collective-permute-start.14 = (bf16[1,2,2,32,1024]{4,3,2,1,0:T(8,128)(2,1)S(1)}, bf16[1,2,2,32,1024]{4,3,2,1,0:T(8,128)(2,1)S(1)}, u32[]{:S(2)}, u32[]{:S(2)}) collective-permute-start(bf16[1,2,2,32,1024]{4,3,2,1,0:T(8,128)(2,1)S(1)} %slice.29), channel_id=1, source_target_pairs={{0,2},{1,3},{2,0},{3,1},{4,6},{5,7},{6,4},{7,5},{8,10},{9,11},{10,... | collective-permute-start | bytes 786440 | tf_op jit(solution)/shard_map/ppermute | solution.py:273
  69.2 1.5 %collective-permute-start.13 = (bf16[1,2,2,32,1024]{4,3,2,1,0:T(8,128)(2,1)S(1)}, bf16[1,2,2,32,1024]{4,3,2,1,0:T(8,128)(2,1)S(1)}, u32[]{:S(2)}, u32[]{:S(2)}) collective-permute-start(bf16[1,2,2,32,1024]{4,3,2,1,0:T(8,128)(2,1)S(1)} %slice.28), channel_id=1, source_target_pairs={{0,4},{1,5},{2,6},{3,7},{4,0},{5,1},{6,2},{7,3},{8,12},{9,13},{10,... | collective-permute-start | bytes 786440 | tf_op jit(solution)/shard_map/ppermute | solution.py:273
  70.7 10.2 %collective-permute-done.14.refs_14_ = bf16[1,2,2,32,1024]{4,3,2,1,0:T(8,128)(2,1)S(1)} collective-permute-done((bf16[1,2,2,32,1024]{4,3,2,1,0:T(8,128)(2,1)S(1)}, bf16[1,2,2,32,1024]{4,3,2,1,0:T(8,128)(2,1)S(1)}, u32[]{:S(2)}, u32[]{:S(2)}) %collective-permute-start.14) | collective-permute-done | bytes 262176 | tf_op jit(solution)/shard_map/ppermute | solution.py:273
  81.8 1.0 collective-permute-done.28.refs_28_
  83.9 11.5 %shard_map.47 = bf16[2048,128]{1,0:T(8,128)(2,1)} custom-call(bf16[256,1024]{1,0:T(8,128)(2,1)} %bitcast.16, bf16[2,1,2,32,1024]{4,3,2,1,0:T(8,128)(2,1)} %copy-done.6, bf16[2,1,2,32,1024]{4,3,2,1,0:T(8,128)(2,1)} %copy-done.10, bf16[2,1,2,32,1024]{4,3,2,1,0:T(8,128)(2,1)} %copy-done.9, bf16[1,1,2,32,1024]{4,3,2,1,0:T(8,128)(2,1)} %copy-done.26, ...), custom_call_target="tpu_custom_call" | custom-call | flops 4294967296 | bytes 8912896 | tf_op jit(solution)/shard_map/pallas_call | solution.py:189
  95.4 0.8 copy-done.5
  96.2 3.8 %all-to-all-start.1 = ((bf16[16,128,128]{2,1,0:T(8,128)(2,1)}), bf16[16,128,128]{2,1,0:T(8,128)(2,1)S(1)}, u32[]{:S(2)}, u32[]{:S(2)}) async-start(bf16[16,128,128]{2,1,0:T(8,128)(2,1)} %bitcast.18), calls=%async_computation.1 | async-start | bytes 1048576 | tf_op jit(solution)/shard_map/all_to_all | solution.py:318
  100.0 10.8 %shard_map.48.right_ref = bf16[256,1024]{1,0:T(8,128)(2,1)} custom-call(bf16[256,1024]{1,0:T(8,128)(2,1)} %bitcast.17, bf16[2,1,2,32,1024]{4,3,2,1,0:T(8,128)(2,1)} %copy-done.6, bf16[2,1,2,32,1024]{4,3,2,1,0:T(8,128)(2,1)} %copy-done.10, bf16[2,1,2,32,1024]{4,3,2,1,0:T(8,128)(2,1)} %copy-done.9, bf16[1,1,2,32,1024]{4,3,2,1,0:T(8,128)(2,1)} %copy-done.26, ...), custom_call_target="tpu_custom_call" | custom-call | flops 4294967296 | bytes 8912896 | tf_op jit(solution)/shard_map/pallas_call | solution.py:189
  110.8 1.0 copy-done
  112.5 16.5 %all_to_all.20 = bf16[32,16,256]{2,1,0:T(8,128)(2,1)S(1)} all-to-all(bf16[32,16,256]{2,1,0:T(8,128)(2,1)S(1)} %bitcast.15), channel_id=1, replica_groups=mesh['cuts'=1,'mode'=32] {'mode'}, dimensions={0} | all-to-all | bytes 524288 | tf_op jit(solution)/shard_map/all_to_all | solution.py:318
  (112 shorter events, 10.4 us)
Async XLA Ops:
  1.1 9.3 %collective-permute-start.3 = (bf16[2,1,2,32,1024]{4,3,2,1,0:T(8,128)(2,1)S(1)}, bf16[2,1,2,32,1024]{4,3,2,1,0:T(8,128)(2,1)S(1)}, u32[]{:S(2)}, u32[]{:S(2)}) collective-permute-start(bf16[2,1,2,32,1024]{4,3,2,1,0:T(8,128)(2,1)S(1)} %maximum_bitcast_fusion.refs_0_), channel_id=1, source_target_pairs={{0,4},{1,5},{2,6},{3,7},{4,0},{5,1},{6,2},{7,3},{8,12},{9,13},{10,... | collective-permute-start | bytes 786440 | tf_op jit(solution)/shard_map/ppermute | solution.py:273
  4.1 8.1 %collective-permute-start.2 = (bf16[2,1,2,32,1024]{4,3,2,1,0:T(8,128)(2,1)S(1)}, bf16[2,1,2,32,1024]{4,3,2,1,0:T(8,128)(2,1)S(1)}, u32[]{:S(2)}, u32[]{:S(2)}) collective-permute-start(bf16[2,1,2,32,1024]{4,3,2,1,0:T(8,128)(2,1)S(1)} %maximum_bitcast_fusion.refs_0_), channel_id=1, source_target_pairs={{0,2},{1,3},{2,0},{3,1},{4,6},{5,7},{6,4},{7,5},{8,10},{9,11},{10,... | collective-permute-start | bytes 786440 | tf_op jit(solution)/shard_map/ppermute | solution.py:273
  5.6 12.0 %collective-permute-start.6 = (bf16[2,1,2,32,1024]{4,3,2,1,0:T(8,128)(2,1)S(1)}, bf16[2,1,2,32,1024]{4,3,2,1,0:T(8,128)(2,1)S(1)}, u32[]{:S(2)}, u32[]{:S(2)}) collective-permute-start(bf16[2,1,2,32,1024]{4,3,2,1,0:T(8,128)(2,1)S(1)} %maximum_bitcast_fusion.refs_0_), channel_id=1, source_target_pairs={{0,8},{1,9},{2,10},{3,11},{4,12},{5,13},{6,14},{7,15},{8,0},{9,1},... | collective-permute-start | bytes 786440 | tf_op jit(solution)/shard_map/ppermute | solution.py:273
  7.2 15.4 %collective-permute-start.1 = (bf16[2,1,2,32,1024]{4,3,2,1,0:T(8,128)(2,1)S(1)}, bf16[2,1,2,32,1024]{4,3,2,1,0:T(8,128)(2,1)S(1)}, u32[]{:S(2)}, u32[]{:S(2)}) collective-permute-start(bf16[2,1,2,32,1024]{4,3,2,1,0:T(8,128)(2,1)S(1)} %maximum_bitcast_fusion.refs_0_), channel_id=1, source_target_pairs={{0,24},{1,25},{2,26},{3,27},{4,28},{5,29},{6,30},{7,31},{8,16},{9,... | collective-permute-start | bytes 786440 | tf_op jit(solution)/shard_map/ppermute | solution.py:273
  9.7 22.4 %collective-permute-start = (bf16[2,1,2,32,1024]{4,3,2,1,0:T(8,128)(2,1)S(1)}, bf16[2,1,2,32,1024]{4,3,2,1,0:T(8,128)(2,1)S(1)}, u32[]{:S(2)}, u32[]{:S(2)}) collective-permute-start(bf16[2,1,2,32,1024]{4,3,2,1,0:T(8,128)(2,1)S(1)} %maximum_bitcast_fusion.refs_0_), channel_id=1, source_target_pairs={{0,16},{1,17},{2,18},{3,19},{4,20},{5,21},{6,22},{7,23},{8,24},{9,... | collective-permute-start | bytes 786440 | tf_op jit(solution)/shard_map/ppermute | solution.py:273
  10.5 7.1 %collective-permute-start.5 = (bf16[1,1,2,32,1024]{4,3,2,1,0:T(8,128)(2,1)S(1)}, bf16[1,1,2,32,1024]{4,3,2,1,0:T(8,128)(2,1)S(1)}, u32[]{:S(2)}, u32[]{:S(2)}) collective-permute-start(bf16[1,1,2,32,1024]{4,3,2,1,0:T(8,128)(2,1)S(1)} %slice.25), channel_id=1, source_target_pairs={{0,2},{1,3},{2,0},{3,1},{4,6},{5,7},{6,4},{7,5},{8,10},{9,11},{10,... | collective-permute-start | bytes 393224 | tf_op jit(solution)/shard_map/ppermute | solution.py:273
  12.2 5.4 %collective-permute-start.4 = (bf16[1,1,2,32,1024]{4,3,2,1,0:T(8,128)(2,1)S(1)}, bf16[1,1,2,32,1024]{4,3,2,1,0:T(8,128)(2,1)S(1)}, u32[]{:S(2)}, u32[]{:S(2)}) collective-permute-start(bf16[1,1,2,32,1024]{4,3,2,1,0:T(8,128)(2,1)S(1)} %slice.24), channel_id=1, source_target_pairs={{0,4},{1,5},{2,6},{3,7},{4,0},{5,1},{6,2},{7,3},{8,12},{9,13},{10,... | collective-permute-start | bytes 393224 | tf_op jit(solution)/shard_map/ppermute | solution.py:273
  17.6 17.5 %collective-permute-start.8 = (bf16[2,1,2,32,1024]{4,3,2,1,0:T(8,128)(2,1)S(1)}, bf16[2,1,2,32,1024]{4,3,2,1,0:T(8,128)(2,1)S(1)}, u32[]{:S(2)}, u32[]{:S(2)}) collective-permute-start(bf16[2,1,2,32,1024]{4,3,2,1,0:T(8,128)(2,1)S(1)} %collective-permute-done.6.refs_5_), channel_id=1, source_target_pairs={{0,4},{1,5},{2,6},{3,7},{4,0},{5,1},{6,2},{7,3},{8,12},{9,13},{10,... | collective-permute-start | bytes 786440 | tf_op jit(solution)/shard_map/ppermute | solution.py:273
  18.8 18.2 %collective-permute-start.7 = (bf16[2,1,2,32,1024]{4,3,2,1,0:T(8,128)(2,1)S(1)}, bf16[2,1,2,32,1024]{4,3,2,1,0:T(8,128)(2,1)}, u32[]{:S(2)}, u32[]{:S(2)}) collective-permute-start(bf16[2,1,2,32,1024]{4,3,2,1,0:T(8,128)(2,1)S(1)} %collective-permute-done.6.refs_5_), channel_id=1, source_target_pairs={{0,2},{1,3},{2,0},{3,1},{4,6},{5,7},{6,4},{7,5},{8,10},{9,11},{10,... | collective-permute-start | bytes 786440 | tf_op jit(solution)/shard_map/ppermute | solution.py:273
  32.1 29.2 %all-to-all-start = ((bf16[32,8,1024]{2,1,0:T(8,128)(2,1)}), bf16[32,8,1024]{2,1,0:T(8,128)(2,1)S(1)}, u32[]{:S(2)}, u32[]{:S(2)}) async-start(bf16[32,8,1024]{2,1,0:T(8,128)(2,1)} %bitcast), calls=%async_computation | async-start | bytes 1048576 | tf_op jit(solution)/shard_map/all_to_all | solution.py:318
  35.2 9.8 %collective-permute-start.10 = (bf16[1,1,2,32,1024]{4,3,2,1,0:T(8,128)(2,1)S(1)}, bf16[1,1,2,32,1024]{4,3,2,1,0:T(8,128)(2,1)S(1)}, u32[]{:S(2)}, u32[]{:S(2)}) collective-permute-start(bf16[1,1,2,32,1024]{4,3,2,1,0:T(8,128)(2,1)S(1)} %slice.27), channel_id=1, source_target_pairs={{0,2},{1,3},{2,0},{3,1},{4,6},{5,7},{6,4},{7,5},{8,10},{9,11},{10,... | collective-permute-start | bytes 393224 | tf_op jit(solution)/shard_map/ppermute | solution.py:273
  37.9 7.7 %collective-permute-start.9 = (bf16[1,1,2,32,1024]{4,3,2,1,0:T(8,128)(2,1)S(1)}, bf16[1,1,2,32,1024]{4,3,2,1,0:T(8,128)(2,1)}, u32[]{:S(2)}, u32[]{:S(2)}) collective-permute-start(bf16[1,1,2,32,1024]{4,3,2,1,0:T(8,128)(2,1)S(1)} %slice.26), channel_id=1, source_target_pairs={{0,4},{1,5},{2,6},{3,7},{4,0},{5,1},{6,2},{7,3},{8,12},{9,13},{10,... | collective-permute-start | bytes 393224 | tf_op jit(solution)/shard_map/ppermute | solution.py:273
  39.5 7.9 %collective-permute-start.15 = (bf16[2,1,2,32,1024]{4,3,2,1,0:T(8,128)(2,1)S(1)}, bf16[2,1,2,32,1024]{4,3,2,1,0:T(8,128)(2,1)S(1)}, u32[]{:S(2)}, u32[]{:S(2)}) collective-permute-start(bf16[2,1,2,32,1024]{4,3,2,1,0:T(8,128)(2,1)S(1)} %maximum_bitcast_fusion.refs_0_), channel_id=1, source_target_pairs={{0,1},{1,0},{2,3},{3,2},{4,5},{5,4},{6,7},{7,6},{8,9},{9,8},{10,11... | collective-permute-start | bytes 786440 | tf_op jit(solution)/shard_map/ppermute | solution.py:273
  39.5 9.5 %collective-permute-start.17 = (bf16[2,1,2,32,1024]{4,3,2,1,0:T(8,128)(2,1)S(1)}, bf16[2,1,2,32,1024]{4,3,2,1,0:T(8,128)(2,1)S(1)}, u32[]{:S(2)}, u32[]{:S(2)}) collective-permute-start(bf16[2,1,2,32,1024]{4,3,2,1,0:T(8,128)(2,1)S(1)} %collective-permute-done.3.refs_2_), channel_id=1, source_target_pairs={{0,1},{1,0},{2,3},{3,2},{4,5},{5,4},{6,7},{7,6},{8,9},{9,8},{10,11... | collective-permute-start | bytes 786440 | tf_op jit(solution)/shard_map/ppermute | solution.py:273
  45.6 14.3 %collective-permute-start.12 = (bf16[2,2,2,32,1024]{4,3,2,1,0:T(8,128)(2,1)S(1)}, bf16[2,2,2,32,1024]{4,3,2,1,0:T(8,128)(2,1)S(1)}, u32[]{:S(2)}, u32[]{:S(2)}) collective-permute-start(bf16[2,2,2,32,1024]{4,3,2,1,0:T(8,128)(2,1)S(1)} %pad_maximum_fusion.refs_10_), channel_id=1, source_target_pairs={{0,4},{1,5},{2,6},{3,7},{4,0},{5,1},{6,2},{7,3},{8,12},{9,13},{10,... | collective-permute-start | bytes 1572872 | tf_op jit(solution)/shard_map/ppermute | solution.py:273
  46.8 13.4 %collective-permute-start.11 = (bf16[2,2,2,32,1024]{4,3,2,1,0:T(8,128)(2,1)S(1)}, bf16[2,2,2,32,1024]{4,3,2,1,0:T(8,128)(2,1)S(1)}, u32[]{:S(2)}, u32[]{:S(2)}) collective-permute-start(bf16[2,2,2,32,1024]{4,3,2,1,0:T(8,128)(2,1)S(1)} %pad_maximum_fusion.refs_10_), channel_id=1, source_target_pairs={{0,2},{1,3},{2,0},{3,1},{4,6},{5,7},{6,4},{7,5},{8,10},{9,11},{10,... | collective-permute-start | bytes 1572872 | tf_op jit(solution)/shard_map/ppermute | solution.py:273
  47.4 3.4 %collective-permute-start.16 = (bf16[2,1,2,32,1024]{4,3,2,1,0:T(8,128)(2,1)S(1)}, bf16[2,1,2,32,1024]{4,3,2,1,0:T(8,128)(2,1)S(1)}, u32[]{:S(2)}, u32[]{:S(2)}) collective-permute-start(bf16[2,1,2,32,1024]{4,3,2,1,0:T(8,128)(2,1)S(1)} %collective-permute-done.2.refs_1_), channel_id=1, source_target_pairs={{0,1},{1,0},{2,3},{3,2},{4,5},{5,4},{6,7},{7,6},{8,9},{9,8},{10,11... | collective-permute-start | bytes 786440 | tf_op jit(solution)/shard_map/ppermute | solution.py:273
  48.9 2.2 %collective-permute-start.20 = (bf16[2,1,2,32,1024]{4,3,2,1,0:T(8,128)(2,1)S(1)}, bf16[2,1,2,32,1024]{4,3,2,1,0:T(8,128)(2,1)S(1)}, u32[]{:S(2)}, u32[]{:S(2)}) collective-permute-start(bf16[2,1,2,32,1024]{4,3,2,1,0:T(8,128)(2,1)S(1)} %copy-done.15), channel_id=1, source_target_pairs={{0,1},{1,0},{2,3},{3,2},{4,5},{5,4},{6,7},{7,6},{8,9},{9,8},{10,11... | collective-permute-start | bytes 786440 | tf_op jit(solution)/shard_map/ppermute | solution.py:273
  49.0 1.6 %collective-permute-start.18 = (bf16[1,1,2,32,1024]{4,3,2,1,0:T(8,128)(2,1)S(1)}, bf16[1,1,2,32,1024]{4,3,2,1,0:T(8,128)(2,1)S(1)}, u32[]{:S(2)}, u32[]{:S(2)}) collective-permute-start(bf16[1,1,2,32,1024]{4,3,2,1,0:T(8,128)(2,1)S(1)} %copy-done.27), channel_id=1, source_target_pairs={{0,1},{1,0},{2,3},{3,2},{4,5},{5,4},{6,7},{7,6},{8,9},{9,8},{10,11... | collective-permute-start | bytes 393224 | tf_op jit(solution)/shard_map/ppermute | solution.py:273
  50.6 10.1 %collective-permute-start.22 = (bf16[2,1,2,32,1024]{4,3,2,1,0:T(8,128)(2,1)S(1)}, bf16[2,1,2,32,1024]{4,3,2,1,0:T(8,128)(2,1)S(1)}, u32[]{:S(2)}, u32[]{:S(2)}) collective-permute-start(bf16[2,1,2,32,1024]{4,3,2,1,0:T(8,128)(2,1)S(1)} %copy-done.12), channel_id=1, source_target_pairs={{0,1},{1,0},{2,3},{3,2},{4,5},{5,4},{6,7},{7,6},{8,9},{9,8},{10,11... | collective-permute-start | bytes 786440 | tf_op jit(solution)/shard_map/ppermute | solution.py:273
  50.8 9.6 %collective-permute-start.24 = (bf16[1,1,2,32,1024]{4,3,2,1,0:T(8,128)(2,1)S(1)}, bf16[1,1,2,32,1024]{4,3,2,1,0:T(8,128)(2,1)S(1)}, u32[]{:S(2)}, u32[]{:S(2)}) collective-permute-start(bf16[1,1,2,32,1024]{4,3,2,1,0:T(8,128)(2,1)S(1)} %collective-permute-done.10.refs_9_), channel_id=1, source_target_pairs={{0,1},{1,0},{2,3},{3,2},{4,5},{5,4},{6,7},{7,6},{8,9},{9,8},{10,11... | collective-permute-start | bytes 393224 | tf_op jit(solution)/shard_map/ppermute | solution.py:273
  51.1 19.6 %collective-permute-start.25 = (bf16[2,2,2,32,1024]{4,3,2,1,0:T(8,128)(2,1)S(1)}, bf16[2,2,2,32,1024]{4,3,2,1,0:T(8,128)(2,1)S(1)}, u32[]{:S(2)}, u32[]{:S(2)}) collective-permute-start(bf16[2,2,2,32,1024]{4,3,2,1,0:T(8,128)(2,1)S(1)} %pad_maximum_fusion.refs_10_), channel_id=1, source_target_pairs={{0,1},{1,0},{2,3},{3,2},{4,5},{5,4},{6,7},{7,6},{8,9},{9,8},{10,11... | collective-permute-start | bytes 1572872 | tf_op jit(solution)/shard_map/ppermute | solution.py:273
  59.9 21.0 %collective-permute-start.27 = (bf16[2,2,2,32,1024]{4,3,2,1,0:T(8,128)(2,1)S(1)}, bf16[2,2,2,32,1024]{4,3,2,1,0:T(8,128)(2,1)}, u32[]{:S(2)}, u32[]{:S(2)}) collective-permute-start(bf16[2,2,2,32,1024]{4,3,2,1,0:T(8,128)(2,1)S(1)} %collective-permute-done.12.refs_12_), channel_id=1, source_target_pairs={{0,1},{1,0},{2,3},{3,2},{4,5},{5,4},{6,7},{7,6},{8,9},{9,8},{10,11... | collective-permute-start | bytes 1572872 | tf_op jit(solution)/shard_map/ppermute | solution.py:273
  60.2 20.8 %collective-permute-start.26 = (bf16[2,2,2,32,1024]{4,3,2,1,0:T(8,128)(2,1)S(1)}, bf16[2,2,2,32,1024]{4,3,2,1,0:T(8,128)(2,1)}, u32[]{:S(2)}, u32[]{:S(2)}) collective-permute-start(bf16[2,2,2,32,1024]{4,3,2,1,0:T(8,128)(2,1)S(1)} %collective-permute-done.11.refs_11_), channel_id=1, source_target_pairs={{0,1},{1,0},{2,3},{3,2},{4,5},{5,4},{6,7},{7,6},{8,9},{9,8},{10,11... | collective-permute-start | bytes 1572872 | tf_op jit(solution)/shard_map/ppermute | solution.py:273
  60.4 8.8 %collective-permute-start.21 = (bf16[2,1,2,32,1024]{4,3,2,1,0:T(8,128)(2,1)}, bf16[2,1,2,32,1024]{4,3,2,1,0:T(8,128)(2,1)}, u32[]{:S(2)}, u32[]{:S(2)}) collective-permute-start(bf16[2,1,2,32,1024]{4,3,2,1,0:T(8,128)(2,1)} %collective-permute-done.7.refs_6_), channel_id=1, source_target_pairs={{0,1},{1,0},{2,3},{3,2},{4,5},{5,4},{6,7},{7,6},{8,9},{9,8},{10,11... | collective-permute-start | bytes 786440 | tf_op jit(solution)/shard_map/ppermute | solution.py:273
  61.1 6.2 %collective-permute-start.23 = (bf16[1,1,2,32,1024]{4,3,2,1,0:T(8,128)(2,1)}, bf16[1,1,2,32,1024]{4,3,2,1,0:T(8,128)(2,1)}, u32[]{:S(2)}, u32[]{:S(2)}) collective-permute-start(bf16[1,1,2,32,1024]{4,3,2,1,0:T(8,128)(2,1)} %collective-permute-done.9.refs_8_), channel_id=1, source_target_pairs={{0,1},{1,0},{2,3},{3,2},{4,5},{5,4},{6,7},{7,6},{8,9},{9,8},{10,11... | collective-permute-start | bytes 393224 | tf_op jit(solution)/shard_map/ppermute | solution.py:273
  62.1 33.2 %all-to-all-start.2 = ((bf16[32,8,1024]{2,1,0:T(8,128)(2,1)}), bf16[32,8,1024]{2,1,0:T(8,128)(2,1)S(1)}, u32[]{:S(2)}, u32[]{:S(2)}) async-start(bf16[32,8,1024]{2,1,0:T(8,128)(2,1)} %bitcast.5), calls=%async_computation.2 | async-start | bytes 1048576 | tf_op jit(solution)/shard_map/all_to_all | solution.py:318
  67.3 13.6 %collective-permute-start.14 = (bf16[1,2,2,32,1024]{4,3,2,1,0:T(8,128)(2,1)S(1)}, bf16[1,2,2,32,1024]{4,3,2,1,0:T(8,128)(2,1)S(1)}, u32[]{:S(2)}, u32[]{:S(2)}) collective-permute-start(bf16[1,2,2,32,1024]{4,3,2,1,0:T(8,128)(2,1)S(1)} %slice.29), channel_id=1, source_target_pairs={{0,2},{1,3},{2,0},{3,1},{4,6},{5,7},{6,4},{7,5},{8,10},{9,11},{10,... | collective-permute-start | bytes 786440 | tf_op jit(solution)/shard_map/ppermute | solution.py:273
  69.2 12.0 %collective-permute-start.13 = (bf16[1,2,2,32,1024]{4,3,2,1,0:T(8,128)(2,1)S(1)}, bf16[1,2,2,32,1024]{4,3,2,1,0:T(8,128)(2,1)S(1)}, u32[]{:S(2)}, u32[]{:S(2)}) collective-permute-start(bf16[1,2,2,32,1024]{4,3,2,1,0:T(8,128)(2,1)S(1)} %slice.28), channel_id=1, source_target_pairs={{0,4},{1,5},{2,6},{3,7},{4,0},{5,1},{6,2},{7,3},{8,12},{9,13},{10,... | collective-permute-start | bytes 786440 | tf_op jit(solution)/shard_map/ppermute | solution.py:273
  81.2 1.5 %collective-permute-start.28 = (bf16[1,2,2,32,1024]{4,3,2,1,0:T(8,128)(2,1)S(1)}, bf16[1,2,2,32,1024]{4,3,2,1,0:T(8,128)(2,1)S(1)}, u32[]{:S(2)}, u32[]{:S(2)}) collective-permute-start(bf16[1,2,2,32,1024]{4,3,2,1,0:T(8,128)(2,1)S(1)} %collective-permute-done.13.refs_13_), channel_id=1, source_target_pairs={{0,1},{1,0},{2,3},{3,2},{4,5},{5,4},{6,7},{7,6},{8,9},{9,8},{10,11... | collective-permute-start | bytes 786440 | tf_op jit(solution)/shard_map/ppermute | solution.py:273
  81.2 1.9 %collective-permute-start.29 = (bf16[1,2,2,32,1024]{4,3,2,1,0:T(8,128)(2,1)S(1)}, bf16[1,2,2,32,1024]{4,3,2,1,0:T(8,128)(2,1)S(1)}, u32[]{:S(2)}, u32[]{:S(2)}) collective-permute-start(bf16[1,2,2,32,1024]{4,3,2,1,0:T(8,128)(2,1)S(1)} %collective-permute-done.14.refs_14_), channel_id=1, source_target_pairs={{0,1},{1,0},{2,3},{3,2},{4,5},{5,4},{6,7},{7,6},{8,9},{9,8},{10,11... | collective-permute-start | bytes 786440 | tf_op jit(solution)/shard_map/ppermute | solution.py:273
  96.2 14.6 %all-to-all-start.1 = ((bf16[16,128,128]{2,1,0:T(8,128)(2,1)}), bf16[16,128,128]{2,1,0:T(8,128)(2,1)S(1)}, u32[]{:S(2)}, u32[]{:S(2)}) async-start(bf16[16,128,128]{2,1,0:T(8,128)(2,1)} %bitcast.18), calls=%async_computation.1 | async-start | bytes 1048576 | tf_op jit(solution)/shard_map/all_to_all | solution.py:318
  (32 other events, 381.9 us)

commit v10 on v8

--- a/solution.py
+++ b/solution.py
@@ -292,25 +292,29 @@
 def spread(gate_a, gate_b, packed):
     bits = lax.axis_size("mode").bit_length() - 1
     own = jnp.stack([gate_a, gate_b])[:, None]
-    blocks = plane(own, ((),))
     far = [()]
     for bit in range(3, bits):
         far += [source + (bit,) for source in far]
-    far = tuple(far[1:])
-    value = jnp.concatenate([flip(own, *source) for source in far], axis=1)
-    states = trade(packed)
-    value, *_ = lax.optimization_barrier((value, packed, blocks[-2][0], blocks[-1][0]))
-    blocks += plane(value, far)
+    came = [flip(own, *source) for source in far[1:]]
+    sets = [(own, ((),)), (came[0], tuple(far[1:2]))]
+    if came[1:]:
+        sets.append((jnp.concatenate(came[1:], axis=1), tuple(far[2:])))
+    blocks = []
+    for number, (value, sources) in enumerate(sets):
+        if number:
+            tied = (blocks[3][0], blocks[4][0]) if number == 1 else (packed, blocks[6][0], blocks[7][0])
+            value, *_ = lax.optimization_barrier((value, *tied))
+        blocks += plane(value, sources)
+    packed, *_ = lax.optimization_barrier((packed, *came[1:], blocks[8][0], blocks[9][0]))
+    last = len(blocks) - 2
     near = []
     for number, (value, sources, gates) in enumerate(blocks):
-        if number >= len(blocks) - 2:
-            value, states, *_ = lax.optimization_barrier(
-                (value, states, *[earlier for earlier, _, _ in near[: len(blocks) - 2]])
-            )
+        if number >= last:
+            value, *_ = lax.optimization_barrier((value, *[earlier for earlier, _, _ in near[:last]]))
         near.append((flip(value, 0), tuple(source + (0,) for source in sources), gates))
     blocks += near
     plan = tuple((sources, gates) for _, sources, gates in blocks)
-    return [value for value, _, _ in blocks], plan, states
+    return [value for value, _, _ in blocks], plan, trade(packed)
 
 
 def trade(value, groups=None):

time: 146 us -> 134 us (0.918)
  waiting for transfers between devices: 69.7 us -> 51.6 us
  starting transfers between devices: 27.8 us -> 33.4 us
  local copies, waits for them, and re-layouts: 6.65 us -> 4.28 us
  blocking collectives: 14.6 us -> 16.4 us
    ppermute x21 -> x30, waiting for transfers between devices: 69.7 us -> 51.6 us  [flip(): return lax.ppermute(value, 'mode', pairs)]
    ppermute x21 -> x30, starting transfers between devices: 16.8 us -> 25.6 us  [flip(): return lax.ppermute(value, 'mode', pairs)]
    all_to_all x2, starting transfers between devices: 11.1 us -> 7.78 us  [trade(): lax.all_to_all(value, 'mode', split_axis=0, concat_axis=0, axis_index_gro...]
    unnamed x50 -> x74, local copies, waits for them, and re-layouts: 5.97 us -> 3.59 us
    all_to_all x1, blocking collectives: 14.6 us -> 16.4 us  [trade(): lax.all_to_all(value, 'mode', split_axis=0, concat_axis=0, axis_index_gro...]
  transfers between devices with their start and end apart: 23 -> 32, of which waited for: 11 -> 14; matrix products, arithmetic and copies ran while one was open for 0% -> 0% of each run, Pallas kernels for 8% -> 10%
where the time goes in v10:
time: 134 us; the launch traced here: 133 us
  waiting for transfers between devices  51.6 us (39%)
  starting transfers between devices  33.4 us (25%)
  Pallas kernels  26.1 us (19%)
  blocking collectives  16.4 us (12%)
  local copies, waits for them, and re-layouts  4.28 us (3%)
    ppermute x30, waiting for transfers between devices, flip(): return lax.ppermute(value, 'mode', pairs)  51.6 us
    pallas_call x4, Pallas kernels, call(): pl.pallas_call(kernel, out_shape=jax.ShapeDtypeStruct(out_shape, jnp.bflo...  26.1 us
    ppermute x30, starting transfers between devices, flip(): return lax.ppermute(value, 'mode', pairs)  25.6 us
    all_to_all x1, blocking collectives, trade(): lax.all_to_all(value, 'mode', split_axis=0, concat_axis=0, axis_index_gro...  16.4 us
    all_to_all x2, starting transfers between devices, trade(): lax.all_to_all(value, 'mode', split_axis=0, concat_axis=0, axis_index_gro...  7.78 us
    unnamed x74, local copies, waits for them, and re-layouts  3.59 us
  transfers between devices with their start and end apart: 32, of which 14 were waited for; matrix products, arithmetic and copies ran while one was open for 0% of the time, Pallas kernels for 10%

profile of v10, /device:TPU:0, one launch (start us, length us, event | category | flops | bytes accessed | tf_op | source)
XLA Modules:
  0.0 133.3 jit_solution(6370568156588638313)
XLA Ops:
  0.0 1.1 maximum_bitcast_fusion.refs_0_
  1.1 3.0 %collective-permute-start.5 = (bf16[2,1,2,32,1024]{4,3,2,1,0:T(8,128)(2,1)S(1)}, bf16[2,1,2,32,1024]{4,3,2,1,0:T(8,128)(2,1)S(1)}, u32[]{:S(2)}, u32[]{:S(2)}) collective-permute-start(bf16[2,1,2,32,1024]{4,3,2,1,0:T(8,128)(2,1)S(1)} %maximum_bitcast_fusion.refs_0_), channel_id=1, source_target_pairs={{0,4},{1,5},{2,6},{3,7},{4,0},{5,1},{6,2},{7,3},{8,12},{9,13},{10,... | collective-permute-start | bytes 786440 | tf_op jit(solution)/shard_map/ppermute | solution.py:276
  4.1 1.5 %collective-permute-start.3 = (bf16[2,1,2,32,1024]{4,3,2,1,0:T(8,128)(2,1)S(1)}, bf16[2,1,2,32,1024]{4,3,2,1,0:T(8,128)(2,1)S(1)}, u32[]{:S(2)}, u32[]{:S(2)}) collective-permute-start(bf16[2,1,2,32,1024]{4,3,2,1,0:T(8,128)(2,1)S(1)} %maximum_bitcast_fusion.refs_0_), channel_id=1, source_target_pairs={{0,2},{1,3},{2,0},{3,1},{4,6},{5,7},{6,4},{7,5},{8,10},{9,11},{10,... | collective-permute-start | bytes 786440 | tf_op jit(solution)/shard_map/ppermute | solution.py:276
  5.6 1.6 %collective-permute-start.2 = (bf16[2,1,2,32,1024]{4,3,2,1,0:T(8,128)(2,1)S(1)}, bf16[2,1,2,32,1024]{4,3,2,1,0:T(8,128)(2,1)S(1)}, u32[]{:S(2)}, u32[]{:S(2)}) collective-permute-start(bf16[2,1,2,32,1024]{4,3,2,1,0:T(8,128)(2,1)S(1)} %maximum_bitcast_fusion.refs_0_), channel_id=1, source_target_pairs={{0,8},{1,9},{2,10},{3,11},{4,12},{5,13},{6,14},{7,15},{8,0},{9,1},... | collective-permute-start | bytes 786440 | tf_op jit(solution)/shard_map/ppermute | solution.py:276
  7.2 3.2 %collective-permute-done.5.refs_2_ = bf16[2,1,2,32,1024]{4,3,2,1,0:T(8,128)(2,1)S(1)} collective-permute-done((bf16[2,1,2,32,1024]{4,3,2,1,0:T(8,128)(2,1)S(1)}, bf16[2,1,2,32,1024]{4,3,2,1,0:T(8,128)(2,1)S(1)}, u32[]{:S(2)}, u32[]{:S(2)}) %collective-permute-start.5) | collective-permute-done | bytes 262176 | tf_op jit(solution)/shard_map/ppermute | solution.py:276
  10.5 1.8 %collective-permute-start.6 = (bf16[1,1,2,32,1024]{4,3,2,1,0:T(8,128)(2,1)S(1)}, bf16[1,1,2,32,1024]{4,3,2,1,0:T(8,128)(2,1)S(1)}, u32[]{:S(2)}, u32[]{:S(2)}) collective-permute-start(bf16[1,1,2,32,1024]{4,3,2,1,0:T(8,128)(2,1)S(1)} %slice.25), channel_id=1, source_target_pairs={{0,2},{1,3},{2,0},{3,1},{4,6},{5,7},{6,4},{7,5},{8,10},{9,11},{10,... | collective-permute-start | bytes 393224 | tf_op jit(solution)/shard_map/ppermute | solution.py:276
  12.2 1.6 %collective-permute-start.4 = (bf16[1,1,2,32,1024]{4,3,2,1,0:T(8,128)(2,1)S(1)}, bf16[1,1,2,32,1024]{4,3,2,1,0:T(8,128)(2,1)S(1)}, u32[]{:S(2)}, u32[]{:S(2)}) collective-permute-start(bf16[1,1,2,32,1024]{4,3,2,1,0:T(8,128)(2,1)S(1)} %slice.24), channel_id=1, source_target_pairs={{0,4},{1,5},{2,6},{3,7},{4,0},{5,1},{6,2},{7,3},{8,12},{9,13},{10,... | collective-permute-start | bytes 393224 | tf_op jit(solution)/shard_map/ppermute | solution.py:276
  13.8 1.6 %collective-permute-done.6.refs_4_ = bf16[1,1,2,32,1024]{4,3,2,1,0:T(8,128)(2,1)S(1)} collective-permute-done((bf16[1,1,2,32,1024]{4,3,2,1,0:T(8,128)(2,1)S(1)}, bf16[1,1,2,32,1024]{4,3,2,1,0:T(8,128)(2,1)S(1)}, u32[]{:S(2)}, u32[]{:S(2)}) %collective-permute-start.6) | collective-permute-done | bytes 131104 | tf_op jit(solution)/shard_map/ppermute | solution.py:276
  15.5 1.8 %collective-permute-done.4.refs_3_ = bf16[1,1,2,32,1024]{4,3,2,1,0:T(8,128)(2,1)S(1)} collective-permute-done((bf16[1,1,2,32,1024]{4,3,2,1,0:T(8,128)(2,1)S(1)}, bf16[1,1,2,32,1024]{4,3,2,1,0:T(8,128)(2,1)S(1)}, u32[]{:S(2)}, u32[]{:S(2)}) %collective-permute-start.4) | collective-permute-done | bytes 131104 | tf_op jit(solution)/shard_map/ppermute | solution.py:276
  17.3 1.5 %collective-permute-start.9 = (bf16[2,1,2,32,1024]{4,3,2,1,0:T(8,128)(2,1)S(1)}, bf16[2,1,2,32,1024]{4,3,2,1,0:T(8,128)(2,1)S(1)}, u32[]{:S(2)}, u32[]{:S(2)}) collective-permute-start(bf16[2,1,2,32,1024]{4,3,2,1,0:T(8,128)(2,1)S(1)} %collective-permute-done.2.refs_5_), channel_id=1, source_target_pairs={{0,4},{1,5},{2,6},{3,7},{4,0},{5,1},{6,2},{7,3},{8,12},{9,13},{10,... | collective-permute-start | bytes 786440 | tf_op jit(solution)/shard_map/ppermute | solution.py:276
  19.3 3.6 %collective-permute-start.1 = (bf16[2,1,2,32,1024]{4,3,2,1,0:T(8,128)(2,1)S(1)}, bf16[2,1,2,32,1024]{4,3,2,1,0:T(8,128)(2,1)S(1)}, u32[]{:S(2)}, u32[]{:S(2)}) collective-permute-start(bf16[2,1,2,32,1024]{4,3,2,1,0:T(8,128)(2,1)S(1)} %maximum_bitcast_fusion.refs_0_), channel_id=1, source_target_pairs={{0,24},{1,25},{2,26},{3,27},{4,28},{5,29},{6,30},{7,31},{8,16},{9,... | collective-permute-start | bytes 786440 | tf_op jit(solution)/shard_map/ppermute | solution.py:276
  22.9 0.7 collective-permute-done.9.refs_7_
  23.7 1.2 collective-permute-start.10
  24.9 1.7 %collective-permute-done.7.refs_6_ = bf16[2,1,2,32,1024]{4,3,2,1,0:T(8,128)(2,1)S(1)} collective-permute-done((bf16[2,1,2,32,1024]{4,3,2,1,0:T(8,128)(2,1)S(1)}, bf16[2,1,2,32,1024]{4,3,2,1,0:T(8,128)(2,1)S(1)}, u32[]{:S(2)}, u32[]{:S(2)}) %collective-permute-start.7) | collective-permute-done | bytes 262176 | tf_op jit(solution)/shard_map/ppermute | solution.py:276
  26.8 2.8 %shard_map.46 = bf16[512,1024]{1,0:T(8,128)(2,1)} custom-call(bf16[4,2,64,1024]{3,2,1,0:T(8,128)(2,1)S(1)} %copy-done.1, s32[4,1024]{1,0:T(4,128)S(1)} %copy-done.2), custom_call_target="tpu_custom_call" | custom-call | flops 2147483648 | bytes 1064960 | tf_op jit(solution)/shard_map/pallas_call | solution.py:193
  29.6 12.8 %collective-permute-done = bf16[2,1,2,32,1024]{4,3,2,1,0:T(8,128)(2,1)S(1)} collective-permute-done((bf16[2,1,2,32,1024]{4,3,2,1,0:T(8,128)(2,1)S(1)}, bf16[2,1,2,32,1024]{4,3,2,1,0:T(8,128)(2,1)S(1)}, u32[]{:S(2)}, u32[]{:S(2)}) %collective-permute-start) | collective-permute-done | bytes 262176 | tf_op jit(solution)/shard_map/ppermute | solution.py:276
  43.1 4.0 %all-to-all-start = ((bf16[32,16,1024]{2,1,0:T(8,128)(2,1)}), bf16[32,16,1024]{2,1,0:T(8,128)(2,1)S(1)}, u32[]{:S(2)}, u32[]{:S(2)}) async-start(bf16[32,16,1024]{2,1,0:T(8,128)(2,1)} %bitcast), calls=%async_computation | async-start | bytes 2097152 | tf_op jit(solution)/shard_map/all_to_all | solution.py:321
  47.9 1.8 %collective-permute-start.12 = (bf16[2,2,2,32,1024]{4,3,2,1,0:T(8,128)(2,1)S(1)}, bf16[2,2,2,32,1024]{4,3,2,1,0:T(8,128)(2,1)S(1)}, u32[]{:S(2)}, u32[]{:S(2)}) collective-permute-start(bf16[2,2,2,32,1024]{4,3,2,1,0:T(8,128)(2,1)S(1)} %pad_maximum_fusion.refs_10_), channel_id=1, source_target_pairs={{0,4},{1,5},{2,6},{3,7},{4,0},{5,1},{6,2},{7,3},{8,12},{9,13},{10,... | collective-permute-start | bytes 1572872 | tf_op jit(solution)/shard_map/ppermute | solution.py:276
  49.7 1.5 %collective-permute-start.11 = (bf16[2,2,2,32,1024]{4,3,2,1,0:T(8,128)(2,1)S(1)}, bf16[2,2,2,32,1024]{4,3,2,1,0:T(8,128)(2,1)S(1)}, u32[]{:S(2)}, u32[]{:S(2)}) collective-permute-start(bf16[2,2,2,32,1024]{4,3,2,1,0:T(8,128)(2,1)S(1)} %pad_maximum_fusion.refs_10_), channel_id=1, source_target_pairs={{0,2},{1,3},{2,0},{3,1},{4,6},{5,7},{6,4},{7,5},{8,10},{9,11},{10,... | collective-permute-start | bytes 1572872 | tf_op jit(solution)/shard_map/ppermute | solution.py:276
  51.7 0.9 collective-permute-done.19.refs_19_
  53.2 1.1 collective-permute-done.18.refs_18_
  55.2 17.2 %collective-permute-done.12.refs_12_ = bf16[2,2,2,32,1024]{4,3,2,1,0:T(8,128)(2,1)S(1)} collective-permute-done((bf16[2,2,2,32,1024]{4,3,2,1,0:T(8,128)(2,1)S(1)}, bf16[2,2,2,32,1024]{4,3,2,1,0:T(8,128)(2,1)S(1)}, u32[]{:S(2)}, u32[]{:S(2)}) %collective-permute-start.12) | collective-permute-done | bytes 524320 | tf_op jit(solution)/shard_map/ppermute | solution.py:276
  74.1 1.4 %collective-permute-done.23.refs_23_ = bf16[1,1,2,32,1024]{4,3,2,1,0:T(8,128)(2,1)S(1)} collective-permute-done((bf16[1,1,2,32,1024]{4,3,2,1,0:T(8,128)(2,1)S(1)}, bf16[1,1,2,32,1024]{4,3,2,1,0:T(8,128)(2,1)S(1)}, u32[]{:S(2)}, u32[]{:S(2)}) %collective-permute-start.23) | collective-permute-done | bytes 131104 | tf_op jit(solution)/shard_map/ppermute | solution.py:276
  75.5 1.3 collective-permute-start.14
  77.3 6.6 %collective-permute-done.14.refs_14_ = bf16[1,2,2,32,1024]{4,3,2,1,0:T(8,128)(2,1)S(1)} collective-permute-done((bf16[1,2,2,32,1024]{4,3,2,1,0:T(8,128)(2,1)S(1)}, bf16[1,2,2,32,1024]{4,3,2,1,0:T(8,128)(2,1)S(1)}, u32[]{:S(2)}, u32[]{:S(2)}) %collective-permute-start.14) | collective-permute-done | bytes 262176 | tf_op jit(solution)/shard_map/ppermute | solution.py:276
  83.9 1.1 collective-permute-done.13.refs_13_
  85.6 1.0 collective-permute-done.28.refs_28_
  88.1 11.7 %shard_map.47 = bf16[2048,128]{1,0:T(8,128)(2,1)} custom-call(bf16[512,1024]{1,0:T(8,128)(2,1)} %bitcast.14, bf16[2,1,2,32,1024]{4,3,2,1,0:T(8,128)(2,1)} %copy-done.5, bf16[2,1,2,32,1024]{4,3,2,1,0:T(8,128)(2,1)} %copy-done.9, bf16[2,1,2,32,1024]{4,3,2,1,0:T(8,128)(2,1)} %copy-done.8, bf16[1,1,2,32,1024]{4,3,2,1,0:T(8,128)(2,1)} %copy-done.28, ...), custom_call_target="tpu_custom_call" | custom-call | flops 4294967296 | bytes 9437184 | tf_op jit(solution)/shard_map/pallas_call | solution.py:193
  99.8 3.8 %all-to-all-start.1 = ((bf16[16,128,128]{2,1,0:T(8,128)(2,1)}), bf16[16,128,128]{2,1,0:T(8,128)(2,1)S(1)}, u32[]{:S(2)}, u32[]{:S(2)}) async-start(bf16[16,128,128]{2,1,0:T(8,128)(2,1)} %bitcast.16), calls=%async_computation.1 | async-start | bytes 1048576 | tf_op jit(solution)/shard_map/all_to_all | solution.py:321
  103.6 11.0 %shard_map.48.right_ref = bf16[256,1024]{1,0:T(8,128)(2,1)} custom-call(bf16[512,1024]{1,0:T(8,128)(2,1)} %bitcast.15, bf16[2,1,2,32,1024]{4,3,2,1,0:T(8,128)(2,1)} %copy-done.5, bf16[2,1,2,32,1024]{4,3,2,1,0:T(8,128)(2,1)} %copy-done.9, bf16[2,1,2,32,1024]{4,3,2,1,0:T(8,128)(2,1)} %copy-done.8, bf16[1,1,2,32,1024]{4,3,2,1,0:T(8,128)(2,1)} %copy-done.28, ...), custom_call_target="tpu_custom_call" | custom-call | flops 4294967296 | bytes 9437184 | tf_op jit(solution)/shard_map/pallas_call | solution.py:193
  114.6 1.0 copy-done
  116.2 16.4 %all_to_all.15 = bf16[32,16,256]{2,1,0:T(8,128)(2,1)S(1)} all-to-all(bf16[32,16,256]{2,1,0:T(8,128)(2,1)S(1)} %bitcast.13), channel_id=1, replica_groups=mesh['cuts'=1,'mode'=32] {'mode'}, dimensions={0} | all-to-all | bytes 524288 | tf_op jit(solution)/shard_map/all_to_all | solution.py:321
  (122 shorter events, 9.5 us)
Async XLA Ops:
  1.1 9.3 %collective-permute-start.5 = (bf16[2,1,2,32,1024]{4,3,2,1,0:T(8,128)(2,1)S(1)}, bf16[2,1,2,32,1024]{4,3,2,1,0:T(8,128)(2,1)S(1)}, u32[]{:S(2)}, u32[]{:S(2)}) collective-permute-start(bf16[2,1,2,32,1024]{4,3,2,1,0:T(8,128)(2,1)S(1)} %maximum_bitcast_fusion.refs_0_), channel_id=1, source_target_pairs={{0,4},{1,5},{2,6},{3,7},{4,0},{5,1},{6,2},{7,3},{8,12},{9,13},{10,... | collective-permute-start | bytes 786440 | tf_op jit(solution)/shard_map/ppermute | solution.py:276
  4.1 8.1 %collective-permute-start.3 = (bf16[2,1,2,32,1024]{4,3,2,1,0:T(8,128)(2,1)S(1)}, bf16[2,1,2,32,1024]{4,3,2,1,0:T(8,128)(2,1)S(1)}, u32[]{:S(2)}, u32[]{:S(2)}) collective-permute-start(bf16[2,1,2,32,1024]{4,3,2,1,0:T(8,128)(2,1)S(1)} %maximum_bitcast_fusion.refs_0_), channel_id=1, source_target_pairs={{0,2},{1,3},{2,0},{3,1},{4,6},{5,7},{6,4},{7,5},{8,10},{9,11},{10,... | collective-permute-start | bytes 786440 | tf_op jit(solution)/shard_map/ppermute | solution.py:276
  5.6 8.2 %collective-permute-start.2 = (bf16[2,1,2,32,1024]{4,3,2,1,0:T(8,128)(2,1)S(1)}, bf16[2,1,2,32,1024]{4,3,2,1,0:T(8,128)(2,1)S(1)}, u32[]{:S(2)}, u32[]{:S(2)}) collective-permute-start(bf16[2,1,2,32,1024]{4,3,2,1,0:T(8,128)(2,1)S(1)} %maximum_bitcast_fusion.refs_0_), channel_id=1, source_target_pairs={{0,8},{1,9},{2,10},{3,11},{4,12},{5,13},{6,14},{7,15},{8,0},{9,1},... | collective-permute-start | bytes 786440 | tf_op jit(solution)/shard_map/ppermute | solution.py:276
  10.5 5.0 %collective-permute-start.6 = (bf16[1,1,2,32,1024]{4,3,2,1,0:T(8,128)(2,1)S(1)}, bf16[1,1,2,32,1024]{4,3,2,1,0:T(8,128)(2,1)S(1)}, u32[]{:S(2)}, u32[]{:S(2)}) collective-permute-start(bf16[1,1,2,32,1024]{4,3,2,1,0:T(8,128)(2,1)S(1)} %slice.25), channel_id=1, source_target_pairs={{0,2},{1,3},{2,0},{3,1},{4,6},{5,7},{6,4},{7,5},{8,10},{9,11},{10,... | collective-permute-start | bytes 393224 | tf_op jit(solution)/shard_map/ppermute | solution.py:276
  12.2 5.0 %collective-permute-start.4 = (bf16[1,1,2,32,1024]{4,3,2,1,0:T(8,128)(2,1)S(1)}, bf16[1,1,2,32,1024]{4,3,2,1,0:T(8,128)(2,1)S(1)}, u32[]{:S(2)}, u32[]{:S(2)}) collective-permute-start(bf16[1,1,2,32,1024]{4,3,2,1,0:T(8,128)(2,1)S(1)} %slice.24), channel_id=1, source_target_pairs={{0,4},{1,5},{2,6},{3,7},{4,0},{5,1},{6,2},{7,3},{8,12},{9,13},{10,... | collective-permute-start | bytes 393224 | tf_op jit(solution)/shard_map/ppermute | solution.py:276
  17.3 6.4 %collective-permute-start.9 = (bf16[2,1,2,32,1024]{4,3,2,1,0:T(8,128)(2,1)S(1)}, bf16[2,1,2,32,1024]{4,3,2,1,0:T(8,128)(2,1)S(1)}, u32[]{:S(2)}, u32[]{:S(2)}) collective-permute-start(bf16[2,1,2,32,1024]{4,3,2,1,0:T(8,128)(2,1)S(1)} %collective-permute-done.2.refs_5_), channel_id=1, source_target_pairs={{0,4},{1,5},{2,6},{3,7},{4,0},{5,1},{6,2},{7,3},{8,12},{9,13},{10,... | collective-permute-start | bytes 786440 | tf_op jit(solution)/shard_map/ppermute | solution.py:276
  18.8 7.8 %collective-permute-start.7 = (bf16[2,1,2,32,1024]{4,3,2,1,0:T(8,128)(2,1)S(1)}, bf16[2,1,2,32,1024]{4,3,2,1,0:T(8,128)(2,1)S(1)}, u32[]{:S(2)}, u32[]{:S(2)}) collective-permute-start(bf16[2,1,2,32,1024]{4,3,2,1,0:T(8,128)(2,1)S(1)} %collective-permute-done.2.refs_5_), channel_id=1, source_target_pairs={{0,2},{1,3},{2,0},{3,1},{4,6},{5,7},{6,4},{7,5},{8,10},{9,11},{10,... | collective-permute-start | bytes 786440 | tf_op jit(solution)/shard_map/ppermute | solution.py:276
  19.3 10.3 %collective-permute-start.1 = (bf16[2,1,2,32,1024]{4,3,2,1,0:T(8,128)(2,1)S(1)}, bf16[2,1,2,32,1024]{4,3,2,1,0:T(8,128)(2,1)S(1)}, u32[]{:S(2)}, u32[]{:S(2)}) collective-permute-start(bf16[2,1,2,32,1024]{4,3,2,1,0:T(8,128)(2,1)S(1)} %maximum_bitcast_fusion.refs_0_), channel_id=1, source_target_pairs={{0,24},{1,25},{2,26},{3,27},{4,28},{5,29},{6,30},{7,31},{8,16},{9,... | collective-permute-start | bytes 786440 | tf_op jit(solution)/shard_map/ppermute | solution.py:276
  22.9 19.5 %collective-permute-start = (bf16[2,1,2,32,1024]{4,3,2,1,0:T(8,128)(2,1)S(1)}, bf16[2,1,2,32,1024]{4,3,2,1,0:T(8,128)(2,1)S(1)}, u32[]{:S(2)}, u32[]{:S(2)}) collective-permute-start(bf16[2,1,2,32,1024]{4,3,2,1,0:T(8,128)(2,1)S(1)} %maximum_bitcast_fusion.refs_0_), channel_id=1, source_target_pairs={{0,16},{1,17},{2,18},{3,19},{4,20},{5,21},{6,22},{7,23},{8,24},{9,... | collective-permute-start | bytes 786440 | tf_op jit(solution)/shard_map/ppermute | solution.py:276
  23.7 18.8 %collective-permute-start.10 = (bf16[1,1,2,32,1024]{4,3,2,1,0:T(8,128)(2,1)S(1)}, bf16[1,1,2,32,1024]{4,3,2,1,0:T(8,128)(2,1)S(1)}, u32[]{:S(2)}, u32[]{:S(2)}) collective-permute-start(bf16[1,1,2,32,1024]{4,3,2,1,0:T(8,128)(2,1)S(1)} %slice.27), channel_id=1, source_target_pairs={{0,2},{1,3},{2,0},{3,1},{4,6},{5,7},{6,4},{7,5},{8,10},{9,11},{10,... | collective-permute-start | bytes 393224 | tf_op jit(solution)/shard_map/ppermute | solution.py:276
  26.6 15.8 %collective-permute-start.8 = (bf16[1,1,2,32,1024]{4,3,2,1,0:T(8,128)(2,1)S(1)}, bf16[1,1,2,32,1024]{4,3,2,1,0:T(8,128)(2,1)S(1)}, u32[]{:S(2)}, u32[]{:S(2)}) collective-permute-start(bf16[1,1,2,32,1024]{4,3,2,1,0:T(8,128)(2,1)S(1)} %slice.26), channel_id=1, source_target_pairs={{0,4},{1,5},{2,6},{3,7},{4,0},{5,1},{6,2},{7,3},{8,12},{9,13},{10,... | collective-permute-start | bytes 393224 | tf_op jit(solution)/shard_map/ppermute | solution.py:276
  43.1 43.8 %all-to-all-start = ((bf16[32,16,1024]{2,1,0:T(8,128)(2,1)}), bf16[32,16,1024]{2,1,0:T(8,128)(2,1)S(1)}, u32[]{:S(2)}, u32[]{:S(2)}) async-start(bf16[32,16,1024]{2,1,0:T(8,128)(2,1)} %bitcast), calls=%async_computation | async-start | bytes 2097152 | tf_op jit(solution)/shard_map/all_to_all | solution.py:321
  47.2 3.9 %collective-permute-start.15 = (bf16[2,1,2,32,1024]{4,3,2,1,0:T(8,128)(2,1)S(1)}, bf16[2,1,2,32,1024]{4,3,2,1,0:T(8,128)(2,1)S(1)}, u32[]{:S(2)}, u32[]{:S(2)}) collective-permute-start(bf16[2,1,2,32,1024]{4,3,2,1,0:T(8,128)(2,1)S(1)} %maximum_bitcast_fusion.refs_0_), channel_id=1, source_target_pairs={{0,1},{1,0},{2,3},{3,2},{4,5},{5,4},{6,7},{7,6},{8,9},{9,8},{10,11... | collective-permute-start | bytes 786440 | tf_op jit(solution)/shard_map/ppermute | solution.py:276
  47.5 5.3 %collective-permute-start.17 = (bf16[2,1,2,32,1024]{4,3,2,1,0:T(8,128)(2,1)S(1)}, bf16[2,1,2,32,1024]{4,3,2,1,0:T(8,128)(2,1)S(1)}, u32[]{:S(2)}, u32[]{:S(2)}) collective-permute-start(bf16[2,1,2,32,1024]{4,3,2,1,0:T(8,128)(2,1)S(1)} %collective-permute-done.5.refs_2_), channel_id=1, source_target_pairs={{0,1},{1,0},{2,3},{3,2},{4,5},{5,4},{6,7},{7,6},{8,9},{9,8},{10,11... | collective-permute-start | bytes 786440 | tf_op jit(solution)/shard_map/ppermute | solution.py:276
  47.9 24.5 %collective-permute-start.12 = (bf16[2,2,2,32,1024]{4,3,2,1,0:T(8,128)(2,1)S(1)}, bf16[2,2,2,32,1024]{4,3,2,1,0:T(8,128)(2,1)S(1)}, u32[]{:S(2)}, u32[]{:S(2)}) collective-permute-start(bf16[2,2,2,32,1024]{4,3,2,1,0:T(8,128)(2,1)S(1)} %pad_maximum_fusion.refs_10_), channel_id=1, source_target_pairs={{0,4},{1,5},{2,6},{3,7},{4,0},{5,1},{6,2},{7,3},{8,12},{9,13},{10,... | collective-permute-start | bytes 1572872 | tf_op jit(solution)/shard_map/ppermute | solution.py:276
  49.7 22.6 %collective-permute-start.11 = (bf16[2,2,2,32,1024]{4,3,2,1,0:T(8,128)(2,1)S(1)}, bf16[2,2,2,32,1024]{4,3,2,1,0:T(8,128)(2,1)S(1)}, u32[]{:S(2)}, u32[]{:S(2)}) collective-permute-start(bf16[2,2,2,32,1024]{4,3,2,1,0:T(8,128)(2,1)S(1)} %pad_maximum_fusion.refs_10_), channel_id=1, source_target_pairs={{0,2},{1,3},{2,0},{3,1},{4,6},{5,7},{6,4},{7,5},{8,10},{9,11},{10,... | collective-permute-start | bytes 1572872 | tf_op jit(solution)/shard_map/ppermute | solution.py:276
  51.2 1.5 %collective-permute-start.19 = (bf16[1,1,2,32,1024]{4,3,2,1,0:T(8,128)(2,1)S(1)}, bf16[1,1,2,32,1024]{4,3,2,1,0:T(8,128)(2,1)}, u32[]{:S(2)}, u32[]{:S(2)}) collective-permute-start(bf16[1,1,2,32,1024]{4,3,2,1,0:T(8,128)(2,1)S(1)} %collective-permute-done.6.refs_4_), channel_id=1, source_target_pairs={{0,1},{1,0},{2,3},{3,2},{4,5},{5,4},{6,7},{7,6},{8,9},{9,8},{10,11... | collective-permute-start | bytes 393224 | tf_op jit(solution)/shard_map/ppermute | solution.py:276
  51.2 3.4 %collective-permute-start.16 = (bf16[2,1,2,32,1024]{4,3,2,1,0:T(8,128)(2,1)S(1)}, bf16[2,1,2,32,1024]{4,3,2,1,0:T(8,128)(2,1)S(1)}, u32[]{:S(2)}, u32[]{:S(2)}) collective-permute-start(bf16[2,1,2,32,1024]{4,3,2,1,0:T(8,128)(2,1)S(1)} %collective-permute-done.3.refs_1_), channel_id=1, source_target_pairs={{0,1},{1,0},{2,3},{3,2},{4,5},{5,4},{6,7},{7,6},{8,9},{9,8},{10,11... | collective-permute-start | bytes 786440 | tf_op jit(solution)/shard_map/ppermute | solution.py:276
  52.6 2.3 %collective-permute-start.20 = (bf16[2,1,2,32,1024]{4,3,2,1,0:T(8,128)(2,1)S(1)}, bf16[2,1,2,32,1024]{4,3,2,1,0:T(8,128)(2,1)S(1)}, u32[]{:S(2)}, u32[]{:S(2)}) collective-permute-start(bf16[2,1,2,32,1024]{4,3,2,1,0:T(8,128)(2,1)S(1)} %copy-done.16), channel_id=1, source_target_pairs={{0,1},{1,0},{2,3},{3,2},{4,5},{5,4},{6,7},{7,6},{8,9},{9,8},{10,11... | collective-permute-start | bytes 786440 | tf_op jit(solution)/shard_map/ppermute | solution.py:276
  52.8 1.6 %collective-permute-start.18 = (bf16[1,1,2,32,1024]{4,3,2,1,0:T(8,128)(2,1)S(1)}, bf16[1,1,2,32,1024]{4,3,2,1,0:T(8,128)(2,1)S(1)}, u32[]{:S(2)}, u32[]{:S(2)}) collective-permute-start(bf16[1,1,2,32,1024]{4,3,2,1,0:T(8,128)(2,1)S(1)} %copy-done.29), channel_id=1, source_target_pairs={{0,1},{1,0},{2,3},{3,2},{4,5},{5,4},{6,7},{7,6},{8,9},{9,8},{10,11... | collective-permute-start | bytes 393224 | tf_op jit(solution)/shard_map/ppermute | solution.py:276
  54.4 18.6 %collective-permute-start.22 = (bf16[2,1,2,32,1024]{4,3,2,1,0:T(8,128)(2,1)S(1)}, bf16[2,1,2,32,1024]{4,3,2,1,0:T(8,128)(2,1)S(1)}, u32[]{:S(2)}, u32[]{:S(2)}) collective-permute-start(bf16[2,1,2,32,1024]{4,3,2,1,0:T(8,128)(2,1)S(1)} %collective-permute-done.9.refs_7_), channel_id=1, source_target_pairs={{0,1},{1,0},{2,3},{3,2},{4,5},{5,4},{6,7},{7,6},{8,9},{9,8},{10,11... | collective-permute-start | bytes 786440 | tf_op jit(solution)/shard_map/ppermute | solution.py:276
  54.6 18.3 %collective-permute-start.24 = (bf16[1,1,2,32,1024]{4,3,2,1,0:T(8,128)(2,1)S(1)}, bf16[1,1,2,32,1024]{4,3,2,1,0:T(8,128)(2,1)S(1)}, u32[]{:S(2)}, u32[]{:S(2)}) collective-permute-start(bf16[1,1,2,32,1024]{4,3,2,1,0:T(8,128)(2,1)S(1)} %copy-done.31), channel_id=1, source_target_pairs={{0,1},{1,0},{2,3},{3,2},{4,5},{5,4},{6,7},{7,6},{8,9},{9,8},{10,11... | collective-permute-start | bytes 393224 | tf_op jit(solution)/shard_map/ppermute | solution.py:276
  55.0 22.4 %collective-permute-start.25 = (bf16[2,2,2,32,1024]{4,3,2,1,0:T(8,128)(2,1)S(1)}, bf16[2,2,2,32,1024]{4,3,2,1,0:T(8,128)(2,1)S(1)}, u32[]{:S(2)}, u32[]{:S(2)}) collective-permute-start(bf16[2,2,2,32,1024]{4,3,2,1,0:T(8,128)(2,1)S(1)} %pad_maximum_fusion.refs_10_), channel_id=1, source_target_pairs={{0,1},{1,0},{2,3},{3,2},{4,5},{5,4},{6,7},{7,6},{8,9},{9,8},{10,11... | collective-permute-start | bytes 1572872 | tf_op jit(solution)/shard_map/ppermute | solution.py:276
  72.3 11.6 %collective-permute-start.27 = (bf16[2,2,2,32,1024]{4,3,2,1,0:T(8,128)(2,1)S(1)}, bf16[2,2,2,32,1024]{4,3,2,1,0:T(8,128)(2,1)S(1)}, u32[]{:S(2)}, u32[]{:S(2)}) collective-permute-start(bf16[2,2,2,32,1024]{4,3,2,1,0:T(8,128)(2,1)S(1)} %collective-permute-done.12.refs_12_), channel_id=1, source_target_pairs={{0,1},{1,0},{2,3},{3,2},{4,5},{5,4},{6,7},{7,6},{8,9},{9,8},{10,11... | collective-permute-start | bytes 1572872 | tf_op jit(solution)/shard_map/ppermute | solution.py:276
  72.3 11.6 %collective-permute-start.26 = (bf16[2,2,2,32,1024]{4,3,2,1,0:T(8,128)(2,1)S(1)}, bf16[2,2,2,32,1024]{4,3,2,1,0:T(8,128)(2,1)S(1)}, u32[]{:S(2)}, u32[]{:S(2)}) collective-permute-start(bf16[2,2,2,32,1024]{4,3,2,1,0:T(8,128)(2,1)S(1)} %collective-permute-done.11.refs_11_), channel_id=1, source_target_pairs={{0,1},{1,0},{2,3},{3,2},{4,5},{5,4},{6,7},{7,6},{8,9},{9,8},{10,11... | collective-permute-start | bytes 1572872 | tf_op jit(solution)/shard_map/ppermute | solution.py:276
  72.8 4.1 %collective-permute-start.21 = (bf16[2,1,2,32,1024]{4,3,2,1,0:T(8,128)(2,1)S(1)}, bf16[2,1,2,32,1024]{4,3,2,1,0:T(8,128)(2,1)S(1)}, u32[]{:S(2)}, u32[]{:S(2)}) collective-permute-start(bf16[2,1,2,32,1024]{4,3,2,1,0:T(8,128)(2,1)S(1)} %collective-permute-done.7.refs_6_), channel_id=1, source_target_pairs={{0,1},{1,0},{2,3},{3,2},{4,5},{5,4},{6,7},{7,6},{8,9},{9,8},{10,11... | collective-permute-start | bytes 786440 | tf_op jit(solution)/shard_map/ppermute | solution.py:276
  73.7 1.8 %collective-permute-start.23 = (bf16[1,1,2,32,1024]{4,3,2,1,0:T(8,128)(2,1)S(1)}, bf16[1,1,2,32,1024]{4,3,2,1,0:T(8,128)(2,1)S(1)}, u32[]{:S(2)}, u32[]{:S(2)}) collective-permute-start(bf16[1,1,2,32,1024]{4,3,2,1,0:T(8,128)(2,1)S(1)} %copy-done.33), channel_id=1, source_target_pairs={{0,1},{1,0},{2,3},{3,2},{4,5},{5,4},{6,7},{7,6},{8,9},{9,8},{10,11... | collective-permute-start | bytes 393224 | tf_op jit(solution)/shard_map/ppermute | solution.py:276
  75.5 8.3 %collective-permute-start.14 = (bf16[1,2,2,32,1024]{4,3,2,1,0:T(8,128)(2,1)S(1)}, bf16[1,2,2,32,1024]{4,3,2,1,0:T(8,128)(2,1)S(1)}, u32[]{:S(2)}, u32[]{:S(2)}) collective-permute-start(bf16[1,2,2,32,1024]{4,3,2,1,0:T(8,128)(2,1)S(1)} %slice.29), channel_id=1, source_target_pairs={{0,2},{1,3},{2,0},{3,1},{4,6},{5,7},{6,4},{7,5},{8,10},{9,11},{10,... | collective-permute-start | bytes 786440 | tf_op jit(solution)/shard_map/ppermute | solution.py:276
  76.9 8.1 %collective-permute-start.13 = (bf16[1,2,2,32,1024]{4,3,2,1,0:T(8,128)(2,1)S(1)}, bf16[1,2,2,32,1024]{4,3,2,1,0:T(8,128)(2,1)S(1)}, u32[]{:S(2)}, u32[]{:S(2)}) collective-permute-start(bf16[1,2,2,32,1024]{4,3,2,1,0:T(8,128)(2,1)S(1)} %slice.28), channel_id=1, source_target_pairs={{0,4},{1,5},{2,6},{3,7},{4,0},{5,1},{6,2},{7,3},{8,12},{9,13},{10,... | collective-permute-start | bytes 786440 | tf_op jit(solution)/shard_map/ppermute | solution.py:276
  85.1 1.5 %collective-permute-start.28 = (bf16[1,2,2,32,1024]{4,3,2,1,0:T(8,128)(2,1)S(1)}, bf16[1,2,2,32,1024]{4,3,2,1,0:T(8,128)(2,1)S(1)}, u32[]{:S(2)}, u32[]{:S(2)}) collective-permute-start(bf16[1,2,2,32,1024]{4,3,2,1,0:T(8,128)(2,1)S(1)} %collective-permute-done.13.refs_13_), channel_id=1, source_target_pairs={{0,1},{1,0},{2,3},{3,2},{4,5},{5,4},{6,7},{7,6},{8,9},{9,8},{10,11... | collective-permute-start | bytes 786440 | tf_op jit(solution)/shard_map/ppermute | solution.py:276
  85.1 1.9 %collective-permute-start.29 = (bf16[1,2,2,32,1024]{4,3,2,1,0:T(8,128)(2,1)S(1)}, bf16[1,2,2,32,1024]{4,3,2,1,0:T(8,128)(2,1)S(1)}, u32[]{:S(2)}, u32[]{:S(2)}) collective-permute-start(bf16[1,2,2,32,1024]{4,3,2,1,0:T(8,128)(2,1)S(1)} %collective-permute-done.14.refs_14_), channel_id=1, source_target_pairs={{0,1},{1,0},{2,3},{3,2},{4,5},{5,4},{6,7},{7,6},{8,9},{9,8},{10,11... | collective-permute-start | bytes 786440 | tf_op jit(solution)/shard_map/ppermute | solution.py:276
  99.8 14.8 %all-to-all-start.1 = ((bf16[16,128,128]{2,1,0:T(8,128)(2,1)}), bf16[16,128,128]{2,1,0:T(8,128)(2,1)S(1)}, u32[]{:S(2)}, u32[]{:S(2)}) async-start(bf16[16,128,128]{2,1,0:T(8,128)(2,1)} %bitcast.16), calls=%async_computation.1 | async-start | bytes 1048576 | tf_op jit(solution)/shard_map/all_to_all | solution.py:321
  (37 other events, 578.8 us)

commit v11 on v9

--- a/solution.py
+++ b/solution.py
@@ -302,7 +302,7 @@
         if number:
             value, *_ = lax.optimization_barrier((value, *packed, blocks[-2][0], blocks[-1][0]))
         blocks += plane(value, sources)
-    right, *_ = lax.optimization_barrier((packed[1], blocks[-4][0], blocks[-3][0]))
+    right, *_ = lax.optimization_barrier((packed[1], blocks[-2][0], blocks[-1][0]))
     last = len(blocks) - 2
     near = []
     for number, (value, sources, gates) in enumerate(blocks):

time: 130 us -> 136 us (1.046)
  waiting for transfers between devices: 41.8 us -> 46.9 us
    ppermute x30, waiting for transfers between devices: 41.8 us -> 46.9 us  [flip(): return lax.ppermute(value, 'mode', pairs)]
    all_to_all x3, starting transfers between devices: 11.9 us -> 13.3 us  [trade(): lax.all_to_all(value, 'mode', split_axis=0, concat_axis=0, axis_index_gro...]
    unnamed x62 -> x60, local copies, waits for them, and re-layouts: 4.53 us -> 4.97 us
  transfers between devices with their start and end apart: 33 -> 33, of which waited for: 13 -> 10; matrix products, arithmetic and copies ran while one was open for 1% -> 1% of each run, Pallas kernels for 20% -> 19%
where the time goes in v11:
time: 136 us
  waiting for transfers between devices  46.9 us (34%)
  starting transfers between devices  38.2 us (28%)
  Pallas kernels  26 us (19%)
  blocking collectives  16.4 us (12%)
  local copies, waits for them, and re-layouts  6.57 us (5%)
    ppermute x30, waiting for transfers between devices, flip(): return lax.ppermute(value, 'mode', pairs)  46.9 us
    pallas_call x4, Pallas kernels, call(): pl.pallas_call(kernel, out_shape=[out] * outputs if outputs else out, in_...  26 us
    ppermute x30, starting transfers between devices, flip(): return lax.ppermute(value, 'mode', pairs)  24.8 us
    all_to_all x1, blocking collectives, trade(): lax.all_to_all(value, 'mode', split_axis=0, concat_axis=0, axis_index_gro...  16.4 us
    all_to_all x3, starting transfers between devices, trade(): lax.all_to_all(value, 'mode', split_axis=0, concat_axis=0, axis_index_gro...  13.3 us
    unnamed x60, local copies, waits for them, and re-layouts  4.97 us
  transfers between devices with their start and end apart: 33, of which 10 were waited for; matrix products, arithmetic and copies ran while one was open for 1% of the time, Pallas kernels for 19%

profile of v11, /device:TPU:0, one launch (start us, length us, event | category | flops | bytes accessed | tf_op | source)
XLA Modules:
  0.0 135.6 jit_solution(18178341159116197368)
XLA Ops:
  0.0 1.1 maximum_bitcast_fusion.refs_0_
  1.1 3.0 %collective-permute-start.3 = (bf16[2,1,2,32,1024]{4,3,2,1,0:T(8,128)(2,1)S(1)}, bf16[2,1,2,32,1024]{4,3,2,1,0:T(8,128)(2,1)S(1)}, u32[]{:S(2)}, u32[]{:S(2)}) collective-permute-start(bf16[2,1,2,32,1024]{4,3,2,1,0:T(8,128)(2,1)S(1)} %maximum_bitcast_fusion.refs_0_), channel_id=1, source_target_pairs={{0,4},{1,5},{2,6},{3,7},{4,0},{5,1},{6,2},{7,3},{8,12},{9,13},{10,... | collective-permute-start | bytes 786440 | tf_op jit(solution)/shard_map/ppermute | solution.py:273
  4.1 1.5 %collective-permute-start.2 = (bf16[2,1,2,32,1024]{4,3,2,1,0:T(8,128)(2,1)S(1)}, bf16[2,1,2,32,1024]{4,3,2,1,0:T(8,128)(2,1)S(1)}, u32[]{:S(2)}, u32[]{:S(2)}) collective-permute-start(bf16[2,1,2,32,1024]{4,3,2,1,0:T(8,128)(2,1)S(1)} %maximum_bitcast_fusion.refs_0_), channel_id=1, source_target_pairs={{0,2},{1,3},{2,0},{3,1},{4,6},{5,7},{6,4},{7,5},{8,10},{9,11},{10,... | collective-permute-start | bytes 786440 | tf_op jit(solution)/shard_map/ppermute | solution.py:273
  5.6 1.6 %collective-permute-start.6 = (bf16[2,1,2,32,1024]{4,3,2,1,0:T(8,128)(2,1)S(1)}, bf16[2,1,2,32,1024]{4,3,2,1,0:T(8,128)(2,1)S(1)}, u32[]{:S(2)}, u32[]{:S(2)}) collective-permute-start(bf16[2,1,2,32,1024]{4,3,2,1,0:T(8,128)(2,1)S(1)} %maximum_bitcast_fusion.refs_0_), channel_id=1, source_target_pairs={{0,8},{1,9},{2,10},{3,11},{4,12},{5,13},{6,14},{7,15},{8,0},{9,1},... | collective-permute-start | bytes 786440 | tf_op jit(solution)/shard_map/ppermute | solution.py:273
  7.2 3.2 %collective-permute-done.3.refs_2_ = bf16[2,1,2,32,1024]{4,3,2,1,0:T(8,128)(2,1)S(1)} collective-permute-done((bf16[2,1,2,32,1024]{4,3,2,1,0:T(8,128)(2,1)S(1)}, bf16[2,1,2,32,1024]{4,3,2,1,0:T(8,128)(2,1)S(1)}, u32[]{:S(2)}, u32[]{:S(2)}) %collective-permute-start.3) | collective-permute-done | bytes 262176 | tf_op jit(solution)/shard_map/ppermute | solution.py:273
  10.5 1.8 %collective-permute-start.5 = (bf16[1,1,2,32,1024]{4,3,2,1,0:T(8,128)(2,1)S(1)}, bf16[1,1,2,32,1024]{4,3,2,1,0:T(8,128)(2,1)S(1)}, u32[]{:S(2)}, u32[]{:S(2)}) collective-permute-start(bf16[1,1,2,32,1024]{4,3,2,1,0:T(8,128)(2,1)S(1)} %slice.25), channel_id=1, source_target_pairs={{0,2},{1,3},{2,0},{3,1},{4,6},{5,7},{6,4},{7,5},{8,10},{9,11},{10,... | collective-permute-start | bytes 393224 | tf_op jit(solution)/shard_map/ppermute | solution.py:273
  12.2 1.6 %collective-permute-start.4 = (bf16[1,1,2,32,1024]{4,3,2,1,0:T(8,128)(2,1)S(1)}, bf16[1,1,2,32,1024]{4,3,2,1,0:T(8,128)(2,1)S(1)}, u32[]{:S(2)}, u32[]{:S(2)}) collective-permute-start(bf16[1,1,2,32,1024]{4,3,2,1,0:T(8,128)(2,1)S(1)} %slice.24), channel_id=1, source_target_pairs={{0,4},{1,5},{2,6},{3,7},{4,0},{5,1},{6,2},{7,3},{8,12},{9,13},{10,... | collective-permute-start | bytes 393224 | tf_op jit(solution)/shard_map/ppermute | solution.py:273
  14.6 3.0 %shard_map.46 = (bf16[256,1024]{1,0:T(8,128)(2,1)}, bf16[256,1024]{1,0:T(8,128)(2,1)}) custom-call(bf16[4,2,64,1024]{3,2,1,0:T(8,128)(2,1)S(1)} %copy-done.1, s32[4,1024]{1,0:T(4,128)S(1)} %copy-done.2), custom_call_target="tpu_custom_call" | custom-call | flops 2147483648 | bytes 1064960 | tf_op jit(solution)/shard_map/pallas_call | solution.py:189
  17.6 1.2 collective-permute-start.8
  19.4 3.6 %collective-permute-start.1 = (bf16[2,1,2,32,1024]{4,3,2,1,0:T(8,128)(2,1)S(1)}, bf16[2,1,2,32,1024]{4,3,2,1,0:T(8,128)(2,1)S(1)}, u32[]{:S(2)}, u32[]{:S(2)}) collective-permute-start(bf16[2,1,2,32,1024]{4,3,2,1,0:T(8,128)(2,1)S(1)} %maximum_bitcast_fusion.refs_0_), channel_id=1, source_target_pairs={{0,24},{1,25},{2,26},{3,27},{4,28},{5,29},{6,30},{7,31},{8,16},{9,... | collective-permute-start | bytes 786440 | tf_op jit(solution)/shard_map/ppermute | solution.py:273
  23.0 1.5 %collective-permute-done.8.refs_7_ = bf16[2,1,2,32,1024]{4,3,2,1,0:T(8,128)(2,1)} collective-permute-done((bf16[2,1,2,32,1024]{4,3,2,1,0:T(8,128)(2,1)S(1)}, bf16[2,1,2,32,1024]{4,3,2,1,0:T(8,128)(2,1)}, u32[]{:S(2)}, u32[]{:S(2)}) %collective-permute-start.8) | collective-permute-done | bytes 262176 | tf_op jit(solution)/shard_map/ppermute | solution.py:273
  24.4 0.9 slice.27
  26.0 1.2 collective-permute-start.9
  27.1 3.0 %collective-permute-done.1 = bf16[2,1,2,32,1024]{4,3,2,1,0:T(8,128)(2,1)S(1)} collective-permute-done((bf16[2,1,2,32,1024]{4,3,2,1,0:T(8,128)(2,1)S(1)}, bf16[2,1,2,32,1024]{4,3,2,1,0:T(8,128)(2,1)S(1)}, u32[]{:S(2)}, u32[]{:S(2)}) %collective-permute-start.1) | collective-permute-done | bytes 262176 | tf_op jit(solution)/shard_map/ppermute | solution.py:273
  30.1 13.1 %collective-permute-done = bf16[2,1,2,32,1024]{4,3,2,1,0:T(8,128)(2,1)S(1)} collective-permute-done((bf16[2,1,2,32,1024]{4,3,2,1,0:T(8,128)(2,1)S(1)}, bf16[2,1,2,32,1024]{4,3,2,1,0:T(8,128)(2,1)S(1)}, u32[]{:S(2)}, u32[]{:S(2)}) %collective-permute-start) | collective-permute-done | bytes 262176 | tf_op jit(solution)/shard_map/ppermute | solution.py:273
  43.2 4.1 %all-to-all-start = ((bf16[32,8,1024]{2,1,0:T(8,128)(2,1)}), bf16[32,8,1024]{2,1,0:T(8,128)(2,1)S(1)}, u32[]{:S(2)}, u32[]{:S(2)}) async-start(bf16[32,8,1024]{2,1,0:T(8,128)(2,1)} %bitcast), calls=%async_computation | async-start | bytes 1048576 | tf_op jit(solution)/shard_map/all_to_all | solution.py:318
  47.5 1.8 %collective-permute-start.12 = (bf16[2,2,2,32,1024]{4,3,2,1,0:T(8,128)(2,1)S(1)}, bf16[2,2,2,32,1024]{4,3,2,1,0:T(8,128)(2,1)S(1)}, u32[]{:S(2)}, u32[]{:S(2)}) collective-permute-start(bf16[2,2,2,32,1024]{4,3,2,1,0:T(8,128)(2,1)S(1)} %pad_maximum_fusion.refs_10_), channel_id=1, source_target_pairs={{0,4},{1,5},{2,6},{3,7},{4,0},{5,1},{6,2},{7,3},{8,12},{9,13},{10,... | collective-permute-start | bytes 1572872 | tf_op jit(solution)/shard_map/ppermute | solution.py:273
  49.3 1.5 %collective-permute-start.11 = (bf16[2,2,2,32,1024]{4,3,2,1,0:T(8,128)(2,1)S(1)}, bf16[2,2,2,32,1024]{4,3,2,1,0:T(8,128)(2,1)S(1)}, u32[]{:S(2)}, u32[]{:S(2)}) collective-permute-start(bf16[2,2,2,32,1024]{4,3,2,1,0:T(8,128)(2,1)S(1)} %pad_maximum_fusion.refs_10_), channel_id=1, source_target_pairs={{0,2},{1,3},{2,0},{3,1},{4,6},{5,7},{6,4},{7,5},{8,10},{9,11},{10,... | collective-permute-start | bytes 1572872 | tf_op jit(solution)/shard_map/ppermute | solution.py:273
  51.4 15.7 %collective-permute-done.12.refs_12_ = bf16[2,2,2,32,1024]{4,3,2,1,0:T(8,128)(2,1)S(1)} collective-permute-done((bf16[2,2,2,32,1024]{4,3,2,1,0:T(8,128)(2,1)S(1)}, bf16[2,2,2,32,1024]{4,3,2,1,0:T(8,128)(2,1)S(1)}, u32[]{:S(2)}, u32[]{:S(2)}) %collective-permute-start.12) | collective-permute-done | bytes 524320 | tf_op jit(solution)/shard_map/ppermute | solution.py:273
  67.8 0.9 copy-done.25
  68.8 1.5 %collective-permute-start.14 = (bf16[1,2,2,32,1024]{4,3,2,1,0:T(8,128)(2,1)S(1)}, bf16[1,2,2,32,1024]{4,3,2,1,0:T(8,128)(2,1)}, u32[]{:S(2)}, u32[]{:S(2)}) collective-permute-start(bf16[1,2,2,32,1024]{4,3,2,1,0:T(8,128)(2,1)S(1)} %slice.29), channel_id=1, source_target_pairs={{0,2},{1,3},{2,0},{3,1},{4,6},{5,7},{6,4},{7,5},{8,10},{9,11},{10,... | collective-permute-start | bytes 786440 | tf_op jit(solution)/shard_map/ppermute | solution.py:273
  71.3 6.1 %collective-permute-done.14.refs_14_ = bf16[1,2,2,32,1024]{4,3,2,1,0:T(8,128)(2,1)} collective-permute-done((bf16[1,2,2,32,1024]{4,3,2,1,0:T(8,128)(2,1)S(1)}, bf16[1,2,2,32,1024]{4,3,2,1,0:T(8,128)(2,1)}, u32[]{:S(2)}, u32[]{:S(2)}) %collective-permute-start.14) | collective-permute-done | bytes 262176 | tf_op jit(solution)/shard_map/ppermute | solution.py:273
  77.5 1.2 collective-permute-done.13.refs_13_
  78.8 0.8 copy-done.4
  79.6 4.2 %all-to-all-start.2 = ((bf16[32,8,1024]{2,1,0:T(8,128)(2,1)}), bf16[32,8,1024]{2,1,0:T(8,128)(2,1)S(1)}, u32[]{:S(2)}, u32[]{:S(2)}) async-start(bf16[32,8,1024]{2,1,0:T(8,128)(2,1)} %bitcast.5), calls=%async_computation.2 | async-start | bytes 1048576 | tf_op jit(solution)/shard_map/all_to_all | solution.py:318
  84.4 1.4 %collective-permute-done.23.refs_23_ = bf16[1,1,2,32,1024]{4,3,2,1,0:T(8,128)(2,1)S(1)} collective-permute-done((bf16[1,1,2,32,1024]{4,3,2,1,0:T(8,128)(2,1)}, bf16[1,1,2,32,1024]{4,3,2,1,0:T(8,128)(2,1)S(1)}, u32[]{:S(2)}, u32[]{:S(2)}) %collective-permute-start.23) | collective-permute-done | bytes 131104 | tf_op jit(solution)/shard_map/ppermute | solution.py:273
  86.5 1.2 collective-permute-done.28.refs_28_
  88.8 11.5 %shard_map.47 = bf16[2048,128]{1,0:T(8,128)(2,1)} custom-call(bf16[256,1024]{1,0:T(8,128)(2,1)} %bitcast.16, bf16[2,1,2,32,1024]{4,3,2,1,0:T(8,128)(2,1)} %copy-done.6, bf16[2,1,2,32,1024]{4,3,2,1,0:T(8,128)(2,1)} %copy-done.10, bf16[2,1,2,32,1024]{4,3,2,1,0:T(8,128)(2,1)} %copy-done.9, bf16[1,1,2,32,1024]{4,3,2,1,0:T(8,128)(2,1)} %copy-done.24, ...), custom_call_target="tpu_custom_call" | custom-call | flops 4294967296 | bytes 8912896 | tf_op jit(solution)/shard_map/pallas_call | solution.py:189
  101.1 5.0 %all-to-all-start.1 = ((bf16[16,128,128]{2,1,0:T(8,128)(2,1)}), bf16[16,128,128]{2,1,0:T(8,128)(2,1)S(1)}, u32[]{:S(2)}, u32[]{:S(2)}) async-start(bf16[16,128,128]{2,1,0:T(8,128)(2,1)} %bitcast.18), calls=%async_computation.1 | async-start | bytes 1048576 | tf_op jit(solution)/shard_map/all_to_all | solution.py:318
  106.1 10.8 %shard_map.48.right_ref = bf16[256,1024]{1,0:T(8,128)(2,1)} custom-call(bf16[256,1024]{1,0:T(8,128)(2,1)} %bitcast.17, bf16[2,1,2,32,1024]{4,3,2,1,0:T(8,128)(2,1)} %copy-done.6, bf16[2,1,2,32,1024]{4,3,2,1,0:T(8,128)(2,1)} %copy-done.10, bf16[2,1,2,32,1024]{4,3,2,1,0:T(8,128)(2,1)} %copy-done.9, bf16[1,1,2,32,1024]{4,3,2,1,0:T(8,128)(2,1)} %copy-done.24, ...), custom_call_target="tpu_custom_call" | custom-call | flops 4294967296 | bytes 8912896 | tf_op jit(solution)/shard_map/pallas_call | solution.py:189
  117.0 1.0 copy-done
  118.6 16.4 %all_to_all.20 = bf16[32,16,256]{2,1,0:T(8,128)(2,1)S(1)} all-to-all(bf16[32,16,256]{2,1,0:T(8,128)(2,1)S(1)} %bitcast.15), channel_id=1, replica_groups=mesh['cuts'=1,'mode'=32] {'mode'}, dimensions={0} | all-to-all | bytes 524288 | tf_op jit(solution)/shard_map/all_to_all | solution.py:318
  (110 shorter events, 8.8 us)
Async XLA Ops:
  1.1 9.3 %collective-permute-start.3 = (bf16[2,1,2,32,1024]{4,3,2,1,0:T(8,128)(2,1)S(1)}, bf16[2,1,2,32,1024]{4,3,2,1,0:T(8,128)(2,1)S(1)}, u32[]{:S(2)}, u32[]{:S(2)}) collective-permute-start(bf16[2,1,2,32,1024]{4,3,2,1,0:T(8,128)(2,1)S(1)} %maximum_bitcast_fusion.refs_0_), channel_id=1, source_target_pairs={{0,4},{1,5},{2,6},{3,7},{4,0},{5,1},{6,2},{7,3},{8,12},{9,13},{10,... | collective-permute-start | bytes 786440 | tf_op jit(solution)/shard_map/ppermute | solution.py:273
  4.1 8.1 %collective-permute-start.2 = (bf16[2,1,2,32,1024]{4,3,2,1,0:T(8,128)(2,1)S(1)}, bf16[2,1,2,32,1024]{4,3,2,1,0:T(8,128)(2,1)S(1)}, u32[]{:S(2)}, u32[]{:S(2)}) collective-permute-start(bf16[2,1,2,32,1024]{4,3,2,1,0:T(8,128)(2,1)S(1)} %maximum_bitcast_fusion.refs_0_), channel_id=1, source_target_pairs={{0,2},{1,3},{2,0},{3,1},{4,6},{5,7},{6,4},{7,5},{8,10},{9,11},{10,... | collective-permute-start | bytes 786440 | tf_op jit(solution)/shard_map/ppermute | solution.py:273
  5.6 12.0 %collective-permute-start.6 = (bf16[2,1,2,32,1024]{4,3,2,1,0:T(8,128)(2,1)S(1)}, bf16[2,1,2,32,1024]{4,3,2,1,0:T(8,128)(2,1)S(1)}, u32[]{:S(2)}, u32[]{:S(2)}) collective-permute-start(bf16[2,1,2,32,1024]{4,3,2,1,0:T(8,128)(2,1)S(1)} %maximum_bitcast_fusion.refs_0_), channel_id=1, source_target_pairs={{0,8},{1,9},{2,10},{3,11},{4,12},{5,13},{6,14},{7,15},{8,0},{9,1},... | collective-permute-start | bytes 786440 | tf_op jit(solution)/shard_map/ppermute | solution.py:273
  10.5 7.1 %collective-permute-start.5 = (bf16[1,1,2,32,1024]{4,3,2,1,0:T(8,128)(2,1)S(1)}, bf16[1,1,2,32,1024]{4,3,2,1,0:T(8,128)(2,1)S(1)}, u32[]{:S(2)}, u32[]{:S(2)}) collective-permute-start(bf16[1,1,2,32,1024]{4,3,2,1,0:T(8,128)(2,1)S(1)} %slice.25), channel_id=1, source_target_pairs={{0,2},{1,3},{2,0},{3,1},{4,6},{5,7},{6,4},{7,5},{8,10},{9,11},{10,... | collective-permute-start | bytes 393224 | tf_op jit(solution)/shard_map/ppermute | solution.py:273
  12.2 5.4 %collective-permute-start.4 = (bf16[1,1,2,32,1024]{4,3,2,1,0:T(8,128)(2,1)S(1)}, bf16[1,1,2,32,1024]{4,3,2,1,0:T(8,128)(2,1)S(1)}, u32[]{:S(2)}, u32[]{:S(2)}) collective-permute-start(bf16[1,1,2,32,1024]{4,3,2,1,0:T(8,128)(2,1)S(1)} %slice.24), channel_id=1, source_target_pairs={{0,4},{1,5},{2,6},{3,7},{4,0},{5,1},{6,2},{7,3},{8,12},{9,13},{10,... | collective-permute-start | bytes 393224 | tf_op jit(solution)/shard_map/ppermute | solution.py:273
  17.6 6.8 %collective-permute-start.8 = (bf16[2,1,2,32,1024]{4,3,2,1,0:T(8,128)(2,1)S(1)}, bf16[2,1,2,32,1024]{4,3,2,1,0:T(8,128)(2,1)}, u32[]{:S(2)}, u32[]{:S(2)}) collective-permute-start(bf16[2,1,2,32,1024]{4,3,2,1,0:T(8,128)(2,1)S(1)} %collective-permute-done.6.refs_5_), channel_id=1, source_target_pairs={{0,4},{1,5},{2,6},{3,7},{4,0},{5,1},{6,2},{7,3},{8,12},{9,13},{10,... | collective-permute-start | bytes 786440 | tf_op jit(solution)/shard_map/ppermute | solution.py:273
  18.8 7.1 %collective-permute-start.7 = (bf16[2,1,2,32,1024]{4,3,2,1,0:T(8,128)(2,1)S(1)}, bf16[2,1,2,32,1024]{4,3,2,1,0:T(8,128)(2,1)S(1)}, u32[]{:S(2)}, u32[]{:S(2)}) collective-permute-start(bf16[2,1,2,32,1024]{4,3,2,1,0:T(8,128)(2,1)S(1)} %collective-permute-done.6.refs_5_), channel_id=1, source_target_pairs={{0,2},{1,3},{2,0},{3,1},{4,6},{5,7},{6,4},{7,5},{8,10},{9,11},{10,... | collective-permute-start | bytes 786440 | tf_op jit(solution)/shard_map/ppermute | solution.py:273
  19.4 10.8 %collective-permute-start.1 = (bf16[2,1,2,32,1024]{4,3,2,1,0:T(8,128)(2,1)S(1)}, bf16[2,1,2,32,1024]{4,3,2,1,0:T(8,128)(2,1)S(1)}, u32[]{:S(2)}, u32[]{:S(2)}) collective-permute-start(bf16[2,1,2,32,1024]{4,3,2,1,0:T(8,128)(2,1)S(1)} %maximum_bitcast_fusion.refs_0_), channel_id=1, source_target_pairs={{0,24},{1,25},{2,26},{3,27},{4,28},{5,29},{6,30},{7,31},{8,16},{9,... | collective-permute-start | bytes 786440 | tf_op jit(solution)/shard_map/ppermute | solution.py:273
  23.0 20.3 %collective-permute-start = (bf16[2,1,2,32,1024]{4,3,2,1,0:T(8,128)(2,1)S(1)}, bf16[2,1,2,32,1024]{4,3,2,1,0:T(8,128)(2,1)S(1)}, u32[]{:S(2)}, u32[]{:S(2)}) collective-permute-start(bf16[2,1,2,32,1024]{4,3,2,1,0:T(8,128)(2,1)S(1)} %maximum_bitcast_fusion.refs_0_), channel_id=1, source_target_pairs={{0,16},{1,17},{2,18},{3,19},{4,20},{5,21},{6,22},{7,23},{8,24},{9,... | collective-permute-start | bytes 786440 | tf_op jit(solution)/shard_map/ppermute | solution.py:273
  25.3 22.1 %collective-permute-start.10 = (bf16[1,1,2,32,1024]{4,3,2,1,0:T(8,128)(2,1)S(1)}, bf16[1,1,2,32,1024]{4,3,2,1,0:T(8,128)(2,1)}, u32[]{:S(2)}, u32[]{:S(2)}) collective-permute-start(bf16[1,1,2,32,1024]{4,3,2,1,0:T(8,128)(2,1)S(1)} %slice.27), channel_id=1, source_target_pairs={{0,2},{1,3},{2,0},{3,1},{4,6},{5,7},{6,4},{7,5},{8,10},{9,11},{10,... | collective-permute-start | bytes 393224 | tf_op jit(solution)/shard_map/ppermute | solution.py:273
  26.0 21.5 %collective-permute-start.9 = (bf16[1,1,2,32,1024]{4,3,2,1,0:T(8,128)(2,1)S(1)}, bf16[1,1,2,32,1024]{4,3,2,1,0:T(8,128)(2,1)}, u32[]{:S(2)}, u32[]{:S(2)}) collective-permute-start(bf16[1,1,2,32,1024]{4,3,2,1,0:T(8,128)(2,1)S(1)} %slice.26), channel_id=1, source_target_pairs={{0,4},{1,5},{2,6},{3,7},{4,0},{5,1},{6,2},{7,3},{8,12},{9,13},{10,... | collective-permute-start | bytes 393224 | tf_op jit(solution)/shard_map/ppermute | solution.py:273
  43.2 35.5 %all-to-all-start = ((bf16[32,8,1024]{2,1,0:T(8,128)(2,1)}), bf16[32,8,1024]{2,1,0:T(8,128)(2,1)S(1)}, u32[]{:S(2)}, u32[]{:S(2)}) async-start(bf16[32,8,1024]{2,1,0:T(8,128)(2,1)} %bitcast), calls=%async_computation | async-start | bytes 1048576 | tf_op jit(solution)/shard_map/all_to_all | solution.py:318
  47.5 19.6 %collective-permute-start.12 = (bf16[2,2,2,32,1024]{4,3,2,1,0:T(8,128)(2,1)S(1)}, bf16[2,2,2,32,1024]{4,3,2,1,0:T(8,128)(2,1)S(1)}, u32[]{:S(2)}, u32[]{:S(2)}) collective-permute-start(bf16[2,2,2,32,1024]{4,3,2,1,0:T(8,128)(2,1)S(1)} %pad_maximum_fusion.refs_10_), channel_id=1, source_target_pairs={{0,4},{1,5},{2,6},{3,7},{4,0},{5,1},{6,2},{7,3},{8,12},{9,13},{10,... | collective-permute-start | bytes 1572872 | tf_op jit(solution)/shard_map/ppermute | solution.py:273
  49.3 17.8 %collective-permute-start.11 = (bf16[2,2,2,32,1024]{4,3,2,1,0:T(8,128)(2,1)S(1)}, bf16[2,2,2,32,1024]{4,3,2,1,0:T(8,128)(2,1)S(1)}, u32[]{:S(2)}, u32[]{:S(2)}) collective-permute-start(bf16[2,2,2,32,1024]{4,3,2,1,0:T(8,128)(2,1)S(1)} %pad_maximum_fusion.refs_10_), channel_id=1, source_target_pairs={{0,2},{1,3},{2,0},{3,1},{4,6},{5,7},{6,4},{7,5},{8,10},{9,11},{10,... | collective-permute-start | bytes 1572872 | tf_op jit(solution)/shard_map/ppermute | solution.py:273
  50.8 17.0 %collective-permute-start.15 = (bf16[2,1,2,32,1024]{4,3,2,1,0:T(8,128)(2,1)S(1)}, bf16[2,1,2,32,1024]{4,3,2,1,0:T(8,128)(2,1)S(1)}, u32[]{:S(2)}, u32[]{:S(2)}) collective-permute-start(bf16[2,1,2,32,1024]{4,3,2,1,0:T(8,128)(2,1)S(1)} %maximum_bitcast_fusion.refs_0_), channel_id=1, source_target_pairs={{0,1},{1,0},{2,3},{3,2},{4,5},{5,4},{6,7},{7,6},{8,9},{9,8},{10,11... | collective-permute-start | bytes 786440 | tf_op jit(solution)/shard_map/ppermute | solution.py:273
  50.8 19.4 %collective-permute-start.17 = (bf16[2,1,2,32,1024]{4,3,2,1,0:T(8,128)(2,1)S(1)}, bf16[2,1,2,32,1024]{4,3,2,1,0:T(8,128)(2,1)S(1)}, u32[]{:S(2)}, u32[]{:S(2)}) collective-permute-start(bf16[2,1,2,32,1024]{4,3,2,1,0:T(8,128)(2,1)S(1)} %collective-permute-done.3.refs_2_), channel_id=1, source_target_pairs={{0,1},{1,0},{2,3},{3,2},{4,5},{5,4},{6,7},{7,6},{8,9},{9,8},{10,11... | collective-permute-start | bytes 786440 | tf_op jit(solution)/shard_map/ppermute | solution.py:273
  51.3 17.4 %collective-permute-start.19 = (bf16[1,1,2,32,1024]{4,3,2,1,0:T(8,128)(2,1)S(1)}, bf16[1,1,2,32,1024]{4,3,2,1,0:T(8,128)(2,1)S(1)}, u32[]{:S(2)}, u32[]{:S(2)}) collective-permute-start(bf16[1,1,2,32,1024]{4,3,2,1,0:T(8,128)(2,1)S(1)} %collective-permute-done.5.refs_4_), channel_id=1, source_target_pairs={{0,1},{1,0},{2,3},{3,2},{4,5},{5,4},{6,7},{7,6},{8,9},{9,8},{10,11... | collective-permute-start | bytes 393224 | tf_op jit(solution)/shard_map/ppermute | solution.py:273
  67.1 3.6 %collective-permute-start.16 = (bf16[2,1,2,32,1024]{4,3,2,1,0:T(8,128)(2,1)S(1)}, bf16[2,1,2,32,1024]{4,3,2,1,0:T(8,128)(2,1)S(1)}, u32[]{:S(2)}, u32[]{:S(2)}) collective-permute-start(bf16[2,1,2,32,1024]{4,3,2,1,0:T(8,128)(2,1)S(1)} %collective-permute-done.2.refs_1_), channel_id=1, source_target_pairs={{0,1},{1,0},{2,3},{3,2},{4,5},{5,4},{6,7},{7,6},{8,9},{9,8},{10,11... | collective-permute-start | bytes 786440 | tf_op jit(solution)/shard_map/ppermute | solution.py:273
  67.2 4.1 %collective-permute-start.20 = (bf16[2,1,2,32,1024]{4,3,2,1,0:T(8,128)(2,1)S(1)}, bf16[2,1,2,32,1024]{4,3,2,1,0:T(8,128)(2,1)S(1)}, u32[]{:S(2)}, u32[]{:S(2)}) collective-permute-start(bf16[2,1,2,32,1024]{4,3,2,1,0:T(8,128)(2,1)S(1)} %copy-done.15), channel_id=1, source_target_pairs={{0,1},{1,0},{2,3},{3,2},{4,5},{5,4},{6,7},{7,6},{8,9},{9,8},{10,11... | collective-permute-start | bytes 786440 | tf_op jit(solution)/shard_map/ppermute | solution.py:273
  68.6 2.0 %collective-permute-start.18 = (bf16[1,1,2,32,1024]{4,3,2,1,0:T(8,128)(2,1)S(1)}, bf16[1,1,2,32,1024]{4,3,2,1,0:T(8,128)(2,1)S(1)}, u32[]{:S(2)}, u32[]{:S(2)}) collective-permute-start(bf16[1,1,2,32,1024]{4,3,2,1,0:T(8,128)(2,1)S(1)} %copy-done.25), channel_id=1, source_target_pairs={{0,1},{1,0},{2,3},{3,2},{4,5},{5,4},{6,7},{7,6},{8,9},{9,8},{10,11... | collective-permute-start | bytes 393224 | tf_op jit(solution)/shard_map/ppermute | solution.py:273
  68.8 8.7 %collective-permute-start.14 = (bf16[1,2,2,32,1024]{4,3,2,1,0:T(8,128)(2,1)S(1)}, bf16[1,2,2,32,1024]{4,3,2,1,0:T(8,128)(2,1)}, u32[]{:S(2)}, u32[]{:S(2)}) collective-permute-start(bf16[1,2,2,32,1024]{4,3,2,1,0:T(8,128)(2,1)S(1)} %slice.29), channel_id=1, source_target_pairs={{0,2},{1,3},{2,0},{3,1},{4,6},{5,7},{6,4},{7,5},{8,10},{9,11},{10,... | collective-permute-start | bytes 786440 | tf_op jit(solution)/shard_map/ppermute | solution.py:273
  70.2 8.4 %collective-permute-start.13 = (bf16[1,2,2,32,1024]{4,3,2,1,0:T(8,128)(2,1)S(1)}, bf16[1,2,2,32,1024]{4,3,2,1,0:T(8,128)(2,1)}, u32[]{:S(2)}, u32[]{:S(2)}) collective-permute-start(bf16[1,2,2,32,1024]{4,3,2,1,0:T(8,128)(2,1)S(1)} %slice.28), channel_id=1, source_target_pairs={{0,4},{1,5},{2,6},{3,7},{4,0},{5,1},{6,2},{7,3},{8,12},{9,13},{10,... | collective-permute-start | bytes 786440 | tf_op jit(solution)/shard_map/ppermute | solution.py:273
  70.6 15.3 %collective-permute-start.25 = (bf16[2,2,2,32,1024]{4,3,2,1,0:T(8,128)(2,1)S(1)}, bf16[2,2,2,32,1024]{4,3,2,1,0:T(8,128)(2,1)}, u32[]{:S(2)}, u32[]{:S(2)}) collective-permute-start(bf16[2,2,2,32,1024]{4,3,2,1,0:T(8,128)(2,1)S(1)} %pad_maximum_fusion.refs_10_), channel_id=1, source_target_pairs={{0,1},{1,0},{2,3},{3,2},{4,5},{5,4},{6,7},{7,6},{8,9},{9,8},{10,11... | collective-permute-start | bytes 1572872 | tf_op jit(solution)/shard_map/ppermute | solution.py:273
  70.7 15.2 %collective-permute-start.27 = (bf16[2,2,2,32,1024]{4,3,2,1,0:T(8,128)(2,1)S(1)}, bf16[2,2,2,32,1024]{4,3,2,1,0:T(8,128)(2,1)S(1)}, u32[]{:S(2)}, u32[]{:S(2)}) collective-permute-start(bf16[2,2,2,32,1024]{4,3,2,1,0:T(8,128)(2,1)S(1)} %collective-permute-done.12.refs_12_), channel_id=1, source_target_pairs={{0,1},{1,0},{2,3},{3,2},{4,5},{5,4},{6,7},{7,6},{8,9},{9,8},{10,11... | collective-permute-start | bytes 1572872 | tf_op jit(solution)/shard_map/ppermute | solution.py:273
  71.3 14.6 %collective-permute-start.26 = (bf16[2,2,2,32,1024]{4,3,2,1,0:T(8,128)(2,1)S(1)}, bf16[2,2,2,32,1024]{4,3,2,1,0:T(8,128)(2,1)}, u32[]{:S(2)}, u32[]{:S(2)}) collective-permute-start(bf16[2,2,2,32,1024]{4,3,2,1,0:T(8,128)(2,1)S(1)} %collective-permute-done.11.refs_11_), channel_id=1, source_target_pairs={{0,1},{1,0},{2,3},{3,2},{4,5},{5,4},{6,7},{7,6},{8,9},{9,8},{10,11... | collective-permute-start | bytes 1572872 | tf_op jit(solution)/shard_map/ppermute | solution.py:273
  77.5 6.7 %collective-permute-start.22 = (bf16[2,1,2,32,1024]{4,3,2,1,0:T(8,128)(2,1)}, bf16[2,1,2,32,1024]{4,3,2,1,0:T(8,128)(2,1)}, u32[]{:S(2)}, u32[]{:S(2)}) collective-permute-start(bf16[2,1,2,32,1024]{4,3,2,1,0:T(8,128)(2,1)} %collective-permute-done.8.refs_7_), channel_id=1, source_target_pairs={{0,1},{1,0},{2,3},{3,2},{4,5},{5,4},{6,7},{7,6},{8,9},{9,8},{10,11... | collective-permute-start | bytes 786440 | tf_op jit(solution)/shard_map/ppermute | solution.py:273
  78.7 5.1 %collective-permute-start.24 = (bf16[1,1,2,32,1024]{4,3,2,1,0:T(8,128)(2,1)}, bf16[1,1,2,32,1024]{4,3,2,1,0:T(8,128)(2,1)S(1)}, u32[]{:S(2)}, u32[]{:S(2)}) collective-permute-start(bf16[1,1,2,32,1024]{4,3,2,1,0:T(8,128)(2,1)} %collective-permute-done.10.refs_9_), channel_id=1, source_target_pairs={{0,1},{1,0},{2,3},{3,2},{4,5},{5,4},{6,7},{7,6},{8,9},{9,8},{10,11... | collective-permute-start | bytes 393224 | tf_op jit(solution)/shard_map/ppermute | solution.py:273
  79.6 20.8 %all-to-all-start.2 = ((bf16[32,8,1024]{2,1,0:T(8,128)(2,1)}), bf16[32,8,1024]{2,1,0:T(8,128)(2,1)S(1)}, u32[]{:S(2)}, u32[]{:S(2)}) async-start(bf16[32,8,1024]{2,1,0:T(8,128)(2,1)} %bitcast.5), calls=%async_computation.2 | async-start | bytes 1048576 | tf_op jit(solution)/shard_map/all_to_all | solution.py:318
  83.9 2.0 %collective-permute-start.21 = (bf16[2,1,2,32,1024]{4,3,2,1,0:T(8,128)(2,1)S(1)}, bf16[2,1,2,32,1024]{4,3,2,1,0:T(8,128)(2,1)S(1)}, u32[]{:S(2)}, u32[]{:S(2)}) collective-permute-start(bf16[2,1,2,32,1024]{4,3,2,1,0:T(8,128)(2,1)S(1)} %copy-done.12), channel_id=1, source_target_pairs={{0,1},{1,0},{2,3},{3,2},{4,5},{5,4},{6,7},{7,6},{8,9},{9,8},{10,11... | collective-permute-start | bytes 786440 | tf_op jit(solution)/shard_map/ppermute | solution.py:273
  85.9 1.8 %collective-permute-start.28 = (bf16[1,2,2,32,1024]{4,3,2,1,0:T(8,128)(2,1)}, bf16[1,2,2,32,1024]{4,3,2,1,0:T(8,128)(2,1)S(1)}, u32[]{:S(2)}, u32[]{:S(2)}) collective-permute-start(bf16[1,2,2,32,1024]{4,3,2,1,0:T(8,128)(2,1)} %collective-permute-done.13.refs_13_), channel_id=1, source_target_pairs={{0,1},{1,0},{2,3},{3,2},{4,5},{5,4},{6,7},{7,6},{8,9},{9,8},{10,11... | collective-permute-start | bytes 786440 | tf_op jit(solution)/shard_map/ppermute | solution.py:273
  86.2 1.9 %collective-permute-start.29 = (bf16[1,2,2,32,1024]{4,3,2,1,0:T(8,128)(2,1)}, bf16[1,2,2,32,1024]{4,3,2,1,0:T(8,128)(2,1)S(1)}, u32[]{:S(2)}, u32[]{:S(2)}) collective-permute-start(bf16[1,2,2,32,1024]{4,3,2,1,0:T(8,128)(2,1)} %collective-permute-done.14.refs_14_), channel_id=1, source_target_pairs={{0,1},{1,0},{2,3},{3,2},{4,5},{5,4},{6,7},{7,6},{8,9},{9,8},{10,11... | collective-permute-start | bytes 786440 | tf_op jit(solution)/shard_map/ppermute | solution.py:273
  101.1 15.8 %all-to-all-start.1 = ((bf16[16,128,128]{2,1,0:T(8,128)(2,1)}), bf16[16,128,128]{2,1,0:T(8,128)(2,1)S(1)}, u32[]{:S(2)}, u32[]{:S(2)}) async-start(bf16[16,128,128]{2,1,0:T(8,128)(2,1)} %bitcast.18), calls=%async_computation.1 | async-start | bytes 1048576 | tf_op jit(solution)/shard_map/all_to_all | solution.py:318
  (31 other events, 396.5 us)

commit v12 on v11

--- a/solution.py
+++ b/solution.py
@@ -293,15 +293,16 @@
     for bit in range(3, bits):
         far += [source + (bit,) for source in far]
     came = [flip(own, *source) for source in far[1:]]
-    left, *rest = lax.optimization_barrier((packed[0], *came[1:]))
-    sets = [(own, ((),)), (came[0], tuple(far[1:2]))]
-    if rest:
-        sets.append((jnp.concatenate(rest, axis=1), tuple(far[2:])))
+    sets = [(own, ((),)), (jnp.concatenate(came[:2], axis=1), tuple(far[1:3]))]
+    if came[2:]:
+        sets.append((jnp.concatenate(came[2:], axis=1), tuple(far[3:])))
     blocks = []
     for number, (value, sources) in enumerate(sets):
         if number:
-            value, *_ = lax.optimization_barrier((value, *packed, blocks[-2][0], blocks[-1][0]))
+            tied = (*packed, blocks[3][0], blocks[4][0]) if number == 1 else (blocks[6][0], blocks[7][0])
+            value, *_ = lax.optimization_barrier((value, *tied))
         blocks += plane(value, sources)
+    left, *_ = lax.optimization_barrier((packed[0], *came[2:], blocks[8][0], blocks[9][0]))
     right, *_ = lax.optimization_barrier((packed[1], blocks[-2][0], blocks[-1][0]))
     last = len(blocks) - 2
     near = []

time: 136 us -> 126 us (0.926)
  waiting for transfers between devices: 46.9 us -> 33.3 us
  starting transfers between devices: 38.2 us -> 42.8 us
  local copies, waits for them, and re-layouts: 6.57 us -> 5.05 us
    ppermute x30, waiting for transfers between devices: 46.9 us -> 33.3 us  [flip(): return lax.ppermute(value, 'mode', pairs)]
    all_to_all x3, starting transfers between devices: 13.3 us -> 15.9 us  [trade(): lax.all_to_all(value, 'mode', split_axis=0, concat_axis=0, axis_index_gro...]
    ppermute x30, starting transfers between devices: 24.8 us -> 27 us  [flip(): return lax.ppermute(value, 'mode', pairs)]
    unnamed x60 -> x56, local copies, waits for them, and re-layouts: 4.97 us -> 4.36 us
  transfers between devices with their start and end apart: 33 -> 33, of which waited for: 10 -> 15; matrix products, arithmetic and copies ran while one was open for 1% -> 0% of each run, Pallas kernels for 19% -> 20%
where the time goes in v12:
time: 126 us; the launch traced here: 125 us
  starting transfers between devices  42.8 us (34%)
  waiting for transfers between devices  33.3 us (26%)
  Pallas kernels  26 us (21%)
  blocking collectives  16.4 us (13%)
  local copies, waits for them, and re-layouts  5.05 us (4%)
    ppermute x30, waiting for transfers between devices, flip(): return lax.ppermute(value, 'mode', pairs)  33.3 us
    ppermute x30, starting transfers between devices, flip(): return lax.ppermute(value, 'mode', pairs)  27 us
    pallas_call x4, Pallas kernels, call(): pl.pallas_call(kernel, out_shape=[out] * outputs if outputs else out, in_...  26 us
    all_to_all x1, blocking collectives, trade(): lax.all_to_all(value, 'mode', split_axis=0, concat_axis=0, axis_index_gro...  16.4 us
    all_to_all x3, starting transfers between devices, trade(): lax.all_to_all(value, 'mode', split_axis=0, concat_axis=0, axis_index_gro...  15.9 us
    unnamed x56, local copies, waits for them, and re-layouts  4.36 us
  transfers between devices with their start and end apart: 33, of which 15 were waited for; matrix products, arithmetic and copies ran while one was open for 0% of the time, Pallas kernels for 20%

profile of v12, /device:TPU:0, one launch (start us, length us, event | category | flops | bytes accessed | tf_op | source)
XLA Modules:
  0.0 125.1 jit_solution(17841590975917711047)
XLA Ops:
  0.0 1.1 maximum_bitcast_fusion.refs_0_
  1.1 3.0 %collective-permute-start.5 = (bf16[2,1,2,32,1024]{4,3,2,1,0:T(8,128)(2,1)S(1)}, bf16[2,1,2,32,1024]{4,3,2,1,0:T(8,128)(2,1)S(1)}, u32[]{:S(2)}, u32[]{:S(2)}) collective-permute-start(bf16[2,1,2,32,1024]{4,3,2,1,0:T(8,128)(2,1)S(1)} %maximum_bitcast_fusion.refs_0_), channel_id=1, source_target_pairs={{0,4},{1,5},{2,6},{3,7},{4,0},{5,1},{6,2},{7,3},{8,12},{9,13},{10,... | collective-permute-start | bytes 786440 | tf_op jit(solution)/shard_map/ppermute | solution.py:273
  4.1 1.5 %collective-permute-start.3 = (bf16[2,1,2,32,1024]{4,3,2,1,0:T(8,128)(2,1)S(1)}, bf16[2,1,2,32,1024]{4,3,2,1,0:T(8,128)(2,1)S(1)}, u32[]{:S(2)}, u32[]{:S(2)}) collective-permute-start(bf16[2,1,2,32,1024]{4,3,2,1,0:T(8,128)(2,1)S(1)} %maximum_bitcast_fusion.refs_0_), channel_id=1, source_target_pairs={{0,2},{1,3},{2,0},{3,1},{4,6},{5,7},{6,4},{7,5},{8,10},{9,11},{10,... | collective-permute-start | bytes 786440 | tf_op jit(solution)/shard_map/ppermute | solution.py:273
  5.6 2.6 %collective-permute-start.2 = (bf16[2,1,2,32,1024]{4,3,2,1,0:T(8,128)(2,1)S(1)}, bf16[2,1,2,32,1024]{4,3,2,1,0:T(8,128)(2,1)S(1)}, u32[]{:S(2)}, u32[]{:S(2)}) collective-permute-start(bf16[2,1,2,32,1024]{4,3,2,1,0:T(8,128)(2,1)S(1)} %maximum_bitcast_fusion.refs_0_), channel_id=1, source_target_pairs={{0,16},{1,17},{2,18},{3,19},{4,20},{5,21},{6,22},{7,23},{8,24},{9,... | collective-permute-start | bytes 786440 | tf_op jit(solution)/shard_map/ppermute | solution.py:273
  8.2 1.6 %collective-permute-start.1 = (bf16[2,1,2,32,1024]{4,3,2,1,0:T(8,128)(2,1)S(1)}, bf16[2,1,2,32,1024]{4,3,2,1,0:T(8,128)(2,1)S(1)}, u32[]{:S(2)}, u32[]{:S(2)}) collective-permute-start(bf16[2,1,2,32,1024]{4,3,2,1,0:T(8,128)(2,1)S(1)} %maximum_bitcast_fusion.refs_0_), channel_id=1, source_target_pairs={{0,8},{1,9},{2,10},{3,11},{4,12},{5,13},{6,14},{7,15},{8,0},{9,1},... | collective-permute-start | bytes 786440 | tf_op jit(solution)/shard_map/ppermute | solution.py:273
  9.8 0.6 collective-permute-done.5.refs_2_
  10.5 1.8 %collective-permute-start.6 = (bf16[1,1,2,32,1024]{4,3,2,1,0:T(8,128)(2,1)S(1)}, bf16[1,1,2,32,1024]{4,3,2,1,0:T(8,128)(2,1)S(1)}, u32[]{:S(2)}, u32[]{:S(2)}) collective-permute-start(bf16[1,1,2,32,1024]{4,3,2,1,0:T(8,128)(2,1)S(1)} %slice.25), channel_id=1, source_target_pairs={{0,2},{1,3},{2,0},{3,1},{4,6},{5,7},{6,4},{7,5},{8,10},{9,11},{10,... | collective-permute-start | bytes 393224 | tf_op jit(solution)/shard_map/ppermute | solution.py:273
  12.2 1.6 %collective-permute-start.4 = (bf16[1,1,2,32,1024]{4,3,2,1,0:T(8,128)(2,1)S(1)}, bf16[1,1,2,32,1024]{4,3,2,1,0:T(8,128)(2,1)S(1)}, u32[]{:S(2)}, u32[]{:S(2)}) collective-permute-start(bf16[1,1,2,32,1024]{4,3,2,1,0:T(8,128)(2,1)S(1)} %slice.24), channel_id=1, source_target_pairs={{0,4},{1,5},{2,6},{3,7},{4,0},{5,1},{6,2},{7,3},{8,12},{9,13},{10,... | collective-permute-start | bytes 393224 | tf_op jit(solution)/shard_map/ppermute | solution.py:273
  13.8 0.7 copy-done.2
  14.6 3.0 %shard_map.46 = (bf16[256,1024]{1,0:T(8,128)(2,1)}, bf16[256,1024]{1,0:T(8,128)(2,1)}) custom-call(bf16[4,2,64,1024]{3,2,1,0:T(8,128)(2,1)S(1)} %copy-done.1, s32[4,1024]{1,0:T(4,128)S(1)} %copy-done.2), custom_call_target="tpu_custom_call" | custom-call | flops 2147483648 | bytes 1064960 | tf_op jit(solution)/shard_map/pallas_call | solution.py:189
  17.6 2.1 %collective-permute-done.2 = bf16[2,1,2,32,1024]{4,3,2,1,0:T(8,128)(2,1)S(1)} collective-permute-done((bf16[2,1,2,32,1024]{4,3,2,1,0:T(8,128)(2,1)S(1)}, bf16[2,1,2,32,1024]{4,3,2,1,0:T(8,128)(2,1)S(1)}, u32[]{:S(2)}, u32[]{:S(2)}) %collective-permute-start.2) | collective-permute-done | bytes 262176 | tf_op jit(solution)/shard_map/ppermute | solution.py:273
  21.1 3.2 %collective-permute-start = (bf16[2,1,2,32,1024]{4,3,2,1,0:T(8,128)(2,1)S(1)}, bf16[2,1,2,32,1024]{4,3,2,1,0:T(8,128)(2,1)}, u32[]{:S(2)}, u32[]{:S(2)}) collective-permute-start(bf16[2,1,2,32,1024]{4,3,2,1,0:T(8,128)(2,1)S(1)} %maximum_bitcast_fusion.refs_0_), channel_id=1, source_target_pairs={{0,24},{1,25},{2,26},{3,27},{4,28},{5,29},{6,30},{7,31},{8,16},{9,... | collective-permute-start | bytes 786440 | tf_op jit(solution)/shard_map/ppermute | solution.py:273
  24.3 8.3 %collective-permute-done.9.refs_7_ = bf16[2,2,2,32,1024]{4,3,2,1,0:T(8,128)(2,1)S(1)} collective-permute-done((bf16[2,2,2,32,1024]{4,3,2,1,0:T(8,128)(2,1)S(1)}, bf16[2,2,2,32,1024]{4,3,2,1,0:T(8,128)(2,1)S(1)}, u32[]{:S(2)}, u32[]{:S(2)}) %collective-permute-start.9) | collective-permute-done | bytes 524320 | tf_op jit(solution)/shard_map/ppermute | solution.py:273
  33.3 1.8 %collective-permute-start.8 = (bf16[1,2,2,32,1024]{4,3,2,1,0:T(8,128)(2,1)S(1)}, bf16[1,2,2,32,1024]{4,3,2,1,0:T(8,128)(2,1)}, u32[]{:S(2)}, u32[]{:S(2)}) collective-permute-start(bf16[1,2,2,32,1024]{4,3,2,1,0:T(8,128)(2,1)S(1)} %slice.26), channel_id=1, source_target_pairs={{0,4},{1,5},{2,6},{3,7},{4,0},{5,1},{6,2},{7,3},{8,12},{9,13},{10,... | collective-permute-start | bytes 786440 | tf_op jit(solution)/shard_map/ppermute | solution.py:273
  35.1 4.1 %collective-permute-done.10.refs_9_ = bf16[1,2,2,32,1024]{4,3,2,1,0:T(8,128)(2,1)} collective-permute-done((bf16[1,2,2,32,1024]{4,3,2,1,0:T(8,128)(2,1)S(1)}, bf16[1,2,2,32,1024]{4,3,2,1,0:T(8,128)(2,1)}, u32[]{:S(2)}, u32[]{:S(2)}) %collective-permute-start.10) | collective-permute-done | bytes 262176 | tf_op jit(solution)/shard_map/ppermute | solution.py:273
  39.8 6.5 %all-to-all-start = ((bf16[32,8,1024]{2,1,0:T(8,128)(2,1)}), bf16[32,8,1024]{2,1,0:T(8,128)(2,1)S(1)}, u32[]{:S(2)}, u32[]{:S(2)}) async-start(bf16[32,8,1024]{2,1,0:T(8,128)(2,1)} %bitcast), calls=%async_computation | async-start | bytes 1048576 | tf_op jit(solution)/shard_map/all_to_all | solution.py:319
  46.7 1.7 %collective-permute-start.12 = (bf16[2,1,2,32,1024]{4,3,2,1,0:T(8,128)(2,1)}, bf16[2,1,2,32,1024]{4,3,2,1,0:T(8,128)(2,1)S(1)}, u32[]{:S(2)}, u32[]{:S(2)}) collective-permute-start(bf16[2,1,2,32,1024]{4,3,2,1,0:T(8,128)(2,1)} %collective-permute-done.refs_10_), channel_id=1, source_target_pairs={{0,4},{1,5},{2,6},{3,7},{4,0},{5,1},{6,2},{7,3},{8,12},{9,13},{10,... | collective-permute-start | bytes 786440 | tf_op jit(solution)/shard_map/ppermute | solution.py:273
  48.4 1.5 %collective-permute-start.11 = (bf16[2,1,2,32,1024]{4,3,2,1,0:T(8,128)(2,1)}, bf16[2,1,2,32,1024]{4,3,2,1,0:T(8,128)(2,1)S(1)}, u32[]{:S(2)}, u32[]{:S(2)}) collective-permute-start(bf16[2,1,2,32,1024]{4,3,2,1,0:T(8,128)(2,1)} %collective-permute-done.refs_10_), channel_id=1, source_target_pairs={{0,2},{1,3},{2,0},{3,1},{4,6},{5,7},{6,4},{7,5},{8,10},{9,11},{10,... | collective-permute-start | bytes 786440 | tf_op jit(solution)/shard_map/ppermute | solution.py:273
  50.5 9.6 %collective-permute-done.12.refs_12_ = bf16[2,1,2,32,1024]{4,3,2,1,0:T(8,128)(2,1)S(1)} collective-permute-done((bf16[2,1,2,32,1024]{4,3,2,1,0:T(8,128)(2,1)}, bf16[2,1,2,32,1024]{4,3,2,1,0:T(8,128)(2,1)S(1)}, u32[]{:S(2)}, u32[]{:S(2)}) %collective-permute-start.12) | collective-permute-done | bytes 262176 | tf_op jit(solution)/shard_map/ppermute | solution.py:273
  61.6 1.3 %collective-permute-start.14 = (bf16[1,1,2,32,1024]{4,3,2,1,0:T(8,128)(2,1)S(1)}, bf16[1,1,2,32,1024]{4,3,2,1,0:T(8,128)(2,1)S(1)}, u32[]{:S(2)}, u32[]{:S(2)}) collective-permute-start(bf16[1,1,2,32,1024]{4,3,2,1,0:T(8,128)(2,1)S(1)} %slice.29), channel_id=1, source_target_pairs={{0,2},{1,3},{2,0},{3,1},{4,6},{5,7},{6,4},{7,5},{8,10},{9,11},{10,... | collective-permute-start | bytes 393224 | tf_op jit(solution)/shard_map/ppermute | solution.py:273
  63.9 3.3 %collective-permute-done.14.refs_14_ = bf16[1,1,2,32,1024]{4,3,2,1,0:T(8,128)(2,1)S(1)} collective-permute-done((bf16[1,1,2,32,1024]{4,3,2,1,0:T(8,128)(2,1)S(1)}, bf16[1,1,2,32,1024]{4,3,2,1,0:T(8,128)(2,1)S(1)}, u32[]{:S(2)}, u32[]{:S(2)}) %collective-permute-start.14) | collective-permute-done | bytes 131104 | tf_op jit(solution)/shard_map/ppermute | solution.py:273
  67.2 1.1 collective-permute-done.13.refs_13_
  68.4 0.8 copy-done.4
  69.2 4.3 %all-to-all-start.2 = ((bf16[32,8,1024]{2,1,0:T(8,128)(2,1)}), bf16[32,8,1024]{2,1,0:T(8,128)(2,1)S(1)}, u32[]{:S(2)}, u32[]{:S(2)}) async-start(bf16[32,8,1024]{2,1,0:T(8,128)(2,1)} %bitcast.4), calls=%async_computation.2 | async-start | bytes 1048576 | tf_op jit(solution)/shard_map/all_to_all | solution.py:319
  74.5 0.9 collective-permute-done.23.refs_23_
  76.4 1.0 collective-permute-done.28.refs_28_
  78.2 11.5 %shard_map.47 = bf16[2048,128]{1,0:T(8,128)(2,1)} custom-call(bf16[256,1024]{1,0:T(8,128)(2,1)} %bitcast.16, bf16[2,1,2,32,1024]{4,3,2,1,0:T(8,128)(2,1)} %copy-done.6, bf16[2,1,2,32,1024]{4,3,2,1,0:T(8,128)(2,1)} %copy-done.10, bf16[2,1,2,32,1024]{4,3,2,1,0:T(8,128)(2,1)} %copy-done.9, bf16[1,1,2,32,1024]{4,3,2,1,0:T(8,128)(2,1)} %copy-done.23, ...), custom_call_target="tpu_custom_call" | custom-call | flops 4294967296 | bytes 8912896 | tf_op jit(solution)/shard_map/pallas_call | solution.py:189
  89.7 0.8 copy-done.5
  90.6 5.0 %all-to-all-start.1 = ((bf16[16,128,128]{2,1,0:T(8,128)(2,1)}), bf16[16,128,128]{2,1,0:T(8,128)(2,1)S(1)}, u32[]{:S(2)}, u32[]{:S(2)}) async-start(bf16[16,128,128]{2,1,0:T(8,128)(2,1)} %bitcast.18), calls=%async_computation.1 | async-start | bytes 1048576 | tf_op jit(solution)/shard_map/all_to_all | solution.py:319
  95.5 10.8 %shard_map.48.right_ref = bf16[256,1024]{1,0:T(8,128)(2,1)} custom-call(bf16[256,1024]{1,0:T(8,128)(2,1)} %bitcast.17, bf16[2,1,2,32,1024]{4,3,2,1,0:T(8,128)(2,1)} %copy-done.6, bf16[2,1,2,32,1024]{4,3,2,1,0:T(8,128)(2,1)} %copy-done.10, bf16[2,1,2,32,1024]{4,3,2,1,0:T(8,128)(2,1)} %copy-done.9, bf16[1,1,2,32,1024]{4,3,2,1,0:T(8,128)(2,1)} %copy-done.23, ...), custom_call_target="tpu_custom_call" | custom-call | flops 4294967296 | bytes 8912896 | tf_op jit(solution)/shard_map/pallas_call | solution.py:189
  106.4 1.0 copy-done
  108.0 16.4 %all_to_all.20 = bf16[32,16,256]{2,1,0:T(8,128)(2,1)S(1)} all-to-all(bf16[32,16,256]{2,1,0:T(8,128)(2,1)S(1)} %bitcast.15), channel_id=1, replica_groups=mesh['cuts'=1,'mode'=32] {'mode'}, dimensions={0} | all-to-all | bytes 524288 | tf_op jit(solution)/shard_map/all_to_all | solution.py:319
  (106 shorter events, 10.0 us)
Async XLA Ops:
  1.1 9.3 %collective-permute-start.5 = (bf16[2,1,2,32,1024]{4,3,2,1,0:T(8,128)(2,1)S(1)}, bf16[2,1,2,32,1024]{4,3,2,1,0:T(8,128)(2,1)S(1)}, u32[]{:S(2)}, u32[]{:S(2)}) collective-permute-start(bf16[2,1,2,32,1024]{4,3,2,1,0:T(8,128)(2,1)S(1)} %maximum_bitcast_fusion.refs_0_), channel_id=1, source_target_pairs={{0,4},{1,5},{2,6},{3,7},{4,0},{5,1},{6,2},{7,3},{8,12},{9,13},{10,... | collective-permute-start | bytes 786440 | tf_op jit(solution)/shard_map/ppermute | solution.py:273
  4.1 8.1 %collective-permute-start.3 = (bf16[2,1,2,32,1024]{4,3,2,1,0:T(8,128)(2,1)S(1)}, bf16[2,1,2,32,1024]{4,3,2,1,0:T(8,128)(2,1)S(1)}, u32[]{:S(2)}, u32[]{:S(2)}) collective-permute-start(bf16[2,1,2,32,1024]{4,3,2,1,0:T(8,128)(2,1)S(1)} %maximum_bitcast_fusion.refs_0_), channel_id=1, source_target_pairs={{0,2},{1,3},{2,0},{3,1},{4,6},{5,7},{6,4},{7,5},{8,10},{9,11},{10,... | collective-permute-start | bytes 786440 | tf_op jit(solution)/shard_map/ppermute | solution.py:273
  5.6 14.1 %collective-permute-start.2 = (bf16[2,1,2,32,1024]{4,3,2,1,0:T(8,128)(2,1)S(1)}, bf16[2,1,2,32,1024]{4,3,2,1,0:T(8,128)(2,1)S(1)}, u32[]{:S(2)}, u32[]{:S(2)}) collective-permute-start(bf16[2,1,2,32,1024]{4,3,2,1,0:T(8,128)(2,1)S(1)} %maximum_bitcast_fusion.refs_0_), channel_id=1, source_target_pairs={{0,16},{1,17},{2,18},{3,19},{4,20},{5,21},{6,22},{7,23},{8,24},{9,... | collective-permute-start | bytes 786440 | tf_op jit(solution)/shard_map/ppermute | solution.py:273
  8.2 11.7 %collective-permute-start.1 = (bf16[2,1,2,32,1024]{4,3,2,1,0:T(8,128)(2,1)S(1)}, bf16[2,1,2,32,1024]{4,3,2,1,0:T(8,128)(2,1)S(1)}, u32[]{:S(2)}, u32[]{:S(2)}) collective-permute-start(bf16[2,1,2,32,1024]{4,3,2,1,0:T(8,128)(2,1)S(1)} %maximum_bitcast_fusion.refs_0_), channel_id=1, source_target_pairs={{0,8},{1,9},{2,10},{3,11},{4,12},{5,13},{6,14},{7,15},{8,0},{9,1},... | collective-permute-start | bytes 786440 | tf_op jit(solution)/shard_map/ppermute | solution.py:273
  10.5 9.5 %collective-permute-start.6 = (bf16[1,1,2,32,1024]{4,3,2,1,0:T(8,128)(2,1)S(1)}, bf16[1,1,2,32,1024]{4,3,2,1,0:T(8,128)(2,1)S(1)}, u32[]{:S(2)}, u32[]{:S(2)}) collective-permute-start(bf16[1,1,2,32,1024]{4,3,2,1,0:T(8,128)(2,1)S(1)} %slice.25), channel_id=1, source_target_pairs={{0,2},{1,3},{2,0},{3,1},{4,6},{5,7},{6,4},{7,5},{8,10},{9,11},{10,... | collective-permute-start | bytes 393224 | tf_op jit(solution)/shard_map/ppermute | solution.py:273
  12.2 7.8 %collective-permute-start.4 = (bf16[1,1,2,32,1024]{4,3,2,1,0:T(8,128)(2,1)S(1)}, bf16[1,1,2,32,1024]{4,3,2,1,0:T(8,128)(2,1)S(1)}, u32[]{:S(2)}, u32[]{:S(2)}) collective-permute-start(bf16[1,1,2,32,1024]{4,3,2,1,0:T(8,128)(2,1)S(1)} %slice.24), channel_id=1, source_target_pairs={{0,4},{1,5},{2,6},{3,7},{4,0},{5,1},{6,2},{7,3},{8,12},{9,13},{10,... | collective-permute-start | bytes 393224 | tf_op jit(solution)/shard_map/ppermute | solution.py:273
  20.0 12.6 %collective-permute-start.9 = (bf16[2,2,2,32,1024]{4,3,2,1,0:T(8,128)(2,1)S(1)}, bf16[2,2,2,32,1024]{4,3,2,1,0:T(8,128)(2,1)S(1)}, u32[]{:S(2)}, u32[]{:S(2)}) collective-permute-start(bf16[2,2,2,32,1024]{4,3,2,1,0:T(8,128)(2,1)S(1)} %pad_maximum_fusion.refs_5_), channel_id=1, source_target_pairs={{0,4},{1,5},{2,6},{3,7},{4,0},{5,1},{6,2},{7,3},{8,12},{9,13},{10,... | collective-permute-start | bytes 1572872 | tf_op jit(solution)/shard_map/ppermute | solution.py:273
  20.6 12.6 %collective-permute-start.7 = (bf16[2,2,2,32,1024]{4,3,2,1,0:T(8,128)(2,1)S(1)}, bf16[2,2,2,32,1024]{4,3,2,1,0:T(8,128)(2,1)S(1)}, u32[]{:S(2)}, u32[]{:S(2)}) collective-permute-start(bf16[2,2,2,32,1024]{4,3,2,1,0:T(8,128)(2,1)S(1)} %pad_maximum_fusion.refs_5_), channel_id=1, source_target_pairs={{0,2},{1,3},{2,0},{3,1},{4,6},{5,7},{6,4},{7,5},{8,10},{9,11},{10,... | collective-permute-start | bytes 1572872 | tf_op jit(solution)/shard_map/ppermute | solution.py:273
  21.1 14.0 %collective-permute-start = (bf16[2,1,2,32,1024]{4,3,2,1,0:T(8,128)(2,1)S(1)}, bf16[2,1,2,32,1024]{4,3,2,1,0:T(8,128)(2,1)}, u32[]{:S(2)}, u32[]{:S(2)}) collective-permute-start(bf16[2,1,2,32,1024]{4,3,2,1,0:T(8,128)(2,1)S(1)} %maximum_bitcast_fusion.refs_0_), channel_id=1, source_target_pairs={{0,24},{1,25},{2,26},{3,27},{4,28},{5,29},{6,30},{7,31},{8,16},{9,... | collective-permute-start | bytes 786440 | tf_op jit(solution)/shard_map/ppermute | solution.py:273
  32.6 6.5 %collective-permute-start.10 = (bf16[1,2,2,32,1024]{4,3,2,1,0:T(8,128)(2,1)S(1)}, bf16[1,2,2,32,1024]{4,3,2,1,0:T(8,128)(2,1)}, u32[]{:S(2)}, u32[]{:S(2)}) collective-permute-start(bf16[1,2,2,32,1024]{4,3,2,1,0:T(8,128)(2,1)S(1)} %slice.27), channel_id=1, source_target_pairs={{0,2},{1,3},{2,0},{3,1},{4,6},{5,7},{6,4},{7,5},{8,10},{9,11},{10,... | collective-permute-start | bytes 786440 | tf_op jit(solution)/shard_map/ppermute | solution.py:273
  33.3 6.5 %collective-permute-start.8 = (bf16[1,2,2,32,1024]{4,3,2,1,0:T(8,128)(2,1)S(1)}, bf16[1,2,2,32,1024]{4,3,2,1,0:T(8,128)(2,1)}, u32[]{:S(2)}, u32[]{:S(2)}) collective-permute-start(bf16[1,2,2,32,1024]{4,3,2,1,0:T(8,128)(2,1)S(1)} %slice.26), channel_id=1, source_target_pairs={{0,4},{1,5},{2,6},{3,7},{4,0},{5,1},{6,2},{7,3},{8,12},{9,13},{10,... | collective-permute-start | bytes 786440 | tf_op jit(solution)/shard_map/ppermute | solution.py:273
  39.8 28.6 %all-to-all-start = ((bf16[32,8,1024]{2,1,0:T(8,128)(2,1)}), bf16[32,8,1024]{2,1,0:T(8,128)(2,1)S(1)}, u32[]{:S(2)}, u32[]{:S(2)}) async-start(bf16[32,8,1024]{2,1,0:T(8,128)(2,1)} %bitcast), calls=%async_computation | async-start | bytes 1048576 | tf_op jit(solution)/shard_map/all_to_all | solution.py:319
  46.4 4.0 %collective-permute-start.15 = (bf16[2,1,2,32,1024]{4,3,2,1,0:T(8,128)(2,1)S(1)}, bf16[2,1,2,32,1024]{4,3,2,1,0:T(8,128)(2,1)S(1)}, u32[]{:S(2)}, u32[]{:S(2)}) collective-permute-start(bf16[2,1,2,32,1024]{4,3,2,1,0:T(8,128)(2,1)S(1)} %maximum_bitcast_fusion.refs_0_), channel_id=1, source_target_pairs={{0,1},{1,0},{2,3},{3,2},{4,5},{5,4},{6,7},{7,6},{8,9},{9,8},{10,11... | collective-permute-start | bytes 786440 | tf_op jit(solution)/shard_map/ppermute | solution.py:273
  46.7 13.4 %collective-permute-start.12 = (bf16[2,1,2,32,1024]{4,3,2,1,0:T(8,128)(2,1)}, bf16[2,1,2,32,1024]{4,3,2,1,0:T(8,128)(2,1)S(1)}, u32[]{:S(2)}, u32[]{:S(2)}) collective-permute-start(bf16[2,1,2,32,1024]{4,3,2,1,0:T(8,128)(2,1)} %collective-permute-done.refs_10_), channel_id=1, source_target_pairs={{0,4},{1,5},{2,6},{3,7},{4,0},{5,1},{6,2},{7,3},{8,12},{9,13},{10,... | collective-permute-start | bytes 786440 | tf_op jit(solution)/shard_map/ppermute | solution.py:273
  48.4 11.9 %collective-permute-start.11 = (bf16[2,1,2,32,1024]{4,3,2,1,0:T(8,128)(2,1)}, bf16[2,1,2,32,1024]{4,3,2,1,0:T(8,128)(2,1)S(1)}, u32[]{:S(2)}, u32[]{:S(2)}) collective-permute-start(bf16[2,1,2,32,1024]{4,3,2,1,0:T(8,128)(2,1)} %collective-permute-done.refs_10_), channel_id=1, source_target_pairs={{0,2},{1,3},{2,0},{3,1},{4,6},{5,7},{6,4},{7,5},{8,10},{9,11},{10,... | collective-permute-start | bytes 786440 | tf_op jit(solution)/shard_map/ppermute | solution.py:273
  49.8 13.0 %collective-permute-start.17 = (bf16[2,1,2,32,1024]{4,3,2,1,0:T(8,128)(2,1)S(1)}, bf16[2,1,2,32,1024]{4,3,2,1,0:T(8,128)(2,1)S(1)}, u32[]{:S(2)}, u32[]{:S(2)}) collective-permute-start(bf16[2,1,2,32,1024]{4,3,2,1,0:T(8,128)(2,1)S(1)} %collective-permute-done.5.refs_2_), channel_id=1, source_target_pairs={{0,1},{1,0},{2,3},{3,2},{4,5},{5,4},{6,7},{7,6},{8,9},{9,8},{10,11... | collective-permute-start | bytes 786440 | tf_op jit(solution)/shard_map/ppermute | solution.py:273
  49.8 13.5 %collective-permute-start.16 = (bf16[2,1,2,32,1024]{4,3,2,1,0:T(8,128)(2,1)S(1)}, bf16[2,1,2,32,1024]{4,3,2,1,0:T(8,128)(2,1)S(1)}, u32[]{:S(2)}, u32[]{:S(2)}) collective-permute-start(bf16[2,1,2,32,1024]{4,3,2,1,0:T(8,128)(2,1)S(1)} %collective-permute-done.3.refs_1_), channel_id=1, source_target_pairs={{0,1},{1,0},{2,3},{3,2},{4,5},{5,4},{6,7},{7,6},{8,9},{9,8},{10,11... | collective-permute-start | bytes 786440 | tf_op jit(solution)/shard_map/ppermute | solution.py:273
  50.4 23.2 %collective-permute-start.20 = (bf16[2,2,2,32,1024]{4,3,2,1,0:T(8,128)(2,1)S(1)}, bf16[2,2,2,32,1024]{4,3,2,1,0:T(8,128)(2,1)}, u32[]{:S(2)}, u32[]{:S(2)}) collective-permute-start(bf16[2,2,2,32,1024]{4,3,2,1,0:T(8,128)(2,1)S(1)} %pad_maximum_fusion.refs_5_), channel_id=1, source_target_pairs={{0,1},{1,0},{2,3},{3,2},{4,5},{5,4},{6,7},{7,6},{8,9},{9,8},{10,11... | collective-permute-start | bytes 1572872 | tf_op jit(solution)/shard_map/ppermute | solution.py:273
  60.1 1.5 %collective-permute-start.19 = (bf16[1,1,2,32,1024]{4,3,2,1,0:T(8,128)(2,1)S(1)}, bf16[1,1,2,32,1024]{4,3,2,1,0:T(8,128)(2,1)}, u32[]{:S(2)}, u32[]{:S(2)}) collective-permute-start(bf16[1,1,2,32,1024]{4,3,2,1,0:T(8,128)(2,1)S(1)} %collective-permute-done.6.refs_4_), channel_id=1, source_target_pairs={{0,1},{1,0},{2,3},{3,2},{4,5},{5,4},{6,7},{7,6},{8,9},{9,8},{10,11... | collective-permute-start | bytes 393224 | tf_op jit(solution)/shard_map/ppermute | solution.py:273
  60.3 3.0 %collective-permute-start.18 = (bf16[1,1,2,32,1024]{4,3,2,1,0:T(8,128)(2,1)S(1)}, bf16[1,1,2,32,1024]{4,3,2,1,0:T(8,128)(2,1)S(1)}, u32[]{:S(2)}, u32[]{:S(2)}) collective-permute-start(bf16[1,1,2,32,1024]{4,3,2,1,0:T(8,128)(2,1)S(1)} %collective-permute-done.4.refs_3_), channel_id=1, source_target_pairs={{0,1},{1,0},{2,3},{3,2},{4,5},{5,4},{6,7},{7,6},{8,9},{9,8},{10,11... | collective-permute-start | bytes 393224 | tf_op jit(solution)/shard_map/ppermute | solution.py:273
  61.6 5.6 %collective-permute-start.14 = (bf16[1,1,2,32,1024]{4,3,2,1,0:T(8,128)(2,1)S(1)}, bf16[1,1,2,32,1024]{4,3,2,1,0:T(8,128)(2,1)S(1)}, u32[]{:S(2)}, u32[]{:S(2)}) collective-permute-start(bf16[1,1,2,32,1024]{4,3,2,1,0:T(8,128)(2,1)S(1)} %slice.29), channel_id=1, source_target_pairs={{0,2},{1,3},{2,0},{3,1},{4,6},{5,7},{6,4},{7,5},{8,10},{9,11},{10,... | collective-permute-start | bytes 393224 | tf_op jit(solution)/shard_map/ppermute | solution.py:273
  62.9 5.4 %collective-permute-start.13 = (bf16[1,1,2,32,1024]{4,3,2,1,0:T(8,128)(2,1)S(1)}, bf16[1,1,2,32,1024]{4,3,2,1,0:T(8,128)(2,1)}, u32[]{:S(2)}, u32[]{:S(2)}) collective-permute-start(bf16[1,1,2,32,1024]{4,3,2,1,0:T(8,128)(2,1)S(1)} %slice.28), channel_id=1, source_target_pairs={{0,4},{1,5},{2,6},{3,7},{4,0},{5,1},{6,2},{7,3},{8,12},{9,13},{10,... | collective-permute-start | bytes 393224 | tf_op jit(solution)/shard_map/ppermute | solution.py:273
  63.3 10.6 %collective-permute-start.25 = (bf16[2,1,2,32,1024]{4,3,2,1,0:T(8,128)(2,1)}, bf16[2,1,2,32,1024]{4,3,2,1,0:T(8,128)(2,1)}, u32[]{:S(2)}, u32[]{:S(2)}) collective-permute-start(bf16[2,1,2,32,1024]{4,3,2,1,0:T(8,128)(2,1)} %collective-permute-done.refs_10_), channel_id=1, source_target_pairs={{0,1},{1,0},{2,3},{3,2},{4,5},{5,4},{6,7},{7,6},{8,9},{9,8},{10,11... | collective-permute-start | bytes 786440 | tf_op jit(solution)/shard_map/ppermute | solution.py:273
  63.3 11.1 %collective-permute-start.22 = (bf16[2,2,2,32,1024]{4,3,2,1,0:T(8,128)(2,1)S(1)}, bf16[2,2,2,32,1024]{4,3,2,1,0:T(8,128)(2,1)}, u32[]{:S(2)}, u32[]{:S(2)}) collective-permute-start(bf16[2,2,2,32,1024]{4,3,2,1,0:T(8,128)(2,1)S(1)} %collective-permute-done.9.refs_7_), channel_id=1, source_target_pairs={{0,1},{1,0},{2,3},{3,2},{4,5},{5,4},{6,7},{7,6},{8,9},{9,8},{10,11... | collective-permute-start | bytes 1572872 | tf_op jit(solution)/shard_map/ppermute | solution.py:273
  67.2 7.0 %collective-permute-start.24 = (bf16[1,2,2,32,1024]{4,3,2,1,0:T(8,128)(2,1)}, bf16[1,2,2,32,1024]{4,3,2,1,0:T(8,128)(2,1)S(1)}, u32[]{:S(2)}, u32[]{:S(2)}) collective-permute-start(bf16[1,2,2,32,1024]{4,3,2,1,0:T(8,128)(2,1)} %collective-permute-done.10.refs_9_), channel_id=1, source_target_pairs={{0,1},{1,0},{2,3},{3,2},{4,5},{5,4},{6,7},{7,6},{8,9},{9,8},{10,11... | collective-permute-start | bytes 786440 | tf_op jit(solution)/shard_map/ppermute | solution.py:273
  68.3 7.6 %collective-permute-start.21 = (bf16[2,2,2,32,1024]{4,3,2,1,0:T(8,128)(2,1)S(1)}, bf16[2,2,2,32,1024]{4,3,2,1,0:T(8,128)(2,1)}, u32[]{:S(2)}, u32[]{:S(2)}) collective-permute-start(bf16[2,2,2,32,1024]{4,3,2,1,0:T(8,128)(2,1)S(1)} %collective-permute-done.7.refs_6_), channel_id=1, source_target_pairs={{0,1},{1,0},{2,3},{3,2},{4,5},{5,4},{6,7},{7,6},{8,9},{9,8},{10,11... | collective-permute-start | bytes 1572872 | tf_op jit(solution)/shard_map/ppermute | solution.py:273
  69.2 20.5 %all-to-all-start.2 = ((bf16[32,8,1024]{2,1,0:T(8,128)(2,1)}), bf16[32,8,1024]{2,1,0:T(8,128)(2,1)S(1)}, u32[]{:S(2)}, u32[]{:S(2)}) async-start(bf16[32,8,1024]{2,1,0:T(8,128)(2,1)} %bitcast.4), calls=%async_computation.2 | async-start | bytes 1048576 | tf_op jit(solution)/shard_map/all_to_all | solution.py:319
  73.6 1.8 %collective-permute-start.23 = (bf16[1,2,2,32,1024]{4,3,2,1,0:T(8,128)(2,1)}, bf16[1,2,2,32,1024]{4,3,2,1,0:T(8,128)(2,1)S(1)}, u32[]{:S(2)}, u32[]{:S(2)}) collective-permute-start(bf16[1,2,2,32,1024]{4,3,2,1,0:T(8,128)(2,1)} %collective-permute-done.8.refs_8_), channel_id=1, source_target_pairs={{0,1},{1,0},{2,3},{3,2},{4,5},{5,4},{6,7},{7,6},{8,9},{9,8},{10,11... | collective-permute-start | bytes 786440 | tf_op jit(solution)/shard_map/ppermute | solution.py:273
  73.9 1.7 %collective-permute-start.27 = (bf16[2,1,2,32,1024]{4,3,2,1,0:T(8,128)(2,1)S(1)}, bf16[2,1,2,32,1024]{4,3,2,1,0:T(8,128)(2,1)S(1)}, u32[]{:S(2)}, u32[]{:S(2)}) collective-permute-start(bf16[2,1,2,32,1024]{4,3,2,1,0:T(8,128)(2,1)S(1)} %copy-done.12), channel_id=1, source_target_pairs={{0,1},{1,0},{2,3},{3,2},{4,5},{5,4},{6,7},{7,6},{8,9},{9,8},{10,11... | collective-permute-start | bytes 786440 | tf_op jit(solution)/shard_map/ppermute | solution.py:273
  74.1 1.8 %collective-permute-start.26 = (bf16[2,1,2,32,1024]{4,3,2,1,0:T(8,128)(2,1)S(1)}, bf16[2,1,2,32,1024]{4,3,2,1,0:T(8,128)(2,1)S(1)}, u32[]{:S(2)}, u32[]{:S(2)}) collective-permute-start(bf16[2,1,2,32,1024]{4,3,2,1,0:T(8,128)(2,1)S(1)} %copy-done.14), channel_id=1, source_target_pairs={{0,1},{1,0},{2,3},{3,2},{4,5},{5,4},{6,7},{7,6},{8,9},{9,8},{10,11... | collective-permute-start | bytes 786440 | tf_op jit(solution)/shard_map/ppermute | solution.py:273
  75.9 1.6 %collective-permute-start.28 = (bf16[1,1,2,32,1024]{4,3,2,1,0:T(8,128)(2,1)}, bf16[1,1,2,32,1024]{4,3,2,1,0:T(8,128)(2,1)S(1)}, u32[]{:S(2)}, u32[]{:S(2)}) collective-permute-start(bf16[1,1,2,32,1024]{4,3,2,1,0:T(8,128)(2,1)} %collective-permute-done.13.refs_13_), channel_id=1, source_target_pairs={{0,1},{1,0},{2,3},{3,2},{4,5},{5,4},{6,7},{7,6},{8,9},{9,8},{10,11... | collective-permute-start | bytes 393224 | tf_op jit(solution)/shard_map/ppermute | solution.py:273
  90.6 15.8 %all-to-all-start.1 = ((bf16[16,128,128]{2,1,0:T(8,128)(2,1)}), bf16[16,128,128]{2,1,0:T(8,128)(2,1)S(1)}, u32[]{:S(2)}, u32[]{:S(2)}) async-start(bf16[16,128,128]{2,1,0:T(8,128)(2,1)} %bitcast.18), calls=%async_computation.1 | async-start | bytes 1048576 | tf_op jit(solution)/shard_map/all_to_all | solution.py:319
  (29 other events, 387.2 us)

commit v13 on v12

--- a/solution.py
+++ b/solution.py
@@ -302,7 +302,7 @@
             tied = (*packed, blocks[3][0], blocks[4][0]) if number == 1 else (blocks[6][0], blocks[7][0])
             value, *_ = lax.optimization_barrier((value, *tied))
         blocks += plane(value, sources)
-    left, *_ = lax.optimization_barrier((packed[0], *came[2:], blocks[8][0], blocks[9][0]))
+    left, *_ = lax.optimization_barrier((packed[0], blocks[8][0], blocks[9][0], blocks[-4][0], blocks[-3][0]))
     right, *_ = lax.optimization_barrier((packed[1], blocks[-2][0], blocks[-1][0]))
     last = len(blocks) - 2
     near = []

time: 126 us -> 124 us (0.984)
  waiting for transfers between devices: 33.3 us -> 30.8 us
  local copies, waits for them, and re-layouts: 5.05 us -> 6.85 us
    ppermute x30, waiting for transfers between devices: 33.3 us -> 27.7 us  [flip(): return lax.ppermute(value, 'mode', pairs)]
    all_to_all x3, waiting for transfers between devices: 0.01 us -> 3.04 us  [trade(): lax.all_to_all(value, 'mode', split_axis=0, concat_axis=0, axis_index_gro...]
    unnamed x56 -> x62, local copies, waits for them, and re-layouts: 4.36 us -> 6.16 us
  transfers between devices with their start and end apart: 33 -> 33, of which waited for: 15 -> 17; matrix products, arithmetic and copies ran while one was open for 0% -> 0% of each run, Pallas kernels for 20% -> 21%
where the time goes in v13:
time: 124 us
  starting transfers between devices  42.2 us (34%)
  waiting for transfers between devices  30.8 us (25%)
  Pallas kernels  25.9 us (21%)
  blocking collectives  16.4 us (13%)
  local copies, waits for them, and re-layouts  6.85 us (6%)
    ppermute x30, waiting for transfers between devices, flip(): return lax.ppermute(value, 'mode', pairs)  27.7 us
    ppermute x30, starting transfers between devices, flip(): return lax.ppermute(value, 'mode', pairs)  27.1 us
    pallas_call x4, Pallas kernels, call(): pl.pallas_call(kernel, out_shape=[out] * outputs if outputs else out, in_...  25.9 us
    all_to_all x1, blocking collectives, trade(): lax.all_to_all(value, 'mode', split_axis=0, concat_axis=0, axis_index_gro...  16.4 us
    all_to_all x3, starting transfers between devices, trade(): lax.all_to_all(value, 'mode', split_axis=0, concat_axis=0, axis_index_gro...  15.1 us
    unnamed x62, local copies, waits for them, and re-layouts  6.16 us
    all_to_all x3, waiting for transfers between devices, trade(): lax.all_to_all(value, 'mode', split_axis=0, concat_axis=0, axis_index_gro...  3.04 us
  transfers between devices with their start and end apart: 33, of which 17 were waited for; matrix products, arithmetic and copies ran while one was open for 0% of the time, Pallas kernels for 21%

profile of v13, /device:TPU:0, one launch (start us, length us, event | category | flops | bytes accessed | tf_op | source)
XLA Modules:
  0.0 123.6 jit_solution(13916990679524161445)
XLA Ops:
  0.0 1.1 maximum_bitcast_fusion.refs_0_
  1.1 3.0 %collective-permute-start.4 = (bf16[2,1,2,32,1024]{4,3,2,1,0:T(8,128)(2,1)S(1)}, bf16[2,1,2,32,1024]{4,3,2,1,0:T(8,128)(2,1)S(1)}, u32[]{:S(2)}, u32[]{:S(2)}) collective-permute-start(bf16[2,1,2,32,1024]{4,3,2,1,0:T(8,128)(2,1)S(1)} %maximum_bitcast_fusion.refs_0_), channel_id=1, source_target_pairs={{0,4},{1,5},{2,6},{3,7},{4,0},{5,1},{6,2},{7,3},{8,12},{9,13},{10,... | collective-permute-start | bytes 786440 | tf_op jit(solution)/shard_map/ppermute | solution.py:273
  4.1 1.5 %collective-permute-start.2 = (bf16[2,1,2,32,1024]{4,3,2,1,0:T(8,128)(2,1)S(1)}, bf16[2,1,2,32,1024]{4,3,2,1,0:T(8,128)(2,1)S(1)}, u32[]{:S(2)}, u32[]{:S(2)}) collective-permute-start(bf16[2,1,2,32,1024]{4,3,2,1,0:T(8,128)(2,1)S(1)} %maximum_bitcast_fusion.refs_0_), channel_id=1, source_target_pairs={{0,2},{1,3},{2,0},{3,1},{4,6},{5,7},{6,4},{7,5},{8,10},{9,11},{10,... | collective-permute-start | bytes 786440 | tf_op jit(solution)/shard_map/ppermute | solution.py:273
  5.6 2.6 %collective-permute-start.1 = (bf16[2,1,2,32,1024]{4,3,2,1,0:T(8,128)(2,1)S(1)}, bf16[2,1,2,32,1024]{4,3,2,1,0:T(8,128)(2,1)S(1)}, u32[]{:S(2)}, u32[]{:S(2)}) collective-permute-start(bf16[2,1,2,32,1024]{4,3,2,1,0:T(8,128)(2,1)S(1)} %maximum_bitcast_fusion.refs_0_), channel_id=1, source_target_pairs={{0,16},{1,17},{2,18},{3,19},{4,20},{5,21},{6,22},{7,23},{8,24},{9,... | collective-permute-start | bytes 786440 | tf_op jit(solution)/shard_map/ppermute | solution.py:273
  8.2 1.6 %collective-permute-start = (bf16[2,1,2,32,1024]{4,3,2,1,0:T(8,128)(2,1)S(1)}, bf16[2,1,2,32,1024]{4,3,2,1,0:T(8,128)(2,1)S(1)}, u32[]{:S(2)}, u32[]{:S(2)}) collective-permute-start(bf16[2,1,2,32,1024]{4,3,2,1,0:T(8,128)(2,1)S(1)} %maximum_bitcast_fusion.refs_0_), channel_id=1, source_target_pairs={{0,8},{1,9},{2,10},{3,11},{4,12},{5,13},{6,14},{7,15},{8,0},{9,1},... | collective-permute-start | bytes 786440 | tf_op jit(solution)/shard_map/ppermute | solution.py:273
  10.5 1.8 %collective-permute-start.5 = (bf16[1,1,2,32,1024]{4,3,2,1,0:T(8,128)(2,1)S(1)}, bf16[1,1,2,32,1024]{4,3,2,1,0:T(8,128)(2,1)S(1)}, u32[]{:S(2)}, u32[]{:S(2)}) collective-permute-start(bf16[1,1,2,32,1024]{4,3,2,1,0:T(8,128)(2,1)S(1)} %slice.25), channel_id=1, source_target_pairs={{0,2},{1,3},{2,0},{3,1},{4,6},{5,7},{6,4},{7,5},{8,10},{9,11},{10,... | collective-permute-start | bytes 393224 | tf_op jit(solution)/shard_map/ppermute | solution.py:273
  12.2 1.6 %collective-permute-start.3 = (bf16[1,1,2,32,1024]{4,3,2,1,0:T(8,128)(2,1)S(1)}, bf16[1,1,2,32,1024]{4,3,2,1,0:T(8,128)(2,1)S(1)}, u32[]{:S(2)}, u32[]{:S(2)}) collective-permute-start(bf16[1,1,2,32,1024]{4,3,2,1,0:T(8,128)(2,1)S(1)} %slice.24), channel_id=1, source_target_pairs={{0,4},{1,5},{2,6},{3,7},{4,0},{5,1},{6,2},{7,3},{8,12},{9,13},{10,... | collective-permute-start | bytes 393224 | tf_op jit(solution)/shard_map/ppermute | solution.py:273
  13.8 0.7 copy-done.2
  14.6 3.0 %shard_map.46 = (bf16[256,1024]{1,0:T(8,128)(2,1)}, bf16[256,1024]{1,0:T(8,128)(2,1)}) custom-call(bf16[4,2,64,1024]{3,2,1,0:T(8,128)(2,1)S(1)} %copy-done.1, s32[4,1024]{1,0:T(4,128)S(1)} %copy-done.2), custom_call_target="tpu_custom_call" | custom-call | flops 2147483648 | bytes 1064960 | tf_op jit(solution)/shard_map/pallas_call | solution.py:189
  17.6 2.1 %collective-permute-done.1 = bf16[2,1,2,32,1024]{4,3,2,1,0:T(8,128)(2,1)S(1)} collective-permute-done((bf16[2,1,2,32,1024]{4,3,2,1,0:T(8,128)(2,1)S(1)}, bf16[2,1,2,32,1024]{4,3,2,1,0:T(8,128)(2,1)S(1)}, u32[]{:S(2)}, u32[]{:S(2)}) %collective-permute-start.1) | collective-permute-done | bytes 262176 | tf_op jit(solution)/shard_map/ppermute | solution.py:273
  20.0 0.7 copy-done.24
  21.7 3.2 %collective-permute-start.10 = (bf16[2,1,2,32,1024]{4,3,2,1,0:T(8,128)(2,1)S(1)}, bf16[2,1,2,32,1024]{4,3,2,1,0:T(8,128)(2,1)}, u32[]{:S(2)}, u32[]{:S(2)}) collective-permute-start(bf16[2,1,2,32,1024]{4,3,2,1,0:T(8,128)(2,1)S(1)} %maximum_bitcast_fusion.refs_0_), channel_id=1, source_target_pairs={{0,24},{1,25},{2,26},{3,27},{4,28},{5,29},{6,30},{7,31},{8,16},{9,... | collective-permute-start | bytes 786440 | tf_op jit(solution)/shard_map/ppermute | solution.py:273
  25.0 8.3 %collective-permute-done.8.refs_7_ = bf16[2,2,2,32,1024]{4,3,2,1,0:T(8,128)(2,1)S(1)} collective-permute-done((bf16[2,2,2,32,1024]{4,3,2,1,0:T(8,128)(2,1)S(1)}, bf16[2,2,2,32,1024]{4,3,2,1,0:T(8,128)(2,1)S(1)}, u32[]{:S(2)}, u32[]{:S(2)}) %collective-permute-start.8) | collective-permute-done | bytes 524320 | tf_op jit(solution)/shard_map/ppermute | solution.py:273
  33.9 1.8 %collective-permute-start.7 = (bf16[1,2,2,32,1024]{4,3,2,1,0:T(8,128)(2,1)S(1)}, bf16[1,2,2,32,1024]{4,3,2,1,0:T(8,128)(2,1)S(1)}, u32[]{:S(2)}, u32[]{:S(2)}) collective-permute-start(bf16[1,2,2,32,1024]{4,3,2,1,0:T(8,128)(2,1)S(1)} %slice.26), channel_id=1, source_target_pairs={{0,4},{1,5},{2,6},{3,7},{4,0},{5,1},{6,2},{7,3},{8,12},{9,13},{10,... | collective-permute-start | bytes 786440 | tf_op jit(solution)/shard_map/ppermute | solution.py:273
  36.0 1.5 %collective-permute-start.11 = (bf16[2,1,2,32,1024]{4,3,2,1,0:T(8,128)(2,1)}, bf16[2,1,2,32,1024]{4,3,2,1,0:T(8,128)(2,1)S(1)}, u32[]{:S(2)}, u32[]{:S(2)}) collective-permute-start(bf16[2,1,2,32,1024]{4,3,2,1,0:T(8,128)(2,1)} %collective-permute-done.10.refs_10_), channel_id=1, source_target_pairs={{0,2},{1,3},{2,0},{3,1},{4,6},{5,7},{6,4},{7,5},{8,10},{9,11},{10,... | collective-permute-start | bytes 786440 | tf_op jit(solution)/shard_map/ppermute | solution.py:273
  37.5 4.8 %collective-permute-done.9.refs_9_ = bf16[1,2,2,32,1024]{4,3,2,1,0:T(8,128)(2,1)} collective-permute-done((bf16[1,2,2,32,1024]{4,3,2,1,0:T(8,128)(2,1)S(1)}, bf16[1,2,2,32,1024]{4,3,2,1,0:T(8,128)(2,1)}, u32[]{:S(2)}, u32[]{:S(2)}) %collective-permute-start.9) | collective-permute-done | bytes 262176 | tf_op jit(solution)/shard_map/ppermute | solution.py:273
  42.6 2.8 %collective-permute-done.12.refs_12_ = bf16[2,1,2,32,1024]{4,3,2,1,0:T(8,128)(2,1)S(1)} collective-permute-done((bf16[2,1,2,32,1024]{4,3,2,1,0:T(8,128)(2,1)}, bf16[2,1,2,32,1024]{4,3,2,1,0:T(8,128)(2,1)S(1)}, u32[]{:S(2)}, u32[]{:S(2)}) %collective-permute-start.12) | collective-permute-done | bytes 262176 | tf_op jit(solution)/shard_map/ppermute | solution.py:273
  45.4 7.1 %all-to-all-start = ((bf16[32,8,1024]{2,1,0:T(8,128)(2,1)}), bf16[32,8,1024]{2,1,0:T(8,128)(2,1)S(1)}, u32[]{:S(2)}, u32[]{:S(2)}) async-start(bf16[32,8,1024]{2,1,0:T(8,128)(2,1)} %bitcast), calls=%async_computation | async-start | bytes 1048576 | tf_op jit(solution)/shard_map/all_to_all | solution.py:319
  55.9 1.6 %collective-permute-start.14 = (bf16[1,1,2,32,1024]{4,3,2,1,0:T(8,128)(2,1)S(1)}, bf16[1,1,2,32,1024]{4,3,2,1,0:T(8,128)(2,1)S(1)}, u32[]{:S(2)}, u32[]{:S(2)}) collective-permute-start(bf16[1,1,2,32,1024]{4,3,2,1,0:T(8,128)(2,1)S(1)} %slice.29), channel_id=1, source_target_pairs={{0,2},{1,3},{2,0},{3,1},{4,6},{5,7},{6,4},{7,5},{8,10},{9,11},{10,... | collective-permute-start | bytes 393224 | tf_op jit(solution)/shard_map/ppermute | solution.py:273
  57.5 1.5 %collective-permute-start.13 = (bf16[1,1,2,32,1024]{4,3,2,1,0:T(8,128)(2,1)S(1)}, bf16[1,1,2,32,1024]{4,3,2,1,0:T(8,128)(2,1)S(1)}, u32[]{:S(2)}, u32[]{:S(2)}) collective-permute-start(bf16[1,1,2,32,1024]{4,3,2,1,0:T(8,128)(2,1)S(1)} %slice.28), channel_id=1, source_target_pairs={{0,4},{1,5},{2,6},{3,7},{4,0},{5,1},{6,2},{7,3},{8,12},{9,13},{10,... | collective-permute-start | bytes 393224 | tf_op jit(solution)/shard_map/ppermute | solution.py:273
  59.5 4.2 %collective-permute-done.14.refs_14_ = bf16[1,1,2,32,1024]{4,3,2,1,0:T(8,128)(2,1)S(1)} collective-permute-done((bf16[1,1,2,32,1024]{4,3,2,1,0:T(8,128)(2,1)S(1)}, bf16[1,1,2,32,1024]{4,3,2,1,0:T(8,128)(2,1)S(1)}, u32[]{:S(2)}, u32[]{:S(2)}) %collective-permute-start.14) | collective-permute-done | bytes 131104 | tf_op jit(solution)/shard_map/ppermute | solution.py:273
  65.1 3.0 %all-to-all-done = bf16[32,8,1024]{2,1,0:T(8,128)(2,1)S(1)} async-done(((bf16[32,8,1024]{2,1,0:T(8,128)(2,1)}), bf16[32,8,1024]{2,1,0:T(8,128)(2,1)S(1)}, u32[]{:S(2)}, u32[]{:S(2)}) %all-to-all-start) | async-done | bytes 524320 | tf_op jit(solution)/shard_map/all_to_all | solution.py:319
  68.1 0.8 copy-done.4
  68.9 3.1 %all-to-all-start.2 = ((bf16[32,8,1024]{2,1,0:T(8,128)(2,1)}), bf16[32,8,1024]{2,1,0:T(8,128)(2,1)S(1)}, u32[]{:S(2)}, u32[]{:S(2)}) async-start(bf16[32,8,1024]{2,1,0:T(8,128)(2,1)} %bitcast.4), calls=%async_computation.2 | async-start | bytes 1048576 | tf_op jit(solution)/shard_map/all_to_all | solution.py:319
  72.9 0.9 collective-permute-done.23.refs_23_
  74.9 1.0 collective-permute-done.28.refs_28_
  76.8 11.5 %shard_map.47 = bf16[2048,128]{1,0:T(8,128)(2,1)} custom-call(bf16[256,1024]{1,0:T(8,128)(2,1)} %bitcast.16, bf16[2,1,2,32,1024]{4,3,2,1,0:T(8,128)(2,1)} %copy-done.6, bf16[2,1,2,32,1024]{4,3,2,1,0:T(8,128)(2,1)} %copy-done.10, bf16[2,1,2,32,1024]{4,3,2,1,0:T(8,128)(2,1)} %copy-done.9, bf16[1,1,2,32,1024]{4,3,2,1,0:T(8,128)(2,1)} %copy-done.24, ...), custom_call_target="tpu_custom_call" | custom-call | flops 4294967296 | bytes 8912896 | tf_op jit(solution)/shard_map/pallas_call | solution.py:189
  88.4 0.8 copy-done.5
  89.2 4.9 %all-to-all-start.1 = ((bf16[16,128,128]{2,1,0:T(8,128)(2,1)}), bf16[16,128,128]{2,1,0:T(8,128)(2,1)S(1)}, u32[]{:S(2)}, u32[]{:S(2)}) async-start(bf16[16,128,128]{2,1,0:T(8,128)(2,1)} %bitcast.18), calls=%async_computation.1 | async-start | bytes 1048576 | tf_op jit(solution)/shard_map/all_to_all | solution.py:319
  94.1 10.8 %shard_map.48.right_ref = bf16[256,1024]{1,0:T(8,128)(2,1)} custom-call(bf16[256,1024]{1,0:T(8,128)(2,1)} %bitcast.17, bf16[2,1,2,32,1024]{4,3,2,1,0:T(8,128)(2,1)} %copy-done.6, bf16[2,1,2,32,1024]{4,3,2,1,0:T(8,128)(2,1)} %copy-done.10, bf16[2,1,2,32,1024]{4,3,2,1,0:T(8,128)(2,1)} %copy-done.9, bf16[1,1,2,32,1024]{4,3,2,1,0:T(8,128)(2,1)} %copy-done.24, ...), custom_call_target="tpu_custom_call" | custom-call | flops 4294967296 | bytes 8912896 | tf_op jit(solution)/shard_map/pallas_call | solution.py:189
  104.9 1.0 copy-done
  106.6 16.4 %all_to_all.20 = bf16[32,16,256]{2,1,0:T(8,128)(2,1)S(1)} all-to-all(bf16[32,16,256]{2,1,0:T(8,128)(2,1)S(1)} %bitcast.15), channel_id=1, replica_groups=mesh['cuts'=1,'mode'=32] {'mode'}, dimensions={0} | all-to-all | bytes 524288 | tf_op jit(solution)/shard_map/all_to_all | solution.py:319
  (112 shorter events, 12.4 us)
Async XLA Ops:
  1.1 9.3 %collective-permute-start.4 = (bf16[2,1,2,32,1024]{4,3,2,1,0:T(8,128)(2,1)S(1)}, bf16[2,1,2,32,1024]{4,3,2,1,0:T(8,128)(2,1)S(1)}, u32[]{:S(2)}, u32[]{:S(2)}) collective-permute-start(bf16[2,1,2,32,1024]{4,3,2,1,0:T(8,128)(2,1)S(1)} %maximum_bitcast_fusion.refs_0_), channel_id=1, source_target_pairs={{0,4},{1,5},{2,6},{3,7},{4,0},{5,1},{6,2},{7,3},{8,12},{9,13},{10,... | collective-permute-start | bytes 786440 | tf_op jit(solution)/shard_map/ppermute | solution.py:273
  4.1 8.1 %collective-permute-start.2 = (bf16[2,1,2,32,1024]{4,3,2,1,0:T(8,128)(2,1)S(1)}, bf16[2,1,2,32,1024]{4,3,2,1,0:T(8,128)(2,1)S(1)}, u32[]{:S(2)}, u32[]{:S(2)}) collective-permute-start(bf16[2,1,2,32,1024]{4,3,2,1,0:T(8,128)(2,1)S(1)} %maximum_bitcast_fusion.refs_0_), channel_id=1, source_target_pairs={{0,2},{1,3},{2,0},{3,1},{4,6},{5,7},{6,4},{7,5},{8,10},{9,11},{10,... | collective-permute-start | bytes 786440 | tf_op jit(solution)/shard_map/ppermute | solution.py:273
  5.6 14.1 %collective-permute-start.1 = (bf16[2,1,2,32,1024]{4,3,2,1,0:T(8,128)(2,1)S(1)}, bf16[2,1,2,32,1024]{4,3,2,1,0:T(8,128)(2,1)S(1)}, u32[]{:S(2)}, u32[]{:S(2)}) collective-permute-start(bf16[2,1,2,32,1024]{4,3,2,1,0:T(8,128)(2,1)S(1)} %maximum_bitcast_fusion.refs_0_), channel_id=1, source_target_pairs={{0,16},{1,17},{2,18},{3,19},{4,20},{5,21},{6,22},{7,23},{8,24},{9,... | collective-permute-start | bytes 786440 | tf_op jit(solution)/shard_map/ppermute | solution.py:273
  8.2 11.7 %collective-permute-start = (bf16[2,1,2,32,1024]{4,3,2,1,0:T(8,128)(2,1)S(1)}, bf16[2,1,2,32,1024]{4,3,2,1,0:T(8,128)(2,1)S(1)}, u32[]{:S(2)}, u32[]{:S(2)}) collective-permute-start(bf16[2,1,2,32,1024]{4,3,2,1,0:T(8,128)(2,1)S(1)} %maximum_bitcast_fusion.refs_0_), channel_id=1, source_target_pairs={{0,8},{1,9},{2,10},{3,11},{4,12},{5,13},{6,14},{7,15},{8,0},{9,1},... | collective-permute-start | bytes 786440 | tf_op jit(solution)/shard_map/ppermute | solution.py:273
  10.5 9.5 %collective-permute-start.5 = (bf16[1,1,2,32,1024]{4,3,2,1,0:T(8,128)(2,1)S(1)}, bf16[1,1,2,32,1024]{4,3,2,1,0:T(8,128)(2,1)S(1)}, u32[]{:S(2)}, u32[]{:S(2)}) collective-permute-start(bf16[1,1,2,32,1024]{4,3,2,1,0:T(8,128)(2,1)S(1)} %slice.25), channel_id=1, source_target_pairs={{0,2},{1,3},{2,0},{3,1},{4,6},{5,7},{6,4},{7,5},{8,10},{9,11},{10,... | collective-permute-start | bytes 393224 | tf_op jit(solution)/shard_map/ppermute | solution.py:273
  12.2 7.8 %collective-permute-start.3 = (bf16[1,1,2,32,1024]{4,3,2,1,0:T(8,128)(2,1)S(1)}, bf16[1,1,2,32,1024]{4,3,2,1,0:T(8,128)(2,1)S(1)}, u32[]{:S(2)}, u32[]{:S(2)}) collective-permute-start(bf16[1,1,2,32,1024]{4,3,2,1,0:T(8,128)(2,1)S(1)} %slice.24), channel_id=1, source_target_pairs={{0,4},{1,5},{2,6},{3,7},{4,0},{5,1},{6,2},{7,3},{8,12},{9,13},{10,... | collective-permute-start | bytes 393224 | tf_op jit(solution)/shard_map/ppermute | solution.py:273
  20.8 12.5 %collective-permute-start.8 = (bf16[2,2,2,32,1024]{4,3,2,1,0:T(8,128)(2,1)S(1)}, bf16[2,2,2,32,1024]{4,3,2,1,0:T(8,128)(2,1)S(1)}, u32[]{:S(2)}, u32[]{:S(2)}) collective-permute-start(bf16[2,2,2,32,1024]{4,3,2,1,0:T(8,128)(2,1)S(1)} %pad_maximum_fusion.refs_5_), channel_id=1, source_target_pairs={{0,4},{1,5},{2,6},{3,7},{4,0},{5,1},{6,2},{7,3},{8,12},{9,13},{10,... | collective-permute-start | bytes 1572872 | tf_op jit(solution)/shard_map/ppermute | solution.py:273
  21.3 12.6 %collective-permute-start.6 = (bf16[2,2,2,32,1024]{4,3,2,1,0:T(8,128)(2,1)S(1)}, bf16[2,2,2,32,1024]{4,3,2,1,0:T(8,128)(2,1)S(1)}, u32[]{:S(2)}, u32[]{:S(2)}) collective-permute-start(bf16[2,2,2,32,1024]{4,3,2,1,0:T(8,128)(2,1)S(1)} %pad_maximum_fusion.refs_5_), channel_id=1, source_target_pairs={{0,2},{1,3},{2,0},{3,1},{4,6},{5,7},{6,4},{7,5},{8,10},{9,11},{10,... | collective-permute-start | bytes 1572872 | tf_op jit(solution)/shard_map/ppermute | solution.py:273
  21.7 12.2 %collective-permute-start.10 = (bf16[2,1,2,32,1024]{4,3,2,1,0:T(8,128)(2,1)S(1)}, bf16[2,1,2,32,1024]{4,3,2,1,0:T(8,128)(2,1)}, u32[]{:S(2)}, u32[]{:S(2)}) collective-permute-start(bf16[2,1,2,32,1024]{4,3,2,1,0:T(8,128)(2,1)S(1)} %maximum_bitcast_fusion.refs_0_), channel_id=1, source_target_pairs={{0,24},{1,25},{2,26},{3,27},{4,28},{5,29},{6,30},{7,31},{8,16},{9,... | collective-permute-start | bytes 786440 | tf_op jit(solution)/shard_map/ppermute | solution.py:273
  33.3 9.1 %collective-permute-start.9 = (bf16[1,2,2,32,1024]{4,3,2,1,0:T(8,128)(2,1)S(1)}, bf16[1,2,2,32,1024]{4,3,2,1,0:T(8,128)(2,1)}, u32[]{:S(2)}, u32[]{:S(2)}) collective-permute-start(bf16[1,2,2,32,1024]{4,3,2,1,0:T(8,128)(2,1)S(1)} %slice.27), channel_id=1, source_target_pairs={{0,2},{1,3},{2,0},{3,1},{4,6},{5,7},{6,4},{7,5},{8,10},{9,11},{10,... | collective-permute-start | bytes 786440 | tf_op jit(solution)/shard_map/ppermute | solution.py:273
  33.9 8.7 %collective-permute-start.7 = (bf16[1,2,2,32,1024]{4,3,2,1,0:T(8,128)(2,1)S(1)}, bf16[1,2,2,32,1024]{4,3,2,1,0:T(8,128)(2,1)S(1)}, u32[]{:S(2)}, u32[]{:S(2)}) collective-permute-start(bf16[1,2,2,32,1024]{4,3,2,1,0:T(8,128)(2,1)S(1)} %slice.26), channel_id=1, source_target_pairs={{0,4},{1,5},{2,6},{3,7},{4,0},{5,1},{6,2},{7,3},{8,12},{9,13},{10,... | collective-permute-start | bytes 786440 | tf_op jit(solution)/shard_map/ppermute | solution.py:273
  35.7 9.7 %collective-permute-start.12 = (bf16[2,1,2,32,1024]{4,3,2,1,0:T(8,128)(2,1)}, bf16[2,1,2,32,1024]{4,3,2,1,0:T(8,128)(2,1)S(1)}, u32[]{:S(2)}, u32[]{:S(2)}) collective-permute-start(bf16[2,1,2,32,1024]{4,3,2,1,0:T(8,128)(2,1)} %collective-permute-done.10.refs_10_), channel_id=1, source_target_pairs={{0,4},{1,5},{2,6},{3,7},{4,0},{5,1},{6,2},{7,3},{8,12},{9,13},{10,... | collective-permute-start | bytes 786440 | tf_op jit(solution)/shard_map/ppermute | solution.py:273
  36.0 9.4 %collective-permute-start.11 = (bf16[2,1,2,32,1024]{4,3,2,1,0:T(8,128)(2,1)}, bf16[2,1,2,32,1024]{4,3,2,1,0:T(8,128)(2,1)S(1)}, u32[]{:S(2)}, u32[]{:S(2)}) collective-permute-start(bf16[2,1,2,32,1024]{4,3,2,1,0:T(8,128)(2,1)} %collective-permute-done.10.refs_10_), channel_id=1, source_target_pairs={{0,2},{1,3},{2,0},{3,1},{4,6},{5,7},{6,4},{7,5},{8,10},{9,11},{10,... | collective-permute-start | bytes 786440 | tf_op jit(solution)/shard_map/ppermute | solution.py:273
  45.4 22.7 %all-to-all-start = ((bf16[32,8,1024]{2,1,0:T(8,128)(2,1)}), bf16[32,8,1024]{2,1,0:T(8,128)(2,1)S(1)}, u32[]{:S(2)}, u32[]{:S(2)}) async-start(bf16[32,8,1024]{2,1,0:T(8,128)(2,1)} %bitcast), calls=%async_computation | async-start | bytes 1048576 | tf_op jit(solution)/shard_map/all_to_all | solution.py:319
  52.6 1.6 %collective-permute-start.15 = (bf16[2,1,2,32,1024]{4,3,2,1,0:T(8,128)(2,1)S(1)}, bf16[2,1,2,32,1024]{4,3,2,1,0:T(8,128)(2,1)S(1)}, u32[]{:S(2)}, u32[]{:S(2)}) collective-permute-start(bf16[2,1,2,32,1024]{4,3,2,1,0:T(8,128)(2,1)S(1)} %maximum_bitcast_fusion.refs_0_), channel_id=1, source_target_pairs={{0,1},{1,0},{2,3},{3,2},{4,5},{5,4},{6,7},{7,6},{8,9},{9,8},{10,11... | collective-permute-start | bytes 786440 | tf_op jit(solution)/shard_map/ppermute | solution.py:273
  52.9 4.6 %collective-permute-start.17 = (bf16[2,1,2,32,1024]{4,3,2,1,0:T(8,128)(2,1)S(1)}, bf16[2,1,2,32,1024]{4,3,2,1,0:T(8,128)(2,1)S(1)}, u32[]{:S(2)}, u32[]{:S(2)}) collective-permute-start(bf16[2,1,2,32,1024]{4,3,2,1,0:T(8,128)(2,1)S(1)} %collective-permute-done.4.refs_2_), channel_id=1, source_target_pairs={{0,1},{1,0},{2,3},{3,2},{4,5},{5,4},{6,7},{7,6},{8,9},{9,8},{10,11... | collective-permute-start | bytes 786440 | tf_op jit(solution)/shard_map/ppermute | solution.py:273
  53.2 18.9 %collective-permute-start.20 = (bf16[2,2,2,32,1024]{4,3,2,1,0:T(8,128)(2,1)S(1)}, bf16[2,2,2,32,1024]{4,3,2,1,0:T(8,128)(2,1)}, u32[]{:S(2)}, u32[]{:S(2)}) collective-permute-start(bf16[2,2,2,32,1024]{4,3,2,1,0:T(8,128)(2,1)S(1)} %pad_maximum_fusion.refs_5_), channel_id=1, source_target_pairs={{0,1},{1,0},{2,3},{3,2},{4,5},{5,4},{6,7},{7,6},{8,9},{9,8},{10,11... | collective-permute-start | bytes 1572872 | tf_op jit(solution)/shard_map/ppermute | solution.py:273
  53.4 5.5 %collective-permute-start.16 = (bf16[2,1,2,32,1024]{4,3,2,1,0:T(8,128)(2,1)S(1)}, bf16[2,1,2,32,1024]{4,3,2,1,0:T(8,128)(2,1)S(1)}, u32[]{:S(2)}, u32[]{:S(2)}) collective-permute-start(bf16[2,1,2,32,1024]{4,3,2,1,0:T(8,128)(2,1)S(1)} %collective-permute-done.2.refs_1_), channel_id=1, source_target_pairs={{0,1},{1,0},{2,3},{3,2},{4,5},{5,4},{6,7},{7,6},{8,9},{9,8},{10,11... | collective-permute-start | bytes 786440 | tf_op jit(solution)/shard_map/ppermute | solution.py:273
  53.7 2.2 %collective-permute-start.19 = (bf16[1,1,2,32,1024]{4,3,2,1,0:T(8,128)(2,1)S(1)}, bf16[1,1,2,32,1024]{4,3,2,1,0:T(8,128)(2,1)S(1)}, u32[]{:S(2)}, u32[]{:S(2)}) collective-permute-start(bf16[1,1,2,32,1024]{4,3,2,1,0:T(8,128)(2,1)S(1)} %collective-permute-done.5.refs_4_), channel_id=1, source_target_pairs={{0,1},{1,0},{2,3},{3,2},{4,5},{5,4},{6,7},{7,6},{8,9},{9,8},{10,11... | collective-permute-start | bytes 393224 | tf_op jit(solution)/shard_map/ppermute | solution.py:273
  54.9 4.0 %collective-permute-start.18 = (bf16[1,1,2,32,1024]{4,3,2,1,0:T(8,128)(2,1)}, bf16[1,1,2,32,1024]{4,3,2,1,0:T(8,128)(2,1)S(1)}, u32[]{:S(2)}, u32[]{:S(2)}) collective-permute-start(bf16[1,1,2,32,1024]{4,3,2,1,0:T(8,128)(2,1)} %copy-done.24), channel_id=1, source_target_pairs={{0,1},{1,0},{2,3},{3,2},{4,5},{5,4},{6,7},{7,6},{8,9},{9,8},{10,11... | collective-permute-start | bytes 393224 | tf_op jit(solution)/shard_map/ppermute | solution.py:273
  55.9 7.8 %collective-permute-start.14 = (bf16[1,1,2,32,1024]{4,3,2,1,0:T(8,128)(2,1)S(1)}, bf16[1,1,2,32,1024]{4,3,2,1,0:T(8,128)(2,1)S(1)}, u32[]{:S(2)}, u32[]{:S(2)}) collective-permute-start(bf16[1,1,2,32,1024]{4,3,2,1,0:T(8,128)(2,1)S(1)} %slice.29), channel_id=1, source_target_pairs={{0,2},{1,3},{2,0},{3,1},{4,6},{5,7},{6,4},{7,5},{8,10},{9,11},{10,... | collective-permute-start | bytes 393224 | tf_op jit(solution)/shard_map/ppermute | solution.py:273
  57.5 6.9 %collective-permute-start.13 = (bf16[1,1,2,32,1024]{4,3,2,1,0:T(8,128)(2,1)S(1)}, bf16[1,1,2,32,1024]{4,3,2,1,0:T(8,128)(2,1)S(1)}, u32[]{:S(2)}, u32[]{:S(2)}) collective-permute-start(bf16[1,1,2,32,1024]{4,3,2,1,0:T(8,128)(2,1)S(1)} %slice.28), channel_id=1, source_target_pairs={{0,4},{1,5},{2,6},{3,7},{4,0},{5,1},{6,2},{7,3},{8,12},{9,13},{10,... | collective-permute-start | bytes 393224 | tf_op jit(solution)/shard_map/ppermute | solution.py:273
  58.9 13.4 %collective-permute-start.25 = (bf16[2,1,2,32,1024]{4,3,2,1,0:T(8,128)(2,1)}, bf16[2,1,2,32,1024]{4,3,2,1,0:T(8,128)(2,1)}, u32[]{:S(2)}, u32[]{:S(2)}) collective-permute-start(bf16[2,1,2,32,1024]{4,3,2,1,0:T(8,128)(2,1)} %collective-permute-done.10.refs_10_), channel_id=1, source_target_pairs={{0,1},{1,0},{2,3},{3,2},{4,5},{5,4},{6,7},{7,6},{8,9},{9,8},{10,11... | collective-permute-start | bytes 786440 | tf_op jit(solution)/shard_map/ppermute | solution.py:273
  59.0 14.0 %collective-permute-start.22 = (bf16[2,2,2,32,1024]{4,3,2,1,0:T(8,128)(2,1)S(1)}, bf16[2,2,2,32,1024]{4,3,2,1,0:T(8,128)(2,1)}, u32[]{:S(2)}, u32[]{:S(2)}) collective-permute-start(bf16[2,2,2,32,1024]{4,3,2,1,0:T(8,128)(2,1)S(1)} %collective-permute-done.8.refs_7_), channel_id=1, source_target_pairs={{0,1},{1,0},{2,3},{3,2},{4,5},{5,4},{6,7},{7,6},{8,9},{9,8},{10,11... | collective-permute-start | bytes 1572872 | tf_op jit(solution)/shard_map/ppermute | solution.py:273
  63.7 8.9 %collective-permute-start.24 = (bf16[1,2,2,32,1024]{4,3,2,1,0:T(8,128)(2,1)}, bf16[1,2,2,32,1024]{4,3,2,1,0:T(8,128)(2,1)S(1)}, u32[]{:S(2)}, u32[]{:S(2)}) collective-permute-start(bf16[1,2,2,32,1024]{4,3,2,1,0:T(8,128)(2,1)} %collective-permute-done.9.refs_9_), channel_id=1, source_target_pairs={{0,1},{1,0},{2,3},{3,2},{4,5},{5,4},{6,7},{7,6},{8,9},{9,8},{10,11... | collective-permute-start | bytes 786440 | tf_op jit(solution)/shard_map/ppermute | solution.py:273
  65.1 9.3 %collective-permute-start.21 = (bf16[2,2,2,32,1024]{4,3,2,1,0:T(8,128)(2,1)S(1)}, bf16[2,2,2,32,1024]{4,3,2,1,0:T(8,128)(2,1)}, u32[]{:S(2)}, u32[]{:S(2)}) collective-permute-start(bf16[2,2,2,32,1024]{4,3,2,1,0:T(8,128)(2,1)S(1)} %collective-permute-done.6.refs_6_), channel_id=1, source_target_pairs={{0,1},{1,0},{2,3},{3,2},{4,5},{5,4},{6,7},{7,6},{8,9},{9,8},{10,11... | collective-permute-start | bytes 1572872 | tf_op jit(solution)/shard_map/ppermute | solution.py:273
  68.9 19.4 %all-to-all-start.2 = ((bf16[32,8,1024]{2,1,0:T(8,128)(2,1)}), bf16[32,8,1024]{2,1,0:T(8,128)(2,1)S(1)}, u32[]{:S(2)}, u32[]{:S(2)}) async-start(bf16[32,8,1024]{2,1,0:T(8,128)(2,1)} %bitcast.4), calls=%async_computation.2 | async-start | bytes 1048576 | tf_op jit(solution)/shard_map/all_to_all | solution.py:319
  72.0 1.8 %collective-permute-start.23 = (bf16[1,2,2,32,1024]{4,3,2,1,0:T(8,128)(2,1)}, bf16[1,2,2,32,1024]{4,3,2,1,0:T(8,128)(2,1)S(1)}, u32[]{:S(2)}, u32[]{:S(2)}) collective-permute-start(bf16[1,2,2,32,1024]{4,3,2,1,0:T(8,128)(2,1)} %copy-done.15), channel_id=1, source_target_pairs={{0,1},{1,0},{2,3},{3,2},{4,5},{5,4},{6,7},{7,6},{8,9},{9,8},{10,11... | collective-permute-start | bytes 786440 | tf_op jit(solution)/shard_map/ppermute | solution.py:273
  72.3 1.7 %collective-permute-start.27 = (bf16[2,1,2,32,1024]{4,3,2,1,0:T(8,128)(2,1)S(1)}, bf16[2,1,2,32,1024]{4,3,2,1,0:T(8,128)(2,1)S(1)}, u32[]{:S(2)}, u32[]{:S(2)}) collective-permute-start(bf16[2,1,2,32,1024]{4,3,2,1,0:T(8,128)(2,1)S(1)} %copy-done.12), channel_id=1, source_target_pairs={{0,1},{1,0},{2,3},{3,2},{4,5},{5,4},{6,7},{7,6},{8,9},{9,8},{10,11... | collective-permute-start | bytes 786440 | tf_op jit(solution)/shard_map/ppermute | solution.py:273
  72.6 1.8 %collective-permute-start.26 = (bf16[2,1,2,32,1024]{4,3,2,1,0:T(8,128)(2,1)S(1)}, bf16[2,1,2,32,1024]{4,3,2,1,0:T(8,128)(2,1)S(1)}, u32[]{:S(2)}, u32[]{:S(2)}) collective-permute-start(bf16[2,1,2,32,1024]{4,3,2,1,0:T(8,128)(2,1)S(1)} %copy-done.14), channel_id=1, source_target_pairs={{0,1},{1,0},{2,3},{3,2},{4,5},{5,4},{6,7},{7,6},{8,9},{9,8},{10,11... | collective-permute-start | bytes 786440 | tf_op jit(solution)/shard_map/ppermute | solution.py:273
  74.4 1.6 %collective-permute-start.28 = (bf16[1,1,2,32,1024]{4,3,2,1,0:T(8,128)(2,1)}, bf16[1,1,2,32,1024]{4,3,2,1,0:T(8,128)(2,1)S(1)}, u32[]{:S(2)}, u32[]{:S(2)}) collective-permute-start(bf16[1,1,2,32,1024]{4,3,2,1,0:T(8,128)(2,1)} %copy-done.28), channel_id=1, source_target_pairs={{0,1},{1,0},{2,3},{3,2},{4,5},{5,4},{6,7},{7,6},{8,9},{9,8},{10,11... | collective-permute-start | bytes 393224 | tf_op jit(solution)/shard_map/ppermute | solution.py:273
  89.2 15.7 %all-to-all-start.1 = ((bf16[16,128,128]{2,1,0:T(8,128)(2,1)}), bf16[16,128,128]{2,1,0:T(8,128)(2,1)S(1)}, u32[]{:S(2)}, u32[]{:S(2)}) async-start(bf16[16,128,128]{2,1,0:T(8,128)(2,1)} %bitcast.18), calls=%async_computation.1 | async-start | bytes 1048576 | tf_op jit(solution)/shard_map/all_to_all | solution.py:319
  (32 other events, 375.7 us)

commit v14 on v13

--- a/solution.py
+++ b/solution.py
@@ -299,7 +299,7 @@
     blocks = []
     for number, (value, sources) in enumerate(sets):
         if number:
-            tied = (*packed, blocks[3][0], blocks[4][0]) if number == 1 else (blocks[6][0], blocks[7][0])
+            tied = (blocks[3][0], blocks[4][0]) if number == 1 else (*packed, blocks[6][0], blocks[7][0])
             value, *_ = lax.optimization_barrier((value, *tied))
         blocks += plane(value, sources)
     left, *_ = lax.optimization_barrier((packed[0], blocks[8][0], blocks[9][0], blocks[-4][0], blocks[-3][0]))

time: 124 us -> 124 us (level)
    unnamed x62 -> x52, local copies, waits for them, and re-layouts: 6.16 us -> 4.06 us
  transfers between devices with their start and end apart: 33 -> 33, of which waited for: 17 -> 15; matrix products, arithmetic and copies ran while one was open for 0% -> 1% of each run, Pallas kernels for 21% -> 21%
where the time goes in v14:
time: 124 us; the launch traced here: 123 us
  starting transfers between devices  42.5 us (34%)
  waiting for transfers between devices  31 us (25%)
  Pallas kernels  26 us (21%)
  blocking collectives  16.4 us (13%)
  local copies, waits for them, and re-layouts  5.66 us (5%)
    ppermute x30, waiting for transfers between devices, flip(): return lax.ppermute(value, 'mode', pairs)  27.5 us
    ppermute x30, starting transfers between devices, flip(): return lax.ppermute(value, 'mode', pairs)  27.4 us
    pallas_call x4, Pallas kernels, call(): pl.pallas_call(kernel, out_shape=[out] * outputs if outputs else out, in_...  26 us
    all_to_all x1, blocking collectives, trade(): lax.all_to_all(value, 'mode', split_axis=0, concat_axis=0, axis_index_gro...  16.4 us
    all_to_all x3, starting transfers between devices, trade(): lax.all_to_all(value, 'mode', split_axis=0, concat_axis=0, axis_index_gro...  15.2 us
    unnamed x52, local copies, waits for them, and re-layouts  4.06 us
    all_to_all x3, waiting for transfers between devices, trade(): lax.all_to_all(value, 'mode', split_axis=0, concat_axis=0, axis_index_gro...  3.49 us
  transfers between devices with their start and end apart: 33, of which 15 were waited for; matrix products, arithmetic and copies ran while one was open for 1% of the time, Pallas kernels for 21%

profile of v14, /device:TPU:0, one launch (start us, length us, event | category | flops | bytes accessed | tf_op | source)
XLA Modules:
  0.0 123.0 jit_solution(5052206245327831984)
XLA Ops:
  0.0 1.1 maximum_bitcast_fusion.refs_0_
  1.1 3.0 %collective-permute-start.4 = (bf16[2,1,2,32,1024]{4,3,2,1,0:T(8,128)(2,1)S(1)}, bf16[2,1,2,32,1024]{4,3,2,1,0:T(8,128)(2,1)S(1)}, u32[]{:S(2)}, u32[]{:S(2)}) collective-permute-start(bf16[2,1,2,32,1024]{4,3,2,1,0:T(8,128)(2,1)S(1)} %maximum_bitcast_fusion.refs_0_), channel_id=1, source_target_pairs={{0,4},{1,5},{2,6},{3,7},{4,0},{5,1},{6,2},{7,3},{8,12},{9,13},{10,... | collective-permute-start | bytes 786440 | tf_op jit(solution)/shard_map/ppermute | solution.py:273
  4.1 1.5 %collective-permute-start.2 = (bf16[2,1,2,32,1024]{4,3,2,1,0:T(8,128)(2,1)S(1)}, bf16[2,1,2,32,1024]{4,3,2,1,0:T(8,128)(2,1)S(1)}, u32[]{:S(2)}, u32[]{:S(2)}) collective-permute-start(bf16[2,1,2,32,1024]{4,3,2,1,0:T(8,128)(2,1)S(1)} %maximum_bitcast_fusion.refs_0_), channel_id=1, source_target_pairs={{0,2},{1,3},{2,0},{3,1},{4,6},{5,7},{6,4},{7,5},{8,10},{9,11},{10,... | collective-permute-start | bytes 786440 | tf_op jit(solution)/shard_map/ppermute | solution.py:273
  5.6 2.6 %collective-permute-start.1 = (bf16[2,1,2,32,1024]{4,3,2,1,0:T(8,128)(2,1)S(1)}, bf16[2,1,2,32,1024]{4,3,2,1,0:T(8,128)(2,1)S(1)}, u32[]{:S(2)}, u32[]{:S(2)}) collective-permute-start(bf16[2,1,2,32,1024]{4,3,2,1,0:T(8,128)(2,1)S(1)} %maximum_bitcast_fusion.refs_0_), channel_id=1, source_target_pairs={{0,16},{1,17},{2,18},{3,19},{4,20},{5,21},{6,22},{7,23},{8,24},{9,... | collective-permute-start | bytes 786440 | tf_op jit(solution)/shard_map/ppermute | solution.py:273
  8.2 1.6 %collective-permute-start = (bf16[2,1,2,32,1024]{4,3,2,1,0:T(8,128)(2,1)S(1)}, bf16[2,1,2,32,1024]{4,3,2,1,0:T(8,128)(2,1)S(1)}, u32[]{:S(2)}, u32[]{:S(2)}) collective-permute-start(bf16[2,1,2,32,1024]{4,3,2,1,0:T(8,128)(2,1)S(1)} %maximum_bitcast_fusion.refs_0_), channel_id=1, source_target_pairs={{0,8},{1,9},{2,10},{3,11},{4,12},{5,13},{6,14},{7,15},{8,0},{9,1},... | collective-permute-start | bytes 786440 | tf_op jit(solution)/shard_map/ppermute | solution.py:273
  10.5 1.8 %collective-permute-start.5 = (bf16[1,1,2,32,1024]{4,3,2,1,0:T(8,128)(2,1)S(1)}, bf16[1,1,2,32,1024]{4,3,2,1,0:T(8,128)(2,1)S(1)}, u32[]{:S(2)}, u32[]{:S(2)}) collective-permute-start(bf16[1,1,2,32,1024]{4,3,2,1,0:T(8,128)(2,1)S(1)} %slice.25), channel_id=1, source_target_pairs={{0,2},{1,3},{2,0},{3,1},{4,6},{5,7},{6,4},{7,5},{8,10},{9,11},{10,... | collective-permute-start | bytes 393224 | tf_op jit(solution)/shard_map/ppermute | solution.py:273
  12.3 1.6 %collective-permute-start.3 = (bf16[1,1,2,32,1024]{4,3,2,1,0:T(8,128)(2,1)S(1)}, bf16[1,1,2,32,1024]{4,3,2,1,0:T(8,128)(2,1)}, u32[]{:S(2)}, u32[]{:S(2)}) collective-permute-start(bf16[1,1,2,32,1024]{4,3,2,1,0:T(8,128)(2,1)S(1)} %slice.24), channel_id=1, source_target_pairs={{0,4},{1,5},{2,6},{3,7},{4,0},{5,1},{6,2},{7,3},{8,12},{9,13},{10,... | collective-permute-start | bytes 393224 | tf_op jit(solution)/shard_map/ppermute | solution.py:273
  13.8 5.9 %collective-permute-done.1 = bf16[2,1,2,32,1024]{4,3,2,1,0:T(8,128)(2,1)S(1)} collective-permute-done((bf16[2,1,2,32,1024]{4,3,2,1,0:T(8,128)(2,1)S(1)}, bf16[2,1,2,32,1024]{4,3,2,1,0:T(8,128)(2,1)S(1)}, u32[]{:S(2)}, u32[]{:S(2)}) %collective-permute-start.1) | collective-permute-done | bytes 262176 | tf_op jit(solution)/shard_map/ppermute | solution.py:273
  21.1 3.2 %collective-permute-start.10 = (bf16[2,1,2,32,1024]{4,3,2,1,0:T(8,128)(2,1)S(1)}, bf16[2,1,2,32,1024]{4,3,2,1,0:T(8,128)(2,1)}, u32[]{:S(2)}, u32[]{:S(2)}) collective-permute-start(bf16[2,1,2,32,1024]{4,3,2,1,0:T(8,128)(2,1)S(1)} %maximum_bitcast_fusion.refs_0_), channel_id=1, source_target_pairs={{0,24},{1,25},{2,26},{3,27},{4,28},{5,29},{6,30},{7,31},{8,16},{9,... | collective-permute-start | bytes 786440 | tf_op jit(solution)/shard_map/ppermute | solution.py:273
  24.3 3.0 %shard_map.46 = (bf16[256,1024]{1,0:T(8,128)(2,1)}, bf16[256,1024]{1,0:T(8,128)(2,1)}) custom-call(bf16[4,2,64,1024]{3,2,1,0:T(8,128)(2,1)S(1)} %copy-done.1, s32[4,1024]{1,0:T(4,128)S(1)} %copy-done.2), custom_call_target="tpu_custom_call" | custom-call | flops 2147483648 | bytes 1064960 | tf_op jit(solution)/shard_map/pallas_call | solution.py:189
  27.4 5.2 %collective-permute-done.8.refs_7_ = bf16[2,2,2,32,1024]{4,3,2,1,0:T(8,128)(2,1)S(1)} collective-permute-done((bf16[2,2,2,32,1024]{4,3,2,1,0:T(8,128)(2,1)S(1)}, bf16[2,2,2,32,1024]{4,3,2,1,0:T(8,128)(2,1)S(1)}, u32[]{:S(2)}, u32[]{:S(2)}) %collective-permute-start.8) | collective-permute-done | bytes 524320 | tf_op jit(solution)/shard_map/ppermute | solution.py:273
  33.2 1.8 %collective-permute-start.7 = (bf16[1,2,2,32,1024]{4,3,2,1,0:T(8,128)(2,1)S(1)}, bf16[1,2,2,32,1024]{4,3,2,1,0:T(8,128)(2,1)}, u32[]{:S(2)}, u32[]{:S(2)}) collective-permute-start(bf16[1,2,2,32,1024]{4,3,2,1,0:T(8,128)(2,1)S(1)} %slice.26), channel_id=1, source_target_pairs={{0,4},{1,5},{2,6},{3,7},{4,0},{5,1},{6,2},{7,3},{8,12},{9,13},{10,... | collective-permute-start | bytes 786440 | tf_op jit(solution)/shard_map/ppermute | solution.py:273
  35.3 1.5 %collective-permute-start.11 = (bf16[2,1,2,32,1024]{4,3,2,1,0:T(8,128)(2,1)}, bf16[2,1,2,32,1024]{4,3,2,1,0:T(8,128)(2,1)}, u32[]{:S(2)}, u32[]{:S(2)}) collective-permute-start(bf16[2,1,2,32,1024]{4,3,2,1,0:T(8,128)(2,1)} %collective-permute-done.10.refs_10_), channel_id=1, source_target_pairs={{0,2},{1,3},{2,0},{3,1},{4,6},{5,7},{6,4},{7,5},{8,10},{9,11},{10,... | collective-permute-start | bytes 786440 | tf_op jit(solution)/shard_map/ppermute | solution.py:273
  36.8 4.8 %collective-permute-done.9.refs_9_ = bf16[1,2,2,32,1024]{4,3,2,1,0:T(8,128)(2,1)} collective-permute-done((bf16[1,2,2,32,1024]{4,3,2,1,0:T(8,128)(2,1)S(1)}, bf16[1,2,2,32,1024]{4,3,2,1,0:T(8,128)(2,1)}, u32[]{:S(2)}, u32[]{:S(2)}) %collective-permute-start.9) | collective-permute-done | bytes 262176 | tf_op jit(solution)/shard_map/ppermute | solution.py:273
  42.0 2.7 %collective-permute-done.12.refs_12_ = bf16[2,1,2,32,1024]{4,3,2,1,0:T(8,128)(2,1)S(1)} collective-permute-done((bf16[2,1,2,32,1024]{4,3,2,1,0:T(8,128)(2,1)}, bf16[2,1,2,32,1024]{4,3,2,1,0:T(8,128)(2,1)S(1)}, u32[]{:S(2)}, u32[]{:S(2)}) %collective-permute-start.12) | collective-permute-done | bytes 262176 | tf_op jit(solution)/shard_map/ppermute | solution.py:273
  44.7 7.1 %all-to-all-start = ((bf16[32,8,1024]{2,1,0:T(8,128)(2,1)}), bf16[32,8,1024]{2,1,0:T(8,128)(2,1)S(1)}, u32[]{:S(2)}, u32[]{:S(2)}) async-start(bf16[32,8,1024]{2,1,0:T(8,128)(2,1)} %bitcast), calls=%async_computation | async-start | bytes 1048576 | tf_op jit(solution)/shard_map/all_to_all | solution.py:319
  54.5 0.9 slice.28
  55.4 1.7 %collective-permute-start.14 = (bf16[1,1,2,32,1024]{4,3,2,1,0:T(8,128)(2,1)S(1)}, bf16[1,1,2,32,1024]{4,3,2,1,0:T(8,128)(2,1)S(1)}, u32[]{:S(2)}, u32[]{:S(2)}) collective-permute-start(bf16[1,1,2,32,1024]{4,3,2,1,0:T(8,128)(2,1)S(1)} %slice.29), channel_id=1, source_target_pairs={{0,2},{1,3},{2,0},{3,1},{4,6},{5,7},{6,4},{7,5},{8,10},{9,11},{10,... | collective-permute-start | bytes 393224 | tf_op jit(solution)/shard_map/ppermute | solution.py:273
  57.2 1.5 %collective-permute-start.13 = (bf16[1,1,2,32,1024]{4,3,2,1,0:T(8,128)(2,1)S(1)}, bf16[1,1,2,32,1024]{4,3,2,1,0:T(8,128)(2,1)}, u32[]{:S(2)}, u32[]{:S(2)}) collective-permute-start(bf16[1,1,2,32,1024]{4,3,2,1,0:T(8,128)(2,1)S(1)} %slice.28), channel_id=1, source_target_pairs={{0,4},{1,5},{2,6},{3,7},{4,0},{5,1},{6,2},{7,3},{8,12},{9,13},{10,... | collective-permute-start | bytes 393224 | tf_op jit(solution)/shard_map/ppermute | solution.py:273
  59.2 3.8 %collective-permute-done.14.refs_14_ = bf16[1,1,2,32,1024]{4,3,2,1,0:T(8,128)(2,1)S(1)} collective-permute-done((bf16[1,1,2,32,1024]{4,3,2,1,0:T(8,128)(2,1)S(1)}, bf16[1,1,2,32,1024]{4,3,2,1,0:T(8,128)(2,1)S(1)}, u32[]{:S(2)}, u32[]{:S(2)}) %collective-permute-start.14) | collective-permute-done | bytes 131104 | tf_op jit(solution)/shard_map/ppermute | solution.py:273
  63.1 0.7 collective-permute-done.13.refs_13_
  63.9 3.5 %all-to-all-done = bf16[32,8,1024]{2,1,0:T(8,128)(2,1)S(1)} async-done(((bf16[32,8,1024]{2,1,0:T(8,128)(2,1)}), bf16[32,8,1024]{2,1,0:T(8,128)(2,1)S(1)}, u32[]{:S(2)}, u32[]{:S(2)}) %all-to-all-start) | async-done | bytes 524320 | tf_op jit(solution)/shard_map/all_to_all | solution.py:319
  67.4 0.8 copy-done.4
  68.2 3.1 %all-to-all-start.2 = ((bf16[32,8,1024]{2,1,0:T(8,128)(2,1)}), bf16[32,8,1024]{2,1,0:T(8,128)(2,1)S(1)}, u32[]{:S(2)}, u32[]{:S(2)}) async-start(bf16[32,8,1024]{2,1,0:T(8,128)(2,1)} %bitcast.4), calls=%async_computation.2 | async-start | bytes 1048576 | tf_op jit(solution)/shard_map/all_to_all | solution.py:319
  72.2 1.0 collective-permute-done.23.refs_23_
  74.4 1.0 collective-permute-done.28.refs_28_
  76.1 11.5 %shard_map.47 = bf16[2048,128]{1,0:T(8,128)(2,1)} custom-call(bf16[256,1024]{1,0:T(8,128)(2,1)} %bitcast.16, bf16[2,1,2,32,1024]{4,3,2,1,0:T(8,128)(2,1)} %copy-done.6, bf16[2,1,2,32,1024]{4,3,2,1,0:T(8,128)(2,1)} %copy-done.10, bf16[2,1,2,32,1024]{4,3,2,1,0:T(8,128)(2,1)} %copy-done.9, bf16[1,1,2,32,1024]{4,3,2,1,0:T(8,128)(2,1)} %collective-permute-done.3.refs_3_, ...), custom_call_target="tpu_custom_call" | custom-call | flops 4294967296 | bytes 8912896 | tf_op jit(solution)/shard_map/pallas_call | solution.py:189
  87.7 0.8 copy-done.5
  88.5 5.0 %all-to-all-start.1 = ((bf16[16,128,128]{2,1,0:T(8,128)(2,1)}), bf16[16,128,128]{2,1,0:T(8,128)(2,1)S(1)}, u32[]{:S(2)}, u32[]{:S(2)}) async-start(bf16[16,128,128]{2,1,0:T(8,128)(2,1)} %bitcast.18), calls=%async_computation.1 | async-start | bytes 1048576 | tf_op jit(solution)/shard_map/all_to_all | solution.py:319
  93.5 10.8 %shard_map.48.right_ref = bf16[256,1024]{1,0:T(8,128)(2,1)} custom-call(bf16[256,1024]{1,0:T(8,128)(2,1)} %bitcast.17, bf16[2,1,2,32,1024]{4,3,2,1,0:T(8,128)(2,1)} %copy-done.6, bf16[2,1,2,32,1024]{4,3,2,1,0:T(8,128)(2,1)} %copy-done.10, bf16[2,1,2,32,1024]{4,3,2,1,0:T(8,128)(2,1)} %copy-done.9, ...), custom_call_target="tpu_custom_call" | custom-call | flops 4294967296 | bytes 8912896 | tf_op jit(solution)/shard_map/pallas_call | solution.py:189
  104.3 1.0 copy-done
  105.9 16.4 %all_to_all.20 = bf16[32,16,256]{2,1,0:T(8,128)(2,1)S(1)} all-to-all(bf16[32,16,256]{2,1,0:T(8,128)(2,1)S(1)} %bitcast.15), channel_id=1, replica_groups=mesh['cuts'=1,'mode'=32] {'mode'}, dimensions={0} | all-to-all | bytes 524288 | tf_op jit(solution)/shard_map/all_to_all | solution.py:319
  (102 shorter events, 10.6 us)
Async XLA Ops:
  1.1 9.3 %collective-permute-start.4 = (bf16[2,1,2,32,1024]{4,3,2,1,0:T(8,128)(2,1)S(1)}, bf16[2,1,2,32,1024]{4,3,2,1,0:T(8,128)(2,1)S(1)}, u32[]{:S(2)}, u32[]{:S(2)}) collective-permute-start(bf16[2,1,2,32,1024]{4,3,2,1,0:T(8,128)(2,1)S(1)} %maximum_bitcast_fusion.refs_0_), channel_id=1, source_target_pairs={{0,4},{1,5},{2,6},{3,7},{4,0},{5,1},{6,2},{7,3},{8,12},{9,13},{10,... | collective-permute-start | bytes 786440 | tf_op jit(solution)/shard_map/ppermute | solution.py:273
  4.1 8.1 %collective-permute-start.2 = (bf16[2,1,2,32,1024]{4,3,2,1,0:T(8,128)(2,1)S(1)}, bf16[2,1,2,32,1024]{4,3,2,1,0:T(8,128)(2,1)S(1)}, u32[]{:S(2)}, u32[]{:S(2)}) collective-permute-start(bf16[2,1,2,32,1024]{4,3,2,1,0:T(8,128)(2,1)S(1)} %maximum_bitcast_fusion.refs_0_), channel_id=1, source_target_pairs={{0,2},{1,3},{2,0},{3,1},{4,6},{5,7},{6,4},{7,5},{8,10},{9,11},{10,... | collective-permute-start | bytes 786440 | tf_op jit(solution)/shard_map/ppermute | solution.py:273
  5.6 14.1 %collective-permute-start.1 = (bf16[2,1,2,32,1024]{4,3,2,1,0:T(8,128)(2,1)S(1)}, bf16[2,1,2,32,1024]{4,3,2,1,0:T(8,128)(2,1)S(1)}, u32[]{:S(2)}, u32[]{:S(2)}) collective-permute-start(bf16[2,1,2,32,1024]{4,3,2,1,0:T(8,128)(2,1)S(1)} %maximum_bitcast_fusion.refs_0_), channel_id=1, source_target_pairs={{0,16},{1,17},{2,18},{3,19},{4,20},{5,21},{6,22},{7,23},{8,24},{9,... | collective-permute-start | bytes 786440 | tf_op jit(solution)/shard_map/ppermute | solution.py:273
  8.2 11.7 %collective-permute-start = (bf16[2,1,2,32,1024]{4,3,2,1,0:T(8,128)(2,1)S(1)}, bf16[2,1,2,32,1024]{4,3,2,1,0:T(8,128)(2,1)S(1)}, u32[]{:S(2)}, u32[]{:S(2)}) collective-permute-start(bf16[2,1,2,32,1024]{4,3,2,1,0:T(8,128)(2,1)S(1)} %maximum_bitcast_fusion.refs_0_), channel_id=1, source_target_pairs={{0,8},{1,9},{2,10},{3,11},{4,12},{5,13},{6,14},{7,15},{8,0},{9,1},... | collective-permute-start | bytes 786440 | tf_op jit(solution)/shard_map/ppermute | solution.py:273
  10.5 9.5 %collective-permute-start.5 = (bf16[1,1,2,32,1024]{4,3,2,1,0:T(8,128)(2,1)S(1)}, bf16[1,1,2,32,1024]{4,3,2,1,0:T(8,128)(2,1)S(1)}, u32[]{:S(2)}, u32[]{:S(2)}) collective-permute-start(bf16[1,1,2,32,1024]{4,3,2,1,0:T(8,128)(2,1)S(1)} %slice.25), channel_id=1, source_target_pairs={{0,2},{1,3},{2,0},{3,1},{4,6},{5,7},{6,4},{7,5},{8,10},{9,11},{10,... | collective-permute-start | bytes 393224 | tf_op jit(solution)/shard_map/ppermute | solution.py:273
  12.3 7.7 %collective-permute-start.3 = (bf16[1,1,2,32,1024]{4,3,2,1,0:T(8,128)(2,1)S(1)}, bf16[1,1,2,32,1024]{4,3,2,1,0:T(8,128)(2,1)}, u32[]{:S(2)}, u32[]{:S(2)}) collective-permute-start(bf16[1,1,2,32,1024]{4,3,2,1,0:T(8,128)(2,1)S(1)} %slice.24), channel_id=1, source_target_pairs={{0,4},{1,5},{2,6},{3,7},{4,0},{5,1},{6,2},{7,3},{8,12},{9,13},{10,... | collective-permute-start | bytes 393224 | tf_op jit(solution)/shard_map/ppermute | solution.py:273
  20.0 12.6 %collective-permute-start.8 = (bf16[2,2,2,32,1024]{4,3,2,1,0:T(8,128)(2,1)S(1)}, bf16[2,2,2,32,1024]{4,3,2,1,0:T(8,128)(2,1)S(1)}, u32[]{:S(2)}, u32[]{:S(2)}) collective-permute-start(bf16[2,2,2,32,1024]{4,3,2,1,0:T(8,128)(2,1)S(1)} %pad_maximum_fusion.refs_5_), channel_id=1, source_target_pairs={{0,4},{1,5},{2,6},{3,7},{4,0},{5,1},{6,2},{7,3},{8,12},{9,13},{10,... | collective-permute-start | bytes 1572872 | tf_op jit(solution)/shard_map/ppermute | solution.py:273
  20.6 12.6 %collective-permute-start.6 = (bf16[2,2,2,32,1024]{4,3,2,1,0:T(8,128)(2,1)S(1)}, bf16[2,2,2,32,1024]{4,3,2,1,0:T(8,128)(2,1)S(1)}, u32[]{:S(2)}, u32[]{:S(2)}) collective-permute-start(bf16[2,2,2,32,1024]{4,3,2,1,0:T(8,128)(2,1)S(1)} %pad_maximum_fusion.refs_5_), channel_id=1, source_target_pairs={{0,2},{1,3},{2,0},{3,1},{4,6},{5,7},{6,4},{7,5},{8,10},{9,11},{10,... | collective-permute-start | bytes 1572872 | tf_op jit(solution)/shard_map/ppermute | solution.py:273
  21.1 14.0 %collective-permute-start.10 = (bf16[2,1,2,32,1024]{4,3,2,1,0:T(8,128)(2,1)S(1)}, bf16[2,1,2,32,1024]{4,3,2,1,0:T(8,128)(2,1)}, u32[]{:S(2)}, u32[]{:S(2)}) collective-permute-start(bf16[2,1,2,32,1024]{4,3,2,1,0:T(8,128)(2,1)S(1)} %maximum_bitcast_fusion.refs_0_), channel_id=1, source_target_pairs={{0,24},{1,25},{2,26},{3,27},{4,28},{5,29},{6,30},{7,31},{8,16},{9,... | collective-permute-start | bytes 786440 | tf_op jit(solution)/shard_map/ppermute | solution.py:273
  32.6 9.1 %collective-permute-start.9 = (bf16[1,2,2,32,1024]{4,3,2,1,0:T(8,128)(2,1)S(1)}, bf16[1,2,2,32,1024]{4,3,2,1,0:T(8,128)(2,1)}, u32[]{:S(2)}, u32[]{:S(2)}) collective-permute-start(bf16[1,2,2,32,1024]{4,3,2,1,0:T(8,128)(2,1)S(1)} %slice.27), channel_id=1, source_target_pairs={{0,2},{1,3},{2,0},{3,1},{4,6},{5,7},{6,4},{7,5},{8,10},{9,11},{10,... | collective-permute-start | bytes 786440 | tf_op jit(solution)/shard_map/ppermute | solution.py:273
  33.2 8.8 %collective-permute-start.7 = (bf16[1,2,2,32,1024]{4,3,2,1,0:T(8,128)(2,1)S(1)}, bf16[1,2,2,32,1024]{4,3,2,1,0:T(8,128)(2,1)}, u32[]{:S(2)}, u32[]{:S(2)}) collective-permute-start(bf16[1,2,2,32,1024]{4,3,2,1,0:T(8,128)(2,1)S(1)} %slice.26), channel_id=1, source_target_pairs={{0,4},{1,5},{2,6},{3,7},{4,0},{5,1},{6,2},{7,3},{8,12},{9,13},{10,... | collective-permute-start | bytes 786440 | tf_op jit(solution)/shard_map/ppermute | solution.py:273
  35.1 9.7 %collective-permute-start.12 = (bf16[2,1,2,32,1024]{4,3,2,1,0:T(8,128)(2,1)}, bf16[2,1,2,32,1024]{4,3,2,1,0:T(8,128)(2,1)S(1)}, u32[]{:S(2)}, u32[]{:S(2)}) collective-permute-start(bf16[2,1,2,32,1024]{4,3,2,1,0:T(8,128)(2,1)} %collective-permute-done.10.refs_10_), channel_id=1, source_target_pairs={{0,4},{1,5},{2,6},{3,7},{4,0},{5,1},{6,2},{7,3},{8,12},{9,13},{10,... | collective-permute-start | bytes 786440 | tf_op jit(solution)/shard_map/ppermute | solution.py:273
  35.3 9.4 %collective-permute-start.11 = (bf16[2,1,2,32,1024]{4,3,2,1,0:T(8,128)(2,1)}, bf16[2,1,2,32,1024]{4,3,2,1,0:T(8,128)(2,1)}, u32[]{:S(2)}, u32[]{:S(2)}) collective-permute-start(bf16[2,1,2,32,1024]{4,3,2,1,0:T(8,128)(2,1)} %collective-permute-done.10.refs_10_), channel_id=1, source_target_pairs={{0,2},{1,3},{2,0},{3,1},{4,6},{5,7},{6,4},{7,5},{8,10},{9,11},{10,... | collective-permute-start | bytes 786440 | tf_op jit(solution)/shard_map/ppermute | solution.py:273
  44.7 22.7 %all-to-all-start = ((bf16[32,8,1024]{2,1,0:T(8,128)(2,1)}), bf16[32,8,1024]{2,1,0:T(8,128)(2,1)S(1)}, u32[]{:S(2)}, u32[]{:S(2)}) async-start(bf16[32,8,1024]{2,1,0:T(8,128)(2,1)} %bitcast), calls=%async_computation | async-start | bytes 1048576 | tf_op jit(solution)/shard_map/all_to_all | solution.py:319
  51.9 1.6 %collective-permute-start.15 = (bf16[2,1,2,32,1024]{4,3,2,1,0:T(8,128)(2,1)S(1)}, bf16[2,1,2,32,1024]{4,3,2,1,0:T(8,128)(2,1)S(1)}, u32[]{:S(2)}, u32[]{:S(2)}) collective-permute-start(bf16[2,1,2,32,1024]{4,3,2,1,0:T(8,128)(2,1)S(1)} %maximum_bitcast_fusion.refs_0_), channel_id=1, source_target_pairs={{0,1},{1,0},{2,3},{3,2},{4,5},{5,4},{6,7},{7,6},{8,9},{9,8},{10,11... | collective-permute-start | bytes 786440 | tf_op jit(solution)/shard_map/ppermute | solution.py:273
  52.2 5.0 %collective-permute-start.17 = (bf16[2,1,2,32,1024]{4,3,2,1,0:T(8,128)(2,1)S(1)}, bf16[2,1,2,32,1024]{4,3,2,1,0:T(8,128)(2,1)S(1)}, u32[]{:S(2)}, u32[]{:S(2)}) collective-permute-start(bf16[2,1,2,32,1024]{4,3,2,1,0:T(8,128)(2,1)S(1)} %collective-permute-done.4.refs_2_), channel_id=1, source_target_pairs={{0,1},{1,0},{2,3},{3,2},{4,5},{5,4},{6,7},{7,6},{8,9},{9,8},{10,11... | collective-permute-start | bytes 786440 | tf_op jit(solution)/shard_map/ppermute | solution.py:273
  52.5 6.2 %collective-permute-start.16 = (bf16[2,1,2,32,1024]{4,3,2,1,0:T(8,128)(2,1)S(1)}, bf16[2,1,2,32,1024]{4,3,2,1,0:T(8,128)(2,1)S(1)}, u32[]{:S(2)}, u32[]{:S(2)}) collective-permute-start(bf16[2,1,2,32,1024]{4,3,2,1,0:T(8,128)(2,1)S(1)} %collective-permute-done.2.refs_1_), channel_id=1, source_target_pairs={{0,1},{1,0},{2,3},{3,2},{4,5},{5,4},{6,7},{7,6},{8,9},{9,8},{10,11... | collective-permute-start | bytes 786440 | tf_op jit(solution)/shard_map/ppermute | solution.py:273
  52.7 18.6 %collective-permute-start.20 = (bf16[2,2,2,32,1024]{4,3,2,1,0:T(8,128)(2,1)S(1)}, bf16[2,2,2,32,1024]{4,3,2,1,0:T(8,128)(2,1)}, u32[]{:S(2)}, u32[]{:S(2)}) collective-permute-start(bf16[2,2,2,32,1024]{4,3,2,1,0:T(8,128)(2,1)S(1)} %pad_maximum_fusion.refs_5_), channel_id=1, source_target_pairs={{0,1},{1,0},{2,3},{3,2},{4,5},{5,4},{6,7},{7,6},{8,9},{9,8},{10,11... | collective-permute-start | bytes 1572872 | tf_op jit(solution)/shard_map/ppermute | solution.py:273
  53.0 2.4 %collective-permute-start.19 = (bf16[1,1,2,32,1024]{4,3,2,1,0:T(8,128)(2,1)S(1)}, bf16[1,1,2,32,1024]{4,3,2,1,0:T(8,128)(2,1)S(1)}, u32[]{:S(2)}, u32[]{:S(2)}) collective-permute-start(bf16[1,1,2,32,1024]{4,3,2,1,0:T(8,128)(2,1)S(1)} %collective-permute-done.5.refs_4_), channel_id=1, source_target_pairs={{0,1},{1,0},{2,3},{3,2},{4,5},{5,4},{6,7},{7,6},{8,9},{9,8},{10,11... | collective-permute-start | bytes 393224 | tf_op jit(solution)/shard_map/ppermute | solution.py:273
  54.2 4.4 %collective-permute-start.18 = (bf16[1,1,2,32,1024]{4,3,2,1,0:T(8,128)(2,1)}, bf16[1,1,2,32,1024]{4,3,2,1,0:T(8,128)(2,1)S(1)}, u32[]{:S(2)}, u32[]{:S(2)}) collective-permute-start(bf16[1,1,2,32,1024]{4,3,2,1,0:T(8,128)(2,1)} %collective-permute-done.3.refs_3_), channel_id=1, source_target_pairs={{0,1},{1,0},{2,3},{3,2},{4,5},{5,4},{6,7},{7,6},{8,9},{9,8},{10,11... | collective-permute-start | bytes 393224 | tf_op jit(solution)/shard_map/ppermute | solution.py:273
  55.4 7.6 %collective-permute-start.14 = (bf16[1,1,2,32,1024]{4,3,2,1,0:T(8,128)(2,1)S(1)}, bf16[1,1,2,32,1024]{4,3,2,1,0:T(8,128)(2,1)S(1)}, u32[]{:S(2)}, u32[]{:S(2)}) collective-permute-start(bf16[1,1,2,32,1024]{4,3,2,1,0:T(8,128)(2,1)S(1)} %slice.29), channel_id=1, source_target_pairs={{0,2},{1,3},{2,0},{3,1},{4,6},{5,7},{6,4},{7,5},{8,10},{9,11},{10,... | collective-permute-start | bytes 393224 | tf_op jit(solution)/shard_map/ppermute | solution.py:273
  57.2 6.7 %collective-permute-start.13 = (bf16[1,1,2,32,1024]{4,3,2,1,0:T(8,128)(2,1)S(1)}, bf16[1,1,2,32,1024]{4,3,2,1,0:T(8,128)(2,1)}, u32[]{:S(2)}, u32[]{:S(2)}) collective-permute-start(bf16[1,1,2,32,1024]{4,3,2,1,0:T(8,128)(2,1)S(1)} %slice.28), channel_id=1, source_target_pairs={{0,4},{1,5},{2,6},{3,7},{4,0},{5,1},{6,2},{7,3},{8,12},{9,13},{10,... | collective-permute-start | bytes 393224 | tf_op jit(solution)/shard_map/ppermute | solution.py:273
  58.6 13.0 %collective-permute-start.25 = (bf16[2,1,2,32,1024]{4,3,2,1,0:T(8,128)(2,1)}, bf16[2,1,2,32,1024]{4,3,2,1,0:T(8,128)(2,1)}, u32[]{:S(2)}, u32[]{:S(2)}) collective-permute-start(bf16[2,1,2,32,1024]{4,3,2,1,0:T(8,128)(2,1)} %collective-permute-done.10.refs_10_), channel_id=1, source_target_pairs={{0,1},{1,0},{2,3},{3,2},{4,5},{5,4},{6,7},{7,6},{8,9},{9,8},{10,11... | collective-permute-start | bytes 786440 | tf_op jit(solution)/shard_map/ppermute | solution.py:273
  58.7 13.5 %collective-permute-start.22 = (bf16[2,2,2,32,1024]{4,3,2,1,0:T(8,128)(2,1)S(1)}, bf16[2,2,2,32,1024]{4,3,2,1,0:T(8,128)(2,1)S(1)}, u32[]{:S(2)}, u32[]{:S(2)}) collective-permute-start(bf16[2,2,2,32,1024]{4,3,2,1,0:T(8,128)(2,1)S(1)} %collective-permute-done.8.refs_7_), channel_id=1, source_target_pairs={{0,1},{1,0},{2,3},{3,2},{4,5},{5,4},{6,7},{7,6},{8,9},{9,8},{10,11... | collective-permute-start | bytes 1572872 | tf_op jit(solution)/shard_map/ppermute | solution.py:273
  63.0 10.1 %collective-permute-start.21 = (bf16[2,2,2,32,1024]{4,3,2,1,0:T(8,128)(2,1)S(1)}, bf16[2,2,2,32,1024]{4,3,2,1,0:T(8,128)(2,1)}, u32[]{:S(2)}, u32[]{:S(2)}) collective-permute-start(bf16[2,2,2,32,1024]{4,3,2,1,0:T(8,128)(2,1)S(1)} %collective-permute-done.6.refs_6_), channel_id=1, source_target_pairs={{0,1},{1,0},{2,3},{3,2},{4,5},{5,4},{6,7},{7,6},{8,9},{9,8},{10,11... | collective-permute-start | bytes 1572872 | tf_op jit(solution)/shard_map/ppermute | solution.py:273
  63.8 8.0 %collective-permute-start.24 = (bf16[1,2,2,32,1024]{4,3,2,1,0:T(8,128)(2,1)}, bf16[1,2,2,32,1024]{4,3,2,1,0:T(8,128)(2,1)}, u32[]{:S(2)}, u32[]{:S(2)}) collective-permute-start(bf16[1,2,2,32,1024]{4,3,2,1,0:T(8,128)(2,1)} %collective-permute-done.9.refs_9_), channel_id=1, source_target_pairs={{0,1},{1,0},{2,3},{3,2},{4,5},{5,4},{6,7},{7,6},{8,9},{9,8},{10,11... | collective-permute-start | bytes 786440 | tf_op jit(solution)/shard_map/ppermute | solution.py:273
  68.2 19.5 %all-to-all-start.2 = ((bf16[32,8,1024]{2,1,0:T(8,128)(2,1)}), bf16[32,8,1024]{2,1,0:T(8,128)(2,1)S(1)}, u32[]{:S(2)}, u32[]{:S(2)}) async-start(bf16[32,8,1024]{2,1,0:T(8,128)(2,1)} %bitcast.4), calls=%async_computation.2 | async-start | bytes 1048576 | tf_op jit(solution)/shard_map/all_to_all | solution.py:319
  71.3 1.8 %collective-permute-start.23 = (bf16[1,2,2,32,1024]{4,3,2,1,0:T(8,128)(2,1)}, bf16[1,2,2,32,1024]{4,3,2,1,0:T(8,128)(2,1)S(1)}, u32[]{:S(2)}, u32[]{:S(2)}) collective-permute-start(bf16[1,2,2,32,1024]{4,3,2,1,0:T(8,128)(2,1)} %collective-permute-done.7.refs_8_), channel_id=1, source_target_pairs={{0,1},{1,0},{2,3},{3,2},{4,5},{5,4},{6,7},{7,6},{8,9},{9,8},{10,11... | collective-permute-start | bytes 786440 | tf_op jit(solution)/shard_map/ppermute | solution.py:273
  71.6 1.7 %collective-permute-start.27 = (bf16[2,1,2,32,1024]{4,3,2,1,0:T(8,128)(2,1)S(1)}, bf16[2,1,2,32,1024]{4,3,2,1,0:T(8,128)(2,1)S(1)}, u32[]{:S(2)}, u32[]{:S(2)}) collective-permute-start(bf16[2,1,2,32,1024]{4,3,2,1,0:T(8,128)(2,1)S(1)} %copy-done.12), channel_id=1, source_target_pairs={{0,1},{1,0},{2,3},{3,2},{4,5},{5,4},{6,7},{7,6},{8,9},{9,8},{10,11... | collective-permute-start | bytes 786440 | tf_op jit(solution)/shard_map/ppermute | solution.py:273
  71.9 2.0 %collective-permute-start.26 = (bf16[2,1,2,32,1024]{4,3,2,1,0:T(8,128)(2,1)}, bf16[2,1,2,32,1024]{4,3,2,1,0:T(8,128)(2,1)S(1)}, u32[]{:S(2)}, u32[]{:S(2)}) collective-permute-start(bf16[2,1,2,32,1024]{4,3,2,1,0:T(8,128)(2,1)} %collective-permute-done.11.refs_11_), channel_id=1, source_target_pairs={{0,1},{1,0},{2,3},{3,2},{4,5},{5,4},{6,7},{7,6},{8,9},{9,8},{10,11... | collective-permute-start | bytes 786440 | tf_op jit(solution)/shard_map/ppermute | solution.py:273
  73.9 1.6 %collective-permute-start.28 = (bf16[1,1,2,32,1024]{4,3,2,1,0:T(8,128)(2,1)}, bf16[1,1,2,32,1024]{4,3,2,1,0:T(8,128)(2,1)S(1)}, u32[]{:S(2)}, u32[]{:S(2)}) collective-permute-start(bf16[1,1,2,32,1024]{4,3,2,1,0:T(8,128)(2,1)} %collective-permute-done.13.refs_13_), channel_id=1, source_target_pairs={{0,1},{1,0},{2,3},{3,2},{4,5},{5,4},{6,7},{7,6},{8,9},{9,8},{10,11... | collective-permute-start | bytes 393224 | tf_op jit(solution)/shard_map/ppermute | solution.py:273
  88.5 15.8 %all-to-all-start.1 = ((bf16[16,128,128]{2,1,0:T(8,128)(2,1)}), bf16[16,128,128]{2,1,0:T(8,128)(2,1)S(1)}, u32[]{:S(2)}, u32[]{:S(2)}) async-start(bf16[16,128,128]{2,1,0:T(8,128)(2,1)} %bitcast.18), calls=%async_computation.1 | async-start | bytes 1048576 | tf_op jit(solution)/shard_map/all_to_all | solution.py:319
  (27 other events, 368.8 us)

commit v15 on v14

--- a/solution.py
+++ b/solution.py
@@ -302,8 +302,9 @@
             tied = (blocks[3][0], blocks[4][0]) if number == 1 else (*packed, blocks[6][0], blocks[7][0])
             value, *_ = lax.optimization_barrier((value, *tied))
         blocks += plane(value, sources)
-    left, *_ = lax.optimization_barrier((packed[0], blocks[8][0], blocks[9][0], blocks[-4][0], blocks[-3][0]))
-    right, *_ = lax.optimization_barrier((packed[1], blocks[-2][0], blocks[-1][0]))
+    left, *_ = lax.optimization_barrier((packed[0], blocks[8][0], blocks[9][0], blocks[-2][0], blocks[-1][0]))
+    left = trade(left)
+    right, left = lax.optimization_barrier((packed[1], left))
     last = len(blocks) - 2
     near = []
     for number, (value, sources, gates) in enumerate(blocks):
@@ -312,7 +313,7 @@
         near.append((flip(value, 0), tuple(source + (0,) for source in sources), gates))
     blocks += near
     plan = tuple((sources, gates) for _, sources, gates in blocks)
-    return [value for value, _, _ in blocks], plan, trade(left), trade(right)
+    return [value for value, _, _ in blocks], plan, left, trade(right)
 
 
 def trade(value, groups=None):

time: 124 us -> 127 us (1.024)
  waiting for transfers between devices: 31 us -> 36.4 us
  starting transfers between devices: 42.5 us -> 40.2 us
    all_to_all x3, waiting for transfers between devices: 3.49 us -> 9.82 us  [trade(): lax.all_to_all(value, 'mode', split_axis=0, concat_axis=0, axis_index_gro...]
    ppermute x30, starting transfers between devices: 27.4 us -> 25.8 us  [flip(): return lax.ppermute(value, 'mode', pairs)]
    unnamed x52 -> x60, local copies, waits for them, and re-layouts: 4.06 us -> 5.11 us
  transfers between devices with their start and end apart: 33 -> 33, of which waited for: 15 -> 17; matrix products, arithmetic and copies ran while one was open for 1% -> 0% of each run, Pallas kernels for 21% -> 20%
where the time goes in v15:
time: 127 us; the launch traced here: 126 us
  starting transfers between devices  40.2 us (32%)
  waiting for transfers between devices  36.4 us (29%)
  Pallas kernels  25.9 us (20%)
  blocking collectives  16.4 us (13%)
  local copies, waits for them, and re-layouts  5.8 us (5%)
    ppermute x30, waiting for transfers between devices, flip(): return lax.ppermute(value, 'mode', pairs)  26.6 us
    pallas_call x4, Pallas kernels, call(): pl.pallas_call(kernel, out_shape=[out] * outputs if outputs else out, in_...  25.9 us
    ppermute x30, starting transfers between devices, flip(): return lax.ppermute(value, 'mode', pairs)  25.8 us
    all_to_all x1, blocking collectives, trade(): lax.all_to_all(value, 'mode', split_axis=0, concat_axis=0, axis_index_gro...  16.4 us
    all_to_all x3, starting transfers between devices, trade(): lax.all_to_all(value, 'mode', split_axis=0, concat_axis=0, axis_index_gro...  14.4 us
    all_to_all x3, waiting for transfers between devices, trade(): lax.all_to_all(value, 'mode', split_axis=0, concat_axis=0, axis_index_gro...  9.82 us
    unnamed x60, local copies, waits for them, and re-layouts  5.11 us
  transfers between devices with their start and end apart: 33, of which 17 were waited for; matrix products, arithmetic and copies ran while one was open for 0% of the time, Pallas kernels for 20%

profile of v15, /device:TPU:0, one launch (start us, length us, event | category | flops | bytes accessed | tf_op | source)
XLA Modules:
  0.0 126.1 jit_solution(11642086459253955187)
XLA Ops:
  0.0 1.1 maximum_bitcast_fusion.refs_0_
  1.1 3.0 %collective-permute-start.4 = (bf16[2,1,2,32,1024]{4,3,2,1,0:T(8,128)(2,1)S(1)}, bf16[2,1,2,32,1024]{4,3,2,1,0:T(8,128)(2,1)S(1)}, u32[]{:S(2)}, u32[]{:S(2)}) collective-permute-start(bf16[2,1,2,32,1024]{4,3,2,1,0:T(8,128)(2,1)S(1)} %maximum_bitcast_fusion.refs_0_), channel_id=1, source_target_pairs={{0,4},{1,5},{2,6},{3,7},{4,0},{5,1},{6,2},{7,3},{8,12},{9,13},{10,... | collective-permute-start | bytes 786440 | tf_op jit(solution)/shard_map/ppermute | solution.py:273
  4.1 1.5 %collective-permute-start.2 = (bf16[2,1,2,32,1024]{4,3,2,1,0:T(8,128)(2,1)S(1)}, bf16[2,1,2,32,1024]{4,3,2,1,0:T(8,128)(2,1)S(1)}, u32[]{:S(2)}, u32[]{:S(2)}) collective-permute-start(bf16[2,1,2,32,1024]{4,3,2,1,0:T(8,128)(2,1)S(1)} %maximum_bitcast_fusion.refs_0_), channel_id=1, source_target_pairs={{0,2},{1,3},{2,0},{3,1},{4,6},{5,7},{6,4},{7,5},{8,10},{9,11},{10,... | collective-permute-start | bytes 786440 | tf_op jit(solution)/shard_map/ppermute | solution.py:273
  5.6 2.6 %collective-permute-start.1 = (bf16[2,1,2,32,1024]{4,3,2,1,0:T(8,128)(2,1)S(1)}, bf16[2,1,2,32,1024]{4,3,2,1,0:T(8,128)(2,1)S(1)}, u32[]{:S(2)}, u32[]{:S(2)}) collective-permute-start(bf16[2,1,2,32,1024]{4,3,2,1,0:T(8,128)(2,1)S(1)} %maximum_bitcast_fusion.refs_0_), channel_id=1, source_target_pairs={{0,16},{1,17},{2,18},{3,19},{4,20},{5,21},{6,22},{7,23},{8,24},{9,... | collective-permute-start | bytes 786440 | tf_op jit(solution)/shard_map/ppermute | solution.py:273
  8.2 1.6 %collective-permute-start = (bf16[2,1,2,32,1024]{4,3,2,1,0:T(8,128)(2,1)S(1)}, bf16[2,1,2,32,1024]{4,3,2,1,0:T(8,128)(2,1)S(1)}, u32[]{:S(2)}, u32[]{:S(2)}) collective-permute-start(bf16[2,1,2,32,1024]{4,3,2,1,0:T(8,128)(2,1)S(1)} %maximum_bitcast_fusion.refs_0_), channel_id=1, source_target_pairs={{0,8},{1,9},{2,10},{3,11},{4,12},{5,13},{6,14},{7,15},{8,0},{9,1},... | collective-permute-start | bytes 786440 | tf_op jit(solution)/shard_map/ppermute | solution.py:273
  10.5 1.8 %collective-permute-start.5 = (bf16[1,1,2,32,1024]{4,3,2,1,0:T(8,128)(2,1)S(1)}, bf16[1,1,2,32,1024]{4,3,2,1,0:T(8,128)(2,1)S(1)}, u32[]{:S(2)}, u32[]{:S(2)}) collective-permute-start(bf16[1,1,2,32,1024]{4,3,2,1,0:T(8,128)(2,1)S(1)} %slice.25), channel_id=1, source_target_pairs={{0,2},{1,3},{2,0},{3,1},{4,6},{5,7},{6,4},{7,5},{8,10},{9,11},{10,... | collective-permute-start | bytes 393224 | tf_op jit(solution)/shard_map/ppermute | solution.py:273
  12.3 1.6 %collective-permute-start.3 = (bf16[1,1,2,32,1024]{4,3,2,1,0:T(8,128)(2,1)S(1)}, bf16[1,1,2,32,1024]{4,3,2,1,0:T(8,128)(2,1)}, u32[]{:S(2)}, u32[]{:S(2)}) collective-permute-start(bf16[1,1,2,32,1024]{4,3,2,1,0:T(8,128)(2,1)S(1)} %slice.24), channel_id=1, source_target_pairs={{0,4},{1,5},{2,6},{3,7},{4,0},{5,1},{6,2},{7,3},{8,12},{9,13},{10,... | collective-permute-start | bytes 393224 | tf_op jit(solution)/shard_map/ppermute | solution.py:273
  13.8 5.9 %collective-permute-done.1 = bf16[2,1,2,32,1024]{4,3,2,1,0:T(8,128)(2,1)S(1)} collective-permute-done((bf16[2,1,2,32,1024]{4,3,2,1,0:T(8,128)(2,1)S(1)}, bf16[2,1,2,32,1024]{4,3,2,1,0:T(8,128)(2,1)S(1)}, u32[]{:S(2)}, u32[]{:S(2)}) %collective-permute-start.1) | collective-permute-done | bytes 262176 | tf_op jit(solution)/shard_map/ppermute | solution.py:273
  21.1 3.2 %collective-permute-start.10 = (bf16[2,1,2,32,1024]{4,3,2,1,0:T(8,128)(2,1)S(1)}, bf16[2,1,2,32,1024]{4,3,2,1,0:T(8,128)(2,1)S(1)}, u32[]{:S(2)}, u32[]{:S(2)}) collective-permute-start(bf16[2,1,2,32,1024]{4,3,2,1,0:T(8,128)(2,1)S(1)} %maximum_bitcast_fusion.refs_0_), channel_id=1, source_target_pairs={{0,24},{1,25},{2,26},{3,27},{4,28},{5,29},{6,30},{7,31},{8,16},{9,... | collective-permute-start | bytes 786440 | tf_op jit(solution)/shard_map/ppermute | solution.py:273
  24.3 3.0 %shard_map.46 = (bf16[256,1024]{1,0:T(8,128)(2,1)}, bf16[256,1024]{1,0:T(8,128)(2,1)}) custom-call(bf16[4,2,64,1024]{3,2,1,0:T(8,128)(2,1)S(1)} %copy-done.1, s32[4,1024]{1,0:T(4,128)S(1)} %copy-done.2), custom_call_target="tpu_custom_call" | custom-call | flops 2147483648 | bytes 1064960 | tf_op jit(solution)/shard_map/pallas_call | solution.py:189
  27.4 3.0 %collective-permute-done.10.refs_10_ = bf16[2,1,2,32,1024]{4,3,2,1,0:T(8,128)(2,1)S(1)} collective-permute-done((bf16[2,1,2,32,1024]{4,3,2,1,0:T(8,128)(2,1)S(1)}, bf16[2,1,2,32,1024]{4,3,2,1,0:T(8,128)(2,1)S(1)}, u32[]{:S(2)}, u32[]{:S(2)}) %collective-permute-start.10) | collective-permute-done | bytes 262176 | tf_op jit(solution)/shard_map/ppermute | solution.py:273
  30.4 2.2 %collective-permute-done.8.refs_7_ = bf16[2,2,2,32,1024]{4,3,2,1,0:T(8,128)(2,1)S(1)} collective-permute-done((bf16[2,2,2,32,1024]{4,3,2,1,0:T(8,128)(2,1)S(1)}, bf16[2,2,2,32,1024]{4,3,2,1,0:T(8,128)(2,1)S(1)}, u32[]{:S(2)}, u32[]{:S(2)}) %collective-permute-start.8) | collective-permute-done | bytes 524320 | tf_op jit(solution)/shard_map/ppermute | solution.py:273
  32.8 1.5 %collective-permute-start.13 = (bf16[2,1,2,32,1024]{4,3,2,1,0:T(8,128)(2,1)S(1)}, bf16[2,1,2,32,1024]{4,3,2,1,0:T(8,128)(2,1)S(1)}, u32[]{:S(2)}, u32[]{:S(2)}) collective-permute-start(bf16[2,1,2,32,1024]{4,3,2,1,0:T(8,128)(2,1)S(1)} %collective-permute-done.10.refs_10_), channel_id=1, source_target_pairs={{0,4},{1,5},{2,6},{3,7},{4,0},{5,1},{6,2},{7,3},{8,12},{9,13},{10,... | collective-permute-start | bytes 786440 | tf_op jit(solution)/shard_map/ppermute | solution.py:273
  34.9 1.6 %collective-permute-start.9 = (bf16[1,2,2,32,1024]{4,3,2,1,0:T(8,128)(2,1)S(1)}, bf16[1,2,2,32,1024]{4,3,2,1,0:T(8,128)(2,1)}, u32[]{:S(2)}, u32[]{:S(2)}) collective-permute-start(bf16[1,2,2,32,1024]{4,3,2,1,0:T(8,128)(2,1)S(1)} %slice.27), channel_id=1, source_target_pairs={{0,2},{1,3},{2,0},{3,1},{4,6},{5,7},{6,4},{7,5},{8,10},{9,11},{10,... | collective-permute-start | bytes 786440 | tf_op jit(solution)/shard_map/ppermute | solution.py:273
  37.1 5.0 %collective-permute-done.13.refs_12_ = bf16[2,1,2,32,1024]{4,3,2,1,0:T(8,128)(2,1)S(1)} collective-permute-done((bf16[2,1,2,32,1024]{4,3,2,1,0:T(8,128)(2,1)S(1)}, bf16[2,1,2,32,1024]{4,3,2,1,0:T(8,128)(2,1)S(1)}, u32[]{:S(2)}, u32[]{:S(2)}) %collective-permute-start.13) | collective-permute-done | bytes 262176 | tf_op jit(solution)/shard_map/ppermute | solution.py:273
  42.6 1.0 collective-permute-done.11.refs_11_
  44.3 2.6 %collective-permute-done.9.refs_9_ = bf16[1,2,2,32,1024]{4,3,2,1,0:T(8,128)(2,1)} collective-permute-done((bf16[1,2,2,32,1024]{4,3,2,1,0:T(8,128)(2,1)S(1)}, bf16[1,2,2,32,1024]{4,3,2,1,0:T(8,128)(2,1)}, u32[]{:S(2)}, u32[]{:S(2)}) %collective-permute-start.9) | collective-permute-done | bytes 262176 | tf_op jit(solution)/shard_map/ppermute | solution.py:273
  46.9 1.3 %collective-permute-done.14.refs_14_ = bf16[1,1,2,32,1024]{4,3,2,1,0:T(8,128)(2,1)S(1)} collective-permute-done((bf16[1,1,2,32,1024]{4,3,2,1,0:T(8,128)(2,1)S(1)}, bf16[1,1,2,32,1024]{4,3,2,1,0:T(8,128)(2,1)S(1)}, u32[]{:S(2)}, u32[]{:S(2)}) %collective-permute-start.14) | collective-permute-done | bytes 131104 | tf_op jit(solution)/shard_map/ppermute | solution.py:273
  48.9 6.4 %all-to-all-start = ((bf16[32,8,1024]{2,1,0:T(8,128)(2,1)}), bf16[32,8,1024]{2,1,0:T(8,128)(2,1)S(1)}, u32[]{:S(2)}, u32[]{:S(2)}) async-start(bf16[32,8,1024]{2,1,0:T(8,128)(2,1)} %bitcast.1), calls=%async_computation | async-start | bytes 1048576 | tf_op jit(solution)/shard_map/all_to_all | solution.py:320
  57.1 1.6 %collective-permute-done.19.refs_19_ = bf16[1,1,2,32,1024]{4,3,2,1,0:T(8,128)(2,1)S(1)} collective-permute-done((bf16[1,1,2,32,1024]{4,3,2,1,0:T(8,128)(2,1)S(1)}, bf16[1,1,2,32,1024]{4,3,2,1,0:T(8,128)(2,1)S(1)}, u32[]{:S(2)}, u32[]{:S(2)}) %collective-permute-start.19) | collective-permute-done | bytes 131104 | tf_op jit(solution)/shard_map/ppermute | solution.py:273
  60.0 0.7 copy-done.19
  61.0 9.8 %all-to-all-done = bf16[32,8,1024]{2,1,0:T(8,128)(2,1)S(1)} async-done(((bf16[32,8,1024]{2,1,0:T(8,128)(2,1)}), bf16[32,8,1024]{2,1,0:T(8,128)(2,1)S(1)}, u32[]{:S(2)}, u32[]{:S(2)}) %all-to-all-start) | async-done | bytes 524320 | tf_op jit(solution)/shard_map/all_to_all | solution.py:320
  70.8 0.8 copy-done.4
  71.6 3.1 %all-to-all-start.2 = ((bf16[32,8,1024]{2,1,0:T(8,128)(2,1)}), bf16[32,8,1024]{2,1,0:T(8,128)(2,1)S(1)}, u32[]{:S(2)}, u32[]{:S(2)}) async-start(bf16[32,8,1024]{2,1,0:T(8,128)(2,1)} %bitcast), calls=%async_computation.2 | async-start | bytes 1048576 | tf_op jit(solution)/shard_map/all_to_all | solution.py:320
  75.5 0.8 collective-permute-done.23.refs_23_
  77.5 1.0 collective-permute-done.28.refs_28_
  79.3 11.5 %shard_map.47 = bf16[2048,128]{1,0:T(8,128)(2,1)} custom-call(bf16[256,1024]{1,0:T(8,128)(2,1)} %bitcast.16, bf16[2,1,2,32,1024]{4,3,2,1,0:T(8,128)(2,1)} %copy-done.6, bf16[2,1,2,32,1024]{4,3,2,1,0:T(8,128)(2,1)} %copy-done.10, bf16[2,1,2,32,1024]{4,3,2,1,0:T(8,128)(2,1)} %copy-done.9, bf16[1,1,2,32,1024]{4,3,2,1,0:T(8,128)(2,1)} %collective-permute-done.3.refs_3_, ...), custom_call_target="tpu_custom_call" | custom-call | flops 4294967296 | bytes 8912896 | tf_op jit(solution)/shard_map/pallas_call | solution.py:189
  90.9 0.8 copy-done.5
  91.7 5.0 %all-to-all-start.1 = ((bf16[16,128,128]{2,1,0:T(8,128)(2,1)}), bf16[16,128,128]{2,1,0:T(8,128)(2,1)S(1)}, u32[]{:S(2)}, u32[]{:S(2)}) async-start(bf16[16,128,128]{2,1,0:T(8,128)(2,1)} %bitcast.18), calls=%async_computation.1 | async-start | bytes 1048576 | tf_op jit(solution)/shard_map/all_to_all | solution.py:320
  96.6 10.8 %shard_map.48.right_ref = bf16[256,1024]{1,0:T(8,128)(2,1)} custom-call(bf16[256,1024]{1,0:T(8,128)(2,1)} %bitcast.17, bf16[2,1,2,32,1024]{4,3,2,1,0:T(8,128)(2,1)} %copy-done.6, bf16[2,1,2,32,1024]{4,3,2,1,0:T(8,128)(2,1)} %copy-done.10, bf16[2,1,2,32,1024]{4,3,2,1,0:T(8,128)(2,1)} %copy-done.9, ...), custom_call_target="tpu_custom_call" | custom-call | flops 4294967296 | bytes 8912896 | tf_op jit(solution)/shard_map/pallas_call | solution.py:189
  107.5 1.0 copy-done
  109.1 16.4 %all_to_all.20 = bf16[32,16,256]{2,1,0:T(8,128)(2,1)S(1)} all-to-all(bf16[32,16,256]{2,1,0:T(8,128)(2,1)S(1)} %bitcast.15), channel_id=1, replica_groups=mesh['cuts'=1,'mode'=32] {'mode'}, dimensions={0} | all-to-all | bytes 524288 | tf_op jit(solution)/shard_map/all_to_all | solution.py:320
  (110 shorter events, 12.7 us)
Async XLA Ops:
  1.1 9.3 %collective-permute-start.4 = (bf16[2,1,2,32,1024]{4,3,2,1,0:T(8,128)(2,1)S(1)}, bf16[2,1,2,32,1024]{4,3,2,1,0:T(8,128)(2,1)S(1)}, u32[]{:S(2)}, u32[]{:S(2)}) collective-permute-start(bf16[2,1,2,32,1024]{4,3,2,1,0:T(8,128)(2,1)S(1)} %maximum_bitcast_fusion.refs_0_), channel_id=1, source_target_pairs={{0,4},{1,5},{2,6},{3,7},{4,0},{5,1},{6,2},{7,3},{8,12},{9,13},{10,... | collective-permute-start | bytes 786440 | tf_op jit(solution)/shard_map/ppermute | solution.py:273
  4.1 8.1 %collective-permute-start.2 = (bf16[2,1,2,32,1024]{4,3,2,1,0:T(8,128)(2,1)S(1)}, bf16[2,1,2,32,1024]{4,3,2,1,0:T(8,128)(2,1)S(1)}, u32[]{:S(2)}, u32[]{:S(2)}) collective-permute-start(bf16[2,1,2,32,1024]{4,3,2,1,0:T(8,128)(2,1)S(1)} %maximum_bitcast_fusion.refs_0_), channel_id=1, source_target_pairs={{0,2},{1,3},{2,0},{3,1},{4,6},{5,7},{6,4},{7,5},{8,10},{9,11},{10,... | collective-permute-start | bytes 786440 | tf_op jit(solution)/shard_map/ppermute | solution.py:273
  5.6 14.1 %collective-permute-start.1 = (bf16[2,1,2,32,1024]{4,3,2,1,0:T(8,128)(2,1)S(1)}, bf16[2,1,2,32,1024]{4,3,2,1,0:T(8,128)(2,1)S(1)}, u32[]{:S(2)}, u32[]{:S(2)}) collective-permute-start(bf16[2,1,2,32,1024]{4,3,2,1,0:T(8,128)(2,1)S(1)} %maximum_bitcast_fusion.refs_0_), channel_id=1, source_target_pairs={{0,16},{1,17},{2,18},{3,19},{4,20},{5,21},{6,22},{7,23},{8,24},{9,... | collective-permute-start | bytes 786440 | tf_op jit(solution)/shard_map/ppermute | solution.py:273
  8.2 11.7 %collective-permute-start = (bf16[2,1,2,32,1024]{4,3,2,1,0:T(8,128)(2,1)S(1)}, bf16[2,1,2,32,1024]{4,3,2,1,0:T(8,128)(2,1)S(1)}, u32[]{:S(2)}, u32[]{:S(2)}) collective-permute-start(bf16[2,1,2,32,1024]{4,3,2,1,0:T(8,128)(2,1)S(1)} %maximum_bitcast_fusion.refs_0_), channel_id=1, source_target_pairs={{0,8},{1,9},{2,10},{3,11},{4,12},{5,13},{6,14},{7,15},{8,0},{9,1},... | collective-permute-start | bytes 786440 | tf_op jit(solution)/shard_map/ppermute | solution.py:273
  10.5 9.5 %collective-permute-start.5 = (bf16[1,1,2,32,1024]{4,3,2,1,0:T(8,128)(2,1)S(1)}, bf16[1,1,2,32,1024]{4,3,2,1,0:T(8,128)(2,1)S(1)}, u32[]{:S(2)}, u32[]{:S(2)}) collective-permute-start(bf16[1,1,2,32,1024]{4,3,2,1,0:T(8,128)(2,1)S(1)} %slice.25), channel_id=1, source_target_pairs={{0,2},{1,3},{2,0},{3,1},{4,6},{5,7},{6,4},{7,5},{8,10},{9,11},{10,... | collective-permute-start | bytes 393224 | tf_op jit(solution)/shard_map/ppermute | solution.py:273
  12.3 7.7 %collective-permute-start.3 = (bf16[1,1,2,32,1024]{4,3,2,1,0:T(8,128)(2,1)S(1)}, bf16[1,1,2,32,1024]{4,3,2,1,0:T(8,128)(2,1)}, u32[]{:S(2)}, u32[]{:S(2)}) collective-permute-start(bf16[1,1,2,32,1024]{4,3,2,1,0:T(8,128)(2,1)S(1)} %slice.24), channel_id=1, source_target_pairs={{0,4},{1,5},{2,6},{3,7},{4,0},{5,1},{6,2},{7,3},{8,12},{9,13},{10,... | collective-permute-start | bytes 393224 | tf_op jit(solution)/shard_map/ppermute | solution.py:273
  20.0 12.6 %collective-permute-start.8 = (bf16[2,2,2,32,1024]{4,3,2,1,0:T(8,128)(2,1)S(1)}, bf16[2,2,2,32,1024]{4,3,2,1,0:T(8,128)(2,1)S(1)}, u32[]{:S(2)}, u32[]{:S(2)}) collective-permute-start(bf16[2,2,2,32,1024]{4,3,2,1,0:T(8,128)(2,1)S(1)} %pad_maximum_fusion.refs_5_), channel_id=1, source_target_pairs={{0,4},{1,5},{2,6},{3,7},{4,0},{5,1},{6,2},{7,3},{8,12},{9,13},{10,... | collective-permute-start | bytes 1572872 | tf_op jit(solution)/shard_map/ppermute | solution.py:273
  20.6 12.2 %collective-permute-start.6 = (bf16[2,2,2,32,1024]{4,3,2,1,0:T(8,128)(2,1)S(1)}, bf16[2,2,2,32,1024]{4,3,2,1,0:T(8,128)(2,1)S(1)}, u32[]{:S(2)}, u32[]{:S(2)}) collective-permute-start(bf16[2,2,2,32,1024]{4,3,2,1,0:T(8,128)(2,1)S(1)} %pad_maximum_fusion.refs_5_), channel_id=1, source_target_pairs={{0,2},{1,3},{2,0},{3,1},{4,6},{5,7},{6,4},{7,5},{8,10},{9,11},{10,... | collective-permute-start | bytes 1572872 | tf_op jit(solution)/shard_map/ppermute | solution.py:273
  21.1 9.3 %collective-permute-start.10 = (bf16[2,1,2,32,1024]{4,3,2,1,0:T(8,128)(2,1)S(1)}, bf16[2,1,2,32,1024]{4,3,2,1,0:T(8,128)(2,1)S(1)}, u32[]{:S(2)}, u32[]{:S(2)}) collective-permute-start(bf16[2,1,2,32,1024]{4,3,2,1,0:T(8,128)(2,1)S(1)} %maximum_bitcast_fusion.refs_0_), channel_id=1, source_target_pairs={{0,24},{1,25},{2,26},{3,27},{4,28},{5,29},{6,30},{7,31},{8,16},{9,... | collective-permute-start | bytes 786440 | tf_op jit(solution)/shard_map/ppermute | solution.py:273
  32.8 9.3 %collective-permute-start.13 = (bf16[2,1,2,32,1024]{4,3,2,1,0:T(8,128)(2,1)S(1)}, bf16[2,1,2,32,1024]{4,3,2,1,0:T(8,128)(2,1)S(1)}, u32[]{:S(2)}, u32[]{:S(2)}) collective-permute-start(bf16[2,1,2,32,1024]{4,3,2,1,0:T(8,128)(2,1)S(1)} %collective-permute-done.10.refs_10_), channel_id=1, source_target_pairs={{0,4},{1,5},{2,6},{3,7},{4,0},{5,1},{6,2},{7,3},{8,12},{9,13},{10,... | collective-permute-start | bytes 786440 | tf_op jit(solution)/shard_map/ppermute | solution.py:273
  34.3 9.2 %collective-permute-start.11 = (bf16[2,1,2,32,1024]{4,3,2,1,0:T(8,128)(2,1)S(1)}, bf16[2,1,2,32,1024]{4,3,2,1,0:T(8,128)(2,1)S(1)}, u32[]{:S(2)}, u32[]{:S(2)}) collective-permute-start(bf16[2,1,2,32,1024]{4,3,2,1,0:T(8,128)(2,1)S(1)} %collective-permute-done.10.refs_10_), channel_id=1, source_target_pairs={{0,2},{1,3},{2,0},{3,1},{4,6},{5,7},{6,4},{7,5},{8,10},{9,11},{10,... | collective-permute-start | bytes 786440 | tf_op jit(solution)/shard_map/ppermute | solution.py:273
  34.9 12.0 %collective-permute-start.9 = (bf16[1,2,2,32,1024]{4,3,2,1,0:T(8,128)(2,1)S(1)}, bf16[1,2,2,32,1024]{4,3,2,1,0:T(8,128)(2,1)}, u32[]{:S(2)}, u32[]{:S(2)}) collective-permute-start(bf16[1,2,2,32,1024]{4,3,2,1,0:T(8,128)(2,1)S(1)} %slice.27), channel_id=1, source_target_pairs={{0,2},{1,3},{2,0},{3,1},{4,6},{5,7},{6,4},{7,5},{8,10},{9,11},{10,... | collective-permute-start | bytes 786440 | tf_op jit(solution)/shard_map/ppermute | solution.py:273
  36.5 10.4 %collective-permute-start.7 = (bf16[1,2,2,32,1024]{4,3,2,1,0:T(8,128)(2,1)S(1)}, bf16[1,2,2,32,1024]{4,3,2,1,0:T(8,128)(2,1)S(1)}, u32[]{:S(2)}, u32[]{:S(2)}) collective-permute-start(bf16[1,2,2,32,1024]{4,3,2,1,0:T(8,128)(2,1)S(1)} %slice.26), channel_id=1, source_target_pairs={{0,4},{1,5},{2,6},{3,7},{4,0},{5,1},{6,2},{7,3},{8,12},{9,13},{10,... | collective-permute-start | bytes 786440 | tf_op jit(solution)/shard_map/ppermute | solution.py:273
  42.1 6.1 %collective-permute-start.14 = (bf16[1,1,2,32,1024]{4,3,2,1,0:T(8,128)(2,1)S(1)}, bf16[1,1,2,32,1024]{4,3,2,1,0:T(8,128)(2,1)S(1)}, u32[]{:S(2)}, u32[]{:S(2)}) collective-permute-start(bf16[1,1,2,32,1024]{4,3,2,1,0:T(8,128)(2,1)S(1)} %slice.29), channel_id=1, source_target_pairs={{0,2},{1,3},{2,0},{3,1},{4,6},{5,7},{6,4},{7,5},{8,10},{9,11},{10,... | collective-permute-start | bytes 393224 | tf_op jit(solution)/shard_map/ppermute | solution.py:273
  43.6 5.2 %collective-permute-start.12 = (bf16[1,1,2,32,1024]{4,3,2,1,0:T(8,128)(2,1)S(1)}, bf16[1,1,2,32,1024]{4,3,2,1,0:T(8,128)(2,1)}, u32[]{:S(2)}, u32[]{:S(2)}) collective-permute-start(bf16[1,1,2,32,1024]{4,3,2,1,0:T(8,128)(2,1)S(1)} %slice.28), channel_id=1, source_target_pairs={{0,4},{1,5},{2,6},{3,7},{4,0},{5,1},{6,2},{7,3},{8,12},{9,13},{10,... | collective-permute-start | bytes 393224 | tf_op jit(solution)/shard_map/ppermute | solution.py:273
  48.9 21.9 %all-to-all-start = ((bf16[32,8,1024]{2,1,0:T(8,128)(2,1)}), bf16[32,8,1024]{2,1,0:T(8,128)(2,1)S(1)}, u32[]{:S(2)}, u32[]{:S(2)}) async-start(bf16[32,8,1024]{2,1,0:T(8,128)(2,1)} %bitcast.1), calls=%async_computation | async-start | bytes 1048576 | tf_op jit(solution)/shard_map/all_to_all | solution.py:320
  55.2 1.6 %collective-permute-start.15 = (bf16[2,1,2,32,1024]{4,3,2,1,0:T(8,128)(2,1)S(1)}, bf16[2,1,2,32,1024]{4,3,2,1,0:T(8,128)(2,1)S(1)}, u32[]{:S(2)}, u32[]{:S(2)}) collective-permute-start(bf16[2,1,2,32,1024]{4,3,2,1,0:T(8,128)(2,1)S(1)} %maximum_bitcast_fusion.refs_0_), channel_id=1, source_target_pairs={{0,1},{1,0},{2,3},{3,2},{4,5},{5,4},{6,7},{7,6},{8,9},{9,8},{10,11... | collective-permute-start | bytes 786440 | tf_op jit(solution)/shard_map/ppermute | solution.py:273
  55.6 3.4 %collective-permute-start.17 = (bf16[2,1,2,32,1024]{4,3,2,1,0:T(8,128)(2,1)S(1)}, bf16[2,1,2,32,1024]{4,3,2,1,0:T(8,128)(2,1)S(1)}, u32[]{:S(2)}, u32[]{:S(2)}) collective-permute-start(bf16[2,1,2,32,1024]{4,3,2,1,0:T(8,128)(2,1)S(1)} %collective-permute-done.4.refs_2_), channel_id=1, source_target_pairs={{0,1},{1,0},{2,3},{3,2},{4,5},{5,4},{6,7},{7,6},{8,9},{9,8},{10,11... | collective-permute-start | bytes 786440 | tf_op jit(solution)/shard_map/ppermute | solution.py:273
  55.8 18.8 %collective-permute-start.20 = (bf16[2,2,2,32,1024]{4,3,2,1,0:T(8,128)(2,1)S(1)}, bf16[2,2,2,32,1024]{4,3,2,1,0:T(8,128)(2,1)}, u32[]{:S(2)}, u32[]{:S(2)}) collective-permute-start(bf16[2,2,2,32,1024]{4,3,2,1,0:T(8,128)(2,1)S(1)} %pad_maximum_fusion.refs_5_), channel_id=1, source_target_pairs={{0,1},{1,0},{2,3},{3,2},{4,5},{5,4},{6,7},{7,6},{8,9},{9,8},{10,11... | collective-permute-start | bytes 1572872 | tf_op jit(solution)/shard_map/ppermute | solution.py:273
  56.1 3.6 %collective-permute-start.16 = (bf16[2,1,2,32,1024]{4,3,2,1,0:T(8,128)(2,1)S(1)}, bf16[2,1,2,32,1024]{4,3,2,1,0:T(8,128)(2,1)S(1)}, u32[]{:S(2)}, u32[]{:S(2)}) collective-permute-start(bf16[2,1,2,32,1024]{4,3,2,1,0:T(8,128)(2,1)S(1)} %collective-permute-done.2.refs_1_), channel_id=1, source_target_pairs={{0,1},{1,0},{2,3},{3,2},{4,5},{5,4},{6,7},{7,6},{8,9},{9,8},{10,11... | collective-permute-start | bytes 786440 | tf_op jit(solution)/shard_map/ppermute | solution.py:273
  56.3 2.4 %collective-permute-start.19 = (bf16[1,1,2,32,1024]{4,3,2,1,0:T(8,128)(2,1)S(1)}, bf16[1,1,2,32,1024]{4,3,2,1,0:T(8,128)(2,1)S(1)}, u32[]{:S(2)}, u32[]{:S(2)}) collective-permute-start(bf16[1,1,2,32,1024]{4,3,2,1,0:T(8,128)(2,1)S(1)} %collective-permute-done.5.refs_4_), channel_id=1, source_target_pairs={{0,1},{1,0},{2,3},{3,2},{4,5},{5,4},{6,7},{7,6},{8,9},{9,8},{10,11... | collective-permute-start | bytes 393224 | tf_op jit(solution)/shard_map/ppermute | solution.py:273
  56.8 2.5 %collective-permute-start.18 = (bf16[1,1,2,32,1024]{4,3,2,1,0:T(8,128)(2,1)}, bf16[1,1,2,32,1024]{4,3,2,1,0:T(8,128)(2,1)S(1)}, u32[]{:S(2)}, u32[]{:S(2)}) collective-permute-start(bf16[1,1,2,32,1024]{4,3,2,1,0:T(8,128)(2,1)} %collective-permute-done.3.refs_3_), channel_id=1, source_target_pairs={{0,1},{1,0},{2,3},{3,2},{4,5},{5,4},{6,7},{7,6},{8,9},{9,8},{10,11... | collective-permute-start | bytes 393224 | tf_op jit(solution)/shard_map/ppermute | solution.py:273
  58.7 16.3 %collective-permute-start.25 = (bf16[2,1,2,32,1024]{4,3,2,1,0:T(8,128)(2,1)}, bf16[2,1,2,32,1024]{4,3,2,1,0:T(8,128)(2,1)}, u32[]{:S(2)}, u32[]{:S(2)}) collective-permute-start(bf16[2,1,2,32,1024]{4,3,2,1,0:T(8,128)(2,1)} %copy-done.14), channel_id=1, source_target_pairs={{0,1},{1,0},{2,3},{3,2},{4,5},{5,4},{6,7},{7,6},{8,9},{9,8},{10,11... | collective-permute-start | bytes 786440 | tf_op jit(solution)/shard_map/ppermute | solution.py:273
  59.0 16.5 %collective-permute-start.22 = (bf16[2,2,2,32,1024]{4,3,2,1,0:T(8,128)(2,1)S(1)}, bf16[2,2,2,32,1024]{4,3,2,1,0:T(8,128)(2,1)}, u32[]{:S(2)}, u32[]{:S(2)}) collective-permute-start(bf16[2,2,2,32,1024]{4,3,2,1,0:T(8,128)(2,1)S(1)} %collective-permute-done.8.refs_7_), channel_id=1, source_target_pairs={{0,1},{1,0},{2,3},{3,2},{4,5},{5,4},{6,7},{7,6},{8,9},{9,8},{10,11... | collective-permute-start | bytes 1572872 | tf_op jit(solution)/shard_map/ppermute | solution.py:273
  59.3 17.0 %collective-permute-start.21 = (bf16[2,2,2,32,1024]{4,3,2,1,0:T(8,128)(2,1)S(1)}, bf16[2,2,2,32,1024]{4,3,2,1,0:T(8,128)(2,1)}, u32[]{:S(2)}, u32[]{:S(2)}) collective-permute-start(bf16[2,2,2,32,1024]{4,3,2,1,0:T(8,128)(2,1)S(1)} %collective-permute-done.6.refs_6_), channel_id=1, source_target_pairs={{0,1},{1,0},{2,3},{3,2},{4,5},{5,4},{6,7},{7,6},{8,9},{9,8},{10,11... | collective-permute-start | bytes 1572872 | tf_op jit(solution)/shard_map/ppermute | solution.py:273
  60.7 14.6 %collective-permute-start.24 = (bf16[1,2,2,32,1024]{4,3,2,1,0:T(8,128)(2,1)}, bf16[1,2,2,32,1024]{4,3,2,1,0:T(8,128)(2,1)}, u32[]{:S(2)}, u32[]{:S(2)}) collective-permute-start(bf16[1,2,2,32,1024]{4,3,2,1,0:T(8,128)(2,1)} %collective-permute-done.9.refs_9_), channel_id=1, source_target_pairs={{0,1},{1,0},{2,3},{3,2},{4,5},{5,4},{6,7},{7,6},{8,9},{9,8},{10,11... | collective-permute-start | bytes 786440 | tf_op jit(solution)/shard_map/ppermute | solution.py:273
  71.6 19.3 %all-to-all-start.2 = ((bf16[32,8,1024]{2,1,0:T(8,128)(2,1)}), bf16[32,8,1024]{2,1,0:T(8,128)(2,1)S(1)}, u32[]{:S(2)}, u32[]{:S(2)}) async-start(bf16[32,8,1024]{2,1,0:T(8,128)(2,1)} %bitcast), calls=%async_computation.2 | async-start | bytes 1048576 | tf_op jit(solution)/shard_map/all_to_all | solution.py:320
  74.7 1.6 %collective-permute-start.23 = (bf16[1,2,2,32,1024]{4,3,2,1,0:T(8,128)(2,1)S(1)}, bf16[1,2,2,32,1024]{4,3,2,1,0:T(8,128)(2,1)S(1)}, u32[]{:S(2)}, u32[]{:S(2)}) collective-permute-start(bf16[1,2,2,32,1024]{4,3,2,1,0:T(8,128)(2,1)S(1)} %copy-done.16), channel_id=1, source_target_pairs={{0,1},{1,0},{2,3},{3,2},{4,5},{5,4},{6,7},{7,6},{8,9},{9,8},{10,11... | collective-permute-start | bytes 786440 | tf_op jit(solution)/shard_map/ppermute | solution.py:273
  75.0 1.7 %collective-permute-start.27 = (bf16[2,1,2,32,1024]{4,3,2,1,0:T(8,128)(2,1)S(1)}, bf16[2,1,2,32,1024]{4,3,2,1,0:T(8,128)(2,1)S(1)}, u32[]{:S(2)}, u32[]{:S(2)}) collective-permute-start(bf16[2,1,2,32,1024]{4,3,2,1,0:T(8,128)(2,1)S(1)} %collective-permute-done.13.refs_12_), channel_id=1, source_target_pairs={{0,1},{1,0},{2,3},{3,2},{4,5},{5,4},{6,7},{7,6},{8,9},{9,8},{10,11... | collective-permute-start | bytes 786440 | tf_op jit(solution)/shard_map/ppermute | solution.py:273
  75.3 1.8 %collective-permute-start.26 = (bf16[2,1,2,32,1024]{4,3,2,1,0:T(8,128)(2,1)S(1)}, bf16[2,1,2,32,1024]{4,3,2,1,0:T(8,128)(2,1)S(1)}, u32[]{:S(2)}, u32[]{:S(2)}) collective-permute-start(bf16[2,1,2,32,1024]{4,3,2,1,0:T(8,128)(2,1)S(1)} %copy-done.13), channel_id=1, source_target_pairs={{0,1},{1,0},{2,3},{3,2},{4,5},{5,4},{6,7},{7,6},{8,9},{9,8},{10,11... | collective-permute-start | bytes 786440 | tf_op jit(solution)/shard_map/ppermute | solution.py:273
  77.0 1.6 %collective-permute-start.28 = (bf16[1,1,2,32,1024]{4,3,2,1,0:T(8,128)(2,1)}, bf16[1,1,2,32,1024]{4,3,2,1,0:T(8,128)(2,1)S(1)}, u32[]{:S(2)}, u32[]{:S(2)}) collective-permute-start(bf16[1,1,2,32,1024]{4,3,2,1,0:T(8,128)(2,1)} %collective-permute-done.12.refs_13_), channel_id=1, source_target_pairs={{0,1},{1,0},{2,3},{3,2},{4,5},{5,4},{6,7},{7,6},{8,9},{9,8},{10,11... | collective-permute-start | bytes 393224 | tf_op jit(solution)/shard_map/ppermute | solution.py:273
  91.7 15.8 %all-to-all-start.1 = ((bf16[16,128,128]{2,1,0:T(8,128)(2,1)}), bf16[16,128,128]{2,1,0:T(8,128)(2,1)S(1)}, u32[]{:S(2)}, u32[]{:S(2)}) async-start(bf16[16,128,128]{2,1,0:T(8,128)(2,1)} %bitcast.18), calls=%async_computation.1 | async-start | bytes 1048576 | tf_op jit(solution)/shard_map/all_to_all | solution.py:320
  (31 other events, 435.7 us)
